TPU v7x, 512 devices: a whole 4x4x16 slice. The times are simulated.
512 devices in a mesh: dp: 64 (over y, z), tensor: 8 (over x, core).
Axes of the slice: x: 4, y: 4, z: 16, core: 2. Of those that a mesh axis runs over, the one named last changes fastest.
Arguments:
- acts: bfloat16 [8192, 1024], P('dp', 'tensor'), may hold values from -6 to 6
- grad_out: bfloat16 [8192, 1024], P('dp', 'tensor'), may hold values from -6 to 6
- master: float32 [3, 1536, 1024], P(None, 'dp', 'tensor'), may hold values from -0.1875 to 0.1875
- moment_one: float32 [3, 1536, 1024], P(None, 'dp', 'tensor'), may hold values from -3 to 3
- moment_two: float32 [3, 1536, 1024], P(None, 'dp', 'tensor'), may hold values from 0.25 to 4
- bit_widths: int32 [3, 24], replicated, may hold values from 2 to 8
- row_dither: int32 [3, 1536], replicated, may hold values from 0 to 1023
- col_dither: int32 [1024], P('tensor'), may hold values from 0 to 1023
Outputs:
- grad_in: bfloat16 [8192, 1024], P('dp', 'tensor')
- new_master: float32 [3, 1536, 1024], P(None, 'dp', 'tensor')
- new_moment_one: float32 [3, 1536, 1024], P(None, 'dp', 'tensor')
- new_moment_two: float32 [3, 1536, 1024], P(None, 'dp', 'tensor')
- new_weights: bfloat16 [3, 1536, 1024], P(None, None, 'tensor')
All inputs are finite; a program needn't handle non-finite values.
Results may differ from a plain program's by a relative error of at most 0.002.
The roundings to bfloat16 on the way count: a program that leaves them out, or rounds other values in their place, can miss the bound.
Values may be sent and summed in bfloat16 or wider, within the bound.
No kernel may reach another device: no remote copies, remote signals or barrier semaphores. Data moves between devices by JAX's collectives and lax.ppermute only.
A program may use at most 64 MiB of HBM per device.

v0:
```python
import math

import jax
import jax.numpy as jnp
from jax import lax
from jax.sharding import PartitionSpec as P

BROWS = 64
QB = 128


BETA_ONE = 0.9
BETA_TWO = 0.95
LEARN_RATE = 0.004
WEIGHT_DECAY = 0.1
ADAM_EPS = 1e-08
RANGE_EPS = 1e-06


def soft_round(value):
    return value - jnp.sin(2.0 * math.pi * value) / (2.0 * math.pi)


def eightbit(weights):
    count, rows, cols = weights.shape
    blocks = weights.reshape(count, rows, cols // QB, QB)
    scale = (jnp.max(jnp.abs(blocks), axis=3, keepdims=True) + RANGE_EPS) / 127.0
    return (soft_round(blocks / scale) * scale).reshape(count, rows, cols).astype(jnp.bfloat16)


def hidden_terms(gate, upper, delta):
    sig = jax.nn.sigmoid(gate)
    active = gate * sig
    dgate = delta * upper * sig * (1.0 + gate * (1.0 - sig))
    dupper = delta * active
    hidden = active * upper
    return jnp.stack([dgate, dupper, hidden]).astype(jnp.bfloat16)


def bucket_max(grads):
    return jnp.max(jnp.abs(grads).reshape(grads.shape[0], grads.shape[1] // BROWS, -1), axis=2)


def rows_times(left, right):
    return lax.dot_general(
        left, right, (((1,), (1,)), ((), ())), preferred_element_type=jnp.float32
    )


def front_grads(terms, acts):
    hidden = terms.shape[1]
    joined = jnp.dot(terms[:2].reshape(2 * hidden, -1), acts, preferred_element_type=jnp.float32)
    return joined.reshape(2, hidden, -1)


def all_grads(terms, acts, grad_out):
    grad_front = front_grads(terms, acts)
    grad_down = jnp.dot(terms[2], grad_out, preferred_element_type=jnp.float32)[None]
    return jnp.concatenate([grad_front, grad_down])


def on_device(acts, grad_out, master, moment_one, moment_two, bit_widths, row_dither, col_dither):
    weights = lax.all_gather(eightbit(master), "dp", axis=1, tiled=True)
    hidden = weights.shape[1]
    width = weights.shape[2]
    front = rows_times(weights[:2].reshape(2 * hidden, width), acts)
    back = rows_times(weights[2], grad_out)
    partial_value = jnp.concatenate([front, back]).reshape(3, hidden, -1)
    summed = lax.psum(partial_value, "tensor")
    terms = hidden_terms(summed[0], summed[1], summed[2])
    tokens = terms.shape[2]
    grads = all_grads(terms, acts, grad_out)
    ranges = lax.pmax(bucket_max(grads), ("dp", "tensor"))
    grad_rows = lax.dot_general(
        terms[:2].reshape(2 * hidden, tokens),
        weights[:2].reshape(2 * hidden, width),
        (((0,), (0,)), ((), ())),
        preferred_element_type=jnp.float32,
    )
    grad_in = grad_rows.astype(jnp.bfloat16)
    levels = jnp.exp2((bit_widths - 1).astype(jnp.float32)) - 1.0
    scale = (ranges + RANGE_EPS) / levels
    scale_rows = jnp.repeat(scale, BROWS, axis=1)[:, :, None]
    replica = lax.axis_index("dp")
    offsets = row_dither[:, :, None] + col_dither[None, None, :] + 389 * replica
    phase = jnp.mod(offsets, 1024).astype(jnp.float32) / 1024.0 - 0.5
    quant = soft_round(grads / scale_rows + phase) - phase
    total = lax.psum_scatter(quant, "dp", scatter_dimension=1, tiled=True)
    shard_rows = total.shape[1]
    local_scale = lax.dynamic_slice_in_dim(scale_rows, replica * shard_rows, shard_rows, 1)
    mean_grad = total * local_scale / lax.axis_size("dp")
    first = BETA_ONE * moment_one + (1.0 - BETA_ONE) * mean_grad
    second = BETA_TWO * moment_two + (1.0 - BETA_TWO) * mean_grad * mean_grad
    updated = master - LEARN_RATE * (first / (jnp.sqrt(second) + ADAM_EPS) + WEIGHT_DECAY * master)
    new_weights = lax.all_gather(eightbit(updated), "dp", axis=1, tiled=True)
    return (grad_in, updated, first, second, new_weights)


def solution(mesh):
    return jax.shard_map(
        on_device,
        mesh=mesh,
        in_specs=(
            P("dp", "tensor"),
            P("dp", "tensor"),
            P(None, "dp", "tensor"),
            P(None, "dp", "tensor"),
            P(None, "dp", "tensor"),
            P(),
            P(),
            P("tensor"),
        ),
        out_specs=(
            P("dp", "tensor"),
            P(None, "dp", "tensor"),
            P(None, "dp", "tensor"),
            P(None, "dp", "tensor"),
            P(None, None, "tensor"),
        ),
        check_vma=False,
    )
```

profile of v0, /device:TPU:6, one launch (start us, length us, event | category | flops | bytes accessed | tf_op | source)
XLA Modules:
  0.0 1099.5 jit_solution(3498556543953979299)
XLA Ops:
  7.2 0.9 abs_reduce_fusion.1
  8.1 1.6 multiply_convert_fusion.4
  9.8 138.7 %all-gather.3.cloned.1.call-done = bf16[3,1536,128]{2,1,0:T(8,128)(2,1)} async-done(((bf16[3,24,128]{2,1,0:T(8,128)(2,1)}), bf16[3,1536,128]{2,1,0:T(8,128)(2,1)}) %all-gather.3.cloned.1.call-update) | async-done | bytes 1179664 | tf_op jit(solution)/shard_map/all_gather | solution.py:63
  148.4 1.2 slice.28
  149.6 0.4 fusion.19
  150.0 1.2 fusion.12
  151.3 0.2 pad_maximum_fusion
  151.4 2.0 copy.15
  153.5 75.5 %all-reduce.2.cloned.1.call-done = f32[3,1536,128]{1,2,0:T(8,128)} async-done(((f32[3,1536,128]{1,2,0:T(8,128)}), f32[3,1536,128]{1,2,0:T(8,128)}) %all-reduce.2.cloned.1.call-update) | async-done | bytes 2359312 | tf_op jit(solution)/shard_map/psum | solution.py:69
  229.0 1.9 fusion.10
  231.0 1.1 concatenate.17
  232.1 0.4 multiply_convert_fusion.2
  232.6 0.7 copy-done.3
  233.4 0.4 fusion.8
  233.9 0.3 concatenate.16
  234.2 1.3 fusion.5
  235.5 105.7 %pmax.7 = f32[3,24]{1,0:T(4,128)S(1)} all-reduce(f32[3,24]{1,0:T(4,128)S(1)} %fusion.5), channel_id=1, replica_groups=mesh['dp'=64,'tensor'=8] {'dp','tensor'}, use_global_device_ids=true, to_apply=%region_3.0 | all-reduce | flops 72 | bytes 576 | tf_op jit(solution)/shard_map/pmax | solution.py:73
  341.4 12.3 %subtract_subtract_fusion = f32[3,1536,128]{2,1,0:T(8,128)} fusion(f32[1,1536,128]{2,1,0:T(8,128)} %bitcast.24, f32[2,1536,128]{2,1,0:T(8,128)S(1)} %fusion.8, s32[]{:T(128)S(6)} %mul_shard_map.3, s32[128]{0:T(128)S(1)} %copy-done.15, s32[3,1536]{1,0:T(4,128)S(1)} %copy-done.13, f32[3,1536]{1,0:T(4,128)S(1)} %div.73), kind=kLoop, calls=%fused_computation.12 | loop fusion | flops 13565952 | bytes 4755972 | tf_op jit(solution)/shard_map/sub | solution.py:87
  354.1 603.4 %reduce-scatter.2.cloned.1.call-done = f32[3,24,128]{2,1,0:T(8,128)} async-done(((f32[3,1536,128]{2,1,0:T(8,128)}), f32[3,24,128]{2,1,0:T(8,128)}) %reduce-scatter.2.cloned.1.call-update) | async-done | bytes 36880 | tf_op jit(solution)/shard_map/reduce_scatter | solution.py:88
  957.5 1.5 abs_reduce_fusion
  959.0 0.8 multiply_convert_fusion.3
  959.9 1.0 fusion.6
  960.8 129.8 %all-gather.5.cloned.1.call-done = bf16[3,1536,128]{2,1,0:T(8,128)(2,1)} async-done(((bf16[3,24,128]{2,1,0:T(8,128)(2,1)}), bf16[3,1536,128]{2,1,0:T(8,128)(2,1)}) %all-gather.5.cloned.1.call-update) | async-done | bytes 1179664 | tf_op jit(solution)/shard_map/all_gather | solution.py:95
  1090.6 2.4 copy.20
  (46 shorter events, 0.8 us)
Async XLA Ops:
  7.2 142.5 %copy-start = (bf16[128,128]{1,0:T(8,128)(2,1)S(1)}, bf16[128,128]{1,0:T(8,128)(2,1)}, u32[]{:S(2)}) copy-start(bf16[128,128]{1,0:T(8,128)(2,1)} %param.8) | copy-start | bytes 98308
  7.2 142.8 %copy-start.12 = (bf16[128,128]{1,0:T(8,128)(2,1)S(1)}, bf16[128,128]{1,0:T(8,128)(2,1)}, u32[]{:S(2)}) copy-start(bf16[128,128]{1,0:T(8,128)(2,1)} %param.9) | copy-start | bytes 98308
  7.2 141.2 %all-gather.3.cloned.1.call-start = ((), (), s32[]{:S(2)}) async-start(), calls=%async_computation.1 | async-start | bytes 1198080 | tf_op jit(solution)/shard_map/all_gather | solution.py:63
  9.7 219.3 %all-reduce.2.cloned.1.call-start = ((), (), s32[]{:S(2)}) async-start(), calls=%async_computation.2 | async-start | bytes 4718592 | tf_op jit(solution)/shard_map/psum | solution.py:69
  153.5 804.0 %reduce-scatter.2.cloned.1.call-start = ((), (), s32[]{:S(2)}) async-start(), calls=%async_computation.3 | async-start | bytes 2396160 | tf_op jit(solution)/shard_map/reduce_scatter | solution.py:88
  229.0 3.1 copy-start.2
  231.0 1.6 copy-start.1
  232.5 0.8 copy-start.3
  232.5 0.9 copy-start.5
  233.9 107.4 %copy-start.14 = (s32[3,24]{1,0:T(4,128)S(1)}, s32[3,24]{1,0:T(4,128)}, u32[]{:S(2)}) copy-start(s32[3,24]{1,0:T(4,128)} %param.13) | copy-start | bytes 868
  233.9 107.6 %copy-start.13 = (s32[3,1536]{1,0:T(4,128)S(1)}, s32[3,1536]{1,0:T(4,128)}, u32[]{:S(2)}) copy-start(s32[3,1536]{1,0:T(4,128)} %param.14) | copy-start | bytes 55300
  233.9 107.6 %copy-start.15 = (s32[128]{0:T(128)S(1)}, s32[128]{0:T(128)}, u32[]{:S(2)}) copy-start(s32[128]{0:T(128)} %param.15) | copy-start | bytes 1540
  353.8 603.7 %copy-start.8 = (f32[3,24,128]{2,1,0:T(8,128)S(1)}, f32[3,24,128]{2,1,0:T(8,128)}, u32[]{:S(2)}) copy-start(f32[3,24,128]{2,1,0:T(8,128)} %param.10) | copy-start | bytes 110596
  353.8 603.7 %copy-start.10 = (f32[3,24,128]{2,1,0:T(8,128)S(1)}, f32[3,24,128]{2,1,0:T(8,128)}, u32[]{:S(2)}) copy-start(f32[3,24,128]{2,1,0:T(8,128)} %param.12) | copy-start | bytes 110596
  353.8 603.7 %copy-start.11 = (f32[3,24,128]{2,1,0:T(8,128)S(1)}, f32[3,24,128]{2,1,0:T(8,128)}, u32[]{:S(2)}) copy-start(f32[3,24,128]{2,1,0:T(8,128)} %param.11) | copy-start | bytes 110596
  353.8 606.0 %copy-start.4 = (bf16[1,1536,128]{1,2,0:T(8,128)(2,1)S(1)}, bf16[1,1536,128]{1,2,0:T(8,128)(2,1)}, u32[]{:S(2)}) copy-start(bf16[1,1536,128]{1,2,0:T(8,128)(2,1)} %copy-done.3) | copy-start | bytes 1179652
  353.8 606.0 %copy-start.6 = (bf16[1,1536,128]{1,2,0:T(8,128)(2,1)S(1)}, bf16[1,1536,128]{1,2,0:T(8,128)(2,1)}, u32[]{:S(2)}) copy-start(bf16[1,1536,128]{1,2,0:T(8,128)(2,1)} %copy-done.5) | copy-start | bytes 1179652
  353.8 606.0 %copy-start.7 = (bf16[3,1536,128]{2,1,0:T(8,128)(2,1)S(1)}, bf16[3,1536,128]{2,1,0:T(8,128)(2,1)}, u32[]{:S(2)}) copy-start(bf16[3,1536,128]{2,1,0:T(8,128)(2,1)} %all-gather.3.cloned.1.call-done) | copy-start | bytes 3538948
  353.8 736.8 %all-gather.5.cloned.1.call-start = ((), (), s32[]{:S(2)}) async-start(), calls=%async_computation.4 | async-start | bytes 1198080 | tf_op jit(solution)/shard_map/all_gather | solution.py:95
  959.0 134.0 %copy-start.9 = (f32[3,24,128]{2,1,0:T(8,128)}, f32[3,24,128]{2,1,0:T(8,128)S(1)}, u32[]{:S(2)}) copy-start(f32[3,24,128]{2,1,0:T(8,128)S(1)} %get-tuple-element.17) | copy-start | bytes 110596
Sparse Core Ops, SparseCore 0:
  11.6 136.8 all-gather.2
  153.6 75.3 all-reduce.1
  354.0 603.4 reduce-scatter.1
  960.9 129.6 all-gather.4
where the time goes:
time: 1100 us
  waiting for transfers between devices  947 us (86%)
  blocking collectives  106 us (10%)
  other arithmetic  19 us (2%)
  between operations  14 us (1%)
    reduce_scatter x1, waiting for transfers between devices, on_device(): total = lax.psum_scatter(quant, 'dp', scatter_dimension=1, tiled=True)  603 us
    all_gather x1, waiting for transfers between devices, on_device(): weights = lax.all_gather(eightbit(master), 'dp', axis=1, tiled=True)  139 us
    all_gather x1, waiting for transfers between devices, on_device(): new_weights = lax.all_gather(eightbit(updated), 'dp', axis=1, tiled=True)  130 us
    pmax x1, blocking collectives, on_device(): ranges = lax.pmax(bucket_max(grads), ('dp', 'tensor'))  106 us
    psum x1, waiting for transfers between devices, on_device(): summed = lax.psum(partial_value, 'tensor')  75.5 us
  transfers between devices with their start and end apart: 4, of which 4 were waited for; matrix products, arithmetic and copies ran while one was open for 0% of the time, Pallas kernels for 0%

commit v1 on v0

v1 whole, which is shorter than its diff:
```python
import jax
import jax.numpy as jnp
from jax import lax
from jax.experimental import pallas as pl
from jax.experimental.pallas import tpu as pltpu
from jax.sharding import Mesh, PartitionSpec as P

F32 = jnp.float32
BF16 = jnp.bfloat16

TOK = 128
BROWS = 64
COLS = 128
SHARD = 24
BLOCK = 48
REPS = 4

BETA_ONE = 0.9
BETA_TWO = 0.95
LEARN_RATE = 0.004
WEIGHT_DECAY = 0.1
ADAM_EPS = 1e-08
RANGE_EPS = 1e-06
N_DP = 64

SINE = (
    0.9999995827674866,
    -6.579691410064697,
    12.986435890197754,
    -12.188101768493652,
    6.558042526245117,
    -1.95303213596344,
)

DP = ("y", "z")
TENSOR = ("xh", "xl", "c")
SIZES = (4, 16, 2, 2, 2)

VMEM_LIMIT = 40 * 1024 * 1024


def turn(value):
    frac = value - jnp.floor(value + 0.5)
    square = frac * frac
    total = jnp.full_like(square, SINE[-1])
    for coef in SINE[-2::-1]:
        total = total * square + coef
    return total * frac


def soft_round(value):
    return value - turn(value)


def eightbit_f32(weights):
    scale = (jnp.max(jnp.abs(weights), axis=-1, keepdims=True) + RANGE_EPS) / 127.0
    return soft_round(weights / scale) * scale


def dot(left, right, left_dim, right_dim):
    return lax.dot_general(
        left, right, (((left_dim,), (right_dim,)), ((), ())), preferred_element_type=F32
    )


def front_kernel(pos_ref, own_ref, other_ref, weights_ref, xs_ref, gs_ref, terms_ref, col_ref, peak_ref):
    core = pos_ref[0]
    for chip in range(4):
        for source, which in ((own_ref, core), (other_ref, 1 - core)):
            cols = pl.ds(pl.multiple_of((2 * chip + which) * COLS, COLS), COLS)
            for rep in range(REPS):
                rows = slice(rep * TOK, (rep + 1) * TOK)
                xs_ref[rows, cols] = source[rep * 4 + chip, 0:TOK, :]
                gs_ref[rows, cols] = source[rep * 4 + chip, TOK : 2 * TOK, :]
            pair = source[chip, 2 * TOK : 2 * TOK + 16, :].astype(F32)
            dither = pair[0:1] * 8.0 + pair[1:2]
            col_ref[:, cols] = jnp.broadcast_to(dither * (1.0 / 1024.0), (8, COLS))
    front = dot(weights_ref[0 : 2 * BLOCK, :], xs_ref[...], 1, 1)
    delta = dot(weights_ref[2 * BLOCK : 3 * BLOCK, :], gs_ref[...], 1, 1)
    gate = front[0:BLOCK]
    upper = front[BLOCK:]
    sig = jax.nn.sigmoid(gate)
    active = gate * sig
    dgate = (delta * upper * sig * (1.0 + gate * (1.0 - sig))).astype(BF16)
    dupper = (delta * active).astype(BF16)
    hidden = (active * upper).astype(BF16)
    peak = jnp.zeros((3 * BLOCK, COLS), F32)
    for rep in range(REPS):
        rows = slice(rep * TOK, (rep + 1) * TOK)
        terms_ref[rep, 0:BLOCK, :] = dgate[:, rows]
        terms_ref[rep, BLOCK : 2 * BLOCK, :] = dupper[:, rows]
        terms_ref[rep, 2 * BLOCK : 3 * BLOCK, :] = hidden[:, rows]
        for part in range(4):
            cols = slice(part * 256, (part + 1) * 256)
            grad_front = dot(terms_ref[rep, 0 : 2 * BLOCK, :], xs_ref[rows, cols], 1, 0)
            grad_down = dot(terms_ref[rep, 2 * BLOCK : 3 * BLOCK, :], gs_ref[rows, cols], 1, 0)
            grads = jnp.abs(jnp.concatenate([grad_front, grad_down], axis=0))
            peak = jnp.maximum(peak, jnp.maximum(grads[:, :COLS], grads[:, COLS:]))
    lane = lax.broadcasted_iota(jnp.int32, (1, COLS), 1)
    packed = jnp.zeros((1, COLS), F32)
    for group in range(9):
        top = jnp.max(peak[group * 16 : (group + 1) * 16], axis=0, keepdims=True)
        top = jnp.max(top, axis=1, keepdims=True)
        packed = jnp.where(lane == group, top, packed)
    peak_ref[...] = jnp.broadcast_to(packed.reshape(1, 1, COLS), peak_ref.shape)


def quant_kernel(pos_ref, xs_ref, gs_ref, terms_ref, peaks_ref, bits_ref, row_ref, col_ref, out_ref):
    spot = pos_ref[1]
    unit = pos_ref[2]
    depth = pos_ref[3]
    lane = lax.broadcasted_iota(jnp.int32, (1, COLS), 1)
    buck = lax.broadcasted_iota(jnp.int32, (1, 24), 1)
    tops = [jnp.max(peaks_ref[i * 16 : (i + 1) * 16], axis=0) for i in range(4)]
    scales = []
    for mat in range(3):
        per_bucket = []
        for bucket in range(3):
            held = jnp.zeros((1, COLS), F32)
            for sub in range(4 * bucket, 4 * bucket + 4):
                held = jnp.maximum(held, jnp.where(lane == mat * 3 + sub % 3, tops[sub // 3], 0.0))
            ranges = jnp.max(held, axis=1, keepdims=True)
            bits = jnp.where(buck == 3 * unit + bucket, bits_ref[mat : mat + 1, :].astype(F32), 0.0)
            bits = jnp.max(bits, axis=1, keepdims=True)
            levels = jnp.ones_like(bits)
            for count in range(3, 9):
                levels = jnp.where(bits == float(count), float(2 ** (count - 1) - 1), levels)
            per_bucket.append((ranges + RANGE_EPS) / levels)
        for sub in range(3):
            which = (3 * spot + sub) // 4
            chosen = jnp.where(which == 0, per_bucket[0], jnp.where(which == 1, per_bucket[1], per_bucket[2]))
            scales.append(jnp.broadcast_to(chosen, (16, COLS)))
    scale = jnp.concatenate(scales, axis=0)
    inverse = 1.0 / scale
    scale = scale * (1.0 / N_DP)
    row_part = row_ref[...]
    for part in range(4):
        cols = slice(part * 256, (part + 1) * 256)
        halves = [jnp.zeros((3 * BLOCK, COLS), F32) for _ in range(2)]
        for rep in range(REPS):
            rows = slice(rep * TOK, (rep + 1) * TOK)
            grad_front = dot(terms_ref[rep, 0 : 2 * BLOCK, :], xs_ref[rows, cols], 1, 0)
            grad_down = dot(terms_ref[rep, 2 * BLOCK : 3 * BLOCK, :], gs_ref[rows, cols], 1, 0)
            grads = jnp.concatenate([grad_front, grad_down], axis=0)
            offset = lax.rem(389 * (rep * 16 + depth), 1024).astype(F32) * (1.0 / 1024.0)
            for half in range(2):
                lanes = slice(half * COLS, (half + 1) * COLS)
                whole = slice(part * 256 + half * COLS, part * 256 + (half + 1) * COLS)
                ratio = grads[:, lanes] * inverse
                phase = row_part + (col_ref[0:1, whole] + offset)
                halves[half] = halves[half] + (ratio + turn(ratio + phase))
        for half in range(2):
            result = halves[half] * scale
            for mat in range(3):
                for low in range(2):
                    start = mat * BLOCK + low * SHARD
                    out_ref[2 * (2 * part + half) + low, mat, :, :] = result[start : start + SHARD]


def adam_kernel(mean_ref, master_ref, one_ref, two_ref, new_master_ref, new_one_ref, new_two_ref, coded_ref):
    mean_grad = mean_ref[...]
    master = master_ref[...]
    first = BETA_ONE * one_ref[...] + (1.0 - BETA_ONE) * mean_grad
    second = BETA_TWO * two_ref[...] + (1.0 - BETA_TWO) * mean_grad * mean_grad
    updated = master - LEARN_RATE * (first / (jnp.sqrt(second) + ADAM_EPS) + WEIGHT_DECAY * master)
    new_one_ref[...] = first
    new_two_ref[...] = second
    new_master_ref[...] = updated
    coded_ref[...] = eightbit_f32(updated)


def back_kernel(terms_ref, weights_ref, out_ref, rows_ref):
    for tensor in range(8):
        for plane in range(4):
            base = (tensor * 4 + plane) * 2 * BLOCK
            start = (8 * plane + tensor) * BLOCK
            rows_ref[base : base + BLOCK, :] = weights_ref[0, start : start + BLOCK, :]
            rows_ref[base + BLOCK : base + 2 * BLOCK, :] = weights_ref[1, start : start + BLOCK, :]
    out_ref[...] = dot(terms_ref[...], rows_ref[...], 0, 0).astype(BF16)


def call(kernel, out_shape, smem=0, operands=(), scratch=()):
    specs = [pl.BlockSpec(memory_space=pltpu.SMEM if i < smem else pltpu.VMEM) for i in range(len(operands))]
    return pl.pallas_call(
        kernel,
        out_shape=out_shape,
        in_specs=specs,
        scratch_shapes=scratch,
        compiler_params=pltpu.CompilerParams(vmem_limit_bytes=VMEM_LIMIT),
    )(*operands)


def struct(shape, dtype=F32):
    return jax.ShapeDtypeStruct(shape, dtype)


def to_all(value, axes, peers):
    return lax.all_to_all(jnp.broadcast_to(value[None], (peers,) + value.shape), axes, 0, 0)


def swap_pairs():
    pairs = []
    for z in range(16):
        for t in range(8):
            pairs.append((z * 8 + t, (2 * t + z % 2) * 8 + z // 2))
    return pairs


def on_device(acts, grad_out, master, moment_one, moment_two, bit_widths, row_dither, col_dither):
    y = lax.axis_index("y")
    z = lax.axis_index("z")
    core = lax.axis_index("c")
    tensor = lax.axis_index(TENSOR)
    spot = tensor % 4
    unit = 2 * y + tensor // 4
    pos = jnp.stack([core, spot, unit, z]).astype(jnp.int32)
    pairs = swap_pairs()

    coded = eightbit_f32(master).astype(BF16)
    moved = lax.ppermute(coded, ("z",) + TENSOR, pairs)
    all_weights = lax.all_gather(coded, DP, axis=1, tiled=True)

    high = (col_dither // 8).astype(BF16)[None]
    low = (col_dither % 8).astype(BF16)[None]
    extra = jnp.concatenate([high, low, jnp.zeros((14, COLS), BF16)])
    packed = jnp.concatenate([acts, grad_out, extra])
    own = to_all(packed, ("y", "xh", "xl"), 16)
    other = lax.ppermute(own, "c", [(0, 1), (1, 0)])

    rows = to_all(moved, "z", 16)
    rows = rows.reshape(8, 2, 3, SHARD, COLS).transpose(2, 1, 3, 0, 4).reshape(3 * BLOCK, 8 * COLS)
    row_part = lax.dynamic_slice(row_dither, (0, BLOCK * (8 * y + tensor)), (3, BLOCK))
    row_part = jnp.broadcast_to(row_part.astype(F32).reshape(3 * BLOCK, 1) * (1.0 / 1024.0), (3 * BLOCK, COLS))

    xs, gs, terms, col_part, peak = call(
        front_kernel,
        (
            struct((REPS * TOK, 1024), BF16),
            struct((REPS * TOK, 1024), BF16),
            struct((REPS, 3 * BLOCK, TOK), BF16),
            struct((8, 1024)),
            struct((64, 1, COLS)),
        ),
        1,
        (pos, own, other, rows),
    )
    peaks = lax.all_to_all(peak, ("xl", "c", "z"), 0, 0)
    mine = lax.all_to_all(terms[:, : 2 * BLOCK], "y", 0, 0)
    mine = to_all(mine, TENSOR, 8)

    shares = call(
        quant_kernel,
        struct((16, 3, SHARD, COLS)),
        1,
        (pos, xs, gs, terms, peaks, bit_widths, row_part, col_part),
    )
    mean_grad = jnp.sum(lax.all_to_all(shares, "z", 0, 0), axis=0)
    mean_grad = lax.ppermute(mean_grad, ("z",) + TENSOR, pairs)

    updated, first, second, new_coded = call(
        adam_kernel,
        tuple(struct((3, SHARD, COLS)) for _ in range(4)),
        0,
        (mean_grad, master, moment_one, moment_two),
    )
    ring = to_all(new_coded.astype(BF16), "z", 16)
    ring = ring.transpose(1, 0, 2, 3).reshape(3, 16 * SHARD, COLS)
    new_weights = to_all(ring, "y", 4).transpose(1, 0, 2, 3).reshape(3, 64 * SHARD, COLS)

    grad_in = call(
        back_kernel,
        struct((TOK, COLS), BF16),
        0,
        (mine.reshape(64 * BLOCK, TOK), all_weights),
        (pltpu.VMEM((64 * BLOCK, COLS), BF16),),
    )
    return (grad_in, updated, first, second, new_weights)


def solution(mesh):
    grid = Mesh(mesh.devices.reshape(SIZES), DP + TENSOR)
    return jax.shard_map(
        on_device,
        mesh=grid,
        in_specs=(
            P(DP, TENSOR),
            P(DP, TENSOR),
            P(None, DP, TENSOR),
            P(None, DP, TENSOR),
            P(None, DP, TENSOR),
            P(),
            P(),
            P(TENSOR),
        ),
        out_specs=(
            P(DP, TENSOR),
            P(None, DP, TENSOR),
            P(None, DP, TENSOR),
            P(None, DP, TENSOR),
            P(None, None, TENSOR),
        ),
        check_vma=False,
    )
```

time: 1100 us -> 314 us (0.29)
  the two profiles are of different devices: /device:TPU:6 before, /device:TPU:16 now
where the time goes in v1:
time: 314 us; the launch traced here: 313 us
  waiting for transfers between devices  202 us (64%)
  starting transfers between devices  74.8 us (24%)
  between operations  14.3 us (5%)
  local copies, waits for them, and re-layouts  12.1 us (4%)
  Pallas kernels  7.96 us (3%)
    all_gather x1, waiting for transfers between devices, on_device(): all_weights = lax.all_gather(coded, DP, axis=1, tiled=True)  93.2 us
    all_to_all x5, waiting for transfers between devices, to_all(): lax.all_to_all(jnp.broadcast_to(value[None], (peers,) + value.shape), axe...  63.8 us
    all_to_all x5, starting transfers between devices, to_all(): lax.all_to_all(jnp.broadcast_to(value[None], (peers,) + value.shape), axe...  55 us
    all_to_all x1, waiting for transfers between devices, on_device(): mean_grad = jnp.sum(lax.all_to_all(shares, 'z', 0, 0), axis=0)  30.7 us
    all_to_all x1, waiting for transfers between devices, on_device(): peaks = lax.all_to_all(peak, ('xl', 'c', 'z'), 0, 0)  12.1 us
    pallas_call x4, Pallas kernels, call(): pl.pallas_call(kernel, out_shape=out_shape, in_specs=specs, scratch_shape...  7.96 us
    all_to_all x1, starting transfers between devices, on_device(): peaks = lax.all_to_all(peak, ('xl', 'c', 'z'), 0, 0)  6.85 us
  transfers between devices with their start and end apart: 12, of which 8 were waited for; matrix products, arithmetic and copies ran while one was open for 2% of the time, Pallas kernels for 1%

profile of v1, /device:TPU:16, one launch (start us, length us, event | category | flops | bytes accessed | tf_op | source)
XLA Modules:
  0.0 313.0 jit_solution(10555575559163406107)
XLA Ops:
  7.8 1.7 concatenate.3
  9.5 1.1 broadcast_in_dim.25
  10.7 9.4 %all-to-all-start = ((bf16[16,272,128]{2,1,0:T(8,128)(2,1)}), bf16[16,272,128]{2,1,0:T(8,128)(2,1)S(1)}, u32[]{:S(2)}, u32[]{:S(2)}) async-start(bf16[16,272,128]{2,1,0:T(8,128)(2,1)} %broadcast_in_dim.25), calls=%async_computation | async-start | bytes 2228224 | tf_op jit(solution)/shard_map/all_to_all | solution.py:198
  20.9 13.0 %all-to-all-done.own_ref = bf16[16,272,128]{2,1,0:T(8,128)(2,1)S(1)} async-done(((bf16[16,272,128]{2,1,0:T(8,128)(2,1)}), bf16[16,272,128]{2,1,0:T(8,128)(2,1)S(1)}, u32[]{:S(2)}, u32[]{:S(2)}) %all-to-all-start) | async-done | bytes 1114144 | tf_op jit(solution)/shard_map/all_to_all | solution.py:198
  34.0 1.9 collective-permute-start
  36.6 15.4 %all-to-all-start.1 = ((bf16[16,3,24,128]{3,2,1,0:T(8,128)(2,1)}), bf16[16,3,24,128]{3,2,1,0:T(8,128)(2,1)S(1)}, u32[]{:S(2)}, u32[]{:S(2)}) async-start(bf16[16,3,24,128]{3,2,1,0:T(8,128)(2,1)} %broadcast_in_dim.54), calls=%async_computation.1 | async-start | bytes 589824 | tf_op jit(solution)/shard_map/all_to_all | solution.py:198
  52.1 20.2 %all-to-all-done.1 = bf16[16,3,24,128]{3,2,1,0:T(8,128)(2,1)S(1)} async-done(((bf16[16,3,24,128]{3,2,1,0:T(8,128)(2,1)}), bf16[16,3,24,128]{3,2,1,0:T(8,128)(2,1)S(1)}, u32[]{:S(2)}, u32[]{:S(2)}) %all-to-all-start.1) | async-done | bytes 294944 | tf_op jit(solution)/shard_map/all_to_all | solution.py:198
  72.4 3.0 shard_map.119
  76.4 6.9 %all-to-all-start.4 = ((f32[64,1,128]{2,1,0:T(1,128)}), f32[64,1,128]{2,1,0:T(1,128)S(1)}, u32[]{:S(2)}, u32[]{:S(2)}) async-start(f32[64,1,128]{2,1,0:T(1,128)} %get-tuple-element.17), calls=%async_computation.4 | async-start | bytes 65536 | tf_op jit(solution)/shard_map/all_to_all | solution.py:247
  84.1 12.1 %all-to-all-done.4.peaks_ref = f32[64,1,128]{2,1,0:T(1,128)S(1)} async-done(((f32[64,1,128]{2,1,0:T(1,128)}), f32[64,1,128]{2,1,0:T(1,128)S(1)}, u32[]{:S(2)}, u32[]{:S(2)}) %all-to-all-start.4) | async-done | bytes 32800 | tf_op jit(solution)/shard_map/all_to_all | solution.py:247
  96.4 1.2 copy-done.2
  97.6 3.2 %shard_map.121 = f32[16,3,24,128]{3,2,1,0:T(8,128)} custom-call(s32[4]{0:T(128)S(1)} %pad_add_fusion.pos_ref, bf16[512,1024]{1,0:T(8,128)(2,1)S(1)} %get-tuple-element.15.xs_ref, bf16[512,1024]{1,0:T(8,128)(2,1)S(1)} %copy-done.2, bf16[4,144,128]{2,1,0:T(8,128)(2,1)S(1)} %get-tuple-element.14.terms_ref, f32[64,1,128]{2,1,0:T(1,128)S(1)} %all-to-all-done.4.peaks_ref, ...), custom_call_target="tpu_custom_call" | custom-call | tf_op jit(solution)/shard_map/pallas_call | solution.py:184
  100.8 3.7 %all-to-all-start.5 = ((f32[16,3,24,128]{3,2,1,0:T(8,128)}), f32[16,3,24,128]{3,2,1,0:T(8,128)S(1)}, u32[]{:S(2)}, u32[]{:S(2)}) async-start(f32[16,3,24,128]{3,2,1,0:T(8,128)} %shard_map.121), calls=%async_computation.5 | async-start | bytes 1179648 | tf_op jit(solution)/shard_map/all_to_all | solution.py:257
  105.2 30.7 %all-to-all-done.5 = f32[16,3,24,128]{3,2,1,0:T(8,128)S(1)} async-done(((f32[16,3,24,128]{3,2,1,0:T(8,128)}), f32[16,3,24,128]{3,2,1,0:T(8,128)S(1)}, u32[]{:S(2)}, u32[]{:S(2)}) %all-to-all-start.5) | async-done | bytes 589856 | tf_op jit(solution)/shard_map/all_to_all | solution.py:257
  135.8 6.0 %all-to-all-start.2 = ((bf16[4,96,128]{2,1,0:T(8,128)(2,1)}), bf16[4,96,128]{2,1,0:T(8,128)(2,1)S(1)}, u32[]{:S(2)}, u32[]{:S(2)}) async-start(bf16[4,96,128]{2,1,0:T(8,128)(2,1)} %slice.3), calls=%async_computation.2 | async-start | bytes 196608 | tf_op jit(solution)/shard_map/all_to_all | solution.py:248
  143.2 1.8 all-to-all-done.2
  145.7 21.9 %all-to-all-start.6 = ((bf16[16,3,24,128]{3,2,1,0:T(8,128)(2,1)}), bf16[16,3,24,128]{3,2,1,0:T(8,128)(2,1)S(1)}, u32[]{:S(2)}, u32[]{:S(2)}) async-start(bf16[16,3,24,128]{3,2,1,0:T(8,128)(2,1)} %broadcast_in_dim.57), calls=%async_computation.6 | async-start | bytes 589824 | tf_op jit(solution)/shard_map/all_to_all | solution.py:198
  168.3 17.6 %all-to-all-done.6 = bf16[16,3,24,128]{3,2,1,0:T(8,128)(2,1)S(1)} async-done(((bf16[16,3,24,128]{3,2,1,0:T(8,128)(2,1)}), bf16[16,3,24,128]{3,2,1,0:T(8,128)(2,1)S(1)}, u32[]{:S(2)}, u32[]{:S(2)}) %all-to-all-start.6) | async-done | bytes 294944 | tf_op jit(solution)/shard_map/all_to_all | solution.py:198
  186.9 3.5 %all-to-all-start.3 = ((bf16[8,4,96,128]{3,2,1,0:T(8,128)(2,1)}), bf16[8,4,96,128]{3,2,1,0:T(8,128)(2,1)S(1)}, u32[]{:S(2)}, u32[]{:S(2)}) async-start(bf16[8,4,96,128]{3,2,1,0:T(8,128)(2,1)} %broadcast_in_dim.55), calls=%async_computation.3 | async-start | bytes 1572864 | tf_op jit(solution)/shard_map/all_to_all | solution.py:198
  190.5 13.0 %all-to-all-done.3 = bf16[8,4,96,128]{3,2,1,0:T(8,128)(2,1)S(1)} async-done(((bf16[8,4,96,128]{3,2,1,0:T(8,128)(2,1)}), bf16[8,4,96,128]{3,2,1,0:T(8,128)(2,1)S(1)}, u32[]{:S(2)}, u32[]{:S(2)}) %all-to-all-start.3) | async-done | bytes 786464 | tf_op jit(solution)/shard_map/all_to_all | solution.py:198
  203.5 1.2 broadcast_in_dim.59
  204.7 4.8 %all-to-all-start.7 = ((bf16[4,3,384,128]{3,2,1,0:T(8,128)(2,1)}), bf16[4,3,384,128]{3,2,1,0:T(8,128)(2,1)S(1)}, u32[]{:S(2)}, u32[]{:S(2)}) async-start(bf16[4,3,384,128]{3,2,1,0:T(8,128)(2,1)} %broadcast_in_dim.59), calls=%async_computation.7 | async-start | bytes 2359296 | tf_op jit(solution)/shard_map/all_to_all | solution.py:198
  209.5 93.2 %all-gather.2.cloned.1.call-done.weights_ref = bf16[3,1536,128]{2,1,0:T(8,128)(2,1)} async-done(((bf16[3,24,128]{2,1,0:T(8,128)(2,1)}), bf16[3,1536,128]{2,1,0:T(8,128)(2,1)}) %all-gather.2.cloned.1.call-update) | async-done | bytes 1179664 | tf_op jit(solution)/shard_map/all_gather | solution.py:221
  302.7 1.3 copy-done
  (43 shorter events, 11.1 us)
Async XLA Ops:
  10.7 9.4 %copy-start.3 = (f32[3,24,128]{2,1,0:T(8,128)S(1)}, f32[3,24,128]{2,1,0:T(8,128)}, u32[]{:S(2)}) copy-start(f32[3,24,128]{2,1,0:T(8,128)} %master_ref.1) | copy-start | bytes 110596
  10.7 23.3 %all-to-all-start = ((bf16[16,272,128]{2,1,0:T(8,128)(2,1)}), bf16[16,272,128]{2,1,0:T(8,128)(2,1)S(1)}, u32[]{:S(2)}, u32[]{:S(2)}) async-start(bf16[16,272,128]{2,1,0:T(8,128)(2,1)} %broadcast_in_dim.25), calls=%async_computation | async-start | bytes 2228224 | tf_op jit(solution)/shard_map/all_to_all | solution.py:198
  20.3 55.2 %copy-start.7 = (bf16[3,24,128]{2,1,0:T(8,128)(2,1)}, bf16[3,24,128]{2,1,0:T(8,128)(2,1)S(1)}, u32[]{:S(2)}) copy-start(bf16[3,24,128]{2,1,0:T(8,128)(2,1)S(1)} %multiply_convert_fusion) | copy-start | bytes 55300
  20.3 15.6 %collective-permute-start.1 = (bf16[3,24,128]{2,1,0:T(8,128)(2,1)S(1)}, bf16[3,24,128]{2,1,0:T(8,128)(2,1)S(1)}, u32[]{:S(2)}, u32[]{:S(2)}) collective-permute-start(bf16[3,24,128]{2,1,0:T(8,128)(2,1)S(1)} %multiply_convert_fusion), channel_id=1, source_target_pairs={{0,0},{1,16},{2,32},{3,48},{4,64},{5,80},{6,96},{7,112},{8,8},{9,2... | collective-permute-start | bytes 55304 | tf_op jit(solution)/shard_map/ppermute | solution.py:220
  34.0 38.4 %collective-permute-start = (bf16[16,272,128]{2,1,0:T(8,128)(2,1)S(1)}, bf16[16,272,128]{2,1,0:T(8,128)(2,1)S(1)}, u32[]{:S(2)}, u32[]{:S(2)}) collective-permute-start(bf16[16,272,128]{2,1,0:T(8,128)(2,1)S(1)} %all-to-all-done.own_ref), channel_id=1, source_target_pairs={{0,1},{1,0},{2,3},{3,2},{4,5},{5,4},{6,7},{7,6},{8,9},{9,8},{10,11... | collective-permute-start | bytes 3342344 | tf_op jit(solution)/shard_map/ppermute | solution.py:228
  36.6 35.6 %all-to-all-start.1 = ((bf16[16,3,24,128]{3,2,1,0:T(8,128)(2,1)}), bf16[16,3,24,128]{3,2,1,0:T(8,128)(2,1)S(1)}, u32[]{:S(2)}, u32[]{:S(2)}) async-start(bf16[16,3,24,128]{3,2,1,0:T(8,128)(2,1)} %broadcast_in_dim.54), calls=%async_computation.1 | async-start | bytes 589824 | tf_op jit(solution)/shard_map/all_to_all | solution.py:198
  72.4 23.9 %copy-start.6 = (s32[3,24]{1,0:T(4,128)S(1)}, s32[3,24]{1,0:T(4,128)}, u32[]{:S(2)}) copy-start(s32[3,24]{1,0:T(4,128)} %bits_ref.1) | copy-start | bytes 868
  75.4 1.0 copy-start.1
  76.4 19.9 %all-to-all-start.4 = ((f32[64,1,128]{2,1,0:T(1,128)}), f32[64,1,128]{2,1,0:T(1,128)S(1)}, u32[]{:S(2)}, u32[]{:S(2)}) async-start(f32[64,1,128]{2,1,0:T(1,128)} %get-tuple-element.17), calls=%async_computation.4 | async-start | bytes 65536 | tf_op jit(solution)/shard_map/all_to_all | solution.py:247
  96.4 1.2 copy-start.2
  100.8 41.7 %copy-start.4 = (f32[3,24,128]{2,1,0:T(8,128)S(1)}, f32[3,24,128]{2,1,0:T(8,128)}, u32[]{:S(2)}) copy-start(f32[3,24,128]{2,1,0:T(8,128)} %one_ref.1) | copy-start | bytes 110596
  100.8 41.7 %copy-start.5 = (f32[3,24,128]{2,1,0:T(8,128)S(1)}, f32[3,24,128]{2,1,0:T(8,128)}, u32[]{:S(2)}) copy-start(f32[3,24,128]{2,1,0:T(8,128)} %two_ref.1) | copy-start | bytes 110596
  100.8 35.0 %all-to-all-start.5 = ((f32[16,3,24,128]{3,2,1,0:T(8,128)}), f32[16,3,24,128]{3,2,1,0:T(8,128)S(1)}, u32[]{:S(2)}, u32[]{:S(2)}) async-start(f32[16,3,24,128]{3,2,1,0:T(8,128)} %shard_map.121), calls=%async_computation.5 | async-start | bytes 1179648 | tf_op jit(solution)/shard_map/all_to_all | solution.py:257
  135.8 9.1 %all-to-all-start.2 = ((bf16[4,96,128]{2,1,0:T(8,128)(2,1)}), bf16[4,96,128]{2,1,0:T(8,128)(2,1)S(1)}, u32[]{:S(2)}, u32[]{:S(2)}) async-start(bf16[4,96,128]{2,1,0:T(8,128)(2,1)} %slice.3), calls=%async_computation.2 | async-start | bytes 196608 | tf_op jit(solution)/shard_map/all_to_all | solution.py:248
  141.8 0.7 collective-permute-start.2
  145.7 40.2 %all-to-all-start.6 = ((bf16[16,3,24,128]{3,2,1,0:T(8,128)(2,1)}), bf16[16,3,24,128]{3,2,1,0:T(8,128)(2,1)S(1)}, u32[]{:S(2)}, u32[]{:S(2)}) async-start(bf16[16,3,24,128]{3,2,1,0:T(8,128)(2,1)} %broadcast_in_dim.57), calls=%async_computation.6 | async-start | bytes 589824 | tf_op jit(solution)/shard_map/all_to_all | solution.py:198
  167.6 135.1 %all-gather.2.cloned.1.call-start = ((), (), s32[]{:S(2)}) async-start(), calls=%async_computation.8 | async-start | bytes 1198080 | tf_op jit(solution)/shard_map/all_gather | solution.py:221
  186.9 16.6 %all-to-all-start.3 = ((bf16[8,4,96,128]{3,2,1,0:T(8,128)(2,1)}), bf16[8,4,96,128]{3,2,1,0:T(8,128)(2,1)S(1)}, u32[]{:S(2)}, u32[]{:S(2)}) async-start(bf16[8,4,96,128]{3,2,1,0:T(8,128)(2,1)} %broadcast_in_dim.55), calls=%async_computation.3 | async-start | bytes 1572864 | tf_op jit(solution)/shard_map/all_to_all | solution.py:198
  204.7 100.4 %all-to-all-start.7 = ((bf16[4,3,384,128]{3,2,1,0:T(8,128)(2,1)}), bf16[4,3,384,128]{3,2,1,0:T(8,128)(2,1)S(1)}, u32[]{:S(2)}, u32[]{:S(2)}) async-start(bf16[4,3,384,128]{3,2,1,0:T(8,128)(2,1)} %broadcast_in_dim.59), calls=%async_computation.7 | async-start | bytes 2359296 | tf_op jit(solution)/shard_map/all_to_all | solution.py:198
  302.7 1.3 copy-start
Sparse Core Ops, SparseCore 0:
  171.4 131.2 all-gather.1

commit v2 on v1

--- a/solution.py
+++ b/solution.py
@@ -36,7 +36,7 @@
 TENSOR = ("xh", "xl", "c")
 SIZES = (4, 16, 2, 2, 2)
 
-VMEM_LIMIT = 40 * 1024 * 1024
+VMEM_LIMIT = 20 * 1024 * 1024
 
 
 def turn(value):
@@ -63,7 +63,25 @@
     )
 
 
-def front_kernel(pos_ref, own_ref, other_ref, weights_ref, xs_ref, gs_ref, terms_ref, col_ref, peak_ref):
+def pack_kernel(acts_ref, grad_ref, dither_ref, master_ref, one_ref, two_ref, packed_ref, state_ref):
+    high = (dither_ref[...] >> 3).astype(F32)
+    low = (dither_ref[...] & 7).astype(F32)
+    row = lax.broadcasted_iota(jnp.int32, (16, COLS), 0)
+    extra = jnp.where(row == 0, high, jnp.where(row == 1, low, 0.0)).astype(BF16)
+    for peer in range(16):
+        packed_ref[peer, 0:TOK, :] = acts_ref[...]
+        packed_ref[peer, TOK : 2 * TOK, :] = grad_ref[...]
+        packed_ref[peer, 2 * TOK : 2 * TOK + 16, :] = extra
+    state_ref[0] = master_ref[...]
+    state_ref[1] = one_ref[...]
+    state_ref[2] = two_ref[...]
+
+
+def code_kernel(state_ref, coded_ref):
+    coded_ref[...] = eightbit_f32(state_ref[0])
+
+
+def front_kernel(pos_ref, own_ref, other_ref, weights_ref, xs_ref, gs_ref, terms_ref, col_ref, peak_ref, keep_ref, give_ref):
     core = pos_ref[0]
     for chip in range(4):
         for source, which in ((own_ref, core), (other_ref, 1 - core)):
@@ -84,6 +102,16 @@
     dgate = (delta * upper * sig * (1.0 + gate * (1.0 - sig))).astype(BF16)
     dupper = (delta * active).astype(BF16)
     hidden = (active * upper).astype(BF16)
+    terms = jnp.concatenate([dgate, dupper], axis=0)
+    for target, which in ((keep_ref, core), (give_ref, 1 - core)):
+        side = []
+        for chip in range(4):
+            cols = pl.ds(pl.multiple_of((2 * chip + which) * COLS, COLS), COLS)
+            side.append(weights_ref[0 : 2 * BLOCK, cols])
+        back = dot(terms, jnp.concatenate(side, axis=1), 0, 0)
+        for rep in range(REPS):
+            for chip in range(4):
+                target[rep * 4 + chip] = back[rep * TOK : (rep + 1) * TOK, chip * COLS : (chip + 1) * COLS]
     peak = jnp.zeros((3 * BLOCK, COLS), F32)
     for rep in range(REPS):
         rows = slice(rep * TOK, (rep + 1) * TOK)
@@ -105,7 +133,12 @@
     peak_ref[...] = jnp.broadcast_to(packed.reshape(1, 1, COLS), peak_ref.shape)
 
 
-def quant_kernel(pos_ref, xs_ref, gs_ref, terms_ref, peaks_ref, bits_ref, row_ref, col_ref, out_ref):
+def quant_kernel(pos_ref, xs_ref, gs_ref, terms_ref, peaks_ref, bits_ref, row_ref, col_ref, keep_ref, got_ref, out_ref, *back_refs):
+    plane = pos_ref[4]
+    for step, back_ref in enumerate(back_refs):
+        first = ((plane + step) % 4) * 4
+        for chip in range(4):
+            back_ref[chip] = keep_ref[first + chip] + got_ref[first + chip]
     spot = pos_ref[1]
     unit = pos_ref[2]
     depth = pos_ref[3]
@@ -157,35 +190,30 @@
                     out_ref[2 * (2 * part + half) + low, mat, :, :] = result[start : start + SHARD]
 
 
-def adam_kernel(mean_ref, master_ref, one_ref, two_ref, new_master_ref, new_one_ref, new_two_ref, coded_ref):
-    mean_grad = mean_ref[...]
-    master = master_ref[...]
-    first = BETA_ONE * one_ref[...] + (1.0 - BETA_ONE) * mean_grad
-    second = BETA_TWO * two_ref[...] + (1.0 - BETA_TWO) * mean_grad * mean_grad
+def adam_kernel(pos_ref, shares_ref, state_ref, own_ref, up_ref, across_ref, down_ref, new_state_ref, coded_ref, *back_refs):
+    chip = pos_ref[5]
+    for step, back_ref in enumerate(back_refs):
+        which = (chip + step) % 4
+        back_ref[...] = (own_ref[which] + up_ref[which]) + (across_ref[which] + down_ref[which])
+    mean_grad = shares_ref[0]
+    for peer in range(1, 16):
+        mean_grad = mean_grad + shares_ref[peer]
+    master = state_ref[0]
+    first = BETA_ONE * state_ref[1] + (1.0 - BETA_ONE) * mean_grad
+    second = BETA_TWO * state_ref[2] + (1.0 - BETA_TWO) * mean_grad * mean_grad
     updated = master - LEARN_RATE * (first / (jnp.sqrt(second) + ADAM_EPS) + WEIGHT_DECAY * master)
-    new_one_ref[...] = first
-    new_two_ref[...] = second
-    new_master_ref[...] = updated
+    new_state_ref[0] = updated
+    new_state_ref[1] = first
+    new_state_ref[2] = second
     coded_ref[...] = eightbit_f32(updated)
 
 
-def back_kernel(terms_ref, weights_ref, out_ref, rows_ref):
-    for tensor in range(8):
-        for plane in range(4):
-            base = (tensor * 4 + plane) * 2 * BLOCK
-            start = (8 * plane + tensor) * BLOCK
-            rows_ref[base : base + BLOCK, :] = weights_ref[0, start : start + BLOCK, :]
-            rows_ref[base + BLOCK : base + 2 * BLOCK, :] = weights_ref[1, start : start + BLOCK, :]
-    out_ref[...] = dot(terms_ref[...], rows_ref[...], 0, 0).astype(BF16)
-
-
-def call(kernel, out_shape, smem=0, operands=(), scratch=()):
+def call(kernel, out_shape, smem=0, operands=()):
     specs = [pl.BlockSpec(memory_space=pltpu.SMEM if i < smem else pltpu.VMEM) for i in range(len(operands))]
     return pl.pallas_call(
         kernel,
         out_shape=out_shape,
         in_specs=specs,
-        scratch_shapes=scratch,
         compiler_params=pltpu.CompilerParams(vmem_limit_bytes=VMEM_LIMIT),
     )(*operands)
 
@@ -196,6 +224,10 @@
 
 def to_all(value, axes, peers):
     return lax.all_to_all(jnp.broadcast_to(value[None], (peers,) + value.shape), axes, 0, 0)
+
+
+def shift(value, axes, step):
+    return lax.ppermute(value, axes, [(i, (i + step) % 4) for i in range(4)])
 
 
 def swap_pairs():
@@ -213,26 +245,26 @@
     tensor = lax.axis_index(TENSOR)
     spot = tensor % 4
     unit = 2 * y + tensor // 4
-    pos = jnp.stack([core, spot, unit, z]).astype(jnp.int32)
+    pos = jnp.stack([core, spot, unit, z, y, tensor // 2]).astype(jnp.int32)
     pairs = swap_pairs()
 
-    coded = eightbit_f32(master).astype(BF16)
-    moved = lax.ppermute(coded, ("z",) + TENSOR, pairs)
-    all_weights = lax.all_gather(coded, DP, axis=1, tiled=True)
-
-    high = (col_dither // 8).astype(BF16)[None]
-    low = (col_dither % 8).astype(BF16)[None]
-    extra = jnp.concatenate([high, low, jnp.zeros((14, COLS), BF16)])
-    packed = jnp.concatenate([acts, grad_out, extra])
-    own = to_all(packed, ("y", "xh", "xl"), 16)
+    packed, state = call(
+        pack_kernel,
+        (struct((16, 2 * TOK + 16, COLS), BF16), struct((3, 3, SHARD, COLS))),
+        0,
+        (acts, grad_out, col_dither[None], master, moment_one, moment_two),
+    )
+    state = lax.ppermute(state, ("z",) + TENSOR, pairs)
+    coded = call(code_kernel, struct((3, SHARD, COLS)), 0, (state,))
+    rows = to_all(coded.astype(BF16), "z", 16)
+    own = lax.all_to_all(packed, ("y", "xh", "xl"), 0, 0)
     other = lax.ppermute(own, "c", [(0, 1), (1, 0)])
 
-    rows = to_all(moved, "z", 16)
     rows = rows.reshape(8, 2, 3, SHARD, COLS).transpose(2, 1, 3, 0, 4).reshape(3 * BLOCK, 8 * COLS)
     row_part = lax.dynamic_slice(row_dither, (0, BLOCK * (8 * y + tensor)), (3, BLOCK))
     row_part = jnp.broadcast_to(row_part.astype(F32).reshape(3 * BLOCK, 1) * (1.0 / 1024.0), (3 * BLOCK, COLS))
 
-    xs, gs, terms, col_part, peak = call(
+    xs, gs, terms, col_part, peak, keep, give = call(
         front_kernel,
         (
             struct((REPS * TOK, 1024), BF16),
@@ -240,41 +272,38 @@
             struct((REPS, 3 * BLOCK, TOK), BF16),
             struct((8, 1024)),
             struct((64, 1, COLS)),
+            struct((16, TOK, COLS)),
+            struct((16, TOK, COLS)),
         ),
         1,
         (pos, own, other, rows),
     )
     peaks = lax.all_to_all(peak, ("xl", "c", "z"), 0, 0)
-    mine = lax.all_to_all(terms[:, : 2 * BLOCK], "y", 0, 0)
-    mine = to_all(mine, TENSOR, 8)
-
-    shares = call(
+    got = lax.ppermute(give, "c", [(0, 1), (1, 0)])
+
+    shares, *back = call(
         quant_kernel,
-        struct((16, 3, SHARD, COLS)),
+        (struct((16, 3, SHARD, COLS)),) + (struct((4, TOK, COLS)),) * 4,
         1,
-        (pos, xs, gs, terms, peaks, bit_widths, row_part, col_part),
-    )
-    mean_grad = jnp.sum(lax.all_to_all(shares, "z", 0, 0), axis=0)
-    mean_grad = lax.ppermute(mean_grad, ("z",) + TENSOR, pairs)
-
-    updated, first, second, new_coded = call(
+        (pos, xs, gs, terms, peaks, bit_widths, row_part, col_part, keep, got),
+    )
+    back = [back[0]] + [shift(back[step], "y", step) for step in (1, 2, 3)]
+    shares = lax.all_to_all(shares, "z", 0, 0)
+
+    new_state, new_coded, *back = call(
         adam_kernel,
-        tuple(struct((3, SHARD, COLS)) for _ in range(4)),
-        0,
-        (mean_grad, master, moment_one, moment_two),
-    )
+        (struct((3, 3, SHARD, COLS)), struct((3, SHARD, COLS))) + (struct((TOK, COLS)),) * 4,
+        1,
+        (pos, shares, state, *back),
+    )
+    back = [back[0]] + [shift(back[step], ("xh", "xl"), step) for step in (1, 2, 3)]
     ring = to_all(new_coded.astype(BF16), "z", 16)
-    ring = ring.transpose(1, 0, 2, 3).reshape(3, 16 * SHARD, COLS)
-    new_weights = to_all(ring, "y", 4).transpose(1, 0, 2, 3).reshape(3, 64 * SHARD, COLS)
-
-    grad_in = call(
-        back_kernel,
-        struct((TOK, COLS), BF16),
-        0,
-        (mine.reshape(64 * BLOCK, TOK), all_weights),
-        (pltpu.VMEM((64 * BLOCK, COLS), BF16),),
-    )
-    return (grad_in, updated, first, second, new_weights)
+    new_state = lax.ppermute(new_state, ("z",) + TENSOR, pairs)
+    grad_in = ((back[0] + back[1]) + (back[2] + back[3])).astype(BF16)
+    ring = jnp.broadcast_to(ring.reshape(1, 8, 2, 3, SHARD, COLS), (4, 8, 2, 3, SHARD, COLS))
+    ring = lax.all_to_all(ring.reshape(32, 2, 3, SHARD, COLS), ("y",) + TENSOR, 0, 0)
+    new_weights = ring.transpose(2, 0, 1, 3, 4).reshape(3, 64 * SHARD, COLS)
+    return (grad_in, new_state[0], new_state[1], new_state[2], new_weights)
 
 
 def solution(mesh):

time: 314 us -> 215 us (0.68)
  the two profiles are of different devices: /device:TPU:16 before, /device:TPU:2 now
where the time goes in v2:
time: 215 us; the launch traced here: 214 us
  waiting for transfers between devices  83.3 us (39%)
  starting transfers between devices  76 us (35%)
  blocking collectives  26.3 us (12%)
  local copies, waits for them, and re-layouts  17.2 us (8%)
  Pallas kernels  8.75 us (4%)
    all_to_all x1, blocking collectives, to_all(): lax.all_to_all(jnp.broadcast_to(value[None], (peers,) + value.shape), axe...  26.3 us
    all_to_all x1, waiting for transfers between devices, to_all(): lax.all_to_all(jnp.broadcast_to(value[None], (peers,) + value.shape), axe...  20.9 us
    ppermute x6, starting transfers between devices, shift(): return lax.ppermute(value, axes, [(i, (i + step) % 4) for i in range(4)])  20.8 us
    ppermute x1, waiting for transfers between devices, on_device(): new_state = lax.ppermute(new_state, ('z',) + TENSOR, pairs)  15.8 us
    unnamed x41, local copies, waits for them, and re-layouts  13.1 us
    all_to_all x1, waiting for transfers between devices, on_device(): shares = lax.all_to_all(shares, 'z', 0, 0)  11.8 us
    all_to_all x1, waiting for transfers between devices, on_device(): peaks = lax.all_to_all(peak, ('xl', 'c', 'z'), 0, 0)  11.5 us
    all_to_all x1, starting transfers between devices, to_all(): lax.all_to_all(jnp.broadcast_to(value[None], (peers,) + value.shape), axe...  10.6 us
  transfers between devices with their start and end apart: 15, of which 11 were waited for; matrix products, arithmetic and copies ran while one was open for 1% of the time, Pallas kernels for 0%

profile of v2, /device:TPU:2, one launch (start us, length us, event | category | flops | bytes accessed | tf_op | source)
XLA Modules:
  0.0 214.0 jit_solution(10884738175556927208)
XLA Ops:
  6.3 9.4 %all-to-all-start = ((bf16[16,272,128]{2,1,0:T(8,128)(2,1)}), bf16[16,272,128]{2,1,0:T(8,128)(2,1)S(1)}, u32[]{:S(2)}, u32[]{:S(2)}) async-start(bf16[16,272,128]{2,1,0:T(8,128)(2,1)} %get-tuple-element.25), calls=%async_computation | async-start | bytes 2228224 | tf_op jit(solution)/shard_map/all_to_all | solution.py:260
  15.6 6.7 %collective-permute-start.1 = (f32[3,3,24,128]{3,2,1,0:T(8,128)S(1)}, f32[3,3,24,128]{3,2,1,0:T(8,128)S(1)}, u32[]{:S(2)}, u32[]{:S(2)}) collective-permute-start(f32[3,3,24,128]{3,2,1,0:T(8,128)S(1)} %get-tuple-element.26), channel_id=1, source_target_pairs={{0,0},{1,16},{2,32},{3,48},{4,64},{5,80},{6,96},{7,112},{8,8},{9,2... | collective-permute-start | bytes 331784 | tf_op jit(solution)/shard_map/ppermute | solution.py:257
  22.4 8.3 %all-to-all-done.own_ref = bf16[16,272,128]{2,1,0:T(8,128)(2,1)S(1)} async-done(((bf16[16,272,128]{2,1,0:T(8,128)(2,1)}), bf16[16,272,128]{2,1,0:T(8,128)(2,1)S(1)}, u32[]{:S(2)}, u32[]{:S(2)}) %all-to-all-start) | async-done | bytes 1114144 | tf_op jit(solution)/shard_map/all_to_all | solution.py:260
  32.6 5.9 %collective-permute-done.1.state_ref = f32[3,3,24,128]{3,2,1,0:T(8,128)S(1)} collective-permute-done((f32[3,3,24,128]{3,2,1,0:T(8,128)S(1)}, f32[3,3,24,128]{3,2,1,0:T(8,128)S(1)}, u32[]{:S(2)}, u32[]{:S(2)}) %collective-permute-start.1) | collective-permute-done | bytes 110624 | tf_op jit(solution)/shard_map/ppermute | solution.py:257
  39.4 10.6 %all-to-all-start.1 = ((bf16[16,3,24,128]{3,2,1,0:T(8,128)(2,1)}), bf16[16,3,24,128]{3,2,1,0:T(8,128)(2,1)S(1)}, u32[]{:S(2)}, u32[]{:S(2)}) async-start(bf16[16,3,24,128]{3,2,1,0:T(8,128)(2,1)} %broadcast_in_dim.13), calls=%async_computation.1 | async-start | bytes 589824 | tf_op jit(solution)/shard_map/all_to_all | solution.py:226
  50.1 20.9 %all-to-all-done.1 = bf16[16,3,24,128]{3,2,1,0:T(8,128)(2,1)S(1)} async-done(((bf16[16,3,24,128]{3,2,1,0:T(8,128)(2,1)}), bf16[16,3,24,128]{3,2,1,0:T(8,128)(2,1)S(1)}, u32[]{:S(2)}, u32[]{:S(2)}) %all-to-all-start.1) | async-done | bytes 294944 | tf_op jit(solution)/shard_map/all_to_all | solution.py:226
  71.1 3.5 %shard_map.121 = (bf16[512,1024]{1,0:T(8,128)(2,1)S(1)}, bf16[512,1024]{1,0:T(8,128)(2,1)S(1)}, bf16[4,144,128]{2,1,0:T(8,128)(2,1)S(1)}, f32[8,1024]{1,0:T(8,12...) custom-call(s32[6]{0:T(128)S(1)} %stack.27.pos_ref, ...), custom_call_target="tpu_custom_call" | custom-call | tf_op jit(solution)/shard_map/pallas_call | solution.py:213
  79.7 8.2 %all-to-all-start.2 = ((f32[64,1,128]{2,1,0:T(1,128)}), f32[64,1,128]{2,1,0:T(1,128)S(1)}, u32[]{:S(2)}, u32[]{:S(2)}) async-start(f32[64,1,128]{2,1,0:T(1,128)} %copy-done.9), calls=%async_computation.2 | async-start | bytes 65536 | tf_op jit(solution)/shard_map/all_to_all | solution.py:281
  88.7 11.5 %all-to-all-done.2.peaks_ref = f32[64,1,128]{2,1,0:T(1,128)S(1)} async-done(((f32[64,1,128]{2,1,0:T(1,128)}), f32[64,1,128]{2,1,0:T(1,128)S(1)}, u32[]{:S(2)}, u32[]{:S(2)}) %all-to-all-start.2) | async-done | bytes 32800 | tf_op jit(solution)/shard_map/all_to_all | solution.py:281
  103.6 3.3 %shard_map.122 = (f32[16,3,24,128]{3,2,1,0:T(8,128)}, f32[4,128,128]{2,1,0:T(8,128)S(1)}, f32[4,128,128]{2,1,0:T(8,128)S(1)}, f32[4,128,128]{2,1,0:T(8,128)S(1)}, f32[4,128,128]{2,1,0:T(8,128)S(1)}) custom-call(s32[6]{0:T(128)S(1)} %stack.27.pos_ref, bf16[512,1024]{1,0:T(8,128)(2,1)S(1)} %get-tuple-element.27.xs_ref, bf16[512,1024]{1,0:T(8,128)(2,1)S(1)} %copy-done.1, ...), custom_call_target="tpu_custom_call" | custom-call | tf_op jit(solution)/shard_map/pallas_call | solution.py:213
  109.0 3.7 %all-to-all-start.3 = ((f32[16,3,24,128]{3,2,1,0:T(8,128)}), f32[16,3,24,128]{3,2,1,0:T(8,128)S(1)}, u32[]{:S(2)}, u32[]{:S(2)}) async-start(f32[16,3,24,128]{3,2,1,0:T(8,128)} %get-tuple-element.34), calls=%async_computation.3 | async-start | bytes 1179648 | tf_op jit(solution)/shard_map/all_to_all | solution.py:291
  112.7 2.4 %collective-permute-start.3 = (f32[4,128,128]{2,1,0:T(8,128)S(1)}, f32[4,128,128]{2,1,0:T(8,128)S(1)}, u32[]{:S(2)}, u32[]{:S(2)}) collective-permute-start(f32[4,128,128]{2,1,0:T(8,128)S(1)} %copy-done.19), channel_id=1, source_target_pairs={{0,128},{128,256},{256,384},{384,0},{1,129},{129,257},{257,385},{3... | collective-permute-start | bytes 786440 | tf_op jit(solution)/shard_map/ppermute | solution.py:230
  115.2 4.6 %collective-permute-start.4 = (f32[4,128,128]{2,1,0:T(8,128)S(1)}, f32[4,128,128]{2,1,0:T(8,128)S(1)}, u32[]{:S(2)}, u32[]{:S(2)}) collective-permute-start(f32[4,128,128]{2,1,0:T(8,128)S(1)} %copy-done.17), channel_id=1, source_target_pairs={{0,256},{128,384},{256,0},{384,128},{1,257},{129,385},{257,1},{385... | collective-permute-start | bytes 786440 | tf_op jit(solution)/shard_map/ppermute | solution.py:230
  119.8 3.4 %collective-permute-start.5 = (f32[4,128,128]{2,1,0:T(8,128)S(1)}, f32[4,128,128]{2,1,0:T(8,128)S(1)}, u32[]{:S(2)}, u32[]{:S(2)}) collective-permute-start(f32[4,128,128]{2,1,0:T(8,128)S(1)} %copy-done.15), channel_id=1, source_target_pairs={{0,384},{128,0},{256,128},{384,256},{1,385},{129,1},{257,129},{385... | collective-permute-start | bytes 786440 | tf_op jit(solution)/shard_map/ppermute | solution.py:230
  125.1 3.9 %collective-permute-done.4.across_ref = f32[4,128,128]{2,1,0:T(8,128)S(1)} collective-permute-done((f32[4,128,128]{2,1,0:T(8,128)S(1)}, f32[4,128,128]{2,1,0:T(8,128)S(1)}, u32[]{:S(2)}, u32[]{:S(2)}) %collective-permute-start.4) | collective-permute-done | bytes 262176 | tf_op jit(solution)/shard_map/ppermute | solution.py:230
  129.1 2.5 %collective-permute-done.5.down_ref = f32[4,128,128]{2,1,0:T(8,128)S(1)} collective-permute-done((f32[4,128,128]{2,1,0:T(8,128)S(1)}, f32[4,128,128]{2,1,0:T(8,128)S(1)}, u32[]{:S(2)}, u32[]{:S(2)}) %collective-permute-start.5) | collective-permute-done | bytes 262176 | tf_op jit(solution)/shard_map/ppermute | solution.py:230
  131.6 11.8 %all-to-all-done.3.shares_ref = f32[16,3,24,128]{3,2,1,0:T(8,128)S(1)} async-done(((f32[16,3,24,128]{3,2,1,0:T(8,128)}), f32[16,3,24,128]{3,2,1,0:T(8,128)S(1)}, u32[]{:S(2)}, u32[]{:S(2)}) %all-to-all-start.3) | async-done | bytes 589856 | tf_op jit(solution)/shard_map/all_to_all | solution.py:291
  144.1 26.3 %all_to_all.30 = bf16[16,3,24,128]{3,2,1,0:T(8,128)(2,1)S(1)} all-to-all(bf16[16,3,24,128]{3,2,1,0:T(8,128)(2,1)S(1)} %broadcast_in_dim.30), channel_id=1, replica_groups=mesh['y'=4,'z'=16,'xh'=2,'xl'=2,'c'=2] {'z'}, dimensions={0} | all-to-all | bytes 589824 | tf_op jit(solution)/shard_map/all_to_all | solution.py:226
  171.7 6.0 %all-to-all-start.5 = ((bf16[32,2,3,24,128]{4,3,1,2,0:T(8,128)(2,1)}), bf16[32,2,3,24,128]{4,3,1,2,0:T(8,128)(2,1)S(1)}, u32[]{:S(2)}, u32[]{:S(2)}) async-start(bf16[32,2,3,24,128]{4,3,1,2,0:T(8,128)(2,1)} %bitcast.13), calls=%async_computation.5 | async-start | bytes 2359296 | tf_op jit(solution)/shard_map/all_to_all | solution.py:304
  177.6 3.4 %collective-permute-start.6 = (f32[128,128]{1,0:T(8,128)S(1)}, f32[128,128]{1,0:T(8,128)S(1)}, u32[]{:S(2)}, u32[]{:S(2)}) collective-permute-start(f32[128,128]{1,0:T(8,128)S(1)} %get-tuple-element.40), channel_id=1, source_target_pairs={{0,2},{2,4},{4,6},{6,0},{1,3},{3,5},{5,7},{7,1},{8,10},{10,12},{12... | collective-permute-start | bytes 196616 | tf_op jit(solution)/shard_map/ppermute | solution.py:230
  181.0 2.7 %collective-permute-start.7 = (f32[128,128]{1,0:T(8,128)S(1)}, f32[128,128]{1,0:T(8,128)S(1)}, u32[]{:S(2)}, u32[]{:S(2)}) collective-permute-start(f32[128,128]{1,0:T(8,128)S(1)} %get-tuple-element.41), channel_id=1, source_target_pairs={{0,4},{2,6},{4,0},{6,2},{1,5},{3,7},{5,1},{7,3},{8,12},{10,14},{12... | collective-permute-start | bytes 196616 | tf_op jit(solution)/shard_map/ppermute | solution.py:230
  183.8 4.3 %collective-permute-start.8 = (f32[128,128]{1,0:T(8,128)S(1)}, f32[128,128]{1,0:T(8,128)S(1)}, u32[]{:S(2)}, u32[]{:S(2)}) collective-permute-start(f32[128,128]{1,0:T(8,128)S(1)} %get-tuple-element.42), channel_id=1, source_target_pairs={{0,6},{2,0},{4,2},{6,4},{1,7},{3,1},{5,3},{7,5},{8,14},{10,8},{12,... | collective-permute-start | bytes 196616 | tf_op jit(solution)/shard_map/ppermute | solution.py:230
  188.1 6.8 %collective-permute-start.9 = (f32[3,3,24,128]{3,2,1,0:T(8,128)S(1)}, f32[3,3,24,128]{3,2,1,0:T(8,128)S(1)}, u32[]{:S(2)}, u32[]{:S(2)}) collective-permute-start(f32[3,3,24,128]{3,2,1,0:T(8,128)S(1)} %get-tuple-element.43), channel_id=1, source_target_pairs={{0,0},{1,16},{2,32},{3,48},{4,64},{5,80},{6,96},{7,112},{8,8},{9,2... | collective-permute-start | bytes 331784 | tf_op jit(solution)/shard_map/ppermute | solution.py:301
  196.3 15.8 %collective-permute-done.9 = f32[3,3,24,128]{3,2,1,0:T(8,128)S(1)} collective-permute-done((f32[3,3,24,128]{3,2,1,0:T(8,128)S(1)}, f32[3,3,24,128]{3,2,1,0:T(8,128)S(1)}, u32[]{:S(2)}, u32[]{:S(2)}) %collective-permute-start.9) | collective-permute-done | bytes 110624 | tf_op jit(solution)/shard_map/ppermute | solution.py:301
  (67 shorter events, 27.1 us)
Async XLA Ops:
  0.6 0.8 copy-start.4
  6.3 24.4 %all-to-all-start = ((bf16[16,272,128]{2,1,0:T(8,128)(2,1)}), bf16[16,272,128]{2,1,0:T(8,128)(2,1)S(1)}, u32[]{:S(2)}, u32[]{:S(2)}) async-start(bf16[16,272,128]{2,1,0:T(8,128)(2,1)} %get-tuple-element.25), calls=%async_computation | async-start | bytes 2228224 | tf_op jit(solution)/shard_map/all_to_all | solution.py:260
  15.6 22.9 %collective-permute-start.1 = (f32[3,3,24,128]{3,2,1,0:T(8,128)S(1)}, f32[3,3,24,128]{3,2,1,0:T(8,128)S(1)}, u32[]{:S(2)}, u32[]{:S(2)}) collective-permute-start(f32[3,3,24,128]{3,2,1,0:T(8,128)S(1)} %get-tuple-element.26), channel_id=1, source_target_pairs={{0,0},{1,16},{2,32},{3,48},{4,64},{5,80},{6,96},{7,112},{8,8},{9,2... | collective-permute-start | bytes 331784 | tf_op jit(solution)/shard_map/ppermute | solution.py:257
  30.7 40.4 %collective-permute-start = (bf16[16,272,128]{2,1,0:T(8,128)(2,1)S(1)}, bf16[16,272,128]{2,1,0:T(8,128)(2,1)S(1)}, u32[]{:S(2)}, u32[]{:S(2)}) collective-permute-start(bf16[16,272,128]{2,1,0:T(8,128)(2,1)S(1)} %all-to-all-done.own_ref), channel_id=1, source_target_pairs={{0,1},{1,0},{2,3},{3,2},{4,5},{5,4},{6,7},{7,6},{8,9},{9,8},{10,11... | collective-permute-start | bytes 3342344 | tf_op jit(solution)/shard_map/ppermute | solution.py:261
  39.4 31.5 %all-to-all-start.1 = ((bf16[16,3,24,128]{3,2,1,0:T(8,128)(2,1)}), bf16[16,3,24,128]{3,2,1,0:T(8,128)(2,1)S(1)}, u32[]{:S(2)}, u32[]{:S(2)}) async-start(bf16[16,3,24,128]{3,2,1,0:T(8,128)(2,1)} %broadcast_in_dim.13), calls=%async_computation.1 | async-start | bytes 589824 | tf_op jit(solution)/shard_map/all_to_all | solution.py:226
  71.1 29.2 %copy-start.12 = (s32[3,24]{1,0:T(4,128)S(1)}, s32[3,24]{1,0:T(4,128)}, u32[]{:S(2)}) copy-start(s32[3,24]{1,0:T(4,128)} %bits_ref.1) | copy-start | bytes 868
  74.6 1.0 copy-start
  75.6 1.0 copy-start.2
  77.8 22.5 %collective-permute-start.2 = (f32[16,128,128]{2,1,0:T(8,128)}, f32[16,128,128]{2,1,0:T(8,128)S(1)}, u32[]{:S(2)}, u32[]{:S(2)}) collective-permute-start(f32[16,128,128]{2,1,0:T(8,128)} %get-tuple-element.33), channel_id=1, source_target_pairs={{0,1},{1,0},{2,3},{3,2},{4,5},{5,4},{6,7},{7,6},{8,9},{9,8},{10,11... | collective-permute-start | bytes 3145736 | tf_op jit(solution)/shard_map/ppermute | solution.py:282
  79.7 20.6 %all-to-all-start.2 = ((f32[64,1,128]{2,1,0:T(1,128)}), f32[64,1,128]{2,1,0:T(1,128)S(1)}, u32[]{:S(2)}, u32[]{:S(2)}) async-start(f32[64,1,128]{2,1,0:T(1,128)} %copy-done.9), calls=%async_computation.2 | async-start | bytes 65536 | tf_op jit(solution)/shard_map/all_to_all | solution.py:281
  100.4 1.2 copy-start.1
  101.6 1.2 copy-start.3
  109.0 3.7 %copy-start.19 = (f32[4,128,128]{2,1,0:T(8,128)S(1)}, f32[4,128,128]{2,1,0:T(8,128)}, u32[]{:S(2)}) copy-start(f32[4,128,128]{2,1,0:T(8,128)} %copy-done.18) | copy-start | bytes 786436
  109.0 6.2 %copy-start.17 = (f32[4,128,128]{2,1,0:T(8,128)S(1)}, f32[4,128,128]{2,1,0:T(8,128)}, u32[]{:S(2)}) copy-start(f32[4,128,128]{2,1,0:T(8,128)} %copy-done.16) | copy-start | bytes 786436
  109.0 10.8 %copy-start.15 = (f32[4,128,128]{2,1,0:T(8,128)S(1)}, f32[4,128,128]{2,1,0:T(8,128)}, u32[]{:S(2)}) copy-start(f32[4,128,128]{2,1,0:T(8,128)} %copy-done.14) | copy-start | bytes 786436
  109.0 34.3 %all-to-all-start.3 = ((f32[16,3,24,128]{3,2,1,0:T(8,128)}), f32[16,3,24,128]{3,2,1,0:T(8,128)S(1)}, u32[]{:S(2)}, u32[]{:S(2)}) async-start(f32[16,3,24,128]{3,2,1,0:T(8,128)} %get-tuple-element.34), calls=%async_computation.3 | async-start | bytes 1179648 | tf_op jit(solution)/shard_map/all_to_all | solution.py:291
  112.7 12.4 %collective-permute-start.3 = (f32[4,128,128]{2,1,0:T(8,128)S(1)}, f32[4,128,128]{2,1,0:T(8,128)S(1)}, u32[]{:S(2)}, u32[]{:S(2)}) collective-permute-start(f32[4,128,128]{2,1,0:T(8,128)S(1)} %copy-done.19), channel_id=1, source_target_pairs={{0,128},{128,256},{256,384},{384,0},{1,129},{129,257},{257,385},{3... | collective-permute-start | bytes 786440 | tf_op jit(solution)/shard_map/ppermute | solution.py:230
  115.2 13.9 %collective-permute-start.4 = (f32[4,128,128]{2,1,0:T(8,128)S(1)}, f32[4,128,128]{2,1,0:T(8,128)S(1)}, u32[]{:S(2)}, u32[]{:S(2)}) collective-permute-start(f32[4,128,128]{2,1,0:T(8,128)S(1)} %copy-done.17), channel_id=1, source_target_pairs={{0,256},{128,384},{256,0},{384,128},{1,257},{129,385},{257,1},{385... | collective-permute-start | bytes 786440 | tf_op jit(solution)/shard_map/ppermute | solution.py:230
  119.8 11.8 %collective-permute-start.5 = (f32[4,128,128]{2,1,0:T(8,128)S(1)}, f32[4,128,128]{2,1,0:T(8,128)S(1)}, u32[]{:S(2)}, u32[]{:S(2)}) collective-permute-start(f32[4,128,128]{2,1,0:T(8,128)S(1)} %copy-done.15), channel_id=1, source_target_pairs={{0,384},{128,0},{256,128},{384,256},{1,385},{129,1},{257,129},{385... | collective-permute-start | bytes 786440 | tf_op jit(solution)/shard_map/ppermute | solution.py:230
  171.7 41.1 %all-to-all-start.5 = ((bf16[32,2,3,24,128]{4,3,1,2,0:T(8,128)(2,1)}), bf16[32,2,3,24,128]{4,3,1,2,0:T(8,128)(2,1)S(1)}, u32[]{:S(2)}, u32[]{:S(2)}) async-start(bf16[32,2,3,24,128]{4,3,1,2,0:T(8,128)(2,1)} %bitcast.13), calls=%async_computation.5 | async-start | bytes 2359296 | tf_op jit(solution)/shard_map/all_to_all | solution.py:304
  177.6 17.3 %collective-permute-start.6 = (f32[128,128]{1,0:T(8,128)S(1)}, f32[128,128]{1,0:T(8,128)S(1)}, u32[]{:S(2)}, u32[]{:S(2)}) collective-permute-start(f32[128,128]{1,0:T(8,128)S(1)} %get-tuple-element.40), channel_id=1, source_target_pairs={{0,2},{2,4},{4,6},{6,0},{1,3},{3,5},{5,7},{7,1},{8,10},{10,12},{12... | collective-permute-start | bytes 196616 | tf_op jit(solution)/shard_map/ppermute | solution.py:230
  181.0 14.3 %collective-permute-start.7 = (f32[128,128]{1,0:T(8,128)S(1)}, f32[128,128]{1,0:T(8,128)S(1)}, u32[]{:S(2)}, u32[]{:S(2)}) collective-permute-start(f32[128,128]{1,0:T(8,128)S(1)} %get-tuple-element.41), channel_id=1, source_target_pairs={{0,4},{2,6},{4,0},{6,2},{1,5},{3,7},{5,1},{7,3},{8,12},{10,14},{12... | collective-permute-start | bytes 196616 | tf_op jit(solution)/shard_map/ppermute | solution.py:230
  183.8 11.9 %collective-permute-start.8 = (f32[128,128]{1,0:T(8,128)S(1)}, f32[128,128]{1,0:T(8,128)S(1)}, u32[]{:S(2)}, u32[]{:S(2)}) collective-permute-start(f32[128,128]{1,0:T(8,128)S(1)} %get-tuple-element.42), channel_id=1, source_target_pairs={{0,6},{2,0},{4,2},{6,4},{1,7},{3,1},{5,3},{7,5},{8,14},{10,8},{12,... | collective-permute-start | bytes 196616 | tf_op jit(solution)/shard_map/ppermute | solution.py:230
  188.1 24.0 %collective-permute-start.9 = (f32[3,3,24,128]{3,2,1,0:T(8,128)S(1)}, f32[3,3,24,128]{3,2,1,0:T(8,128)S(1)}, u32[]{:S(2)}, u32[]{:S(2)}) collective-permute-start(f32[3,3,24,128]{3,2,1,0:T(8,128)S(1)} %get-tuple-element.43), channel_id=1, source_target_pairs={{0,0},{1,16},{2,32},{3,48},{4,64},{5,80},{6,96},{7,112},{8,8},{9,2... | collective-permute-start | bytes 331784 | tf_op jit(solution)/shard_map/ppermute | solution.py:301
  (11 other events, 7.8 us)

commit v3 on v2

--- a/solution.py
+++ b/solution.py
@@ -32,11 +32,13 @@
     -1.95303213596344,
 )
 
-DP = ("y", "z")
+Z = ("zh", "zl")
+DP = ("y",) + Z
 TENSOR = ("xh", "xl", "c")
-SIZES = (4, 16, 2, 2, 2)
-
-VMEM_LIMIT = 20 * 1024 * 1024
+SIZES = (4, 4, 4, 2, 2, 2)
+
+SMALL_LIMIT = 20 * 1024 * 1024
+LARGE_LIMIT = 60 * 1024 * 1024
 
 
 def turn(value):
@@ -81,7 +83,16 @@
     coded_ref[...] = eightbit_f32(state_ref[0])
 
 
-def front_kernel(pos_ref, own_ref, other_ref, weights_ref, xs_ref, gs_ref, terms_ref, col_ref, peak_ref, keep_ref, give_ref):
+def spread_kernel(own_ref, *refs):
+    parts, (_, out_ref, wide_ref) = refs[:4], refs[4:]
+    for step, part in enumerate(parts):
+        wide_ref[step * 3 * SHARD : (step + 1) * 3 * SHARD, :] = part[...].astype(F32)
+    narrow = wide_ref[...].astype(BF16)
+    for peer in range(4):
+        out_ref[peer] = narrow
+
+
+def front_kernel(pos_ref, own_ref, other_ref, rows_ref, xs_ref, gs_ref, terms_ref, col_ref, peak_ref, keep_ref, give_ref, wide_ref, full_ref, weights_ref):
     core = pos_ref[0]
     for chip in range(4):
         for source, which in ((own_ref, core), (other_ref, 1 - core)):
@@ -93,6 +104,16 @@
             pair = source[chip, 2 * TOK : 2 * TOK + 16, :].astype(F32)
             dither = pair[0:1] * 8.0 + pair[1:2]
             col_ref[:, cols] = jnp.broadcast_to(dither * (1.0 / 1024.0), (8, COLS))
+    wide_ref[...] = rows_ref[...].astype(F32)
+    for low in range(4):
+        for step in range(4):
+            column = 2 * ((pos_ref[6] + 4 - step) % 4) + low // 2
+            cols = pl.ds(pl.multiple_of(column * COLS, COLS), COLS)
+            for mat in range(3):
+                source = ((low * 4 + step) * 3 + mat) * SHARD
+                target = mat * BLOCK + (low % 2) * SHARD
+                full_ref[target : target + SHARD, cols] = wide_ref[source : source + SHARD, :]
+    weights_ref[...] = full_ref[...].astype(BF16)
     front = dot(weights_ref[0 : 2 * BLOCK, :], xs_ref[...], 1, 1)
     delta = dot(weights_ref[2 * BLOCK : 3 * BLOCK, :], gs_ref[...], 1, 1)
     gate = front[0:BLOCK]
@@ -208,13 +229,40 @@
     coded_ref[...] = eightbit_f32(updated)
 
 
-def call(kernel, out_shape, smem=0, operands=()):
-    specs = [pl.BlockSpec(memory_space=pltpu.SMEM if i < smem else pltpu.VMEM) for i in range(len(operands))]
+def call(kernel, out_shape, smem=0, operands=(), scratch=(), limit=SMALL_LIMIT):
+    single = not isinstance(out_shape, tuple)
+    outs = (out_shape,) if single else out_shape
+    n_in = len(operands) - smem
+    n_out = len(outs)
+
+    def body(*refs):
+        small = refs[:smem]
+        sources = refs[smem : smem + n_in]
+        targets = refs[smem + n_in : smem + n_in + n_out]
+        held = refs[smem + n_in + n_out :]
+        taken, made, rest, sems = held[:n_in], held[n_in : n_in + n_out], held[n_in + n_out : -1], held[-1]
+        loads = [pltpu.make_async_copy(sources[i], taken[i], sems.at[i]) for i in range(n_in)]
+        for load in loads:
+            load.start()
+        for load in loads:
+            load.wait()
+        kernel(*small, *taken, *made, *rest)
+        stores = [pltpu.make_async_copy(made[i], targets[i], sems.at[n_in + i]) for i in range(n_out)]
+        for store in stores:
+            store.start()
+        for store in stores:
+            store.wait()
+
+    anywhere = pl.BlockSpec(memory_space=pl.ANY)
+    specs = [pl.BlockSpec(memory_space=pltpu.SMEM)] * smem + [anywhere] * n_in
+    buffers = [pltpu.VMEM(item.shape, item.dtype) for item in tuple(operands[smem:]) + outs]
     return pl.pallas_call(
-        kernel,
+        body,
         out_shape=out_shape,
         in_specs=specs,
-        compiler_params=pltpu.CompilerParams(vmem_limit_bytes=VMEM_LIMIT),
+        out_specs=anywhere if single else (anywhere,) * n_out,
+        scratch_shapes=buffers + list(scratch) + [pltpu.SemaphoreType.DMA((n_in + n_out,))],
+        compiler_params=pltpu.CompilerParams(vmem_limit_bytes=limit),
     )(*operands)
 
 
@@ -240,12 +288,12 @@
 
 def on_device(acts, grad_out, master, moment_one, moment_two, bit_widths, row_dither, col_dither):
     y = lax.axis_index("y")
-    z = lax.axis_index("z")
+    z = lax.axis_index(Z)
     core = lax.axis_index("c")
     tensor = lax.axis_index(TENSOR)
     spot = tensor % 4
     unit = 2 * y + tensor // 4
-    pos = jnp.stack([core, spot, unit, z, y, tensor // 2]).astype(jnp.int32)
+    pos = jnp.stack([core, spot, unit, z, y, tensor // 2, z // 4]).astype(jnp.int32)
     pairs = swap_pairs()
 
     packed, state = call(
@@ -253,14 +301,25 @@
         (struct((16, 2 * TOK + 16, COLS), BF16), struct((3, 3, SHARD, COLS))),
         0,
         (acts, grad_out, col_dither[None], master, moment_one, moment_two),
-    )
-    state = lax.ppermute(state, ("z",) + TENSOR, pairs)
+        limit=LARGE_LIMIT,
+    )
+    state = lax.ppermute(state, Z + TENSOR, pairs)
     coded = call(code_kernel, struct((3, SHARD, COLS)), 0, (state,))
-    rows = to_all(coded.astype(BF16), "z", 16)
+    coded = coded.astype(BF16).reshape(3 * SHARD, COLS)
+    parts = [coded] + [shift(coded, "zh", step) for step in (1, 2, 3)]
     own = lax.all_to_all(packed, ("y", "xh", "xl"), 0, 0)
+    own, rows = pl.pallas_call(
+        spread_kernel,
+        out_shape=(struct(own.shape, BF16), struct((4, 12 * SHARD, COLS), BF16)),
+        in_specs=[pl.BlockSpec(memory_space=pl.ANY)] + [pl.BlockSpec(memory_space=pltpu.VMEM)] * 4,
+        out_specs=(pl.BlockSpec(memory_space=pl.ANY), pl.BlockSpec(memory_space=pltpu.VMEM)),
+        scratch_shapes=[pltpu.VMEM((12 * SHARD, COLS), F32)],
+        input_output_aliases={0: 0},
+        compiler_params=pltpu.CompilerParams(vmem_limit_bytes=SMALL_LIMIT),
+    )(own, *parts)
+    rows = lax.all_to_all(rows, "zl", 0, 0).reshape(16 * 3 * SHARD, COLS)
     other = lax.ppermute(own, "c", [(0, 1), (1, 0)])
 
-    rows = rows.reshape(8, 2, 3, SHARD, COLS).transpose(2, 1, 3, 0, 4).reshape(3 * BLOCK, 8 * COLS)
     row_part = lax.dynamic_slice(row_dither, (0, BLOCK * (8 * y + tensor)), (3, BLOCK))
     row_part = jnp.broadcast_to(row_part.astype(F32).reshape(3 * BLOCK, 1) * (1.0 / 1024.0), (3 * BLOCK, COLS))
 
@@ -277,8 +336,14 @@
         ),
         1,
         (pos, own, other, rows),
-    )
-    peaks = lax.all_to_all(peak, ("xl", "c", "z"), 0, 0)
+        (
+            pltpu.VMEM((48 * SHARD, COLS), F32),
+            pltpu.VMEM((3 * BLOCK, 1024), F32),
+            pltpu.VMEM((3 * BLOCK, 1024), BF16),
+        ),
+        limit=LARGE_LIMIT,
+    )
+    peaks = lax.all_to_all(peak, ("xl", "c") + Z, 0, 0)
     got = lax.ppermute(give, "c", [(0, 1), (1, 0)])
 
     shares, *back = call(
@@ -286,9 +351,10 @@
         (struct((16, 3, SHARD, COLS)),) + (struct((4, TOK, COLS)),) * 4,
         1,
         (pos, xs, gs, terms, peaks, bit_widths, row_part, col_part, keep, got),
+        limit=LARGE_LIMIT,
     )
     back = [back[0]] + [shift(back[step], "y", step) for step in (1, 2, 3)]
-    shares = lax.all_to_all(shares, "z", 0, 0)
+    shares = lax.all_to_all(shares, Z, 0, 0)
 
     new_state, new_coded, *back = call(
         adam_kernel,
@@ -297,8 +363,8 @@
         (pos, shares, state, *back),
     )
     back = [back[0]] + [shift(back[step], ("xh", "xl"), step) for step in (1, 2, 3)]
-    ring = to_all(new_coded.astype(BF16), "z", 16)
-    new_state = lax.ppermute(new_state, ("z",) + TENSOR, pairs)
+    ring = to_all(new_coded.astype(BF16), Z, 16)
+    new_state = lax.ppermute(new_state, Z + TENSOR, pairs)
     grad_in = ((back[0] + back[1]) + (back[2] + back[3])).astype(BF16)
     ring = jnp.broadcast_to(ring.reshape(1, 8, 2, 3, SHARD, COLS), (4, 8, 2, 3, SHARD, COLS))
     ring = lax.all_to_all(ring.reshape(32, 2, 3, SHARD, COLS), ("y",) + TENSOR, 0, 0)

time: 215 us -> 224 us (1.042)
  starting transfers between devices: 76 us -> 94.1 us
  local copies, waits for them, and re-layouts: 17.2 us -> 5.93 us
  Pallas kernels: 8.75 us -> 16.8 us
  waiting for transfers between devices: 83.3 us -> 77.7 us
    ppermute x6 -> x9, starting transfers between devices: 20.8 us -> 39.5 us  [shift(): return lax.ppermute(value, axes, [(i, (i + step) % 4) for i in range(4)])]
    unnamed x41 -> x22, local copies, waits for them, and re-layouts: 13.1 us -> 1.28 us
    all_to_all x3, waiting for transfers between devices: 44.2 us -> 32.7 us  [the longest x1 11.6 us: on_device(): shares = lax.all_to_all(shares, Z, 0, 0)]
    ppermute x2, waiting for transfers between devices: 21.8 us -> 31.4 us  [the longest x1 16.2 us: on_device(): state = lax.ppermute(state, Z + TENSOR, pairs)]
    all_to_all x1, waiting for transfers between devices: 8.33 us -> 0.01 us  [on_device(): own = lax.all_to_all(packed, ('y', 'xh', 'xl'), 0, 0)]
    pallas_call x5 -> x6, Pallas kernels: 8.75 us -> 16.8 us  [the longest x5 16 us: call(): pl.pallas_call(body, out_shape=out_shape, in_specs=specs, out_specs=anywh...]
    ppermute x6 -> x9, waiting for transfers between devices: 9.09 us -> 13.6 us  [shift(): return lax.ppermute(value, axes, [(i, (i + step) % 4) for i in range(4)])]
    all_to_all x3, starting transfers between devices: 22.4 us -> 18.5 us  [the longest x1 10.9 us: on_device(): peaks = lax.all_to_all(peak, ('xl', 'c') + Z, 0, 0)]
  transfers between devices with their start and end apart: 15 -> 18, of which waited for: 11 -> 10; matrix products, arithmetic and copies ran while one was open for 1% -> 1% of each run, Pallas kernels for 0% -> 0%
where the time goes in v3:
time: 224 us; the launch traced here: 223 us
  starting transfers between devices  94.1 us (42%)
  waiting for transfers between devices  77.7 us (35%)
  blocking collectives  26.4 us (12%)
  Pallas kernels  16.8 us (8%)
  local copies, waits for them, and re-layouts  5.93 us (3%)
    ppermute x9, starting transfers between devices, shift(): return lax.ppermute(value, axes, [(i, (i + step) % 4) for i in range(4)])  39.5 us
    all_to_all x1, blocking collectives, to_all(): lax.all_to_all(jnp.broadcast_to(value[None], (peers,) + value.shape), axe...  26.4 us
    ppermute x1, waiting for transfers between devices, on_device(): state = lax.ppermute(state, Z + TENSOR, pairs)  16.2 us
    pallas_call x5, Pallas kernels, call(): pl.pallas_call(body, out_shape=out_shape, in_specs=specs, out_specs=anywh...  16 us
    ppermute x1, waiting for transfers between devices, on_device(): new_state = lax.ppermute(new_state, Z + TENSOR, pairs)  15.2 us
    ppermute x9, waiting for transfers between devices, shift(): return lax.ppermute(value, axes, [(i, (i + step) % 4) for i in range(4)])  13.6 us
    all_to_all x1, waiting for transfers between devices, on_device(): shares = lax.all_to_all(shares, Z, 0, 0)  11.6 us
    all_to_all x1, waiting for transfers between devices, on_device(): peaks = lax.all_to_all(peak, ('xl', 'c') + Z, 0, 0)  11.5 us
  transfers between devices with their start and end apart: 18, of which 10 were waited for; matrix products, arithmetic and copies ran while one was open for 1% of the time, Pallas kernels for 0%

profile of v3, /device:TPU:2, one launch (start us, length us, event | category | flops | bytes accessed | tf_op | source)
XLA Modules:
  0.0 223.3 jit_solution(10773718508649843129)
XLA Ops:
  2.7 9.5 %all-to-all-start = ((bf16[16,272,128]{2,1,0:T(8,128)(2,1)}), bf16[16,272,128]{2,1,0:T(8,128)(2,1)S(1)}, u32[]{:S(2)}, u32[]{:S(2)}) async-start(bf16[16,272,128]{2,1,0:T(8,128)(2,1)} %get-tuple-element.27), calls=%async_computation | async-start | bytes 2228224 | tf_op jit(solution)/shard_map/all_to_all | solution.py:310
  12.3 6.7 %collective-permute-start = (f32[3,3,24,128]{3,2,1,0:T(8,128)S(1)}, f32[3,3,24,128]{3,2,1,0:T(8,128)S(1)}, u32[]{:S(2)}, u32[]{:S(2)}) collective-permute-start(f32[3,3,24,128]{3,2,1,0:T(8,128)S(1)} %copy-done.10), channel_id=1, source_target_pairs={{0,0},{1,16},{2,32},{3,48},{4,64},{5,80},{6,96},{7,112},{8,8},{9,2... | collective-permute-start | bytes 331784 | tf_op jit(solution)/shard_map/ppermute | solution.py:306
  19.0 16.2 %collective-permute-done.refs_0_.refs_2_ = f32[3,3,24,128]{3,2,1,0:T(8,128)S(1)} collective-permute-done((f32[3,3,24,128]{3,2,1,0:T(8,128)S(1)}, f32[3,3,24,128]{3,2,1,0:T(8,128)S(1)}, u32[]{:S(2)}, u32[]{:S(2)}) %collective-permute-start) | collective-permute-done | bytes 110624 | tf_op jit(solution)/shard_map/ppermute | solution.py:306
  37.4 11.3 %collective-permute-start.2 = (bf16[72,128]{1,0:T(8,128)(2,1)S(1)}, bf16[72,128]{1,0:T(8,128)(2,1)S(1)}, u32[]{:S(2)}, u32[]{:S(2)}) collective-permute-start(bf16[72,128]{1,0:T(8,128)(2,1)S(1)} %bitcast.22), channel_id=1, source_target_pairs={{0,64},{32,96},{64,0},{96,32},{1,65},{33,97},{65,1},{97,33},{2,66}... | collective-permute-start | bytes 55304 | tf_op jit(solution)/shard_map/ppermute | solution.py:278
  48.7 4.6 %collective-permute-start.3 = (bf16[72,128]{1,0:T(8,128)(2,1)S(1)}, bf16[72,128]{1,0:T(8,128)(2,1)S(1)}, u32[]{:S(2)}, u32[]{:S(2)}) collective-permute-start(bf16[72,128]{1,0:T(8,128)(2,1)S(1)} %bitcast.23), channel_id=1, source_target_pairs={{0,96},{32,0},{64,32},{96,64},{1,97},{33,1},{65,33},{97,65},{2,98}... | collective-permute-start | bytes 55304 | tf_op jit(solution)/shard_map/ppermute | solution.py:278
  53.4 5.1 %collective-permute-done.3.refs_3_ = bf16[72,128]{1,0:T(8,128)(2,1)S(1)} collective-permute-done((bf16[72,128]{1,0:T(8,128)(2,1)S(1)}, bf16[72,128]{1,0:T(8,128)(2,1)S(1)}, u32[]{:S(2)}, u32[]{:S(2)}) %collective-permute-start.3) | collective-permute-done | bytes 18464 | tf_op jit(solution)/shard_map/ppermute | solution.py:278
  61.1 3.9 %all-to-all-start.1 = ((bf16[4,288,128]{2,1,0:T(8,128)(2,1)}), bf16[4,288,128]{2,1,0:T(8,128)(2,1)S(1)}, u32[]{:S(2)}, u32[]{:S(2)}) async-start(bf16[4,288,128]{2,1,0:T(8,128)(2,1)} %get-tuple-element.30), calls=%async_computation.1 | async-start | bytes 589824 | tf_op jit(solution)/shard_map/all_to_all | solution.py:320
  65.6 9.6 %all-to-all-done.1 = bf16[4,288,128]{2,1,0:T(8,128)(2,1)S(1)} async-done(((bf16[4,288,128]{2,1,0:T(8,128)(2,1)}), bf16[4,288,128]{2,1,0:T(8,128)(2,1)S(1)}, u32[]{:S(2)}, u32[]{:S(2)}) %all-to-all-start.1) | async-done | bytes 294944 | tf_op jit(solution)/shard_map/all_to_all | solution.py:320
  76.4 5.9 %shard_map.122 = (bf16[512,1024]{1,0:T(8,128)(2,1)}, bf16[512,1024]{1,0:T(8,128)(2,1)}, bf16[4,144,128]{2,1,0:T(8,128)(2,1)}, f32[8,1024]{1,0:T(8,128)}, f32[64,...) custom-call(s32[7]{0:T(128)} %stack.31.refs_0_, bf16[16,272,128]{2,1,0:T(8,128)(2,1)} %copy-done, ...), custom_call_target="tpu_custom_call" | custom-call | tf_op jit(solution)/shard_map/pallas_call | solution.py:259
  84.2 10.9 %all-to-all-start.2 = ((f32[64,1,128]{2,1,0:T(1,128)}), f32[64,1,128]{2,1,0:T(1,128)S(1)}, u32[]{:S(2)}, u32[]{:S(2)}) async-start(f32[64,1,128]{2,1,0:T(1,128)} %get-tuple-element.34), calls=%async_computation.2 | async-start | bytes 65536 | tf_op jit(solution)/shard_map/all_to_all | solution.py:346
  96.0 11.5 %all-to-all-done.2.refs_4_ = f32[64,1,128]{2,1,0:T(1,128)S(1)} async-done(((f32[64,1,128]{2,1,0:T(1,128)}), f32[64,1,128]{2,1,0:T(1,128)S(1)}, u32[]{:S(2)}, u32[]{:S(2)}) %all-to-all-start.2) | async-done | bytes 32800 | tf_op jit(solution)/shard_map/all_to_all | solution.py:346
  108.5 6.1 %shard_map.123 = (f32[16,3,24,128]{3,2,1,0:T(8,128)}, f32[4,128,128]{2,1,0:T(8,128)}, f32[4,128,128]{2,1,0:T(8,128)}, f32[4,128,128]{2,1,0:T(8,128)}, f32[4,128,128]{2,1,0:T(8,128)}) custom-call(s32[7]{0:T(128)} %stack.31.refs_0_, bf16[512,1024]{1,0:T(8,128)(2,1)} %get-tuple-element.31.refs_1_, bf16[512,1024]{1,0:T(8,128)(2,1)} %get-tuple-element.32.refs_2_, ...), custom_call_target="tpu_custom_call" | custom-call | tf_op jit(solution)/shard_map/pallas_call | solution.py:259
  114.6 3.7 %all-to-all-start.3 = ((f32[16,3,24,128]{3,2,1,0:T(8,128)}), f32[16,3,24,128]{3,2,1,0:T(8,128)S(1)}, u32[]{:S(2)}, u32[]{:S(2)}) async-start(f32[16,3,24,128]{3,2,1,0:T(8,128)} %get-tuple-element.38), calls=%async_computation.3 | async-start | bytes 1179648 | tf_op jit(solution)/shard_map/all_to_all | solution.py:357
  118.4 3.8 %collective-permute-start.6 = (f32[4,128,128]{2,1,0:T(8,128)S(1)}, f32[4,128,128]{2,1,0:T(8,128)S(1)}, u32[]{:S(2)}, u32[]{:S(2)}) collective-permute-start(f32[4,128,128]{2,1,0:T(8,128)S(1)} %copy-done.9), channel_id=1, source_target_pairs={{0,128},{128,256},{256,384},{384,0},{1,129},{129,257},{257,385},{3... | collective-permute-start | bytes 786440 | tf_op jit(solution)/shard_map/ppermute | solution.py:278
  122.2 4.6 %collective-permute-start.7 = (f32[4,128,128]{2,1,0:T(8,128)S(1)}, f32[4,128,128]{2,1,0:T(8,128)S(1)}, u32[]{:S(2)}, u32[]{:S(2)}) collective-permute-start(f32[4,128,128]{2,1,0:T(8,128)S(1)} %copy-done.8), channel_id=1, source_target_pairs={{0,256},{128,384},{256,0},{384,128},{1,257},{129,385},{257,1},{385... | collective-permute-start | bytes 786440 | tf_op jit(solution)/shard_map/ppermute | solution.py:278
  126.8 3.4 %collective-permute-start.8 = (f32[4,128,128]{2,1,0:T(8,128)S(1)}, f32[4,128,128]{2,1,0:T(8,128)S(1)}, u32[]{:S(2)}, u32[]{:S(2)}) collective-permute-start(f32[4,128,128]{2,1,0:T(8,128)S(1)} %copy-done.7), channel_id=1, source_target_pairs={{0,384},{128,0},{256,128},{384,256},{1,385},{129,1},{257,129},{385... | collective-permute-start | bytes 786440 | tf_op jit(solution)/shard_map/ppermute | solution.py:278
  130.2 5.8 %collective-permute-done.7.refs_5_ = f32[4,128,128]{2,1,0:T(8,128)S(1)} collective-permute-done((f32[4,128,128]{2,1,0:T(8,128)S(1)}, f32[4,128,128]{2,1,0:T(8,128)S(1)}, u32[]{:S(2)}, u32[]{:S(2)}) %collective-permute-start.7) | collective-permute-done | bytes 262176 | tf_op jit(solution)/shard_map/ppermute | solution.py:278
  137.4 11.6 %all-to-all-done.3.refs_1_ = f32[16,3,24,128]{3,2,1,0:T(8,128)S(1)} async-done(((f32[16,3,24,128]{3,2,1,0:T(8,128)}), f32[16,3,24,128]{3,2,1,0:T(8,128)S(1)}, u32[]{:S(2)}, u32[]{:S(2)}) %all-to-all-start.3) | async-done | bytes 589856 | tf_op jit(solution)/shard_map/all_to_all | solution.py:357
  150.8 26.4 %all_to_all.30 = bf16[16,3,24,128]{3,2,1,0:T(8,128)(2,1)S(1)} all-to-all(bf16[16,3,24,128]{3,2,1,0:T(8,128)(2,1)S(1)} %broadcast_in_dim.23), channel_id=1, replica_groups=mesh['y'=4,'zh'=4,'zl'=4,'xh'=2,'xl'=2,'c'=2] {'zh','zl'}, dimensions={0} | all-to-all | bytes 589824 | tf_op jit(solution)/shard_map/all_to_all | solution.py:274
  178.3 9.3 %all-to-all-start.5 = ((bf16[32,2,3,24,128]{4,3,1,2,0:T(8,128)(2,1)}), bf16[32,2,3,24,128]{4,3,1,2,0:T(8,128)(2,1)S(1)}, u32[]{:S(2)}, u32[]{:S(2)}) async-start(bf16[32,2,3,24,128]{4,3,1,2,0:T(8,128)(2,1)} %bitcast.14), calls=%async_computation.5 | async-start | bytes 2359296 | tf_op jit(solution)/shard_map/all_to_all | solution.py:370
  187.6 4.0 %collective-permute-start.10 = (f32[128,128]{1,0:T(8,128)S(1)}, f32[128,128]{1,0:T(8,128)S(1)}, u32[]{:S(2)}, u32[]{:S(2)}) collective-permute-start(f32[128,128]{1,0:T(8,128)S(1)} %get-tuple-element.45), channel_id=1, source_target_pairs={{0,4},{2,6},{4,0},{6,2},{1,5},{3,7},{5,1},{7,3},{8,12},{10,14},{12... | collective-permute-start | bytes 196616 | tf_op jit(solution)/shard_map/ppermute | solution.py:278
  191.6 3.4 %collective-permute-start.11 = (f32[128,128]{1,0:T(8,128)S(1)}, f32[128,128]{1,0:T(8,128)S(1)}, u32[]{:S(2)}, u32[]{:S(2)}) collective-permute-start(f32[128,128]{1,0:T(8,128)S(1)} %get-tuple-element.46), channel_id=1, source_target_pairs={{0,6},{2,0},{4,2},{6,4},{1,7},{3,1},{5,3},{7,5},{8,14},{10,8},{12,... | collective-permute-start | bytes 196616 | tf_op jit(solution)/shard_map/ppermute | solution.py:278
  197.4 6.8 %collective-permute-start.12 = (f32[3,3,24,128]{3,2,1,0:T(8,128)S(1)}, f32[3,3,24,128]{3,2,1,0:T(8,128)S(1)}, u32[]{:S(2)}, u32[]{:S(2)}) collective-permute-start(f32[3,3,24,128]{3,2,1,0:T(8,128)S(1)} %get-tuple-element.47), channel_id=1, source_target_pairs={{0,0},{1,16},{2,32},{3,48},{4,64},{5,80},{6,96},{7,112},{8,8},{9,2... | collective-permute-start | bytes 331784 | tf_op jit(solution)/shard_map/ppermute | solution.py:367
  206.2 15.2 %collective-permute-done.12 = f32[3,3,24,128]{3,2,1,0:T(8,128)S(1)} collective-permute-done((f32[3,3,24,128]{3,2,1,0:T(8,128)S(1)}, f32[3,3,24,128]{3,2,1,0:T(8,128)S(1)}, u32[]{:S(2)}, u32[]{:S(2)}) %collective-permute-start.12) | collective-permute-done | bytes 110624 | tf_op jit(solution)/shard_map/ppermute | solution.py:367
  (53 shorter events, 23.0 us)
Async XLA Ops:
  2.7 9.6 %copy-start.10 = (f32[3,3,24,128]{3,2,1,0:T(8,128)S(1)}, f32[3,3,24,128]{3,2,1,0:T(8,128)}, u32[]{:S(2)}) copy-start(f32[3,3,24,128]{3,2,1,0:T(8,128)} %get-tuple-element.28) | copy-start | bytes 331780
  2.7 55.8 %all-to-all-start = ((bf16[16,272,128]{2,1,0:T(8,128)(2,1)}), bf16[16,272,128]{2,1,0:T(8,128)(2,1)S(1)}, u32[]{:S(2)}, u32[]{:S(2)}) async-start(bf16[16,272,128]{2,1,0:T(8,128)(2,1)} %get-tuple-element.27), calls=%async_computation | async-start | bytes 2228224 | tf_op jit(solution)/shard_map/all_to_all | solution.py:310
  12.3 22.9 %collective-permute-start = (f32[3,3,24,128]{3,2,1,0:T(8,128)S(1)}, f32[3,3,24,128]{3,2,1,0:T(8,128)S(1)}, u32[]{:S(2)}, u32[]{:S(2)}) collective-permute-start(f32[3,3,24,128]{3,2,1,0:T(8,128)S(1)} %copy-done.10), channel_id=1, source_target_pairs={{0,0},{1,16},{2,32},{3,48},{4,64},{5,80},{6,96},{7,112},{8,8},{9,2... | collective-permute-start | bytes 331784 | tf_op jit(solution)/shard_map/ppermute | solution.py:306
  35.5 17.9 %collective-permute-start.1 = (bf16[72,128]{1,0:T(8,128)(2,1)S(1)}, bf16[72,128]{1,0:T(8,128)(2,1)S(1)}, u32[]{:S(2)}, u32[]{:S(2)}) collective-permute-start(bf16[72,128]{1,0:T(8,128)(2,1)S(1)} %bitcast.21), channel_id=1, source_target_pairs={{0,32},{32,64},{64,96},{96,0},{1,33},{33,65},{65,97},{97,1},{2,34}... | collective-permute-start | bytes 55304 | tf_op jit(solution)/shard_map/ppermute | solution.py:278
  37.4 16.0 %collective-permute-start.2 = (bf16[72,128]{1,0:T(8,128)(2,1)S(1)}, bf16[72,128]{1,0:T(8,128)(2,1)S(1)}, u32[]{:S(2)}, u32[]{:S(2)}) collective-permute-start(bf16[72,128]{1,0:T(8,128)(2,1)S(1)} %bitcast.22), channel_id=1, source_target_pairs={{0,64},{32,96},{64,0},{96,32},{1,65},{33,97},{65,1},{97,33},{2,66}... | collective-permute-start | bytes 55304 | tf_op jit(solution)/shard_map/ppermute | solution.py:278
  48.7 9.8 %collective-permute-start.3 = (bf16[72,128]{1,0:T(8,128)(2,1)S(1)}, bf16[72,128]{1,0:T(8,128)(2,1)S(1)}, u32[]{:S(2)}, u32[]{:S(2)}) collective-permute-start(bf16[72,128]{1,0:T(8,128)(2,1)S(1)} %bitcast.23), channel_id=1, source_target_pairs={{0,96},{32,0},{64,32},{96,64},{1,97},{33,1},{65,33},{97,65},{2,98}... | collective-permute-start | bytes 55304 | tf_op jit(solution)/shard_map/ppermute | solution.py:278
  59.2 16.0 %copy-start = (bf16[16,272,128]{2,1,0:T(8,128)(2,1)}, bf16[16,272,128]{2,1,0:T(8,128)(2,1)S(1)}, u32[]{:S(2)}) copy-start(bf16[16,272,128]{2,1,0:T(8,128)(2,1)S(1)} %get-tuple-element.29.refs_1_) | copy-start | bytes 3342340
  59.2 16.0 %collective-permute-start.4 = (bf16[16,272,128]{2,1,0:T(8,128)(2,1)S(1)}, bf16[16,272,128]{2,1,0:T(8,128)(2,1)S(1)}, u32[]{:S(2)}, u32[]{:S(2)}) collective-permute-start(bf16[16,272,128]{2,1,0:T(8,128)(2,1)S(1)} %get-tuple-element.29.refs_1_), channel_id=1, source_target_pairs={{0,1},{1,0},{2,3},{3,2},{4,5},{5,4},{6,7},{7,6},{8,9},{9,8},{10,11... | collective-permute-start | bytes 3342344 | tf_op jit(solution)/shard_map/ppermute | solution.py:321
  61.1 14.1 %all-to-all-start.1 = ((bf16[4,288,128]{2,1,0:T(8,128)(2,1)}), bf16[4,288,128]{2,1,0:T(8,128)(2,1)S(1)}, u32[]{:S(2)}, u32[]{:S(2)}) async-start(bf16[4,288,128]{2,1,0:T(8,128)(2,1)} %get-tuple-element.30), calls=%async_computation.1 | async-start | bytes 589824 | tf_op jit(solution)/shard_map/all_to_all | solution.py:320
  82.3 25.2 %collective-permute-start.5 = (f32[16,128,128]{2,1,0:T(8,128)}, f32[16,128,128]{2,1,0:T(8,128)S(1)}, u32[]{:S(2)}, u32[]{:S(2)}) collective-permute-start(f32[16,128,128]{2,1,0:T(8,128)} %get-tuple-element.37), channel_id=1, source_target_pairs={{0,1},{1,0},{2,3},{3,2},{4,5},{5,4},{6,7},{7,6},{8,9},{9,8},{10,11... | collective-permute-start | bytes 3145736 | tf_op jit(solution)/shard_map/ppermute | solution.py:347
  84.2 23.3 %all-to-all-start.2 = ((f32[64,1,128]{2,1,0:T(1,128)}), f32[64,1,128]{2,1,0:T(1,128)S(1)}, u32[]{:S(2)}, u32[]{:S(2)}) async-start(f32[64,1,128]{2,1,0:T(1,128)} %get-tuple-element.34), calls=%async_computation.2 | async-start | bytes 65536 | tf_op jit(solution)/shard_map/all_to_all | solution.py:346
  114.6 7.6 %copy-start.8 = (f32[4,128,128]{2,1,0:T(8,128)S(1)}, f32[4,128,128]{2,1,0:T(8,128)}, u32[]{:S(2)}) copy-start(f32[4,128,128]{2,1,0:T(8,128)} %get-tuple-element.41) | copy-start | bytes 786436
  114.6 12.2 %copy-start.7 = (f32[4,128,128]{2,1,0:T(8,128)S(1)}, f32[4,128,128]{2,1,0:T(8,128)}, u32[]{:S(2)}) copy-start(f32[4,128,128]{2,1,0:T(8,128)} %get-tuple-element.42) | copy-start | bytes 786436
  114.6 34.4 %copy-start.1 = (f32[4,128,128]{2,1,0:T(8,128)S(1)}, f32[4,128,128]{2,1,0:T(8,128)}, u32[]{:S(2)}) copy-start(f32[4,128,128]{2,1,0:T(8,128)} %get-tuple-element.39.refs_3_) | copy-start | bytes 786436
  114.6 34.4 %copy-start.2 = (s32[7]{0:T(128)S(1)}, s32[7]{0:T(128)}, u32[]{:S(2)}) copy-start(s32[7]{0:T(128)} %stack.31.refs_0_) | copy-start | bytes 88
  114.6 34.4 %all-to-all-start.3 = ((f32[16,3,24,128]{3,2,1,0:T(8,128)}), f32[16,3,24,128]{3,2,1,0:T(8,128)S(1)}, u32[]{:S(2)}, u32[]{:S(2)}) async-start(f32[16,3,24,128]{3,2,1,0:T(8,128)} %get-tuple-element.38), calls=%async_computation.3 | async-start | bytes 1179648 | tf_op jit(solution)/shard_map/all_to_all | solution.py:357
  118.4 11.8 %collective-permute-start.6 = (f32[4,128,128]{2,1,0:T(8,128)S(1)}, f32[4,128,128]{2,1,0:T(8,128)S(1)}, u32[]{:S(2)}, u32[]{:S(2)}) collective-permute-start(f32[4,128,128]{2,1,0:T(8,128)S(1)} %copy-done.9), channel_id=1, source_target_pairs={{0,128},{128,256},{256,384},{384,0},{1,129},{129,257},{257,385},{3... | collective-permute-start | bytes 786440 | tf_op jit(solution)/shard_map/ppermute | solution.py:278
  122.2 13.8 %collective-permute-start.7 = (f32[4,128,128]{2,1,0:T(8,128)S(1)}, f32[4,128,128]{2,1,0:T(8,128)S(1)}, u32[]{:S(2)}, u32[]{:S(2)}) collective-permute-start(f32[4,128,128]{2,1,0:T(8,128)S(1)} %copy-done.8), channel_id=1, source_target_pairs={{0,256},{128,384},{256,0},{384,128},{1,257},{129,385},{257,1},{385... | collective-permute-start | bytes 786440 | tf_op jit(solution)/shard_map/ppermute | solution.py:278
  126.8 10.6 %collective-permute-start.8 = (f32[4,128,128]{2,1,0:T(8,128)S(1)}, f32[4,128,128]{2,1,0:T(8,128)S(1)}, u32[]{:S(2)}, u32[]{:S(2)}) collective-permute-start(f32[4,128,128]{2,1,0:T(8,128)S(1)} %copy-done.7), channel_id=1, source_target_pairs={{0,384},{128,0},{256,128},{384,256},{1,385},{129,1},{257,129},{385... | collective-permute-start | bytes 786440 | tf_op jit(solution)/shard_map/ppermute | solution.py:278
  178.3 43.8 %all-to-all-start.5 = ((bf16[32,2,3,24,128]{4,3,1,2,0:T(8,128)(2,1)}), bf16[32,2,3,24,128]{4,3,1,2,0:T(8,128)(2,1)S(1)}, u32[]{:S(2)}, u32[]{:S(2)}) async-start(bf16[32,2,3,24,128]{4,3,1,2,0:T(8,128)(2,1)} %bitcast.14), calls=%async_computation.5 | async-start | bytes 2359296 | tf_op jit(solution)/shard_map/all_to_all | solution.py:370
  187.6 17.7 %collective-permute-start.10 = (f32[128,128]{1,0:T(8,128)S(1)}, f32[128,128]{1,0:T(8,128)S(1)}, u32[]{:S(2)}, u32[]{:S(2)}) collective-permute-start(f32[128,128]{1,0:T(8,128)S(1)} %get-tuple-element.45), channel_id=1, source_target_pairs={{0,4},{2,6},{4,0},{6,2},{1,5},{3,7},{5,1},{7,3},{8,12},{10,14},{12... | collective-permute-start | bytes 196616 | tf_op jit(solution)/shard_map/ppermute | solution.py:278
  191.6 14.0 %collective-permute-start.11 = (f32[128,128]{1,0:T(8,128)S(1)}, f32[128,128]{1,0:T(8,128)S(1)}, u32[]{:S(2)}, u32[]{:S(2)}) collective-permute-start(f32[128,128]{1,0:T(8,128)S(1)} %get-tuple-element.46), channel_id=1, source_target_pairs={{0,6},{2,0},{4,2},{6,4},{1,7},{3,1},{5,3},{7,5},{8,14},{10,8},{12,... | collective-permute-start | bytes 196616 | tf_op jit(solution)/shard_map/ppermute | solution.py:278
  194.9 10.6 %collective-permute-start.9 = (f32[128,128]{1,0:T(8,128)S(1)}, f32[128,128]{1,0:T(8,128)S(1)}, u32[]{:S(2)}, u32[]{:S(2)}) collective-permute-start(f32[128,128]{1,0:T(8,128)S(1)} %get-tuple-element.44), channel_id=1, source_target_pairs={{0,2},{2,4},{4,6},{6,0},{1,3},{3,5},{5,7},{7,1},{8,10},{10,12},{12... | collective-permute-start | bytes 196616 | tf_op jit(solution)/shard_map/ppermute | solution.py:278
  197.4 24.0 %collective-permute-start.12 = (f32[3,3,24,128]{3,2,1,0:T(8,128)S(1)}, f32[3,3,24,128]{3,2,1,0:T(8,128)S(1)}, u32[]{:S(2)}, u32[]{:S(2)}) collective-permute-start(f32[3,3,24,128]{3,2,1,0:T(8,128)S(1)} %get-tuple-element.47), channel_id=1, source_target_pairs={{0,0},{1,16},{2,32},{3,48},{4,64},{5,80},{6,96},{7,112},{8,8},{9,2... | collective-permute-start | bytes 331784 | tf_op jit(solution)/shard_map/ppermute | solution.py:367
  (5 other events, 7.5 us)

commit v4 on v3

--- a/solution.py
+++ b/solution.py
@@ -13,6 +13,7 @@
 COLS = 128
 SHARD = 24
 BLOCK = 48
+PACK = 2 * TOK + 16
 REPS = 4
 
 BETA_ONE = 0.9
@@ -70,50 +71,56 @@
     low = (dither_ref[...] & 7).astype(F32)
     row = lax.broadcasted_iota(jnp.int32, (16, COLS), 0)
     extra = jnp.where(row == 0, high, jnp.where(row == 1, low, 0.0)).astype(BF16)
-    for peer in range(16):
-        packed_ref[peer, 0:TOK, :] = acts_ref[...]
-        packed_ref[peer, TOK : 2 * TOK, :] = grad_ref[...]
-        packed_ref[peer, 2 * TOK : 2 * TOK + 16, :] = extra
+    packed_ref[0:TOK, :] = acts_ref[...]
+    packed_ref[TOK : 2 * TOK, :] = grad_ref[...]
+    packed_ref[2 * TOK : PACK, :] = extra
     state_ref[0] = master_ref[...]
     state_ref[1] = one_ref[...]
     state_ref[2] = two_ref[...]
 
 
-def code_kernel(state_ref, coded_ref):
-    coded_ref[...] = eightbit_f32(state_ref[0])
-
-
-def spread_kernel(own_ref, *refs):
-    parts, (_, out_ref, wide_ref) = refs[:4], refs[4:]
+def spread_kernel(state_ref, *refs):
+    parts, (coded_ref, joined_ref, wide_ref) = refs[:4], refs[4:]
+    coded = eightbit_f32(state_ref[0])
+    for mat in range(6):
+        wide_ref[mat * SHARD : (mat + 1) * SHARD, :] = coded[mat % 3]
+    narrow = wide_ref[...].astype(BF16)
+    for pair in range(8):
+        coded_ref[pair * 6 * SHARD : (pair + 1) * 6 * SHARD, :] = narrow
     for step, part in enumerate(parts):
-        wide_ref[step * 3 * SHARD : (step + 1) * 3 * SHARD, :] = part[...].astype(F32)
-    narrow = wide_ref[...].astype(BF16)
-    for peer in range(4):
-        out_ref[peer] = narrow
-
-
-def front_kernel(pos_ref, own_ref, other_ref, rows_ref, xs_ref, gs_ref, terms_ref, col_ref, peak_ref, keep_ref, give_ref, wide_ref, full_ref, weights_ref):
+        joined_ref[step] = part[...]
+
+
+def front_kernel(need, done, pos_ref, *refs):
+    planes, refs = (refs[:4], refs[4:8]), refs[8:]
+    rows_ref, xs_ref, gs_ref, terms_ref, col_ref, peak_ref, keep_ref, give_ref = refs[:8]
+    wide_ref, full_ref, weights_ref = refs[8:]
     core = pos_ref[0]
-    for chip in range(4):
-        for source, which in ((own_ref, core), (other_ref, 1 - core)):
-            cols = pl.ds(pl.multiple_of((2 * chip + which) * COLS, COLS), COLS)
-            for rep in range(REPS):
-                rows = slice(rep * TOK, (rep + 1) * TOK)
-                xs_ref[rows, cols] = source[rep * 4 + chip, 0:TOK, :]
-                gs_ref[rows, cols] = source[rep * 4 + chip, TOK : 2 * TOK, :]
-            pair = source[chip, 2 * TOK : 2 * TOK + 16, :].astype(F32)
-            dither = pair[0:1] * 8.0 + pair[1:2]
-            col_ref[:, cols] = jnp.broadcast_to(dither * (1.0 / 1024.0), (8, COLS))
+    need(8)
     wide_ref[...] = rows_ref[...].astype(F32)
-    for low in range(4):
-        for step in range(4):
-            column = 2 * ((pos_ref[6] + 4 - step) % 4) + low // 2
-            cols = pl.ds(pl.multiple_of(column * COLS, COLS), COLS)
-            for mat in range(3):
-                source = ((low * 4 + step) * 3 + mat) * SHARD
-                target = mat * BLOCK + (low % 2) * SHARD
-                full_ref[target : target + SHARD, cols] = wide_ref[source : source + SHARD, :]
+    for depth in range(16):
+        cols = slice((depth // 2) * COLS, (depth // 2 + 1) * COLS)
+        for mat in range(3):
+            source = (depth * 3 + mat) * SHARD
+            target = mat * BLOCK + (depth % 2) * SHARD
+            full_ref[target : target + SHARD, cols] = wide_ref[source : source + SHARD, :]
     weights_ref[...] = full_ref[...].astype(BF16)
+    for step in range(REPS):
+        rep = (pos_ref[4] + 4 - step) % 4
+        rows = pl.ds(pl.multiple_of(rep * TOK, TOK), TOK)
+        for side, which in ((0, core), (1, 1 - core)):
+            group = planes[side]
+            need(4 * side + step)
+            for chip in range(4):
+                column = (pos_ref[5] + 4 - chip) % 4
+                cols = pl.ds(pl.multiple_of((2 * column + which) * COLS, COLS), COLS)
+                xs_ref[rows, cols] = group[step][chip, 0:TOK, :]
+                gs_ref[rows, cols] = group[step][chip, TOK : 2 * TOK, :]
+                if step == 0:
+                    pair = group[0][chip, 2 * TOK : PACK, :].astype(F32)
+                    dither = pair[0:1] * 8.0 + pair[1:2]
+                    col_ref[:, cols] = jnp.broadcast_to(dither * (1.0 / 1024.0), (8, COLS))
+    done(0, 1, 3)
     front = dot(weights_ref[0 : 2 * BLOCK, :], xs_ref[...], 1, 1)
     delta = dot(weights_ref[2 * BLOCK : 3 * BLOCK, :], gs_ref[...], 1, 1)
     gate = front[0:BLOCK]
@@ -123,6 +130,12 @@
     dgate = (delta * upper * sig * (1.0 + gate * (1.0 - sig))).astype(BF16)
     dupper = (delta * active).astype(BF16)
     hidden = (active * upper).astype(BF16)
+    for rep in range(REPS):
+        rows = slice(rep * TOK, (rep + 1) * TOK)
+        terms_ref[rep, 0:BLOCK, :] = dgate[:, rows]
+        terms_ref[rep, BLOCK : 2 * BLOCK, :] = dupper[:, rows]
+        terms_ref[rep, 2 * BLOCK : 3 * BLOCK, :] = hidden[:, rows]
+    done(2)
     terms = jnp.concatenate([dgate, dupper], axis=0)
     for target, which in ((keep_ref, core), (give_ref, 1 - core)):
         side = []
@@ -133,12 +146,10 @@
         for rep in range(REPS):
             for chip in range(4):
                 target[rep * 4 + chip] = back[rep * TOK : (rep + 1) * TOK, chip * COLS : (chip + 1) * COLS]
+    done(5, 6)
     peak = jnp.zeros((3 * BLOCK, COLS), F32)
     for rep in range(REPS):
         rows = slice(rep * TOK, (rep + 1) * TOK)
-        terms_ref[rep, 0:BLOCK, :] = dgate[:, rows]
-        terms_ref[rep, BLOCK : 2 * BLOCK, :] = dupper[:, rows]
-        terms_ref[rep, 2 * BLOCK : 3 * BLOCK, :] = hidden[:, rows]
         for part in range(4):
             cols = slice(part * 256, (part + 1) * 256)
             grad_front = dot(terms_ref[rep, 0 : 2 * BLOCK, :], xs_ref[rows, cols], 1, 0)
@@ -152,14 +163,11 @@
         top = jnp.max(top, axis=1, keepdims=True)
         packed = jnp.where(lane == group, top, packed)
     peak_ref[...] = jnp.broadcast_to(packed.reshape(1, 1, COLS), peak_ref.shape)
-
-
-def quant_kernel(pos_ref, xs_ref, gs_ref, terms_ref, peaks_ref, bits_ref, row_ref, col_ref, keep_ref, got_ref, out_ref, *back_refs):
-    plane = pos_ref[4]
-    for step, back_ref in enumerate(back_refs):
-        first = ((plane + step) % 4) * 4
-        for chip in range(4):
-            back_ref[chip] = keep_ref[first + chip] + got_ref[first + chip]
+    done(4)
+
+
+def quant_kernel(need, done, pos_ref, xs_ref, gs_ref, terms_ref, peaks_ref, bits_ref, row_ref, col_ref, keep_ref, got_ref, out_ref, *back_refs):
+    need(3, 4)
     spot = pos_ref[1]
     unit = pos_ref[2]
     depth = pos_ref[3]
@@ -187,6 +195,7 @@
     scale = jnp.concatenate(scales, axis=0)
     inverse = 1.0 / scale
     scale = scale * (1.0 / N_DP)
+    need(0, 1, 2, 5, 6)
     row_part = row_ref[...]
     for part in range(4):
         cols = slice(part * 256, (part + 1) * 256)
@@ -209,6 +218,14 @@
                 for low in range(2):
                     start = mat * BLOCK + low * SHARD
                     out_ref[2 * (2 * part + half) + low, mat, :, :] = result[start : start + SHARD]
+    done(0)
+    need(7, 8)
+    plane = pos_ref[4]
+    for step, back_ref in enumerate(back_refs):
+        first = ((plane + step) % 4) * 4
+        for chip in range(4):
+            back_ref[chip] = keep_ref[first + chip] + got_ref[first + chip]
+        done(1 + step)
 
 
 def adam_kernel(pos_ref, shares_ref, state_ref, own_ref, up_ref, across_ref, down_ref, new_state_ref, coded_ref, *back_refs):
@@ -229,7 +246,7 @@
     coded_ref[...] = eightbit_f32(updated)
 
 
-def call(kernel, out_shape, smem=0, operands=(), scratch=(), limit=SMALL_LIMIT):
+def call(kernel, out_shape, smem=0, operands=(), scratch=(), limit=SMALL_LIMIT, first=None):
     single = not isinstance(out_shape, tuple)
     outs = (out_shape,) if single else out_shape
     n_in = len(operands) - smem
@@ -242,14 +259,28 @@
         held = refs[smem + n_in + n_out :]
         taken, made, rest, sems = held[:n_in], held[n_in : n_in + n_out], held[n_in + n_out : -1], held[-1]
         loads = [pltpu.make_async_copy(sources[i], taken[i], sems.at[i]) for i in range(n_in)]
-        for load in loads:
-            load.start()
-        for load in loads:
-            load.wait()
-        kernel(*small, *taken, *made, *rest)
         stores = [pltpu.make_async_copy(made[i], targets[i], sems.at[n_in + i]) for i in range(n_out)]
-        for store in stores:
-            store.start()
+        if first is None:
+            for load in loads:
+                load.start()
+            for load in loads:
+                load.wait()
+            kernel(*small, *taken, *made, *rest)
+            for store in stores:
+                store.start()
+        else:
+            for i in first:
+                loads[i].start()
+
+            def need(*which):
+                for i in which:
+                    loads[i].wait()
+
+            def done(*which):
+                for i in which:
+                    stores[i].start()
+
+            kernel(need, done, *small, *taken, *made, *rest)
         for store in stores:
             store.wait()
 
@@ -293,32 +324,28 @@
     tensor = lax.axis_index(TENSOR)
     spot = tensor % 4
     unit = 2 * y + tensor // 4
-    pos = jnp.stack([core, spot, unit, z, y, tensor // 2, z // 4]).astype(jnp.int32)
+    pos = jnp.stack([core, spot, unit, z, y, tensor // 2]).astype(jnp.int32)
     pairs = swap_pairs()
 
     packed, state = call(
         pack_kernel,
-        (struct((16, 2 * TOK + 16, COLS), BF16), struct((3, 3, SHARD, COLS))),
+        (struct((PACK, COLS), BF16), struct((3, 3, SHARD, COLS))),
         0,
         (acts, grad_out, col_dither[None], master, moment_one, moment_two),
         limit=LARGE_LIMIT,
     )
     state = lax.ppermute(state, Z + TENSOR, pairs)
-    coded = call(code_kernel, struct((3, SHARD, COLS)), 0, (state,))
-    coded = coded.astype(BF16).reshape(3 * SHARD, COLS)
-    parts = [coded] + [shift(coded, "zh", step) for step in (1, 2, 3)]
-    own = lax.all_to_all(packed, ("y", "xh", "xl"), 0, 0)
-    own, rows = pl.pallas_call(
+    parts = [packed] + [shift(packed, ("xh", "xl"), step) for step in (1, 2, 3)]
+    coded, joined = call(
         spread_kernel,
-        out_shape=(struct(own.shape, BF16), struct((4, 12 * SHARD, COLS), BF16)),
-        in_specs=[pl.BlockSpec(memory_space=pl.ANY)] + [pl.BlockSpec(memory_space=pltpu.VMEM)] * 4,
-        out_specs=(pl.BlockSpec(memory_space=pl.ANY), pl.BlockSpec(memory_space=pltpu.VMEM)),
-        scratch_shapes=[pltpu.VMEM((12 * SHARD, COLS), F32)],
-        input_output_aliases={0: 0},
-        compiler_params=pltpu.CompilerParams(vmem_limit_bytes=SMALL_LIMIT),
-    )(own, *parts)
-    rows = lax.all_to_all(rows, "zl", 0, 0).reshape(16 * 3 * SHARD, COLS)
-    other = lax.ppermute(own, "c", [(0, 1), (1, 0)])
+        (struct((48 * SHARD, COLS), BF16), struct((4, PACK, COLS), BF16)),
+        0,
+        (state, *parts),
+        (pltpu.VMEM((6 * SHARD, COLS), F32),),
+    )
+    rows = lax.all_to_all(coded.reshape(16, 3 * SHARD, COLS), Z, 0, 0).reshape(48 * SHARD, COLS)
+    own = [joined] + [shift(joined, "y", step) for step in (1, 2, 3)]
+    other = [lax.ppermute(plane, "c", [(0, 1), (1, 0)]) for plane in own]
 
     row_part = lax.dynamic_slice(row_dither, (0, BLOCK * (8 * y + tensor)), (3, BLOCK))
     row_part = jnp.broadcast_to(row_part.astype(F32).reshape(3 * BLOCK, 1) * (1.0 / 1024.0), (3 * BLOCK, COLS))
@@ -335,13 +362,14 @@
             struct((16, TOK, COLS)),
         ),
         1,
-        (pos, own, other, rows),
+        (pos, *own, *other, rows),
         (
             pltpu.VMEM((48 * SHARD, COLS), F32),
             pltpu.VMEM((3 * BLOCK, 1024), F32),
             pltpu.VMEM((3 * BLOCK, 1024), BF16),
         ),
         limit=LARGE_LIMIT,
+        first=(8, 0, 4, 1, 5, 2, 6, 3, 7),
     )
     peaks = lax.all_to_all(peak, ("xl", "c") + Z, 0, 0)
     got = lax.ppermute(give, "c", [(0, 1), (1, 0)])
@@ -352,6 +380,7 @@
         1,
         (pos, xs, gs, terms, peaks, bit_widths, row_part, col_part, keep, got),
         limit=LARGE_LIMIT,
+        first=(3, 4, 2, 0, 1, 5, 6, 7, 8),
     )
     back = [back[0]] + [shift(back[step], "y", step) for step in (1, 2, 3)]
     shares = lax.all_to_all(shares, Z, 0, 0)

time: 224 us -> 216 us (0.964)
  waiting for transfers between devices: 77.7 us -> 60.6 us
  starting transfers between devices: 94.1 us -> 104 us
    ppermute x1, waiting for transfers between devices: 16.2 us -> 0.01 us  [on_device(): state = lax.ppermute(state, Z + TENSOR, pairs)]
    all_to_all x2 -> x1, waiting for transfers between devices: 9.62 us -> 0.01 us  [on_device(): lax.all_to_all(coded.reshape(16, 3 * SHARD, COLS), Z, 0, 0)]
    ppermute x9 -> x12, waiting for transfers between devices: 13.6 us -> 20.8 us  [shift(): return lax.ppermute(value, axes, [(i, (i + step) % 4) for i in range(4)])]
    ppermute x1 -> x4, starting transfers between devices: 1.91 us -> 9.07 us  [on_device(): other = [lax.ppermute(plane, 'c', [(0, 1), (1, 0)]) for plane in own]]
    ppermute x9 -> x12, starting transfers between devices: 39.5 us -> 46.3 us  [shift(): return lax.ppermute(value, axes, [(i, (i + step) % 4) for i in range(4)])]
    all_to_all x2 -> x1, starting transfers between devices: 13.4 us -> 6.92 us  [on_device(): lax.all_to_all(coded.reshape(16, 3 * SHARD, COLS), Z, 0, 0)]
    all_to_all x1, starting transfers between devices: 9.26 us -> 5.55 us  [on_device(): lax.all_to_all(ring.reshape(32, 2, 3, SHARD, COLS), ('y',) + TENSOR, 0, 0)]
    all_to_all x1, starting transfers between devices: 10.9 us -> 14.2 us  [on_device(): peaks = lax.all_to_all(peak, ('xl', 'c') + Z, 0, 0)]
  transfers between devices with their start and end apart: 18 -> 23, of which waited for: 10 -> 11; matrix products, arithmetic and copies ran while one was open for 1% -> 1% of each run, Pallas kernels for 0% -> 0%
where the time goes in v4:
time: 216 us; the launch traced here: 215 us
  starting transfers between devices  104 us (48%)
  waiting for transfers between devices  60.6 us (28%)
  blocking collectives  26.3 us (12%)
  Pallas kernels  15 us (7%)
  local copies, waits for them, and re-layouts  6.51 us (3%)
    ppermute x12, starting transfers between devices, shift(): return lax.ppermute(value, axes, [(i, (i + step) % 4) for i in range(4)])  46.3 us
    all_to_all x1, blocking collectives, to_all(): lax.all_to_all(jnp.broadcast_to(value[None], (peers,) + value.shape), axe...  26.3 us
    ppermute x12, waiting for transfers between devices, shift(): return lax.ppermute(value, axes, [(i, (i + step) % 4) for i in range(4)])  20.8 us
    ppermute x1, waiting for transfers between devices, on_device(): new_state = lax.ppermute(new_state, Z + TENSOR, pairs)  15.8 us
    pallas_call x5, Pallas kernels, call(): pl.pallas_call(body, out_shape=out_shape, in_specs=specs, out_specs=anywh...  15 us
    all_to_all x1, starting transfers between devices, on_device(): peaks = lax.all_to_all(peak, ('xl', 'c') + Z, 0, 0)  14.2 us
    all_to_all x1, waiting for transfers between devices, on_device(): shares = lax.all_to_all(shares, Z, 0, 0)  11.7 us
    all_to_all x1, waiting for transfers between devices, on_device(): peaks = lax.all_to_all(peak, ('xl', 'c') + Z, 0, 0)  11.5 us
  transfers between devices with their start and end apart: 23, of which 11 were waited for; matrix products, arithmetic and copies ran while one was open for 1% of the time, Pallas kernels for 0%

profile of v4, /device:TPU:2, one launch (start us, length us, event | category | flops | bytes accessed | tf_op | source)
XLA Modules:
  0.0 214.7 jit_solution(244041794145800476)
XLA Ops:
  2.2 9.1 %collective-permute-start = (f32[3,3,24,128]{3,2,1,0:T(8,128)}, f32[3,3,24,128]{3,2,1,0:T(8,128)S(1)}, u32[]{:S(2)}, u32[]{:S(2)}) collective-permute-start(f32[3,3,24,128]{3,2,1,0:T(8,128)} %get-tuple-element.27), channel_id=1, source_target_pairs={{0,0},{1,16},{2,32},{3,48},{4,64},{5,80},{6,96},{7,112},{8,8},{9,2... | collective-permute-start | bytes 331784 | tf_op jit(solution)/shard_map/ppermute | solution.py:337
  11.3 10.0 %collective-permute-start.1 = (bf16[272,128]{1,0:T(8,128)(2,1)}, bf16[272,128]{1,0:T(8,128)(2,1)S(1)}, u32[]{:S(2)}, u32[]{:S(2)}) collective-permute-start(bf16[272,128]{1,0:T(8,128)(2,1)} %get-tuple-element.28.refs_1_), channel_id=1, source_target_pairs={{0,2},{2,4},{4,6},{6,0},{1,3},{3,5},{5,7},{7,1},{8,10},{10,12},{12... | collective-permute-start | bytes 208904 | tf_op jit(solution)/shard_map/ppermute | solution.py:309
  23.3 4.0 %collective-permute-start.3 = (bf16[272,128]{1,0:T(8,128)(2,1)}, bf16[272,128]{1,0:T(8,128)(2,1)S(1)}, u32[]{:S(2)}, u32[]{:S(2)}) collective-permute-start(bf16[272,128]{1,0:T(8,128)(2,1)} %get-tuple-element.28.refs_1_), channel_id=1, source_target_pairs={{0,6},{2,0},{4,2},{6,4},{1,7},{3,1},{5,3},{7,5},{8,14},{10,8},{12,... | collective-permute-start | bytes 208904 | tf_op jit(solution)/shard_map/ppermute | solution.py:309
  32.5 6.9 %all-to-all-start = ((bf16[16,72,128]{2,1,0:T(8,128)(2,1)}), bf16[16,72,128]{2,1,0:T(8,128)(2,1)S(1)}, u32[]{:S(2)}, u32[]{:S(2)}) async-start(bf16[16,72,128]{2,1,0:T(8,128)(2,1)} %bitcast.7), calls=%async_computation | async-start | bytes 589824 | tf_op jit(solution)/shard_map/all_to_all | solution.py:346
  39.4 4.9 %collective-permute-start.6 = (bf16[4,272,128]{2,1,0:T(8,128)(2,1)S(1)}, bf16[4,272,128]{2,1,0:T(8,128)(2,1)S(1)}, u32[]{:S(2)}, u32[]{:S(2)}) collective-permute-start(bf16[4,272,128]{2,1,0:T(8,128)(2,1)S(1)} %get-tuple-element.29.refs_1_), channel_id=1, source_target_pairs={{0,384},{128,0},{256,128},{384,256},{1,385},{129,1},{257,129},{385... | collective-permute-start | bytes 835592 | tf_op jit(solution)/shard_map/ppermute | solution.py:309
  46.3 4.1 %collective-permute-start.5 = (bf16[4,272,128]{2,1,0:T(8,128)(2,1)S(1)}, bf16[4,272,128]{2,1,0:T(8,128)(2,1)S(1)}, u32[]{:S(2)}, u32[]{:S(2)}) collective-permute-start(bf16[4,272,128]{2,1,0:T(8,128)(2,1)S(1)} %get-tuple-element.29.refs_1_), channel_id=1, source_target_pairs={{0,256},{128,384},{256,0},{384,128},{1,257},{129,385},{257,1},{385... | collective-permute-start | bytes 835592 | tf_op jit(solution)/shard_map/ppermute | solution.py:309
  50.4 2.8 %collective-permute-start.7 = (bf16[4,272,128]{2,1,0:T(8,128)(2,1)S(1)}, bf16[4,272,128]{2,1,0:T(8,128)(2,1)S(1)}, u32[]{:S(2)}, u32[]{:S(2)}) collective-permute-start(bf16[4,272,128]{2,1,0:T(8,128)(2,1)S(1)} %get-tuple-element.29.refs_1_), channel_id=1, source_target_pairs={{0,1},{1,0},{2,3},{3,2},{4,5},{5,4},{6,7},{7,6},{8,9},{9,8},{10,11... | collective-permute-start | bytes 835592 | tf_op jit(solution)/shard_map/ppermute | solution.py:348
  55.2 7.3 %collective-permute-done.4.refs_2_ = bf16[4,272,128]{2,1,0:T(8,128)(2,1)S(1)} collective-permute-done((bf16[4,272,128]{2,1,0:T(8,128)(2,1)S(1)}, bf16[4,272,128]{2,1,0:T(8,128)(2,1)S(1)}, u32[]{:S(2)}, u32[]{:S(2)}) %collective-permute-start.4) | collective-permute-done | bytes 278560 | tf_op jit(solution)/shard_map/ppermute | solution.py:309
  69.0 4.9 %shard_map.121 = (bf16[512,1024]{1,0:T(8,128)(2,1)}, bf16[512,1024]{1,0:T(8,128)(2,1)}, bf16[4,144,128]{2,1,0:T(8,128)(2,1)}, f32[8,1024]{1,0:T(8,128)}, f32[64,...) custom-call(s32[6]{0:T(128)} %stack.27.refs_0_, bf16[4,272,128]{2,1,0:T(8,128)(2,1)} %copy-done, ...), custom_call_target="tpu_custom_call" | custom-call | tf_op jit(solution)/shard_map/pallas_call | solution.py:290
  76.0 14.2 %all-to-all-start.1 = ((f32[64,1,128]{2,1,0:T(1,128)}), f32[64,1,128]{2,1,0:T(1,128)S(1)}, u32[]{:S(2)}, u32[]{:S(2)}) async-start(f32[64,1,128]{2,1,0:T(1,128)} %get-tuple-element.34), calls=%async_computation.1 | async-start | bytes 65536 | tf_op jit(solution)/shard_map/all_to_all | solution.py:374
  91.1 11.5 %all-to-all-done.1.refs_4_ = f32[64,1,128]{2,1,0:T(1,128)S(1)} async-done(((f32[64,1,128]{2,1,0:T(1,128)}), f32[64,1,128]{2,1,0:T(1,128)S(1)}, u32[]{:S(2)}, u32[]{:S(2)}) %all-to-all-start.1) | async-done | bytes 32800 | tf_op jit(solution)/shard_map/all_to_all | solution.py:374
  103.6 5.4 %shard_map.122 = (f32[16,3,24,128]{3,2,1,0:T(8,128)}, f32[4,128,128]{2,1,0:T(8,128)}, f32[4,128,128]{2,1,0:T(8,128)}, f32[4,128,128]{2,1,0:T(8,128)}, f32[4,128,128]{2,1,0:T(8,128)}) custom-call(s32[6]{0:T(128)} %stack.27.refs_0_, bf16[512,1024]{1,0:T(8,128)(2,1)} %get-tuple-element.31.refs_1_, bf16[512,1024]{1,0:T(8,128)(2,1)} %get-tuple-element.32.refs_2_, ...), custom_call_target="tpu_custom_call" | custom-call | tf_op jit(solution)/shard_map/pallas_call | solution.py:290
  109.1 3.7 %all-to-all-start.2 = ((f32[16,3,24,128]{3,2,1,0:T(8,128)}), f32[16,3,24,128]{3,2,1,0:T(8,128)S(1)}, u32[]{:S(2)}, u32[]{:S(2)}) async-start(f32[16,3,24,128]{3,2,1,0:T(8,128)} %get-tuple-element.38), calls=%async_computation.2 | async-start | bytes 1179648 | tf_op jit(solution)/shard_map/all_to_all | solution.py:386
  114.8 2.9 %collective-permute-start.13 = (f32[4,128,128]{2,1,0:T(8,128)S(1)}, f32[4,128,128]{2,1,0:T(8,128)S(1)}, u32[]{:S(2)}, u32[]{:S(2)}) collective-permute-start(f32[4,128,128]{2,1,0:T(8,128)S(1)} %copy-done.15), channel_id=1, source_target_pairs={{0,256},{128,384},{256,0},{384,128},{1,257},{129,385},{257,1},{385... | collective-permute-start | bytes 786440 | tf_op jit(solution)/shard_map/ppermute | solution.py:309
  117.7 4.2 %collective-permute-start.14 = (f32[4,128,128]{2,1,0:T(8,128)S(1)}, f32[4,128,128]{2,1,0:T(8,128)S(1)}, u32[]{:S(2)}, u32[]{:S(2)}) collective-permute-start(f32[4,128,128]{2,1,0:T(8,128)S(1)} %copy-done.14), channel_id=1, source_target_pairs={{0,384},{128,0},{256,128},{384,256},{1,385},{129,1},{257,129},{385... | collective-permute-start | bytes 786440 | tf_op jit(solution)/shard_map/ppermute | solution.py:309
  121.9 7.3 %collective-permute-done.12.refs_4_ = f32[4,128,128]{2,1,0:T(8,128)S(1)} collective-permute-done((f32[4,128,128]{2,1,0:T(8,128)S(1)}, f32[4,128,128]{2,1,0:T(8,128)S(1)}, u32[]{:S(2)}, u32[]{:S(2)}) %collective-permute-start.12) | collective-permute-done | bytes 262176 | tf_op jit(solution)/shard_map/ppermute | solution.py:309
  131.7 11.7 %all-to-all-done.2.refs_1_ = f32[16,3,24,128]{3,2,1,0:T(8,128)S(1)} async-done(((f32[16,3,24,128]{3,2,1,0:T(8,128)}), f32[16,3,24,128]{3,2,1,0:T(8,128)S(1)}, u32[]{:S(2)}, u32[]{:S(2)}) %all-to-all-start.2) | async-done | bytes 589856 | tf_op jit(solution)/shard_map/all_to_all | solution.py:386
  145.2 26.3 %all_to_all.25 = bf16[16,3,24,128]{3,2,1,0:T(8,128)(2,1)S(1)} all-to-all(bf16[16,3,24,128]{3,2,1,0:T(8,128)(2,1)S(1)} %broadcast_in_dim.23), channel_id=1, replica_groups=mesh['y'=4,'zh'=4,'zl'=4,'xh'=2,'xl'=2,'c'=2] {'zh','zl'}, dimensions={0} | all-to-all | bytes 589824 | tf_op jit(solution)/shard_map/all_to_all | solution.py:305
  172.8 5.6 %all-to-all-start.4 = ((bf16[32,2,3,24,128]{4,3,1,2,0:T(8,128)(2,1)}), bf16[32,2,3,24,128]{4,3,1,2,0:T(8,128)(2,1)S(1)}, u32[]{:S(2)}, u32[]{:S(2)}) async-start(bf16[32,2,3,24,128]{4,3,1,2,0:T(8,128)(2,1)} %bitcast.13), calls=%async_computation.4 | async-start | bytes 2359296 | tf_op jit(solution)/shard_map/all_to_all | solution.py:399
  178.4 3.4 %collective-permute-start.15 = (f32[128,128]{1,0:T(8,128)S(1)}, f32[128,128]{1,0:T(8,128)S(1)}, u32[]{:S(2)}, u32[]{:S(2)}) collective-permute-start(f32[128,128]{1,0:T(8,128)S(1)} %get-tuple-element.44), channel_id=1, source_target_pairs={{0,2},{2,4},{4,6},{6,0},{1,3},{3,5},{5,7},{7,1},{8,10},{10,12},{12... | collective-permute-start | bytes 196616 | tf_op jit(solution)/shard_map/ppermute | solution.py:309
  181.7 2.8 %collective-permute-start.16 = (f32[128,128]{1,0:T(8,128)S(1)}, f32[128,128]{1,0:T(8,128)S(1)}, u32[]{:S(2)}, u32[]{:S(2)}) collective-permute-start(f32[128,128]{1,0:T(8,128)S(1)} %get-tuple-element.45), channel_id=1, source_target_pairs={{0,4},{2,6},{4,0},{6,2},{1,5},{3,7},{5,1},{7,3},{8,12},{10,14},{12... | collective-permute-start | bytes 196616 | tf_op jit(solution)/shard_map/ppermute | solution.py:309
  184.6 4.2 %collective-permute-start.17 = (f32[128,128]{1,0:T(8,128)S(1)}, f32[128,128]{1,0:T(8,128)S(1)}, u32[]{:S(2)}, u32[]{:S(2)}) collective-permute-start(f32[128,128]{1,0:T(8,128)S(1)} %get-tuple-element.46), channel_id=1, source_target_pairs={{0,6},{2,0},{4,2},{6,4},{1,7},{3,1},{5,3},{7,5},{8,14},{10,8},{12,... | collective-permute-start | bytes 196616 | tf_op jit(solution)/shard_map/ppermute | solution.py:309
  188.8 6.8 %collective-permute-start.18 = (f32[3,3,24,128]{3,2,1,0:T(8,128)S(1)}, f32[3,3,24,128]{3,2,1,0:T(8,128)S(1)}, u32[]{:S(2)}, u32[]{:S(2)}) collective-permute-start(f32[3,3,24,128]{3,2,1,0:T(8,128)S(1)} %get-tuple-element.47), channel_id=1, source_target_pairs={{0,0},{1,16},{2,32},{3,48},{4,64},{5,80},{6,96},{7,112},{8,8},{9,2... | collective-permute-start | bytes 331784 | tf_op jit(solution)/shard_map/ppermute | solution.py:396
  197.0 15.8 %collective-permute-done.18 = f32[3,3,24,128]{3,2,1,0:T(8,128)S(1)} collective-permute-done((f32[3,3,24,128]{3,2,1,0:T(8,128)S(1)}, f32[3,3,24,128]{3,2,1,0:T(8,128)S(1)}, u32[]{:S(2)}, u32[]{:S(2)}) %collective-permute-start.18) | collective-permute-done | bytes 110624 | tf_op jit(solution)/shard_map/ppermute | solution.py:396
  (73 shorter events, 33.6 us)
Async XLA Ops:
  2.2 28.0 %collective-permute-start = (f32[3,3,24,128]{3,2,1,0:T(8,128)}, f32[3,3,24,128]{3,2,1,0:T(8,128)S(1)}, u32[]{:S(2)}, u32[]{:S(2)}) collective-permute-start(f32[3,3,24,128]{3,2,1,0:T(8,128)} %get-tuple-element.27), channel_id=1, source_target_pairs={{0,0},{1,16},{2,32},{3,48},{4,64},{5,80},{6,96},{7,112},{8,8},{9,2... | collective-permute-start | bytes 331784 | tf_op jit(solution)/shard_map/ppermute | solution.py:337
  11.3 15.9 %collective-permute-start.1 = (bf16[272,128]{1,0:T(8,128)(2,1)}, bf16[272,128]{1,0:T(8,128)(2,1)S(1)}, u32[]{:S(2)}, u32[]{:S(2)}) collective-permute-start(bf16[272,128]{1,0:T(8,128)(2,1)} %get-tuple-element.28.refs_1_), channel_id=1, source_target_pairs={{0,2},{2,4},{4,6},{6,0},{1,3},{3,5},{5,7},{7,1},{8,10},{10,12},{12... | collective-permute-start | bytes 208904 | tf_op jit(solution)/shard_map/ppermute | solution.py:309
  21.3 8.7 %collective-permute-start.2 = (bf16[272,128]{1,0:T(8,128)(2,1)}, bf16[272,128]{1,0:T(8,128)(2,1)S(1)}, u32[]{:S(2)}, u32[]{:S(2)}) collective-permute-start(bf16[272,128]{1,0:T(8,128)(2,1)} %get-tuple-element.28.refs_1_), channel_id=1, source_target_pairs={{0,4},{2,6},{4,0},{6,2},{1,5},{3,7},{5,1},{7,3},{8,12},{10,14},{12... | collective-permute-start | bytes 208904 | tf_op jit(solution)/shard_map/ppermute | solution.py:309
  23.3 6.9 %collective-permute-start.3 = (bf16[272,128]{1,0:T(8,128)(2,1)}, bf16[272,128]{1,0:T(8,128)(2,1)S(1)}, u32[]{:S(2)}, u32[]{:S(2)}) collective-permute-start(bf16[272,128]{1,0:T(8,128)(2,1)} %get-tuple-element.28.refs_1_), channel_id=1, source_target_pairs={{0,6},{2,0},{4,2},{6,4},{1,7},{3,1},{5,3},{7,5},{8,14},{10,8},{12,... | collective-permute-start | bytes 208904 | tf_op jit(solution)/shard_map/ppermute | solution.py:309
  32.5 35.7 %copy-start = (bf16[4,272,128]{2,1,0:T(8,128)(2,1)}, bf16[4,272,128]{2,1,0:T(8,128)(2,1)S(1)}, u32[]{:S(2)}) copy-start(bf16[4,272,128]{2,1,0:T(8,128)(2,1)S(1)} %get-tuple-element.29.refs_1_) | copy-start | bytes 835588
  32.5 35.7 %all-to-all-start = ((bf16[16,72,128]{2,1,0:T(8,128)(2,1)}), bf16[16,72,128]{2,1,0:T(8,128)(2,1)S(1)}, u32[]{:S(2)}, u32[]{:S(2)}) async-start(bf16[16,72,128]{2,1,0:T(8,128)(2,1)} %bitcast.7), calls=%async_computation | async-start | bytes 589824 | tf_op jit(solution)/shard_map/all_to_all | solution.py:346
  39.4 13.8 %collective-permute-start.6 = (bf16[4,272,128]{2,1,0:T(8,128)(2,1)S(1)}, bf16[4,272,128]{2,1,0:T(8,128)(2,1)S(1)}, u32[]{:S(2)}, u32[]{:S(2)}) collective-permute-start(bf16[4,272,128]{2,1,0:T(8,128)(2,1)S(1)} %get-tuple-element.29.refs_1_), channel_id=1, source_target_pairs={{0,384},{128,0},{256,128},{384,256},{1,385},{129,1},{257,129},{385... | collective-permute-start | bytes 835592 | tf_op jit(solution)/shard_map/ppermute | solution.py:309
  44.3 18.2 %collective-permute-start.4 = (bf16[4,272,128]{2,1,0:T(8,128)(2,1)S(1)}, bf16[4,272,128]{2,1,0:T(8,128)(2,1)S(1)}, u32[]{:S(2)}, u32[]{:S(2)}) collective-permute-start(bf16[4,272,128]{2,1,0:T(8,128)(2,1)S(1)} %get-tuple-element.29.refs_1_), channel_id=1, source_target_pairs={{0,128},{128,256},{256,384},{384,0},{1,129},{129,257},{257,385},{3... | collective-permute-start | bytes 835592 | tf_op jit(solution)/shard_map/ppermute | solution.py:309
  46.3 18.4 %collective-permute-start.5 = (bf16[4,272,128]{2,1,0:T(8,128)(2,1)S(1)}, bf16[4,272,128]{2,1,0:T(8,128)(2,1)S(1)}, u32[]{:S(2)}, u32[]{:S(2)}) collective-permute-start(bf16[4,272,128]{2,1,0:T(8,128)(2,1)S(1)} %get-tuple-element.29.refs_1_), channel_id=1, source_target_pairs={{0,256},{128,384},{256,0},{384,128},{1,257},{129,385},{257,1},{385... | collective-permute-start | bytes 835592 | tf_op jit(solution)/shard_map/ppermute | solution.py:309
  50.4 17.2 %collective-permute-start.7 = (bf16[4,272,128]{2,1,0:T(8,128)(2,1)S(1)}, bf16[4,272,128]{2,1,0:T(8,128)(2,1)S(1)}, u32[]{:S(2)}, u32[]{:S(2)}) collective-permute-start(bf16[4,272,128]{2,1,0:T(8,128)(2,1)S(1)} %get-tuple-element.29.refs_1_), channel_id=1, source_target_pairs={{0,1},{1,0},{2,3},{3,2},{4,5},{5,4},{6,7},{7,6},{8,9},{9,8},{10,11... | collective-permute-start | bytes 835592 | tf_op jit(solution)/shard_map/ppermute | solution.py:348
  53.2 14.3 %collective-permute-start.10 = (bf16[4,272,128]{2,1,0:T(8,128)(2,1)S(1)}, bf16[4,272,128]{2,1,0:T(8,128)(2,1)S(1)}, u32[]{:S(2)}, u32[]{:S(2)}) collective-permute-start(bf16[4,272,128]{2,1,0:T(8,128)(2,1)S(1)} %collective-permute-done.6.refs_4_), channel_id=1, source_target_pairs={{0,1},{1,0},{2,3},{3,2},{4,5},{5,4},{6,7},{7,6},{8,9},{9,8},{10,11... | collective-permute-start | bytes 835592 | tf_op jit(solution)/shard_map/ppermute | solution.py:348
  62.5 5.0 %collective-permute-start.8 = (bf16[4,272,128]{2,1,0:T(8,128)(2,1)S(1)}, bf16[4,272,128]{2,1,0:T(8,128)(2,1)S(1)}, u32[]{:S(2)}, u32[]{:S(2)}) collective-permute-start(bf16[4,272,128]{2,1,0:T(8,128)(2,1)S(1)} %collective-permute-done.4.refs_2_), channel_id=1, source_target_pairs={{0,1},{1,0},{2,3},{3,2},{4,5},{5,4},{6,7},{7,6},{8,9},{9,8},{10,11... | collective-permute-start | bytes 835592 | tf_op jit(solution)/shard_map/ppermute | solution.py:348
  64.7 3.5 %collective-permute-start.9 = (bf16[4,272,128]{2,1,0:T(8,128)(2,1)S(1)}, bf16[4,272,128]{2,1,0:T(8,128)(2,1)S(1)}, u32[]{:S(2)}, u32[]{:S(2)}) collective-permute-start(bf16[4,272,128]{2,1,0:T(8,128)(2,1)S(1)} %collective-permute-done.5.refs_3_), channel_id=1, source_target_pairs={{0,1},{1,0},{2,3},{3,2},{4,5},{5,4},{6,7},{7,6},{8,9},{9,8},{10,11... | collective-permute-start | bytes 835592 | tf_op jit(solution)/shard_map/ppermute | solution.py:348
  73.8 28.8 %collective-permute-start.11 = (f32[16,128,128]{2,1,0:T(8,128)}, f32[16,128,128]{2,1,0:T(8,128)S(1)}, u32[]{:S(2)}, u32[]{:S(2)}) collective-permute-start(f32[16,128,128]{2,1,0:T(8,128)} %get-tuple-element.37), channel_id=1, source_target_pairs={{0,1},{1,0},{2,3},{3,2},{4,5},{5,4},{6,7},{7,6},{8,9},{9,8},{10,11... | collective-permute-start | bytes 3145736 | tf_op jit(solution)/shard_map/ppermute | solution.py:375
  76.0 26.6 %all-to-all-start.1 = ((f32[64,1,128]{2,1,0:T(1,128)}), f32[64,1,128]{2,1,0:T(1,128)S(1)}, u32[]{:S(2)}, u32[]{:S(2)}) async-start(f32[64,1,128]{2,1,0:T(1,128)} %get-tuple-element.34), calls=%async_computation.1 | async-start | bytes 65536 | tf_op jit(solution)/shard_map/all_to_all | solution.py:374
  109.1 34.3 %all-to-all-start.2 = ((f32[16,3,24,128]{3,2,1,0:T(8,128)}), f32[16,3,24,128]{3,2,1,0:T(8,128)S(1)}, u32[]{:S(2)}, u32[]{:S(2)}) async-start(f32[16,3,24,128]{3,2,1,0:T(8,128)} %get-tuple-element.38), calls=%async_computation.2 | async-start | bytes 1179648 | tf_op jit(solution)/shard_map/all_to_all | solution.py:386
  112.9 16.3 %collective-permute-start.12 = (f32[4,128,128]{2,1,0:T(8,128)S(1)}, f32[4,128,128]{2,1,0:T(8,128)S(1)}, u32[]{:S(2)}, u32[]{:S(2)}) collective-permute-start(f32[4,128,128]{2,1,0:T(8,128)S(1)} %copy-done.16), channel_id=1, source_target_pairs={{0,128},{128,256},{256,384},{384,0},{1,129},{129,257},{257,385},{3... | collective-permute-start | bytes 786440 | tf_op jit(solution)/shard_map/ppermute | solution.py:309
  114.8 14.4 %collective-permute-start.13 = (f32[4,128,128]{2,1,0:T(8,128)S(1)}, f32[4,128,128]{2,1,0:T(8,128)S(1)}, u32[]{:S(2)}, u32[]{:S(2)}) collective-permute-start(f32[4,128,128]{2,1,0:T(8,128)S(1)} %copy-done.15), channel_id=1, source_target_pairs={{0,256},{128,384},{256,0},{384,128},{1,257},{129,385},{257,1},{385... | collective-permute-start | bytes 786440 | tf_op jit(solution)/shard_map/ppermute | solution.py:309
  117.7 14.0 %collective-permute-start.14 = (f32[4,128,128]{2,1,0:T(8,128)S(1)}, f32[4,128,128]{2,1,0:T(8,128)S(1)}, u32[]{:S(2)}, u32[]{:S(2)}) collective-permute-start(f32[4,128,128]{2,1,0:T(8,128)S(1)} %copy-done.14), channel_id=1, source_target_pairs={{0,384},{128,0},{256,128},{384,256},{1,385},{129,1},{257,129},{385... | collective-permute-start | bytes 786440 | tf_op jit(solution)/shard_map/ppermute | solution.py:309
  172.8 40.7 %all-to-all-start.4 = ((bf16[32,2,3,24,128]{4,3,1,2,0:T(8,128)(2,1)}), bf16[32,2,3,24,128]{4,3,1,2,0:T(8,128)(2,1)S(1)}, u32[]{:S(2)}, u32[]{:S(2)}) async-start(bf16[32,2,3,24,128]{4,3,1,2,0:T(8,128)(2,1)} %bitcast.13), calls=%async_computation.4 | async-start | bytes 2359296 | tf_op jit(solution)/shard_map/all_to_all | solution.py:399
  178.4 17.3 %collective-permute-start.15 = (f32[128,128]{1,0:T(8,128)S(1)}, f32[128,128]{1,0:T(8,128)S(1)}, u32[]{:S(2)}, u32[]{:S(2)}) collective-permute-start(f32[128,128]{1,0:T(8,128)S(1)} %get-tuple-element.44), channel_id=1, source_target_pairs={{0,2},{2,4},{4,6},{6,0},{1,3},{3,5},{5,7},{7,1},{8,10},{10,12},{12... | collective-permute-start | bytes 196616 | tf_op jit(solution)/shard_map/ppermute | solution.py:309
  181.7 14.4 %collective-permute-start.16 = (f32[128,128]{1,0:T(8,128)S(1)}, f32[128,128]{1,0:T(8,128)S(1)}, u32[]{:S(2)}, u32[]{:S(2)}) collective-permute-start(f32[128,128]{1,0:T(8,128)S(1)} %get-tuple-element.45), channel_id=1, source_target_pairs={{0,4},{2,6},{4,0},{6,2},{1,5},{3,7},{5,1},{7,3},{8,12},{10,14},{12... | collective-permute-start | bytes 196616 | tf_op jit(solution)/shard_map/ppermute | solution.py:309
  184.6 11.8 %collective-permute-start.17 = (f32[128,128]{1,0:T(8,128)S(1)}, f32[128,128]{1,0:T(8,128)S(1)}, u32[]{:S(2)}, u32[]{:S(2)}) collective-permute-start(f32[128,128]{1,0:T(8,128)S(1)} %get-tuple-element.46), channel_id=1, source_target_pairs={{0,6},{2,0},{4,2},{6,4},{1,7},{3,1},{5,3},{7,5},{8,14},{10,8},{12,... | collective-permute-start | bytes 196616 | tf_op jit(solution)/shard_map/ppermute | solution.py:309
  188.8 24.0 %collective-permute-start.18 = (f32[3,3,24,128]{3,2,1,0:T(8,128)S(1)}, f32[3,3,24,128]{3,2,1,0:T(8,128)S(1)}, u32[]{:S(2)}, u32[]{:S(2)}) collective-permute-start(f32[3,3,24,128]{3,2,1,0:T(8,128)S(1)} %get-tuple-element.47), channel_id=1, source_target_pairs={{0,0},{1,16},{2,32},{3,48},{4,64},{5,80},{6,96},{7,112},{8,8},{9,2... | collective-permute-start | bytes 331784 | tf_op jit(solution)/shard_map/ppermute | solution.py:396
  (16 other events, 117.7 us)

commit v5 on v4

--- a/solution.py
+++ b/solution.py
@@ -66,7 +66,7 @@
     )
 
 
-def pack_kernel(acts_ref, grad_ref, dither_ref, master_ref, one_ref, two_ref, packed_ref, state_ref):
+def pack_kernel(acts_ref, grad_ref, dither_ref, master_ref, one_ref, two_ref, packed_ref, coded_ref, state_ref, wide_ref):
     high = (dither_ref[...] >> 3).astype(F32)
     low = (dither_ref[...] & 7).astype(F32)
     row = lax.broadcasted_iota(jnp.int32, (16, COLS), 0)
@@ -74,21 +74,15 @@
     packed_ref[0:TOK, :] = acts_ref[...]
     packed_ref[TOK : 2 * TOK, :] = grad_ref[...]
     packed_ref[2 * TOK : PACK, :] = extra
-    state_ref[0] = master_ref[...]
-    state_ref[1] = one_ref[...]
-    state_ref[2] = two_ref[...]
-
-
-def spread_kernel(state_ref, *refs):
-    parts, (coded_ref, joined_ref, wide_ref) = refs[:4], refs[4:]
-    coded = eightbit_f32(state_ref[0])
+    coded = eightbit_f32(master_ref[...])
     for mat in range(6):
         wide_ref[mat * SHARD : (mat + 1) * SHARD, :] = coded[mat % 3]
     narrow = wide_ref[...].astype(BF16)
     for pair in range(8):
         coded_ref[pair * 6 * SHARD : (pair + 1) * 6 * SHARD, :] = narrow
-    for step, part in enumerate(parts):
-        joined_ref[step] = part[...]
+    state_ref[0] = master_ref[...]
+    state_ref[1] = one_ref[...]
+    state_ref[2] = two_ref[...]
 
 
 def front_kernel(need, done, pos_ref, *refs):
@@ -246,6 +240,15 @@
     coded_ref[...] = eightbit_f32(updated)
 
 
+def finish_kernel(ring_ref, state_ref, own_ref, right_ref, across_ref, left_ref, *outs):
+    spread_ref, grad_ref, state_outs = outs[0], outs[1], outs[2:]
+    for plane in range(4):
+        spread_ref[plane] = ring_ref[...]
+    grad_ref[...] = ((own_ref[...] + right_ref[...]) + (across_ref[...] + left_ref[...])).astype(BF16)
+    for which, out_ref in enumerate(state_outs):
+        out_ref[...] = state_ref[which]
+
+
 def call(kernel, out_shape, smem=0, operands=(), scratch=(), limit=SMALL_LIMIT, first=None):
     single = not isinstance(out_shape, tuple)
     outs = (out_shape,) if single else out_shape
@@ -327,23 +330,17 @@
     pos = jnp.stack([core, spot, unit, z, y, tensor // 2]).astype(jnp.int32)
     pairs = swap_pairs()
 
-    packed, state = call(
+    packed, coded, state = call(
         pack_kernel,
-        (struct((PACK, COLS), BF16), struct((3, 3, SHARD, COLS))),
+        (struct((PACK, COLS), BF16), struct((48 * SHARD, COLS), BF16), struct((3, 3, SHARD, COLS))),
         0,
         (acts, grad_out, col_dither[None], master, moment_one, moment_two),
+        (pltpu.VMEM((6 * SHARD, COLS), F32),),
         limit=LARGE_LIMIT,
     )
-    state = lax.ppermute(state, Z + TENSOR, pairs)
-    parts = [packed] + [shift(packed, ("xh", "xl"), step) for step in (1, 2, 3)]
-    coded, joined = call(
-        spread_kernel,
-        (struct((48 * SHARD, COLS), BF16), struct((4, PACK, COLS), BF16)),
-        0,
-        (state, *parts),
-        (pltpu.VMEM((6 * SHARD, COLS), F32),),
-    )
-    rows = lax.all_to_all(coded.reshape(16, 3 * SHARD, COLS), Z, 0, 0).reshape(48 * SHARD, COLS)
+    rows = lax.all_to_all(coded.reshape(16, 3 * SHARD, COLS), Z, 0, 0)
+    rows = lax.all_to_all(rows.reshape(8, 6 * SHARD, COLS), TENSOR, 0, 0).reshape(48 * SHARD, COLS)
+    joined = jnp.stack([packed] + [shift(packed, ("xh", "xl"), step) for step in (1, 2, 3)])
     own = [joined] + [shift(joined, "y", step) for step in (1, 2, 3)]
     other = [lax.ppermute(plane, "c", [(0, 1), (1, 0)]) for plane in own]
 
@@ -382,6 +379,7 @@
         limit=LARGE_LIMIT,
         first=(3, 4, 2, 0, 1, 5, 6, 7, 8),
     )
+    state = lax.ppermute(state, Z + TENSOR, pairs)
     back = [back[0]] + [shift(back[step], "y", step) for step in (1, 2, 3)]
     shares = lax.all_to_all(shares, Z, 0, 0)
 
@@ -392,13 +390,17 @@
         (pos, shares, state, *back),
     )
     back = [back[0]] + [shift(back[step], ("xh", "xl"), step) for step in (1, 2, 3)]
-    ring = to_all(new_coded.astype(BF16), Z, 16)
     new_state = lax.ppermute(new_state, Z + TENSOR, pairs)
-    grad_in = ((back[0] + back[1]) + (back[2] + back[3])).astype(BF16)
-    ring = jnp.broadcast_to(ring.reshape(1, 8, 2, 3, SHARD, COLS), (4, 8, 2, 3, SHARD, COLS))
-    ring = lax.all_to_all(ring.reshape(32, 2, 3, SHARD, COLS), ("y",) + TENSOR, 0, 0)
-    new_weights = ring.transpose(2, 0, 1, 3, 4).reshape(3, 64 * SHARD, COLS)
-    return (grad_in, new_state[0], new_state[1], new_state[2], new_weights)
+    ring = to_all(new_coded.astype(BF16), Z, 16).reshape(48 * SHARD, COLS)
+    ring, grad_in, updated, first, second = call(
+        finish_kernel,
+        (struct((4, 48 * SHARD, COLS), BF16), struct((TOK, COLS), BF16)) + (struct((3, SHARD, COLS)),) * 3,
+        0,
+        (ring, new_state, *back),
+    )
+    ring = lax.all_to_all(ring.reshape(32, 6 * SHARD, COLS), ("y",) + TENSOR, 0, 0)
+    new_weights = ring.reshape(32, 2, 3, SHARD, COLS).transpose(2, 0, 1, 3, 4).reshape(3, 64 * SHARD, COLS)
+    return (grad_in, updated, first, second, new_weights)
 
 
 def solution(mesh):

time: 216 us -> 226 us (1.046)
  the two profiles are of different devices: /device:TPU:2 before, /device:TPU:129 now
where the time goes in v5:
time: 226 us; the launch traced here: 225 us
  starting transfers between devices  119 us (53%)
  waiting for transfers between devices  50.6 us (22%)
  blocking collectives  32.9 us (15%)
  Pallas kernels  15.5 us (7%)
  local copies, waits for them, and re-layouts  4.42 us (2%)
    ppermute x12, starting transfers between devices, shift(): return lax.ppermute(value, axes, [(i, (i + step) % 4) for i in range(4)])  45.5 us
    all_to_all x1, blocking collectives, on_device(): lax.all_to_all(ring.reshape(32, 6 * SHARD, COLS), ('y',) + TENSOR, 0, 0)  32.9 us
    ppermute x1, waiting for transfers between devices, on_device(): state = lax.ppermute(state, Z + TENSOR, pairs)  24.6 us
    pallas_call x5, Pallas kernels, call(): pl.pallas_call(body, out_shape=out_shape, in_specs=specs, out_specs=anywh...  15.5 us
    all_to_all x1, starting transfers between devices, on_device(): rows = lax.all_to_all(coded.reshape(16, 3 * SHARD, COLS), Z, 0, 0)  13.3 us
    ppermute x4, starting transfers between devices, on_device(): other = [lax.ppermute(plane, 'c', [(0, 1), (1, 0)]) for plane in own]  12.4 us
    all_to_all x1, starting transfers between devices, on_device(): peaks = lax.all_to_all(peak, ('xl', 'c') + Z, 0, 0)  12.2 us
    all_to_all x1, starting transfers between devices, to_all(): lax.all_to_all(jnp.broadcast_to(value[None], (peers,) + value.shape), axe...  10.6 us
  transfers between devices with their start and end apart: 24, of which 7 were waited for; matrix products, arithmetic and copies ran while one was open for 1% of the time, Pallas kernels for 0%

profile of v5, /device:TPU:129, one launch (start us, length us, event | category | flops | bytes accessed | tf_op | source)
XLA Modules:
  0.0 225.1 jit_solution(8706246157903658001)
XLA Ops:
  2.4 13.3 %all-to-all-start = ((bf16[16,72,128]{2,1,0:T(8,128)(2,1)}), bf16[16,72,128]{2,1,0:T(8,128)(2,1)}, u32[]{:S(2)}, u32[]{:S(2)}) async-start(bf16[16,72,128]{2,1,0:T(8,128)(2,1)} %bitcast.25), calls=%async_computation | async-start | bytes 589824 | tf_op jit(solution)/shard_map/all_to_all | solution.py:341
  15.7 4.4 %collective-permute-start.2 = (bf16[272,128]{1,0:T(8,128)(2,1)}, bf16[272,128]{1,0:T(8,128)(2,1)S(1)}, u32[]{:S(2)}, u32[]{:S(2)}) collective-permute-start(bf16[272,128]{1,0:T(8,128)(2,1)} %get-tuple-element.31), channel_id=1, source_target_pairs={{0,6},{2,0},{4,2},{6,4},{1,7},{3,1},{5,3},{7,5},{8,14},{10,8},{12,... | collective-permute-start | bytes 208904 | tf_op jit(solution)/shard_map/ppermute | solution.py:312
  22.1 3.6 %collective-permute-start.1 = (bf16[272,128]{1,0:T(8,128)(2,1)}, bf16[272,128]{1,0:T(8,128)(2,1)S(1)}, u32[]{:S(2)}, u32[]{:S(2)}) collective-permute-start(bf16[272,128]{1,0:T(8,128)(2,1)} %get-tuple-element.31), channel_id=1, source_target_pairs={{0,4},{2,6},{4,0},{6,2},{1,5},{3,7},{5,1},{7,3},{8,12},{10,14},{12... | collective-permute-start | bytes 208904 | tf_op jit(solution)/shard_map/ppermute | solution.py:312
  33.4 4.5 %collective-permute-start.4 = (bf16[4,272,128]{2,1,0:T(8,128)(2,1)S(1)}, bf16[4,272,128]{2,1,0:T(8,128)(2,1)S(1)}, u32[]{:S(2)}, u32[]{:S(2)}) collective-permute-start(bf16[4,272,128]{2,1,0:T(8,128)(2,1)S(1)} %pad_maximum_fusion.refs_1_), channel_id=1, source_target_pairs={{0,256},{128,384},{256,0},{384,128},{1,257},{129,385},{257,1},{385... | collective-permute-start | bytes 835592 | tf_op jit(solution)/shard_map/ppermute | solution.py:312
  40.9 5.0 %collective-permute-start.6 = (bf16[4,272,128]{2,1,0:T(8,128)(2,1)S(1)}, bf16[4,272,128]{2,1,0:T(8,128)(2,1)S(1)}, u32[]{:S(2)}, u32[]{:S(2)}) collective-permute-start(bf16[4,272,128]{2,1,0:T(8,128)(2,1)S(1)} %pad_maximum_fusion.refs_1_), channel_id=1, source_target_pairs={{0,1},{1,0},{2,3},{3,2},{4,5},{5,4},{6,7},{7,6},{8,9},{9,8},{10,11... | collective-permute-start | bytes 835592 | tf_op jit(solution)/shard_map/ppermute | solution.py:345
  47.9 3.6 %collective-permute-start.8 = (bf16[4,272,128]{2,1,0:T(8,128)(2,1)S(1)}, bf16[4,272,128]{2,1,0:T(8,128)(2,1)S(1)}, u32[]{:S(2)}, u32[]{:S(2)}) collective-permute-start(bf16[4,272,128]{2,1,0:T(8,128)(2,1)S(1)} %collective-permute-done.4.refs_3_), channel_id=1, source_target_pairs={{0,1},{1,0},{2,3},{3,2},{4,5},{5,4},{6,7},{7,6},{8,9},{9,8},{10,11... | collective-permute-start | bytes 835592 | tf_op jit(solution)/shard_map/ppermute | solution.py:345
  53.4 4.7 %all-to-all-start.1 = ((bf16[8,144,128]{2,1,0:T(8,128)(2,1)}), bf16[8,144,128]{2,1,0:T(8,128)(2,1)S(1)}, u32[]{:S(2)}, u32[]{:S(2)}) async-start(bf16[8,144,128]{2,1,0:T(8,128)(2,1)} %bitcast.12), calls=%async_computation.1 | async-start | bytes 589824 | tf_op jit(solution)/shard_map/all_to_all | solution.py:342
  58.9 6.1 %all-to-all-done.1 = bf16[8,144,128]{2,1,0:T(8,128)(2,1)S(1)} async-done(((bf16[8,144,128]{2,1,0:T(8,128)(2,1)}), bf16[8,144,128]{2,1,0:T(8,128)(2,1)S(1)}, u32[]{:S(2)}, u32[]{:S(2)}) %all-to-all-start.1) | async-done | bytes 294944 | tf_op jit(solution)/shard_map/all_to_all | solution.py:342
  65.7 4.9 %shard_map.120 = (bf16[512,1024]{1,0:T(8,128)(2,1)}, bf16[512,1024]{1,0:T(8,128)(2,1)}, bf16[4,144,128]{2,1,0:T(8,128)(2,1)}, f32[8,1024]{1,0:T(8,128)}, f32[64,...) custom-call(s32[6]{0:T(128)} %stack.42.refs_0_, bf16[4,272,128]{2,1,0:T(8,128)(2,1)} %copy-done.3, ...), custom_call_target="tpu_custom_call" | custom-call | tf_op jit(solution)/shard_map/pallas_call | solution.py:293
  73.5 12.2 %all-to-all-start.2 = ((f32[64,1,128]{2,1,0:T(1,128)}), f32[64,1,128]{2,1,0:T(1,128)S(1)}, u32[]{:S(2)}, u32[]{:S(2)}) async-start(f32[64,1,128]{2,1,0:T(1,128)} %get-tuple-element.36), calls=%async_computation.2 | async-start | bytes 65536 | tf_op jit(solution)/shard_map/all_to_all | solution.py:371
  86.6 7.4 %all-to-all-done.2.refs_4_ = f32[64,1,128]{2,1,0:T(1,128)S(1)} async-done(((f32[64,1,128]{2,1,0:T(1,128)}), f32[64,1,128]{2,1,0:T(1,128)S(1)}, u32[]{:S(2)}, u32[]{:S(2)}) %all-to-all-start.2) | async-done | bytes 32800 | tf_op jit(solution)/shard_map/all_to_all | solution.py:371
  95.0 5.4 %shard_map.121 = (f32[16,3,24,128]{3,2,1,0:T(8,128)}, f32[4,128,128]{2,1,0:T(8,128)}, f32[4,128,128]{2,1,0:T(8,128)}, f32[4,128,128]{2,1,0:T(8,128)}, f32[4,128,128]{2,1,0:T(8,128)}) custom-call(s32[6]{0:T(128)} %stack.42.refs_0_, bf16[512,1024]{1,0:T(8,128)(2,1)} %get-tuple-element.33.refs_1_, bf16[512,1024]{1,0:T(8,128)(2,1)} %get-tuple-element.34.refs_2_, ...), custom_call_target="tpu_custom_call" | custom-call | tf_op jit(solution)/shard_map/pallas_call | solution.py:293
  100.5 8.4 %all-to-all-start.3 = ((f32[16,3,24,128]{3,2,1,0:T(8,128)}), f32[16,3,24,128]{3,2,1,0:T(8,128)S(1)}, u32[]{:S(2)}, u32[]{:S(2)}) async-start(f32[16,3,24,128]{3,2,1,0:T(8,128)} %get-tuple-element.40), calls=%async_computation.3 | async-start | bytes 1179648 | tf_op jit(solution)/shard_map/all_to_all | solution.py:384
  112.0 3.6 %collective-permute-start.13 = (f32[4,128,128]{2,1,0:T(8,128)S(1)}, f32[4,128,128]{2,1,0:T(8,128)S(1)}, u32[]{:S(2)}, u32[]{:S(2)}) collective-permute-start(f32[4,128,128]{2,1,0:T(8,128)S(1)} %copy-done.14), channel_id=1, source_target_pairs={{0,256},{128,384},{256,0},{384,128},{1,257},{129,385},{257,1},{385... | collective-permute-start | bytes 786440 | tf_op jit(solution)/shard_map/ppermute | solution.py:312
  115.7 3.7 %collective-permute-start.14 = (f32[4,128,128]{2,1,0:T(8,128)S(1)}, f32[4,128,128]{2,1,0:T(8,128)S(1)}, u32[]{:S(2)}, u32[]{:S(2)}) collective-permute-start(f32[4,128,128]{2,1,0:T(8,128)S(1)} %copy-done.13), channel_id=1, source_target_pairs={{0,384},{128,0},{256,128},{384,256},{1,385},{129,1},{257,129},{385... | collective-permute-start | bytes 786440 | tf_op jit(solution)/shard_map/ppermute | solution.py:312
  119.4 4.1 %collective-permute-start.11 = (f32[3,3,24,128]{3,2,1,0:T(8,128)S(1)}, f32[3,3,24,128]{3,2,1,0:T(8,128)S(1)}, u32[]{:S(2)}, u32[]{:S(2)}) collective-permute-start(f32[3,3,24,128]{3,2,1,0:T(8,128)S(1)} %copy-done.16), channel_id=1, source_target_pairs={{0,0},{1,16},{2,32},{3,48},{4,64},{5,80},{6,96},{7,112},{8,8},{9,2... | collective-permute-start | bytes 331784 | tf_op jit(solution)/shard_map/ppermute | solution.py:382
  123.5 24.6 %collective-permute-done.11.refs_2_ = f32[3,3,24,128]{3,2,1,0:T(8,128)S(1)} collective-permute-done((f32[3,3,24,128]{3,2,1,0:T(8,128)S(1)}, f32[3,3,24,128]{3,2,1,0:T(8,128)S(1)}, u32[]{:S(2)}, u32[]{:S(2)}) %collective-permute-start.11) | collective-permute-done | bytes 110624 | tf_op jit(solution)/shard_map/ppermute | solution.py:382
  150.6 10.6 %all-to-all-start.4 = ((bf16[16,3,24,128]{3,2,1,0:T(8,128)(2,1)}), bf16[16,3,24,128]{3,2,1,0:T(8,128)(2,1)S(1)}, u32[]{:S(2)}, u32[]{:S(2)}) async-start(bf16[16,3,24,128]{3,2,1,0:T(8,128)(2,1)} %broadcast_in_dim.16), calls=%async_computation.4 | async-start | bytes 589824 | tf_op jit(solution)/shard_map/all_to_all | solution.py:308
  161.2 4.7 %collective-permute-start.15 = (f32[3,3,24,128]{3,2,1,0:T(8,128)S(1)}, f32[3,3,24,128]{3,2,1,0:T(8,128)S(1)}, u32[]{:S(2)}, u32[]{:S(2)}) collective-permute-start(f32[3,3,24,128]{3,2,1,0:T(8,128)S(1)} %get-tuple-element.47), channel_id=1, source_target_pairs={{0,0},{1,16},{2,32},{3,48},{4,64},{5,80},{6,96},{7,112},{8,8},{9,2... | collective-permute-start | bytes 331784 | tf_op jit(solution)/shard_map/ppermute | solution.py:393
  165.9 4.0 %collective-permute-start.16 = (f32[128,128]{1,0:T(8,128)S(1)}, f32[128,128]{1,0:T(8,128)S(1)}, u32[]{:S(2)}, u32[]{:S(2)}) collective-permute-start(f32[128,128]{1,0:T(8,128)S(1)} %get-tuple-element.49), channel_id=1, source_target_pairs={{0,2},{2,4},{4,6},{6,0},{1,3},{3,5},{5,7},{7,1},{8,10},{10,12},{12... | collective-permute-start | bytes 196616 | tf_op jit(solution)/shard_map/ppermute | solution.py:312
  169.9 6.4 %collective-permute-start.17 = (f32[128,128]{1,0:T(8,128)S(1)}, f32[128,128]{1,0:T(8,128)S(1)}, u32[]{:S(2)}, u32[]{:S(2)}) collective-permute-start(f32[128,128]{1,0:T(8,128)S(1)} %get-tuple-element.50), channel_id=1, source_target_pairs={{0,4},{2,6},{4,0},{6,2},{1,5},{3,7},{5,1},{7,3},{8,12},{10,14},{12... | collective-permute-start | bytes 196616 | tf_op jit(solution)/shard_map/ppermute | solution.py:312
  176.3 4.0 %collective-permute-start.18 = (f32[128,128]{1,0:T(8,128)S(1)}, f32[128,128]{1,0:T(8,128)S(1)}, u32[]{:S(2)}, u32[]{:S(2)}) collective-permute-start(f32[128,128]{1,0:T(8,128)S(1)} %get-tuple-element.51), channel_id=1, source_target_pairs={{0,6},{2,0},{4,2},{6,4},{1,7},{3,1},{5,3},{7,5},{8,14},{10,8},{12,... | collective-permute-start | bytes 196616 | tf_op jit(solution)/shard_map/ppermute | solution.py:312
  182.3 7.0 %collective-permute-done.15.refs_1_ = f32[3,3,24,128]{3,2,1,0:T(8,128)S(1)} collective-permute-done((f32[3,3,24,128]{3,2,1,0:T(8,128)S(1)}, f32[3,3,24,128]{3,2,1,0:T(8,128)S(1)}, u32[]{:S(2)}, u32[]{:S(2)}) %collective-permute-start.15) | collective-permute-done | bytes 110624 | tf_op jit(solution)/shard_map/ppermute | solution.py:393
  191.0 32.9 %all_to_all.30 = bf16[32,144,128]{2,1,0:T(8,128)(2,1)S(1)} all-to-all(bf16[32,144,128]{2,1,0:T(8,128)(2,1)S(1)} %bitcast.20), channel_id=1, replica_groups=mesh['y'=4,'zh'=4,'zl'=4,'xh'=2,'xl'=2,'c'=2] {'y','xh','xl','c'}, dimensions={0} | all-to-all | bytes 2359296 | tf_op jit(solution)/shard_map/all_to_all | solution.py:401
  (72 shorter events, 34.9 us)
Async XLA Ops:
  2.4 51.0 %all-to-all-start = ((bf16[16,72,128]{2,1,0:T(8,128)(2,1)}), bf16[16,72,128]{2,1,0:T(8,128)(2,1)}, u32[]{:S(2)}, u32[]{:S(2)}) async-start(bf16[16,72,128]{2,1,0:T(8,128)(2,1)} %bitcast.25), calls=%async_computation | async-start | bytes 589824 | tf_op jit(solution)/shard_map/all_to_all | solution.py:341
  15.7 9.9 %collective-permute-start.2 = (bf16[272,128]{1,0:T(8,128)(2,1)}, bf16[272,128]{1,0:T(8,128)(2,1)S(1)}, u32[]{:S(2)}, u32[]{:S(2)}) collective-permute-start(bf16[272,128]{1,0:T(8,128)(2,1)} %get-tuple-element.31), channel_id=1, source_target_pairs={{0,6},{2,0},{4,2},{6,4},{1,7},{3,1},{5,3},{7,5},{8,14},{10,8},{12,... | collective-permute-start | bytes 208904 | tf_op jit(solution)/shard_map/ppermute | solution.py:312
  20.1 6.9 %collective-permute-start = (bf16[272,128]{1,0:T(8,128)(2,1)}, bf16[272,128]{1,0:T(8,128)(2,1)S(1)}, u32[]{:S(2)}, u32[]{:S(2)}) collective-permute-start(bf16[272,128]{1,0:T(8,128)(2,1)} %get-tuple-element.31), channel_id=1, source_target_pairs={{0,2},{2,4},{4,6},{6,0},{1,3},{3,5},{5,7},{7,1},{8,10},{10,12},{12... | collective-permute-start | bytes 208904 | tf_op jit(solution)/shard_map/ppermute | solution.py:312
  22.1 7.2 %collective-permute-start.1 = (bf16[272,128]{1,0:T(8,128)(2,1)}, bf16[272,128]{1,0:T(8,128)(2,1)S(1)}, u32[]{:S(2)}, u32[]{:S(2)}) collective-permute-start(bf16[272,128]{1,0:T(8,128)(2,1)} %get-tuple-element.31), channel_id=1, source_target_pairs={{0,4},{2,6},{4,0},{6,2},{1,5},{3,7},{5,1},{7,3},{8,12},{10,14},{12... | collective-permute-start | bytes 208904 | tf_op jit(solution)/shard_map/ppermute | solution.py:312
  30.2 15.8 %collective-permute-start.3 = (bf16[4,272,128]{2,1,0:T(8,128)(2,1)S(1)}, bf16[4,272,128]{2,1,0:T(8,128)(2,1)S(1)}, u32[]{:S(2)}, u32[]{:S(2)}) collective-permute-start(bf16[4,272,128]{2,1,0:T(8,128)(2,1)S(1)} %pad_maximum_fusion.refs_1_), channel_id=1, source_target_pairs={{0,128},{128,256},{256,384},{384,0},{1,129},{129,257},{257,385},{3... | collective-permute-start | bytes 835592 | tf_op jit(solution)/shard_map/ppermute | solution.py:312
  33.4 14.5 %collective-permute-start.4 = (bf16[4,272,128]{2,1,0:T(8,128)(2,1)S(1)}, bf16[4,272,128]{2,1,0:T(8,128)(2,1)S(1)}, u32[]{:S(2)}, u32[]{:S(2)}) collective-permute-start(bf16[4,272,128]{2,1,0:T(8,128)(2,1)S(1)} %pad_maximum_fusion.refs_1_), channel_id=1, source_target_pairs={{0,256},{128,384},{256,0},{384,128},{1,257},{129,385},{257,1},{385... | collective-permute-start | bytes 835592 | tf_op jit(solution)/shard_map/ppermute | solution.py:312
  37.9 13.5 %collective-permute-start.5 = (bf16[4,272,128]{2,1,0:T(8,128)(2,1)S(1)}, bf16[4,272,128]{2,1,0:T(8,128)(2,1)S(1)}, u32[]{:S(2)}, u32[]{:S(2)}) collective-permute-start(bf16[4,272,128]{2,1,0:T(8,128)(2,1)S(1)} %pad_maximum_fusion.refs_1_), channel_id=1, source_target_pairs={{0,384},{128,0},{256,128},{384,256},{1,385},{129,1},{257,129},{385... | collective-permute-start | bytes 835592 | tf_op jit(solution)/shard_map/ppermute | solution.py:312
  40.9 17.9 %collective-permute-start.6 = (bf16[4,272,128]{2,1,0:T(8,128)(2,1)S(1)}, bf16[4,272,128]{2,1,0:T(8,128)(2,1)S(1)}, u32[]{:S(2)}, u32[]{:S(2)}) collective-permute-start(bf16[4,272,128]{2,1,0:T(8,128)(2,1)S(1)} %pad_maximum_fusion.refs_1_), channel_id=1, source_target_pairs={{0,1},{1,0},{2,3},{3,2},{4,5},{5,4},{6,7},{7,6},{8,9},{9,8},{10,11... | collective-permute-start | bytes 835592 | tf_op jit(solution)/shard_map/ppermute | solution.py:345
  45.9 12.9 %collective-permute-start.7 = (bf16[4,272,128]{2,1,0:T(8,128)(2,1)S(1)}, bf16[4,272,128]{2,1,0:T(8,128)(2,1)S(1)}, u32[]{:S(2)}, u32[]{:S(2)}) collective-permute-start(bf16[4,272,128]{2,1,0:T(8,128)(2,1)S(1)} %collective-permute-done.3.refs_2_), channel_id=1, source_target_pairs={{0,1},{1,0},{2,3},{3,2},{4,5},{5,4},{6,7},{7,6},{8,9},{9,8},{10,11... | collective-permute-start | bytes 835592 | tf_op jit(solution)/shard_map/ppermute | solution.py:345
  47.9 10.9 %collective-permute-start.8 = (bf16[4,272,128]{2,1,0:T(8,128)(2,1)S(1)}, bf16[4,272,128]{2,1,0:T(8,128)(2,1)S(1)}, u32[]{:S(2)}, u32[]{:S(2)}) collective-permute-start(bf16[4,272,128]{2,1,0:T(8,128)(2,1)S(1)} %collective-permute-done.4.refs_3_), channel_id=1, source_target_pairs={{0,1},{1,0},{2,3},{3,2},{4,5},{5,4},{6,7},{7,6},{8,9},{9,8},{10,11... | collective-permute-start | bytes 835592 | tf_op jit(solution)/shard_map/ppermute | solution.py:345
  51.5 7.4 %collective-permute-start.9 = (bf16[4,272,128]{2,1,0:T(8,128)(2,1)S(1)}, bf16[4,272,128]{2,1,0:T(8,128)(2,1)S(1)}, u32[]{:S(2)}, u32[]{:S(2)}) collective-permute-start(bf16[4,272,128]{2,1,0:T(8,128)(2,1)S(1)} %collective-permute-done.5.refs_4_), channel_id=1, source_target_pairs={{0,1},{1,0},{2,3},{3,2},{4,5},{5,4},{6,7},{7,6},{8,9},{9,8},{10,11... | collective-permute-start | bytes 835592 | tf_op jit(solution)/shard_map/ppermute | solution.py:345
  53.4 11.5 %all-to-all-start.1 = ((bf16[8,144,128]{2,1,0:T(8,128)(2,1)}), bf16[8,144,128]{2,1,0:T(8,128)(2,1)S(1)}, u32[]{:S(2)}, u32[]{:S(2)}) async-start(bf16[8,144,128]{2,1,0:T(8,128)(2,1)} %bitcast.12), calls=%async_computation.1 | async-start | bytes 589824 | tf_op jit(solution)/shard_map/all_to_all | solution.py:342
  70.5 23.5 %collective-permute-start.10 = (f32[16,128,128]{2,1,0:T(8,128)}, f32[16,128,128]{2,1,0:T(8,128)S(1)}, u32[]{:S(2)}, u32[]{:S(2)}) collective-permute-start(f32[16,128,128]{2,1,0:T(8,128)} %get-tuple-element.39), channel_id=1, source_target_pairs={{0,1},{1,0},{2,3},{3,2},{4,5},{5,4},{6,7},{7,6},{8,9},{9,8},{10,11... | collective-permute-start | bytes 3145736 | tf_op jit(solution)/shard_map/ppermute | solution.py:372
  73.5 20.5 %all-to-all-start.2 = ((f32[64,1,128]{2,1,0:T(1,128)}), f32[64,1,128]{2,1,0:T(1,128)S(1)}, u32[]{:S(2)}, u32[]{:S(2)}) async-start(f32[64,1,128]{2,1,0:T(1,128)} %get-tuple-element.36), calls=%async_computation.2 | async-start | bytes 65536 | tf_op jit(solution)/shard_map/all_to_all | solution.py:371
  100.5 47.6 %all-to-all-start.3 = ((f32[16,3,24,128]{3,2,1,0:T(8,128)}), f32[16,3,24,128]{3,2,1,0:T(8,128)S(1)}, u32[]{:S(2)}, u32[]{:S(2)}) async-start(f32[16,3,24,128]{3,2,1,0:T(8,128)} %get-tuple-element.40), calls=%async_computation.3 | async-start | bytes 1179648 | tf_op jit(solution)/shard_map/all_to_all | solution.py:384
  108.8 39.2 %collective-permute-start.12 = (f32[4,128,128]{2,1,0:T(8,128)S(1)}, f32[4,128,128]{2,1,0:T(8,128)S(1)}, u32[]{:S(2)}, u32[]{:S(2)}) collective-permute-start(f32[4,128,128]{2,1,0:T(8,128)S(1)} %copy-done.15), channel_id=1, source_target_pairs={{0,128},{128,256},{256,384},{384,0},{1,129},{129,257},{257,385},{3... | collective-permute-start | bytes 786440 | tf_op jit(solution)/shard_map/ppermute | solution.py:312
  112.0 36.1 %collective-permute-start.13 = (f32[4,128,128]{2,1,0:T(8,128)S(1)}, f32[4,128,128]{2,1,0:T(8,128)S(1)}, u32[]{:S(2)}, u32[]{:S(2)}) collective-permute-start(f32[4,128,128]{2,1,0:T(8,128)S(1)} %copy-done.14), channel_id=1, source_target_pairs={{0,256},{128,384},{256,0},{384,128},{1,257},{129,385},{257,1},{385... | collective-permute-start | bytes 786440 | tf_op jit(solution)/shard_map/ppermute | solution.py:312
  115.7 32.4 %collective-permute-start.14 = (f32[4,128,128]{2,1,0:T(8,128)S(1)}, f32[4,128,128]{2,1,0:T(8,128)S(1)}, u32[]{:S(2)}, u32[]{:S(2)}) collective-permute-start(f32[4,128,128]{2,1,0:T(8,128)S(1)} %copy-done.13), channel_id=1, source_target_pairs={{0,384},{128,0},{256,128},{384,256},{1,385},{129,1},{257,129},{385... | collective-permute-start | bytes 786440 | tf_op jit(solution)/shard_map/ppermute | solution.py:312
  119.4 28.7 %collective-permute-start.11 = (f32[3,3,24,128]{3,2,1,0:T(8,128)S(1)}, f32[3,3,24,128]{3,2,1,0:T(8,128)S(1)}, u32[]{:S(2)}, u32[]{:S(2)}) collective-permute-start(f32[3,3,24,128]{3,2,1,0:T(8,128)S(1)} %copy-done.16), channel_id=1, source_target_pairs={{0,0},{1,16},{2,32},{3,48},{4,64},{5,80},{6,96},{7,112},{8,8},{9,2... | collective-permute-start | bytes 331784 | tf_op jit(solution)/shard_map/ppermute | solution.py:382
  150.6 38.7 %all-to-all-start.4 = ((bf16[16,3,24,128]{3,2,1,0:T(8,128)(2,1)}), bf16[16,3,24,128]{3,2,1,0:T(8,128)(2,1)S(1)}, u32[]{:S(2)}, u32[]{:S(2)}) async-start(bf16[16,3,24,128]{3,2,1,0:T(8,128)(2,1)} %broadcast_in_dim.16), calls=%async_computation.4 | async-start | bytes 589824 | tf_op jit(solution)/shard_map/all_to_all | solution.py:308
  161.2 28.1 %collective-permute-start.15 = (f32[3,3,24,128]{3,2,1,0:T(8,128)S(1)}, f32[3,3,24,128]{3,2,1,0:T(8,128)S(1)}, u32[]{:S(2)}, u32[]{:S(2)}) collective-permute-start(f32[3,3,24,128]{3,2,1,0:T(8,128)S(1)} %get-tuple-element.47), channel_id=1, source_target_pairs={{0,0},{1,16},{2,32},{3,48},{4,64},{5,80},{6,96},{7,112},{8,8},{9,2... | collective-permute-start | bytes 331784 | tf_op jit(solution)/shard_map/ppermute | solution.py:393
  165.9 14.4 %collective-permute-start.16 = (f32[128,128]{1,0:T(8,128)S(1)}, f32[128,128]{1,0:T(8,128)S(1)}, u32[]{:S(2)}, u32[]{:S(2)}) collective-permute-start(f32[128,128]{1,0:T(8,128)S(1)} %get-tuple-element.49), channel_id=1, source_target_pairs={{0,2},{2,4},{4,6},{6,0},{1,3},{3,5},{5,7},{7,1},{8,10},{10,12},{12... | collective-permute-start | bytes 196616 | tf_op jit(solution)/shard_map/ppermute | solution.py:312
  169.9 10.4 %collective-permute-start.17 = (f32[128,128]{1,0:T(8,128)S(1)}, f32[128,128]{1,0:T(8,128)S(1)}, u32[]{:S(2)}, u32[]{:S(2)}) collective-permute-start(f32[128,128]{1,0:T(8,128)S(1)} %get-tuple-element.50), channel_id=1, source_target_pairs={{0,4},{2,6},{4,0},{6,2},{1,5},{3,7},{5,1},{7,3},{8,12},{10,14},{12... | collective-permute-start | bytes 196616 | tf_op jit(solution)/shard_map/ppermute | solution.py:312
  176.3 6.0 %collective-permute-start.18 = (f32[128,128]{1,0:T(8,128)S(1)}, f32[128,128]{1,0:T(8,128)S(1)}, u32[]{:S(2)}, u32[]{:S(2)}) collective-permute-start(f32[128,128]{1,0:T(8,128)S(1)} %get-tuple-element.51), channel_id=1, source_target_pairs={{0,6},{2,0},{4,2},{6,4},{1,7},{3,1},{5,3},{7,5},{8,14},{10,8},{12,... | collective-permute-start | bytes 196616 | tf_op jit(solution)/shard_map/ppermute | solution.py:312
  (17 other events, 261.2 us)

commit v6 on v5

--- a/solution.py
+++ b/solution.py
@@ -66,7 +66,15 @@
     )
 
 
-def pack_kernel(acts_ref, grad_ref, dither_ref, master_ref, one_ref, two_ref, packed_ref, coded_ref, state_ref, wide_ref):
+def spread_coded(coded, coded_ref, wide_ref):
+    for mat in range(6):
+        wide_ref[mat * SHARD : (mat + 1) * SHARD, :] = coded[mat % 3]
+    narrow = wide_ref[...].astype(BF16)
+    for pair in range(8):
+        coded_ref[pair * 6 * SHARD : (pair + 1) * 6 * SHARD, :] = narrow
+
+
+def pack_kernel(acts_ref, grad_ref, dither_ref, master_ref, packed_ref, coded_ref, wide_ref):
     high = (dither_ref[...] >> 3).astype(F32)
     low = (dither_ref[...] & 7).astype(F32)
     row = lax.broadcasted_iota(jnp.int32, (16, COLS), 0)
@@ -74,23 +82,28 @@
     packed_ref[0:TOK, :] = acts_ref[...]
     packed_ref[TOK : 2 * TOK, :] = grad_ref[...]
     packed_ref[2 * TOK : PACK, :] = extra
-    coded = eightbit_f32(master_ref[...])
-    for mat in range(6):
-        wide_ref[mat * SHARD : (mat + 1) * SHARD, :] = coded[mat % 3]
-    narrow = wide_ref[...].astype(BF16)
-    for pair in range(8):
-        coded_ref[pair * 6 * SHARD : (pair + 1) * 6 * SHARD, :] = narrow
-    state_ref[0] = master_ref[...]
-    state_ref[1] = one_ref[...]
-    state_ref[2] = two_ref[...]
+    spread_coded(eightbit_f32(master_ref[...]), coded_ref, wide_ref)
+
+
+def join_kernel(_, *refs):
+    parts, joined_ref, sems = refs[:-2], refs[-2], refs[-1]
+    size = joined_ref.shape[0] // len(parts)
+    copies = [
+        pltpu.make_async_copy(part, joined_ref.at[pl.ds(i * size, size)], sems.at[i])
+        for i, part in enumerate(parts)
+    ]
+    for copy in copies:
+        copy.start()
+    for copy in copies:
+        copy.wait()
 
 
 def front_kernel(need, done, pos_ref, *refs):
-    planes, refs = (refs[:4], refs[4:8]), refs[8:]
+    near, far, refs = refs[0:3:2], refs[1:4:2], refs[4:]
     rows_ref, xs_ref, gs_ref, terms_ref, col_ref, peak_ref, keep_ref, give_ref = refs[:8]
     wide_ref, full_ref, weights_ref = refs[8:]
     core = pos_ref[0]
-    need(8)
+    need(4)
     wide_ref[...] = rows_ref[...].astype(F32)
     for depth in range(16):
         cols = slice((depth // 2) * COLS, (depth // 2 + 1) * COLS)
@@ -103,15 +116,16 @@
         rep = (pos_ref[4] + 4 - step) % 4
         rows = pl.ds(pl.multiple_of(rep * TOK, TOK), TOK)
         for side, which in ((0, core), (1, 1 - core)):
-            group = planes[side]
-            need(4 * side + step)
+            if step < 2:
+                need(2 * side + step)
             for chip in range(4):
+                source = far[side].at[(step - 1) * 4 + chip] if step else near[side].at[chip]
                 column = (pos_ref[5] + 4 - chip) % 4
                 cols = pl.ds(pl.multiple_of((2 * column + which) * COLS, COLS), COLS)
-                xs_ref[rows, cols] = group[step][chip, 0:TOK, :]
-                gs_ref[rows, cols] = group[step][chip, TOK : 2 * TOK, :]
+                xs_ref[rows, cols] = source[0:TOK, :]
+                gs_ref[rows, cols] = source[TOK : 2 * TOK, :]
                 if step == 0:
-                    pair = group[0][chip, 2 * TOK : PACK, :].astype(F32)
+                    pair = source[2 * TOK : PACK, :].astype(F32)
                     dither = pair[0:1] * 8.0 + pair[1:2]
                     col_ref[:, cols] = jnp.broadcast_to(dither * (1.0 / 1024.0), (8, COLS))
     done(0, 1, 3)
@@ -222,31 +236,32 @@
         done(1 + step)
 
 
-def adam_kernel(pos_ref, shares_ref, state_ref, own_ref, up_ref, across_ref, down_ref, new_state_ref, coded_ref, *back_refs):
-    chip = pos_ref[5]
-    for step, back_ref in enumerate(back_refs):
-        which = (chip + step) % 4
-        back_ref[...] = (own_ref[which] + up_ref[which]) + (across_ref[which] + down_ref[which])
+def sum_kernel(pos_ref, shares_ref, own_ref, up_ref, across_ref, down_ref, mean_ref, *back_refs):
     mean_grad = shares_ref[0]
     for peer in range(1, 16):
         mean_grad = mean_grad + shares_ref[peer]
-    master = state_ref[0]
-    first = BETA_ONE * state_ref[1] + (1.0 - BETA_ONE) * mean_grad
-    second = BETA_TWO * state_ref[2] + (1.0 - BETA_TWO) * mean_grad * mean_grad
+    mean_ref[...] = mean_grad
+    for step, back_ref in enumerate(back_refs):
+        which = (pos_ref[5] + step) % 4
+        back_ref[...] = (own_ref[which] + up_ref[which]) + (across_ref[which] + down_ref[which])
+
+
+def adam_kernel(mean_ref, master_ref, one_ref, two_ref, new_master_ref, new_one_ref, new_two_ref, coded_ref, wide_ref):
+    mean_grad = mean_ref[...]
+    master = master_ref[...]
+    first = BETA_ONE * one_ref[...] + (1.0 - BETA_ONE) * mean_grad
+    second = BETA_TWO * two_ref[...] + (1.0 - BETA_TWO) * mean_grad * mean_grad
     updated = master - LEARN_RATE * (first / (jnp.sqrt(second) + ADAM_EPS) + WEIGHT_DECAY * master)
-    new_state_ref[0] = updated
-    new_state_ref[1] = first
-    new_state_ref[2] = second
-    coded_ref[...] = eightbit_f32(updated)
-
-
-def finish_kernel(ring_ref, state_ref, own_ref, right_ref, across_ref, left_ref, *outs):
-    spread_ref, grad_ref, state_outs = outs[0], outs[1], outs[2:]
+    new_master_ref[...] = updated
+    new_one_ref[...] = first
+    new_two_ref[...] = second
+    spread_coded(eightbit_f32(updated), coded_ref, wide_ref)
+
+
+def finish_kernel(ring_ref, own_ref, right_ref, across_ref, left_ref, spread_ref, grad_ref):
     for plane in range(4):
         spread_ref[plane] = ring_ref[...]
     grad_ref[...] = ((own_ref[...] + right_ref[...]) + (across_ref[...] + left_ref[...])).astype(BF16)
-    for which, out_ref in enumerate(state_outs):
-        out_ref[...] = state_ref[which]
 
 
 def call(kernel, out_shape, smem=0, operands=(), scratch=(), limit=SMALL_LIMIT, first=None):
@@ -300,12 +315,21 @@
     )(*operands)
 
 
+def join(after, parts):
+    shape = (len(parts) * parts[0].shape[0],) + parts[0].shape[1:]
+    anywhere = pl.BlockSpec(memory_space=pl.ANY)
+    return pl.pallas_call(
+        join_kernel,
+        out_shape=struct(shape, parts[0].dtype),
+        in_specs=[anywhere] * (1 + len(parts)),
+        out_specs=anywhere,
+        scratch_shapes=[pltpu.SemaphoreType.DMA((len(parts),))],
+        compiler_params=pltpu.CompilerParams(vmem_limit_bytes=SMALL_LIMIT),
+    )(after, *parts)
+
+
 def struct(shape, dtype=F32):
     return jax.ShapeDtypeStruct(shape, dtype)
-
-
-def to_all(value, axes, peers):
-    return lax.all_to_all(jnp.broadcast_to(value[None], (peers,) + value.shape), axes, 0, 0)
 
 
 def shift(value, axes, step):
@@ -330,19 +354,20 @@
     pos = jnp.stack([core, spot, unit, z, y, tensor // 2]).astype(jnp.int32)
     pairs = swap_pairs()
 
-    packed, coded, state = call(
+    packed, coded = call(
         pack_kernel,
-        (struct((PACK, COLS), BF16), struct((48 * SHARD, COLS), BF16), struct((3, 3, SHARD, COLS))),
+        (struct((PACK, COLS), BF16), struct((48 * SHARD, COLS), BF16)),
         0,
-        (acts, grad_out, col_dither[None], master, moment_one, moment_two),
+        (acts, grad_out, col_dither[None], master),
         (pltpu.VMEM((6 * SHARD, COLS), F32),),
         limit=LARGE_LIMIT,
     )
-    rows = lax.all_to_all(coded.reshape(16, 3 * SHARD, COLS), Z, 0, 0)
+    rows = lax.all_to_all(coded.reshape(16, 3 * SHARD, COLS), Z, 0, 0).reshape(48 * SHARD, COLS)
+    joined = join(rows, [packed[None]] + [shift(packed[None], ("xh", "xl"), step) for step in (1, 2, 3)])
     rows = lax.all_to_all(rows.reshape(8, 6 * SHARD, COLS), TENSOR, 0, 0).reshape(48 * SHARD, COLS)
-    joined = jnp.stack([packed] + [shift(packed, ("xh", "xl"), step) for step in (1, 2, 3)])
-    own = [joined] + [shift(joined, "y", step) for step in (1, 2, 3)]
-    other = [lax.ppermute(plane, "c", [(0, 1), (1, 0)]) for plane in own]
+    joined_other = lax.ppermute(joined, "c", [(0, 1), (1, 0)])
+    bundle = join(rows, [shift(joined, "y", step) for step in (1, 2, 3)])
+    bundle_other = lax.ppermute(bundle, "c", [(0, 1), (1, 0)])
 
     row_part = lax.dynamic_slice(row_dither, (0, BLOCK * (8 * y + tensor)), (3, BLOCK))
     row_part = jnp.broadcast_to(row_part.astype(F32).reshape(3 * BLOCK, 1) * (1.0 / 1024.0), (3 * BLOCK, COLS))
@@ -359,14 +384,14 @@
             struct((16, TOK, COLS)),
         ),
         1,
-        (pos, *own, *other, rows),
+        (pos, joined, bundle, joined_other, bundle_other, rows),
         (
             pltpu.VMEM((48 * SHARD, COLS), F32),
             pltpu.VMEM((3 * BLOCK, 1024), F32),
             pltpu.VMEM((3 * BLOCK, 1024), BF16),
         ),
         limit=LARGE_LIMIT,
-        first=(8, 0, 4, 1, 5, 2, 6, 3, 7),
+        first=(4, 0, 2, 1, 3),
     )
     peaks = lax.all_to_all(peak, ("xl", "c") + Z, 0, 0)
     got = lax.ppermute(give, "c", [(0, 1), (1, 0)])
@@ -379,27 +404,34 @@
         limit=LARGE_LIMIT,
         first=(3, 4, 2, 0, 1, 5, 6, 7, 8),
     )
-    state = lax.ppermute(state, Z + TENSOR, pairs)
     back = [back[0]] + [shift(back[step], "y", step) for step in (1, 2, 3)]
     shares = lax.all_to_all(shares, Z, 0, 0)
 
-    new_state, new_coded, *back = call(
+    mean_grad, *back = call(
+        sum_kernel,
+        (struct((3, SHARD, COLS)),) + (struct((TOK, COLS)),) * 4,
+        1,
+        (pos, shares, *back),
+    )
+    mean_grad = lax.ppermute(mean_grad, Z + TENSOR, pairs)
+    back = [back[0]] + [shift(back[step], ("xh", "xl"), step) for step in (1, 2, 3)]
+
+    updated, first, second, ring = call(
         adam_kernel,
-        (struct((3, 3, SHARD, COLS)), struct((3, SHARD, COLS))) + (struct((TOK, COLS)),) * 4,
-        1,
-        (pos, shares, state, *back),
-    )
-    back = [back[0]] + [shift(back[step], ("xh", "xl"), step) for step in (1, 2, 3)]
-    new_state = lax.ppermute(new_state, Z + TENSOR, pairs)
-    ring = to_all(new_coded.astype(BF16), Z, 16).reshape(48 * SHARD, COLS)
-    ring, grad_in, updated, first, second = call(
+        (struct((3, SHARD, COLS)),) * 3 + (struct((48 * SHARD, COLS), BF16),),
+        0,
+        (mean_grad, master, moment_one, moment_two),
+        (pltpu.VMEM((6 * SHARD, COLS), F32),),
+    )
+    ring = lax.all_to_all(ring.reshape(16, 3 * SHARD, COLS), Z, 0, 0).reshape(48 * SHARD, COLS)
+    ring, grad_in = call(
         finish_kernel,
-        (struct((4, 48 * SHARD, COLS), BF16), struct((TOK, COLS), BF16)) + (struct((3, SHARD, COLS)),) * 3,
+        (struct((4, 48 * SHARD, COLS), BF16), struct((TOK, COLS), BF16)),
         0,
-        (ring, new_state, *back),
-    )
-    ring = lax.all_to_all(ring.reshape(32, 6 * SHARD, COLS), ("y",) + TENSOR, 0, 0)
-    new_weights = ring.reshape(32, 2, 3, SHARD, COLS).transpose(2, 0, 1, 3, 4).reshape(3, 64 * SHARD, COLS)
+        (ring, *back),
+    )
+    ring = lax.all_to_all(ring, "y", 0, 0)
+    new_weights = ring.reshape(64, 3, SHARD, COLS).transpose(1, 0, 2, 3).reshape(3, 64 * SHARD, COLS)
     return (grad_in, updated, first, second, new_weights)
 
 

time: 226 us -> 205 us (0.907)
  the two profiles are of different devices: /device:TPU:129 before, /device:TPU:32 now
where the time goes in v6:
time: 205 us; the launch traced here: 204 us
  starting transfers between devices  99.1 us (48%)
  waiting for transfers between devices  51.6 us (25%)
  blocking collectives  28.6 us (14%)
  Pallas kernels  17 us (8%)
  local copies, waits for them, and re-layouts  5.5 us (3%)
    ppermute x12, starting transfers between devices, shift(): return lax.ppermute(value, axes, [(i, (i + step) % 4) for i in range(4)])  41 us
    all_to_all x1, starting transfers between devices, on_device(): lax.all_to_all(ring.reshape(16, 3 * SHARD, COLS), Z, 0, 0)  22.9 us
    all_to_all x1, blocking collectives, on_device(): ring = lax.all_to_all(ring, 'y', 0, 0)  16.6 us
    pallas_call x6, Pallas kernels, call(): pl.pallas_call(body, out_shape=out_shape, in_specs=specs, out_specs=anywh...  16.4 us
    all_to_all x1, starting transfers between devices, on_device(): lax.all_to_all(coded.reshape(16, 3 * SHARD, COLS), Z, 0, 0)  15.2 us
    ppermute x12, waiting for transfers between devices, shift(): return lax.ppermute(value, axes, [(i, (i + step) % 4) for i in range(4)])  14.8 us
    all_to_all x1, waiting for transfers between devices, on_device(): shares = lax.all_to_all(shares, Z, 0, 0)  14.4 us
    all_to_all x1, blocking collectives, on_device(): lax.all_to_all(rows.reshape(8, 6 * SHARD, COLS), TENSOR, 0, 0)  12 us
  transfers between devices with their start and end apart: 20, of which 11 were waited for; matrix products, arithmetic and copies ran while one was open for 1% of the time, Pallas kernels for 0%

profile of v6, /device:TPU:32, one launch (start us, length us, event | category | flops | bytes accessed | tf_op | source)
XLA Modules:
  0.0 203.7 jit_solution(2087081098844368125)
XLA Ops:
  2.3 15.2 %all-to-all-start = ((bf16[16,72,128]{2,1,0:T(8,128)(2,1)}), bf16[16,72,128]{2,1,0:T(8,128)(2,1)S(1)}, u32[]{:S(2)}, u32[]{:S(2)}) async-start(bf16[16,72,128]{2,1,0:T(8,128)(2,1)} %bitcast.29), calls=%async_computation | async-start | bytes 589824 | tf_op jit(solution)/shard_map/all_to_all | solution.py:365
  17.6 3.4 %collective-permute-start = (bf16[1,272,128]{2,1,0:T(8,128)(2,1)}, bf16[1,272,128]{2,1,0:T(8,128)(2,1)S(1)}, u32[]{:S(2)}, u32[]{:S(2)}) collective-permute-start(bf16[1,272,128]{2,1,0:T(8,128)(2,1)} %bitcast.23), channel_id=1, source_target_pairs={{0,2},{2,4},{4,6},{6,0},{1,3},{3,5},{5,7},{7,1},{8,10},{10,12},{12... | collective-permute-start | bytes 208904 | tf_op jit(solution)/shard_map/ppermute | solution.py:336
  21.0 4.6 %collective-permute-start.1 = (bf16[1,272,128]{2,1,0:T(8,128)(2,1)}, bf16[1,272,128]{2,1,0:T(8,128)(2,1)S(1)}, u32[]{:S(2)}, u32[]{:S(2)}) collective-permute-start(bf16[1,272,128]{2,1,0:T(8,128)(2,1)} %bitcast.24), channel_id=1, source_target_pairs={{0,4},{2,6},{4,0},{6,2},{1,5},{3,7},{5,1},{7,3},{8,12},{10,14},{12... | collective-permute-start | bytes 208904 | tf_op jit(solution)/shard_map/ppermute | solution.py:336
  25.6 3.3 %collective-permute-start.2 = (bf16[1,272,128]{2,1,0:T(8,128)(2,1)}, bf16[1,272,128]{2,1,0:T(8,128)(2,1)S(1)}, u32[]{:S(2)}, u32[]{:S(2)}) collective-permute-start(bf16[1,272,128]{2,1,0:T(8,128)(2,1)} %bitcast.25), channel_id=1, source_target_pairs={{0,6},{2,0},{4,2},{6,4},{1,7},{3,1},{5,3},{7,5},{8,14},{10,8},{12,... | collective-permute-start | bytes 208904 | tf_op jit(solution)/shard_map/ppermute | solution.py:336
  29.0 3.0 %collective-permute-done.2.refs_3_ = bf16[1,272,128]{2,1,0:T(8,128)(2,1)S(1)} collective-permute-done((bf16[1,272,128]{2,1,0:T(8,128)(2,1)}, bf16[1,272,128]{2,1,0:T(8,128)(2,1)S(1)}, u32[]{:S(2)}, u32[]{:S(2)}) %collective-permute-start.2) | collective-permute-done | bytes 69664 | tf_op jit(solution)/shard_map/ppermute | solution.py:336
  32.0 4.3 %all-to-all-done = bf16[16,72,128]{2,1,0:T(8,128)(2,1)S(1)} async-done(((bf16[16,72,128]{2,1,0:T(8,128)(2,1)}), bf16[16,72,128]{2,1,0:T(8,128)(2,1)S(1)}, u32[]{:S(2)}, u32[]{:S(2)}) %all-to-all-start) | async-done | bytes 294944 | tf_op jit(solution)/shard_map/all_to_all | solution.py:365
  37.6 3.5 %collective-permute-start.3 = (bf16[4,272,128]{2,1,0:T(8,128)(2,1)S(1)}, bf16[4,272,128]{2,1,0:T(8,128)(2,1)S(1)}, u32[]{:S(2)}, u32[]{:S(2)}) collective-permute-start(bf16[4,272,128]{2,1,0:T(8,128)(2,1)S(1)} %shard_map.120.refs_1_), channel_id=1, source_target_pairs={{0,128},{128,256},{256,384},{384,0},{1,129},{129,257},{257,385},{3... | collective-permute-start | bytes 835592 | tf_op jit(solution)/shard_map/ppermute | solution.py:336
  41.1 4.8 %collective-permute-start.4 = (bf16[4,272,128]{2,1,0:T(8,128)(2,1)S(1)}, bf16[4,272,128]{2,1,0:T(8,128)(2,1)S(1)}, u32[]{:S(2)}, u32[]{:S(2)}) collective-permute-start(bf16[4,272,128]{2,1,0:T(8,128)(2,1)S(1)} %shard_map.120.refs_1_), channel_id=1, source_target_pairs={{0,256},{128,384},{256,0},{384,128},{1,257},{129,385},{257,1},{385... | collective-permute-start | bytes 835592 | tf_op jit(solution)/shard_map/ppermute | solution.py:336
  45.9 3.3 %collective-permute-start.5 = (bf16[4,272,128]{2,1,0:T(8,128)(2,1)S(1)}, bf16[4,272,128]{2,1,0:T(8,128)(2,1)S(1)}, u32[]{:S(2)}, u32[]{:S(2)}) collective-permute-start(bf16[4,272,128]{2,1,0:T(8,128)(2,1)S(1)} %shard_map.120.refs_1_), channel_id=1, source_target_pairs={{0,384},{128,0},{256,128},{384,256},{1,385},{129,1},{257,129},{385... | collective-permute-start | bytes 835592 | tf_op jit(solution)/shard_map/ppermute | solution.py:336
  49.2 12.0 %all_to_all.30 = bf16[8,144,128]{2,1,0:T(8,128)(2,1)S(1)} all-to-all(bf16[8,144,128]{2,1,0:T(8,128)(2,1)S(1)} %bitcast.19), channel_id=1, replica_groups=mesh['y'=4,'zh'=4,'zl'=4,'xh'=2,'xl'=2,'c'=2] {'xh','xl','c'}, dimensions={0} | all-to-all | bytes 589824 | tf_op jit(solution)/shard_map/all_to_all | solution.py:367
  68.5 5.4 %shard_map.122 = (bf16[512,1024]{1,0:T(8,128)(2,1)}, bf16[512,1024]{1,0:T(8,128)(2,1)}, bf16[4,144,128]{2,1,0:T(8,128)(2,1)}, f32[8,1024]{1,0:T(8,128)}, f32[64,...) custom-call(s32[6]{0:T(128)} %stack.27.refs_0_, bf16[4,272,128]{2,1,0:T(8,128)(2,1)} %copy-done.2, ...), custom_call_target="tpu_custom_call" | custom-call | tf_op jit(solution)/shard_map/pallas_call | solution.py:308
  76.2 7.9 %all-to-all-start.2 = ((f32[64,1,128]{2,1,0:T(1,128)}), f32[64,1,128]{2,1,0:T(1,128)S(1)}, u32[]{:S(2)}, u32[]{:S(2)}) async-start(f32[64,1,128]{2,1,0:T(1,128)} %get-tuple-element.35), calls=%async_computation.2 | async-start | bytes 65536 | tf_op jit(solution)/shard_map/all_to_all | solution.py:396
  85.0 11.2 %all-to-all-done.2.refs_4_ = f32[64,1,128]{2,1,0:T(1,128)S(1)} async-done(((f32[64,1,128]{2,1,0:T(1,128)}), f32[64,1,128]{2,1,0:T(1,128)S(1)}, u32[]{:S(2)}, u32[]{:S(2)}) %all-to-all-start.2) | async-done | bytes 32800 | tf_op jit(solution)/shard_map/all_to_all | solution.py:396
  97.2 5.4 %shard_map.123 = (f32[16,3,24,128]{3,2,1,0:T(8,128)}, f32[4,128,128]{2,1,0:T(8,128)}, f32[4,128,128]{2,1,0:T(8,128)}, f32[4,128,128]{2,1,0:T(8,128)}, f32[4,128,128]{2,1,0:T(8,128)}) custom-call(s32[6]{0:T(128)} %stack.27.refs_0_, bf16[512,1024]{1,0:T(8,128)(2,1)} %get-tuple-element.32.refs_1_, bf16[512,1024]{1,0:T(8,128)(2,1)} %get-tuple-element.33.refs_2_, ...), custom_call_target="tpu_custom_call" | custom-call | tf_op jit(solution)/shard_map/pallas_call | solution.py:308
  102.7 4.9 %all-to-all-start.3 = ((f32[16,3,24,128]{3,2,1,0:T(8,128)}), f32[16,3,24,128]{3,2,1,0:T(8,128)S(1)}, u32[]{:S(2)}, u32[]{:S(2)}) async-start(f32[16,3,24,128]{3,2,1,0:T(8,128)} %get-tuple-element.39), calls=%async_computation.3 | async-start | bytes 1179648 | tf_op jit(solution)/shard_map/all_to_all | solution.py:408
  109.9 4.9 %collective-permute-start.11 = (f32[4,128,128]{2,1,0:T(8,128)S(1)}, f32[4,128,128]{2,1,0:T(8,128)S(1)}, u32[]{:S(2)}, u32[]{:S(2)}) collective-permute-start(f32[4,128,128]{2,1,0:T(8,128)S(1)} %copy-done.14), channel_id=1, source_target_pairs={{0,384},{128,0},{256,128},{384,256},{1,385},{129,1},{257,129},{385... | collective-permute-start | bytes 786440 | tf_op jit(solution)/shard_map/ppermute | solution.py:336
  119.2 2.8 %collective-permute-done.11.refs_5_ = f32[4,128,128]{2,1,0:T(8,128)S(1)} collective-permute-done((f32[4,128,128]{2,1,0:T(8,128)S(1)}, f32[4,128,128]{2,1,0:T(8,128)S(1)}, u32[]{:S(2)}, u32[]{:S(2)}) %collective-permute-start.11) | collective-permute-done | bytes 262176 | tf_op jit(solution)/shard_map/ppermute | solution.py:336
  122.1 3.3 %collective-permute-done.9.refs_3_ = f32[4,128,128]{2,1,0:T(8,128)S(1)} collective-permute-done((f32[4,128,128]{2,1,0:T(8,128)S(1)}, f32[4,128,128]{2,1,0:T(8,128)S(1)}, u32[]{:S(2)}, u32[]{:S(2)}) %collective-permute-start.9) | collective-permute-done | bytes 262176 | tf_op jit(solution)/shard_map/ppermute | solution.py:336
  125.4 14.4 %all-to-all-done.3.refs_1_ = f32[16,3,24,128]{3,2,1,0:T(8,128)S(1)} async-done(((f32[16,3,24,128]{3,2,1,0:T(8,128)}), f32[16,3,24,128]{3,2,1,0:T(8,128)S(1)}, u32[]{:S(2)}, u32[]{:S(2)}) %all-to-all-start.3) | async-done | bytes 589856 | tf_op jit(solution)/shard_map/all_to_all | solution.py:408
  142.9 22.9 %all-to-all-start.4 = ((bf16[16,72,128]{2,1,0:T(8,128)(2,1)}), bf16[16,72,128]{2,1,0:T(8,128)(2,1)S(1)}, u32[]{:S(2)}, u32[]{:S(2)}) async-start(bf16[16,72,128]{2,1,0:T(8,128)(2,1)} %bitcast.12), calls=%async_computation.4 | async-start | bytes 589824 | tf_op jit(solution)/shard_map/all_to_all | solution.py:426
  167.7 3.9 %collective-permute-start.14 = (f32[128,128]{1,0:T(8,128)S(1)}, f32[128,128]{1,0:T(8,128)S(1)}, u32[]{:S(2)}, u32[]{:S(2)}) collective-permute-start(f32[128,128]{1,0:T(8,128)S(1)} %get-tuple-element.48), channel_id=1, source_target_pairs={{0,4},{2,6},{4,0},{6,2},{1,5},{3,7},{5,1},{7,3},{8,12},{10,14},{12... | collective-permute-start | bytes 196616 | tf_op jit(solution)/shard_map/ppermute | solution.py:336
  171.7 3.1 %collective-permute-start.15 = (f32[128,128]{1,0:T(8,128)S(1)}, f32[128,128]{1,0:T(8,128)S(1)}, u32[]{:S(2)}, u32[]{:S(2)}) collective-permute-start(f32[128,128]{1,0:T(8,128)S(1)} %get-tuple-element.49), channel_id=1, source_target_pairs={{0,6},{2,0},{4,2},{6,4},{1,7},{3,1},{5,3},{7,5},{8,14},{10,8},{12,... | collective-permute-start | bytes 196616 | tf_op jit(solution)/shard_map/ppermute | solution.py:336
  177.9 6.5 %all-to-all-done.4 = bf16[16,72,128]{2,1,0:T(8,128)(2,1)S(1)} async-done(((bf16[16,72,128]{2,1,0:T(8,128)(2,1)}), bf16[16,72,128]{2,1,0:T(8,128)(2,1)S(1)}, u32[]{:S(2)}, u32[]{:S(2)}) %all-to-all-start.4) | async-done | bytes 294944 | tf_op jit(solution)/shard_map/all_to_all | solution.py:426
  185.8 16.6 %all_to_all.31 = bf16[4,1152,128]{2,1,0:T(8,128)(2,1)S(1)} all-to-all(bf16[4,1152,128]{2,1,0:T(8,128)(2,1)S(1)} %get-tuple-element.54), channel_id=1, replica_groups=mesh['y'=4,'zh'=4,'zl'=4,'xh'=2,'xl'=2,'c'=2] {'y'}, dimensions={0} | all-to-all | bytes 2359296 | tf_op jit(solution)/shard_map/all_to_all | solution.py:433
  (63 shorter events, 31.8 us)
Async XLA Ops:
  2.3 34.0 %all-to-all-start = ((bf16[16,72,128]{2,1,0:T(8,128)(2,1)}), bf16[16,72,128]{2,1,0:T(8,128)(2,1)S(1)}, u32[]{:S(2)}, u32[]{:S(2)}) async-start(bf16[16,72,128]{2,1,0:T(8,128)(2,1)} %bitcast.29), calls=%async_computation | async-start | bytes 589824 | tf_op jit(solution)/shard_map/all_to_all | solution.py:365
  17.6 11.4 %collective-permute-start = (bf16[1,272,128]{2,1,0:T(8,128)(2,1)}, bf16[1,272,128]{2,1,0:T(8,128)(2,1)S(1)}, u32[]{:S(2)}, u32[]{:S(2)}) collective-permute-start(bf16[1,272,128]{2,1,0:T(8,128)(2,1)} %bitcast.23), channel_id=1, source_target_pairs={{0,2},{2,4},{4,6},{6,0},{1,3},{3,5},{5,7},{7,1},{8,10},{10,12},{12... | collective-permute-start | bytes 208904 | tf_op jit(solution)/shard_map/ppermute | solution.py:336
  21.0 8.0 %collective-permute-start.1 = (bf16[1,272,128]{2,1,0:T(8,128)(2,1)}, bf16[1,272,128]{2,1,0:T(8,128)(2,1)S(1)}, u32[]{:S(2)}, u32[]{:S(2)}) collective-permute-start(bf16[1,272,128]{2,1,0:T(8,128)(2,1)} %bitcast.24), channel_id=1, source_target_pairs={{0,4},{2,6},{4,0},{6,2},{1,5},{3,7},{5,1},{7,3},{8,12},{10,14},{12... | collective-permute-start | bytes 208904 | tf_op jit(solution)/shard_map/ppermute | solution.py:336
  25.6 6.4 %collective-permute-start.2 = (bf16[1,272,128]{2,1,0:T(8,128)(2,1)}, bf16[1,272,128]{2,1,0:T(8,128)(2,1)S(1)}, u32[]{:S(2)}, u32[]{:S(2)}) collective-permute-start(bf16[1,272,128]{2,1,0:T(8,128)(2,1)} %bitcast.25), channel_id=1, source_target_pairs={{0,6},{2,0},{4,2},{6,4},{1,7},{3,1},{5,3},{7,5},{8,14},{10,8},{12,... | collective-permute-start | bytes 208904 | tf_op jit(solution)/shard_map/ppermute | solution.py:336
  37.6 23.6 %collective-permute-start.3 = (bf16[4,272,128]{2,1,0:T(8,128)(2,1)S(1)}, bf16[4,272,128]{2,1,0:T(8,128)(2,1)S(1)}, u32[]{:S(2)}, u32[]{:S(2)}) collective-permute-start(bf16[4,272,128]{2,1,0:T(8,128)(2,1)S(1)} %shard_map.120.refs_1_), channel_id=1, source_target_pairs={{0,128},{128,256},{256,384},{384,0},{1,129},{129,257},{257,385},{3... | collective-permute-start | bytes 835592 | tf_op jit(solution)/shard_map/ppermute | solution.py:336
  41.1 20.1 %collective-permute-start.4 = (bf16[4,272,128]{2,1,0:T(8,128)(2,1)S(1)}, bf16[4,272,128]{2,1,0:T(8,128)(2,1)S(1)}, u32[]{:S(2)}, u32[]{:S(2)}) collective-permute-start(bf16[4,272,128]{2,1,0:T(8,128)(2,1)S(1)} %shard_map.120.refs_1_), channel_id=1, source_target_pairs={{0,256},{128,384},{256,0},{384,128},{1,257},{129,385},{257,1},{385... | collective-permute-start | bytes 835592 | tf_op jit(solution)/shard_map/ppermute | solution.py:336
  45.9 15.3 %collective-permute-start.5 = (bf16[4,272,128]{2,1,0:T(8,128)(2,1)S(1)}, bf16[4,272,128]{2,1,0:T(8,128)(2,1)S(1)}, u32[]{:S(2)}, u32[]{:S(2)}) collective-permute-start(bf16[4,272,128]{2,1,0:T(8,128)(2,1)S(1)} %shard_map.120.refs_1_), channel_id=1, source_target_pairs={{0,384},{128,0},{256,128},{384,256},{1,385},{129,1},{257,129},{385... | collective-permute-start | bytes 835592 | tf_op jit(solution)/shard_map/ppermute | solution.py:336
  61.4 5.5 %collective-permute-start.7 = (bf16[12,272,128]{2,1,0:T(8,128)(2,1)S(1)}, bf16[12,272,128]{2,1,0:T(8,128)(2,1)S(1)}, u32[]{:S(2)}, u32[]{:S(2)}) collective-permute-start(bf16[12,272,128]{2,1,0:T(8,128)(2,1)S(1)} %shard_map.121.refs_2_), channel_id=1, source_target_pairs={{0,1},{1,0},{2,3},{3,2},{4,5},{5,4},{6,7},{7,6},{8,9},{9,8},{10,11... | collective-permute-start | bytes 2506760 | tf_op jit(solution)/shard_map/ppermute | solution.py:370
  63.3 3.6 %collective-permute-start.6 = (bf16[4,272,128]{2,1,0:T(8,128)(2,1)S(1)}, bf16[4,272,128]{2,1,0:T(8,128)(2,1)S(1)}, u32[]{:S(2)}, u32[]{:S(2)}) collective-permute-start(bf16[4,272,128]{2,1,0:T(8,128)(2,1)S(1)} %shard_map.120.refs_1_), channel_id=1, source_target_pairs={{0,1},{1,0},{2,3},{3,2},{4,5},{5,4},{6,7},{7,6},{8,9},{9,8},{10,11... | collective-permute-start | bytes 835592 | tf_op jit(solution)/shard_map/ppermute | solution.py:368
  73.9 22.3 %collective-permute-start.8 = (f32[16,128,128]{2,1,0:T(8,128)}, f32[16,128,128]{2,1,0:T(8,128)S(1)}, u32[]{:S(2)}, u32[]{:S(2)}) collective-permute-start(f32[16,128,128]{2,1,0:T(8,128)} %get-tuple-element.38), channel_id=1, source_target_pairs={{0,1},{1,0},{2,3},{3,2},{4,5},{5,4},{6,7},{7,6},{8,9},{9,8},{10,11... | collective-permute-start | bytes 3145736 | tf_op jit(solution)/shard_map/ppermute | solution.py:397
  76.2 20.0 %all-to-all-start.2 = ((f32[64,1,128]{2,1,0:T(1,128)}), f32[64,1,128]{2,1,0:T(1,128)S(1)}, u32[]{:S(2)}, u32[]{:S(2)}) async-start(f32[64,1,128]{2,1,0:T(1,128)} %get-tuple-element.35), calls=%async_computation.2 | async-start | bytes 65536 | tf_op jit(solution)/shard_map/all_to_all | solution.py:396
  102.7 37.1 %copy-start.3 = (f32[4,128,128]{2,1,0:T(8,128)S(1)}, f32[4,128,128]{2,1,0:T(8,128)}, u32[]{:S(2)}) copy-start(f32[4,128,128]{2,1,0:T(8,128)} %get-tuple-element.40.refs_2_) | copy-start | bytes 786436
  102.7 39.1 %copy-start.4 = (f32[3,24,128]{2,1,0:T(8,128)S(1)}, f32[3,24,128]{2,1,0:T(8,128)}, u32[]{:S(2)}) copy-start(f32[3,24,128]{2,1,0:T(8,128)} %refs_1_.3) | copy-start | bytes 110596
  102.7 39.1 %copy-start.6 = (f32[3,24,128]{2,1,0:T(8,128)S(1)}, f32[3,24,128]{2,1,0:T(8,128)}, u32[]{:S(2)}) copy-start(f32[3,24,128]{2,1,0:T(8,128)} %refs_2_.1) | copy-start | bytes 110596
  102.7 39.1 %copy-start.7 = (f32[3,24,128]{2,1,0:T(8,128)S(1)}, f32[3,24,128]{2,1,0:T(8,128)}, u32[]{:S(2)}) copy-start(f32[3,24,128]{2,1,0:T(8,128)} %refs_3_.3) | copy-start | bytes 110596
  102.7 37.1 %all-to-all-start.3 = ((f32[16,3,24,128]{3,2,1,0:T(8,128)}), f32[16,3,24,128]{3,2,1,0:T(8,128)S(1)}, u32[]{:S(2)}, u32[]{:S(2)}) async-start(f32[16,3,24,128]{3,2,1,0:T(8,128)} %get-tuple-element.39), calls=%async_computation.3 | async-start | bytes 1179648 | tf_op jit(solution)/shard_map/all_to_all | solution.py:408
  107.6 11.6 %collective-permute-start.10 = (f32[4,128,128]{2,1,0:T(8,128)S(1)}, f32[4,128,128]{2,1,0:T(8,128)S(1)}, u32[]{:S(2)}, u32[]{:S(2)}) collective-permute-start(f32[4,128,128]{2,1,0:T(8,128)S(1)} %copy-done.15), channel_id=1, source_target_pairs={{0,256},{128,384},{256,0},{384,128},{1,257},{129,385},{257,1},{385... | collective-permute-start | bytes 786440 | tf_op jit(solution)/shard_map/ppermute | solution.py:336
  109.9 12.2 %collective-permute-start.11 = (f32[4,128,128]{2,1,0:T(8,128)S(1)}, f32[4,128,128]{2,1,0:T(8,128)S(1)}, u32[]{:S(2)}, u32[]{:S(2)}) collective-permute-start(f32[4,128,128]{2,1,0:T(8,128)S(1)} %copy-done.14), channel_id=1, source_target_pairs={{0,384},{128,0},{256,128},{384,256},{1,385},{129,1},{257,129},{385... | collective-permute-start | bytes 786440 | tf_op jit(solution)/shard_map/ppermute | solution.py:336
  114.8 10.6 %collective-permute-start.9 = (f32[4,128,128]{2,1,0:T(8,128)S(1)}, f32[4,128,128]{2,1,0:T(8,128)S(1)}, u32[]{:S(2)}, u32[]{:S(2)}) collective-permute-start(f32[4,128,128]{2,1,0:T(8,128)S(1)} %copy-done.13), channel_id=1, source_target_pairs={{0,128},{128,256},{256,384},{384,0},{1,129},{129,257},{257,385},{3... | collective-permute-start | bytes 786440 | tf_op jit(solution)/shard_map/ppermute | solution.py:336
  141.1 0.7 collective-permute-start.12
  142.9 41.4 %all-to-all-start.4 = ((bf16[16,72,128]{2,1,0:T(8,128)(2,1)}), bf16[16,72,128]{2,1,0:T(8,128)(2,1)S(1)}, u32[]{:S(2)}, u32[]{:S(2)}) async-start(bf16[16,72,128]{2,1,0:T(8,128)(2,1)} %bitcast.12), calls=%async_computation.4 | async-start | bytes 589824 | tf_op jit(solution)/shard_map/all_to_all | solution.py:426
  165.8 9.0 %collective-permute-start.13 = (f32[128,128]{1,0:T(8,128)S(1)}, f32[128,128]{1,0:T(8,128)S(1)}, u32[]{:S(2)}, u32[]{:S(2)}) collective-permute-start(f32[128,128]{1,0:T(8,128)S(1)} %get-tuple-element.47), channel_id=1, source_target_pairs={{0,2},{2,4},{4,6},{6,0},{1,3},{3,5},{5,7},{7,1},{8,10},{10,12},{12... | collective-permute-start | bytes 196616 | tf_op jit(solution)/shard_map/ppermute | solution.py:336
  167.7 7.7 %collective-permute-start.14 = (f32[128,128]{1,0:T(8,128)S(1)}, f32[128,128]{1,0:T(8,128)S(1)}, u32[]{:S(2)}, u32[]{:S(2)}) collective-permute-start(f32[128,128]{1,0:T(8,128)S(1)} %get-tuple-element.48), channel_id=1, source_target_pairs={{0,4},{2,6},{4,0},{6,2},{1,5},{3,7},{5,1},{7,3},{8,12},{10,14},{12... | collective-permute-start | bytes 196616 | tf_op jit(solution)/shard_map/ppermute | solution.py:336
  171.7 6.2 %collective-permute-start.15 = (f32[128,128]{1,0:T(8,128)S(1)}, f32[128,128]{1,0:T(8,128)S(1)}, u32[]{:S(2)}, u32[]{:S(2)}) collective-permute-start(f32[128,128]{1,0:T(8,128)S(1)} %get-tuple-element.49), channel_id=1, source_target_pairs={{0,6},{2,0},{4,2},{6,4},{1,7},{3,1},{5,3},{7,5},{8,14},{10,8},{12,... | collective-permute-start | bytes 196616 | tf_op jit(solution)/shard_map/ppermute | solution.py:336
  (12 other events, 102.8 us)

commit v7 on v5

--- a/solution.py
+++ b/solution.py
@@ -66,31 +66,37 @@
     )
 
 
-def pack_kernel(acts_ref, grad_ref, dither_ref, master_ref, one_ref, two_ref, packed_ref, coded_ref, state_ref, wide_ref):
-    high = (dither_ref[...] >> 3).astype(F32)
-    low = (dither_ref[...] & 7).astype(F32)
-    row = lax.broadcasted_iota(jnp.int32, (16, COLS), 0)
-    extra = jnp.where(row == 0, high, jnp.where(row == 1, low, 0.0)).astype(BF16)
-    packed_ref[0:TOK, :] = acts_ref[...]
-    packed_ref[TOK : 2 * TOK, :] = grad_ref[...]
-    packed_ref[2 * TOK : PACK, :] = extra
-    coded = eightbit_f32(master_ref[...])
+def spread_coded(coded, coded_ref, wide_ref):
     for mat in range(6):
         wide_ref[mat * SHARD : (mat + 1) * SHARD, :] = coded[mat % 3]
     narrow = wide_ref[...].astype(BF16)
     for pair in range(8):
         coded_ref[pair * 6 * SHARD : (pair + 1) * 6 * SHARD, :] = narrow
+
+
+def pack_kernel(acts_ref, grad_ref, dither_ref, master_ref, one_ref, two_ref, packed_ref, state_ref):
+    high = (dither_ref[...] >> 3).astype(F32)
+    low = (dither_ref[...] & 7).astype(F32)
+    row = lax.broadcasted_iota(jnp.int32, (16, COLS), 0)
+    extra = jnp.where(row == 0, high, jnp.where(row == 1, low, 0.0)).astype(BF16)
+    for peer in range(16):
+        packed_ref[peer, 0:TOK, :] = acts_ref[...]
+        packed_ref[peer, TOK : 2 * TOK, :] = grad_ref[...]
+        packed_ref[peer, 2 * TOK : PACK, :] = extra
     state_ref[0] = master_ref[...]
     state_ref[1] = one_ref[...]
     state_ref[2] = two_ref[...]
 
 
+def code_kernel(state_ref, coded_ref, wide_ref):
+    spread_coded(eightbit_f32(state_ref[0]), coded_ref, wide_ref)
+
+
 def front_kernel(need, done, pos_ref, *refs):
-    planes, refs = (refs[:4], refs[4:8]), refs[8:]
-    rows_ref, xs_ref, gs_ref, terms_ref, col_ref, peak_ref, keep_ref, give_ref = refs[:8]
-    wide_ref, full_ref, weights_ref = refs[8:]
+    rows_ref, xs_ref, gs_ref, terms_ref, col_ref, peak_ref, keep_ref, give_ref = refs[2:10]
+    wide_ref, full_ref, weights_ref = refs[10:]
     core = pos_ref[0]
-    need(8)
+    need(2)
     wide_ref[...] = rows_ref[...].astype(F32)
     for depth in range(16):
         cols = slice((depth // 2) * COLS, (depth // 2 + 1) * COLS)
@@ -99,21 +105,17 @@
             target = mat * BLOCK + (depth % 2) * SHARD
             full_ref[target : target + SHARD, cols] = wide_ref[source : source + SHARD, :]
     weights_ref[...] = full_ref[...].astype(BF16)
-    for step in range(REPS):
-        rep = (pos_ref[4] + 4 - step) % 4
-        rows = pl.ds(pl.multiple_of(rep * TOK, TOK), TOK)
-        for side, which in ((0, core), (1, 1 - core)):
-            group = planes[side]
-            need(4 * side + step)
-            for chip in range(4):
-                column = (pos_ref[5] + 4 - chip) % 4
-                cols = pl.ds(pl.multiple_of((2 * column + which) * COLS, COLS), COLS)
-                xs_ref[rows, cols] = group[step][chip, 0:TOK, :]
-                gs_ref[rows, cols] = group[step][chip, TOK : 2 * TOK, :]
-                if step == 0:
-                    pair = group[0][chip, 2 * TOK : PACK, :].astype(F32)
-                    dither = pair[0:1] * 8.0 + pair[1:2]
-                    col_ref[:, cols] = jnp.broadcast_to(dither * (1.0 / 1024.0), (8, COLS))
+    for side, which in ((0, core), (1, 1 - core)):
+        need(side)
+        for chip in range(4):
+            cols = pl.ds(pl.multiple_of((2 * chip + which) * COLS, COLS), COLS)
+            for rep in range(REPS):
+                rows = slice(rep * TOK, (rep + 1) * TOK)
+                xs_ref[rows, cols] = refs[side][rep * 4 + chip, 0:TOK, :]
+                gs_ref[rows, cols] = refs[side][rep * 4 + chip, TOK : 2 * TOK, :]
+            pair = refs[side][chip, 2 * TOK : PACK, :].astype(F32)
+            dither = pair[0:1] * 8.0 + pair[1:2]
+            col_ref[:, cols] = jnp.broadcast_to(dither * (1.0 / 1024.0), (8, COLS))
     done(0, 1, 3)
     front = dot(weights_ref[0 : 2 * BLOCK, :], xs_ref[...], 1, 1)
     delta = dot(weights_ref[2 * BLOCK : 3 * BLOCK, :], gs_ref[...], 1, 1)
@@ -222,11 +224,8 @@
         done(1 + step)
 
 
-def adam_kernel(pos_ref, shares_ref, state_ref, own_ref, up_ref, across_ref, down_ref, new_state_ref, coded_ref, *back_refs):
-    chip = pos_ref[5]
-    for step, back_ref in enumerate(back_refs):
-        which = (chip + step) % 4
-        back_ref[...] = (own_ref[which] + up_ref[which]) + (across_ref[which] + down_ref[which])
+def adam_kernel(pos_ref, shares_ref, state_ref, own_ref, up_ref, across_ref, down_ref, new_state_ref, coded_ref, *refs):
+    wide_ref = refs[-1]
     mean_grad = shares_ref[0]
     for peer in range(1, 16):
         mean_grad = mean_grad + shares_ref[peer]
@@ -237,16 +236,16 @@
     new_state_ref[0] = updated
     new_state_ref[1] = first
     new_state_ref[2] = second
-    coded_ref[...] = eightbit_f32(updated)
-
-
-def finish_kernel(ring_ref, state_ref, own_ref, right_ref, across_ref, left_ref, *outs):
-    spread_ref, grad_ref, state_outs = outs[0], outs[1], outs[2:]
+    spread_coded(eightbit_f32(updated), coded_ref, wide_ref)
+    for step, back_ref in enumerate(refs[:-1]):
+        which = (pos_ref[5] + step) % 4
+        back_ref[...] = (own_ref[which] + up_ref[which]) + (across_ref[which] + down_ref[which])
+
+
+def finish_kernel(ring_ref, own_ref, right_ref, across_ref, left_ref, spread_ref, grad_ref):
     for plane in range(4):
         spread_ref[plane] = ring_ref[...]
     grad_ref[...] = ((own_ref[...] + right_ref[...]) + (across_ref[...] + left_ref[...])).astype(BF16)
-    for which, out_ref in enumerate(state_outs):
-        out_ref[...] = state_ref[which]
 
 
 def call(kernel, out_shape, smem=0, operands=(), scratch=(), limit=SMALL_LIMIT, first=None):
@@ -304,10 +303,6 @@
     return jax.ShapeDtypeStruct(shape, dtype)
 
 
-def to_all(value, axes, peers):
-    return lax.all_to_all(jnp.broadcast_to(value[None], (peers,) + value.shape), axes, 0, 0)
-
-
 def shift(value, axes, step):
     return lax.ppermute(value, axes, [(i, (i + step) % 4) for i in range(4)])
 
@@ -330,19 +325,19 @@
     pos = jnp.stack([core, spot, unit, z, y, tensor // 2]).astype(jnp.int32)
     pairs = swap_pairs()
 
-    packed, coded, state = call(
+    packed, state = call(
         pack_kernel,
-        (struct((PACK, COLS), BF16), struct((48 * SHARD, COLS), BF16), struct((3, 3, SHARD, COLS))),
+        (struct((16, PACK, COLS), BF16), struct((3, 3, SHARD, COLS))),
         0,
         (acts, grad_out, col_dither[None], master, moment_one, moment_two),
-        (pltpu.VMEM((6 * SHARD, COLS), F32),),
         limit=LARGE_LIMIT,
     )
-    rows = lax.all_to_all(coded.reshape(16, 3 * SHARD, COLS), Z, 0, 0)
-    rows = lax.all_to_all(rows.reshape(8, 6 * SHARD, COLS), TENSOR, 0, 0).reshape(48 * SHARD, COLS)
-    joined = jnp.stack([packed] + [shift(packed, ("xh", "xl"), step) for step in (1, 2, 3)])
-    own = [joined] + [shift(joined, "y", step) for step in (1, 2, 3)]
-    other = [lax.ppermute(plane, "c", [(0, 1), (1, 0)]) for plane in own]
+    state = lax.ppermute(state, Z + TENSOR, pairs)
+    wide = (pltpu.VMEM((6 * SHARD, COLS), F32),)
+    coded = call(code_kernel, struct((48 * SHARD, COLS), BF16), 0, (state,), wide)
+    rows = lax.all_to_all(coded.reshape(16, 3 * SHARD, COLS), Z, 0, 0).reshape(48 * SHARD, COLS)
+    own = lax.all_to_all(packed, ("y", "xh", "xl"), 0, 0)
+    other = lax.ppermute(own, "c", [(0, 1), (1, 0)])
 
     row_part = lax.dynamic_slice(row_dither, (0, BLOCK * (8 * y + tensor)), (3, BLOCK))
     row_part = jnp.broadcast_to(row_part.astype(F32).reshape(3 * BLOCK, 1) * (1.0 / 1024.0), (3 * BLOCK, COLS))
@@ -359,14 +354,14 @@
             struct((16, TOK, COLS)),
         ),
         1,
-        (pos, *own, *other, rows),
+        (pos, own, other, rows),
         (
             pltpu.VMEM((48 * SHARD, COLS), F32),
             pltpu.VMEM((3 * BLOCK, 1024), F32),
             pltpu.VMEM((3 * BLOCK, 1024), BF16),
         ),
         limit=LARGE_LIMIT,
-        first=(8, 0, 4, 1, 5, 2, 6, 3, 7),
+        first=(2, 0, 1),
     )
     peaks = lax.all_to_all(peak, ("xl", "c") + Z, 0, 0)
     got = lax.ppermute(give, "c", [(0, 1), (1, 0)])
@@ -379,28 +374,28 @@
         limit=LARGE_LIMIT,
         first=(3, 4, 2, 0, 1, 5, 6, 7, 8),
     )
-    state = lax.ppermute(state, Z + TENSOR, pairs)
     back = [back[0]] + [shift(back[step], "y", step) for step in (1, 2, 3)]
     shares = lax.all_to_all(shares, Z, 0, 0)
 
-    new_state, new_coded, *back = call(
+    new_state, ring, *back = call(
         adam_kernel,
-        (struct((3, 3, SHARD, COLS)), struct((3, SHARD, COLS))) + (struct((TOK, COLS)),) * 4,
+        (struct((3, 3, SHARD, COLS)), struct((48 * SHARD, COLS), BF16)) + (struct((TOK, COLS)),) * 4,
         1,
         (pos, shares, state, *back),
+        wide,
     )
     back = [back[0]] + [shift(back[step], ("xh", "xl"), step) for step in (1, 2, 3)]
+    ring = lax.all_to_all(ring.reshape(16, 3 * SHARD, COLS), Z, 0, 0).reshape(48 * SHARD, COLS)
+    ring, grad_in = call(
+        finish_kernel,
+        (struct((4, 48 * SHARD, COLS), BF16), struct((TOK, COLS), BF16)),
+        0,
+        (ring, *back),
+    )
     new_state = lax.ppermute(new_state, Z + TENSOR, pairs)
-    ring = to_all(new_coded.astype(BF16), Z, 16).reshape(48 * SHARD, COLS)
-    ring, grad_in, updated, first, second = call(
-        finish_kernel,
-        (struct((4, 48 * SHARD, COLS), BF16), struct((TOK, COLS), BF16)) + (struct((3, SHARD, COLS)),) * 3,
-        0,
-        (ring, new_state, *back),
-    )
     ring = lax.all_to_all(ring.reshape(32, 6 * SHARD, COLS), ("y",) + TENSOR, 0, 0)
     new_weights = ring.reshape(32, 2, 3, SHARD, COLS).transpose(2, 0, 1, 3, 4).reshape(3, 64 * SHARD, COLS)
-    return (grad_in, updated, first, second, new_weights)
+    return (grad_in, new_state[0], new_state[1], new_state[2], new_weights)
 
 
 def solution(mesh):

time: 226 us -> 201 us (0.89)
  the two profiles are of different devices: /device:TPU:129 before, /device:TPU:2 now
where the time goes in v7:
time: 201 us; the launch traced here: 200 us
  waiting for transfers between devices  94.3 us (47%)
  starting transfers between devices  81.4 us (40%)
  Pallas kernels  17.8 us (9%)
  local copies, waits for them, and re-layouts  4.73 us (2%)
    all_to_all x1, waiting for transfers between devices, on_device(): lax.all_to_all(coded.reshape(16, 3 * SHARD, COLS), Z, 0, 0)  20.2 us
    ppermute x6, starting transfers between devices, shift(): return lax.ppermute(value, axes, [(i, (i + step) % 4) for i in range(4)])  19.8 us
    ppermute x1, waiting for transfers between devices, on_device(): new_state = lax.ppermute(new_state, Z + TENSOR, pairs)  18.4 us
    pallas_call x6, Pallas kernels, call(): pl.pallas_call(body, out_shape=out_shape, in_specs=specs, out_specs=anywh...  17.8 us
    ppermute x6, waiting for transfers between devices, shift(): return lax.ppermute(value, axes, [(i, (i + step) % 4) for i in range(4)])  12.6 us
    all_to_all x1, waiting for transfers between devices, on_device(): shares = lax.all_to_all(shares, Z, 0, 0)  11.8 us
    all_to_all x1, waiting for transfers between devices, on_device(): peaks = lax.all_to_all(peak, ('xl', 'c') + Z, 0, 0)  11.5 us
    all_to_all x1, starting transfers between devices, on_device(): lax.all_to_all(coded.reshape(16, 3 * SHARD, COLS), Z, 0, 0)  10.6 us
  transfers between devices with their start and end apart: 16, of which 12 were waited for; matrix products, arithmetic and copies ran while one was open for 1% of the time, Pallas kernels for 0%

profile of v7, /device:TPU:2, one launch (start us, length us, event | category | flops | bytes accessed | tf_op | source)
XLA Modules:
  0.0 199.9 jit_solution(2840520495029488505)
XLA Ops:
  2.7 9.5 %all-to-all-start = ((bf16[16,272,128]{2,1,0:T(8,128)(2,1)}), bf16[16,272,128]{2,1,0:T(8,128)(2,1)S(1)}, u32[]{:S(2)}, u32[]{:S(2)}) async-start(bf16[16,272,128]{2,1,0:T(8,128)(2,1)} %get-tuple-element.27), calls=%async_computation | async-start | bytes 2228224 | tf_op jit(solution)/shard_map/all_to_all | solution.py:339
  12.3 6.7 %collective-permute-start.1 = (f32[3,3,24,128]{3,2,1,0:T(8,128)S(1)}, f32[3,3,24,128]{3,2,1,0:T(8,128)S(1)}, u32[]{:S(2)}, u32[]{:S(2)}) collective-permute-start(f32[3,3,24,128]{3,2,1,0:T(8,128)S(1)} %copy-done.10), channel_id=1, source_target_pairs={{0,0},{1,16},{2,32},{3,48},{4,64},{5,80},{6,96},{7,112},{8,8},{9,2... | collective-permute-start | bytes 331784 | tf_op jit(solution)/shard_map/ppermute | solution.py:335
  19.0 8.3 %all-to-all-done.refs_1_ = bf16[16,272,128]{2,1,0:T(8,128)(2,1)S(1)} async-done(((bf16[16,272,128]{2,1,0:T(8,128)(2,1)}), bf16[16,272,128]{2,1,0:T(8,128)(2,1)S(1)}, u32[]{:S(2)}, u32[]{:S(2)}) %all-to-all-start) | async-done | bytes 1114144 | tf_op jit(solution)/shard_map/all_to_all | solution.py:339
  29.2 5.9 %collective-permute-done.1.refs_0_.refs_2_ = f32[3,3,24,128]{3,2,1,0:T(8,128)S(1)} collective-permute-done((f32[3,3,24,128]{3,2,1,0:T(8,128)S(1)}, f32[3,3,24,128]{3,2,1,0:T(8,128)S(1)}, u32[]{:S(2)}, u32[]{:S(2)}) %collective-permute-start.1) | collective-permute-done | bytes 110624 | tf_op jit(solution)/shard_map/ppermute | solution.py:335
  36.1 10.6 %all-to-all-start.1 = ((bf16[16,72,128]{2,1,0:T(8,128)(2,1)}), bf16[16,72,128]{2,1,0:T(8,128)(2,1)S(1)}, u32[]{:S(2)}, u32[]{:S(2)}) async-start(bf16[16,72,128]{2,1,0:T(8,128)(2,1)} %bitcast.7), calls=%async_computation.1 | async-start | bytes 589824 | tf_op jit(solution)/shard_map/all_to_all | solution.py:338
  47.4 20.2 %all-to-all-done.1 = bf16[16,72,128]{2,1,0:T(8,128)(2,1)S(1)} async-done(((bf16[16,72,128]{2,1,0:T(8,128)(2,1)}), bf16[16,72,128]{2,1,0:T(8,128)(2,1)S(1)}, u32[]{:S(2)}, u32[]{:S(2)}) %all-to-all-start.1) | async-done | bytes 294944 | tf_op jit(solution)/shard_map/all_to_all | solution.py:338
  68.8 5.6 %shard_map.121 = (bf16[512,1024]{1,0:T(8,128)(2,1)}, bf16[512,1024]{1,0:T(8,128)(2,1)}, bf16[4,144,128]{2,1,0:T(8,128)(2,1)}, f32[8,1024]{1,0:T(8,128)}, f32[64,...) custom-call(s32[6]{0:T(128)} %stack.27.refs_0_, bf16[16,272,128]{2,1,0:T(8,128)(2,1)} %copy-done.2, ...), custom_call_target="tpu_custom_call" | custom-call | tf_op jit(solution)/shard_map/pallas_call | solution.py:292
  76.3 8.2 %all-to-all-start.2 = ((f32[64,1,128]{2,1,0:T(1,128)}), f32[64,1,128]{2,1,0:T(1,128)S(1)}, u32[]{:S(2)}, u32[]{:S(2)}) async-start(f32[64,1,128]{2,1,0:T(1,128)} %get-tuple-element.32), calls=%async_computation.2 | async-start | bytes 65536 | tf_op jit(solution)/shard_map/all_to_all | solution.py:366
  85.4 11.5 %all-to-all-done.2.refs_4_ = f32[64,1,128]{2,1,0:T(1,128)S(1)} async-done(((f32[64,1,128]{2,1,0:T(1,128)}), f32[64,1,128]{2,1,0:T(1,128)S(1)}, u32[]{:S(2)}, u32[]{:S(2)}) %all-to-all-start.2) | async-done | bytes 32800 | tf_op jit(solution)/shard_map/all_to_all | solution.py:366
  97.9 5.4 %shard_map.122 = (f32[16,3,24,128]{3,2,1,0:T(8,128)}, f32[4,128,128]{2,1,0:T(8,128)}, f32[4,128,128]{2,1,0:T(8,128)}, f32[4,128,128]{2,1,0:T(8,128)}, f32[4,128,128]{2,1,0:T(8,128)}) custom-call(s32[6]{0:T(128)} %stack.27.refs_0_, bf16[512,1024]{1,0:T(8,128)(2,1)} %get-tuple-element.29.refs_1_, bf16[512,1024]{1,0:T(8,128)(2,1)} %get-tuple-element.30.refs_2_, ...), custom_call_target="tpu_custom_call" | custom-call | tf_op jit(solution)/shard_map/pallas_call | solution.py:292
  103.4 3.7 %all-to-all-start.3 = ((f32[16,3,24,128]{3,2,1,0:T(8,128)}), f32[16,3,24,128]{3,2,1,0:T(8,128)S(1)}, u32[]{:S(2)}, u32[]{:S(2)}) async-start(f32[16,3,24,128]{3,2,1,0:T(8,128)} %get-tuple-element.36), calls=%async_computation.3 | async-start | bytes 1179648 | tf_op jit(solution)/shard_map/all_to_all | solution.py:378
  107.2 2.4 %collective-permute-start.3 = (f32[4,128,128]{2,1,0:T(8,128)S(1)}, f32[4,128,128]{2,1,0:T(8,128)S(1)}, u32[]{:S(2)}, u32[]{:S(2)}) collective-permute-start(f32[4,128,128]{2,1,0:T(8,128)S(1)} %copy-done.9), channel_id=1, source_target_pairs={{0,128},{128,256},{256,384},{384,0},{1,129},{129,257},{257,385},{3... | collective-permute-start | bytes 786440 | tf_op jit(solution)/shard_map/ppermute | solution.py:307
  109.6 4.6 %collective-permute-start.4 = (f32[4,128,128]{2,1,0:T(8,128)S(1)}, f32[4,128,128]{2,1,0:T(8,128)S(1)}, u32[]{:S(2)}, u32[]{:S(2)}) collective-permute-start(f32[4,128,128]{2,1,0:T(8,128)S(1)} %copy-done.8), channel_id=1, source_target_pairs={{0,256},{128,384},{256,0},{384,128},{1,257},{129,385},{257,1},{385... | collective-permute-start | bytes 786440 | tf_op jit(solution)/shard_map/ppermute | solution.py:307
  114.2 3.4 %collective-permute-start.5 = (f32[4,128,128]{2,1,0:T(8,128)S(1)}, f32[4,128,128]{2,1,0:T(8,128)S(1)}, u32[]{:S(2)}, u32[]{:S(2)}) collective-permute-start(f32[4,128,128]{2,1,0:T(8,128)S(1)} %copy-done.7), channel_id=1, source_target_pairs={{0,384},{128,0},{256,128},{384,256},{1,385},{129,1},{257,129},{385... | collective-permute-start | bytes 786440 | tf_op jit(solution)/shard_map/ppermute | solution.py:307
  119.6 3.9 %collective-permute-done.4.refs_5_ = f32[4,128,128]{2,1,0:T(8,128)S(1)} collective-permute-done((f32[4,128,128]{2,1,0:T(8,128)S(1)}, f32[4,128,128]{2,1,0:T(8,128)S(1)}, u32[]{:S(2)}, u32[]{:S(2)}) %collective-permute-start.4) | collective-permute-done | bytes 262176 | tf_op jit(solution)/shard_map/ppermute | solution.py:307
  123.5 2.5 %collective-permute-done.5.refs_6_ = f32[4,128,128]{2,1,0:T(8,128)S(1)} collective-permute-done((f32[4,128,128]{2,1,0:T(8,128)S(1)}, f32[4,128,128]{2,1,0:T(8,128)S(1)}, u32[]{:S(2)}, u32[]{:S(2)}) %collective-permute-start.5) | collective-permute-done | bytes 262176 | tf_op jit(solution)/shard_map/ppermute | solution.py:307
  126.0 11.8 %all-to-all-done.3.refs_1_ = f32[16,3,24,128]{3,2,1,0:T(8,128)S(1)} async-done(((f32[16,3,24,128]{3,2,1,0:T(8,128)}), f32[16,3,24,128]{3,2,1,0:T(8,128)S(1)}, u32[]{:S(2)}, u32[]{:S(2)}) %all-to-all-start.3) | async-done | bytes 589856 | tf_op jit(solution)/shard_map/all_to_all | solution.py:378
  139.8 7.4 %all-to-all-start.4 = ((bf16[16,72,128]{2,1,0:T(8,128)(2,1)}), bf16[16,72,128]{2,1,0:T(8,128)(2,1)S(1)}, u32[]{:S(2)}, u32[]{:S(2)}) async-start(bf16[16,72,128]{2,1,0:T(8,128)(2,1)} %bitcast.9), calls=%async_computation.4 | async-start | bytes 589824 | tf_op jit(solution)/shard_map/all_to_all | solution.py:388
  149.1 5.6 %collective-permute-start.7 = (f32[128,128]{1,0:T(8,128)S(1)}, f32[128,128]{1,0:T(8,128)S(1)}, u32[]{:S(2)}, u32[]{:S(2)}) collective-permute-start(f32[128,128]{1,0:T(8,128)S(1)} %get-tuple-element.44), channel_id=1, source_target_pairs={{0,4},{2,6},{4,0},{6,2},{1,5},{3,7},{5,1},{7,3},{8,12},{10,14},{12... | collective-permute-start | bytes 196616 | tf_op jit(solution)/shard_map/ppermute | solution.py:307
  157.0 3.9 %collective-permute-done.8.refs_4_ = f32[128,128]{1,0:T(8,128)S(1)} collective-permute-done((f32[128,128]{1,0:T(8,128)S(1)}, f32[128,128]{1,0:T(8,128)S(1)}, u32[]{:S(2)}, u32[]{:S(2)}) %collective-permute-start.8) | collective-permute-done | bytes 65568 | tf_op jit(solution)/shard_map/ppermute | solution.py:307
  160.9 5.5 %all-to-all-done.4 = bf16[16,72,128]{2,1,0:T(8,128)(2,1)S(1)} async-done(((bf16[16,72,128]{2,1,0:T(8,128)(2,1)}), bf16[16,72,128]{2,1,0:T(8,128)(2,1)S(1)}, u32[]{:S(2)}, u32[]{:S(2)}) %all-to-all-start.4) | async-done | bytes 294944 | tf_op jit(solution)/shard_map/all_to_all | solution.py:388
  168.0 6.0 %all-to-all-start.5 = ((bf16[32,144,128]{2,1,0:T(8,128)(2,1)}), bf16[32,144,128]{2,1,0:T(8,128)(2,1)S(1)}, u32[]{:S(2)}, u32[]{:S(2)}) async-start(bf16[32,144,128]{2,1,0:T(8,128)(2,1)} %bitcast.14), calls=%async_computation.5 | async-start | bytes 2359296 | tf_op jit(solution)/shard_map/all_to_all | solution.py:396
  174.0 5.6 %collective-permute-start.9 = (f32[3,3,24,128]{3,2,1,0:T(8,128)S(1)}, f32[3,3,24,128]{3,2,1,0:T(8,128)S(1)}, u32[]{:S(2)}, u32[]{:S(2)}) collective-permute-start(f32[3,3,24,128]{3,2,1,0:T(8,128)S(1)} %get-tuple-element.47), channel_id=1, source_target_pairs={{0,0},{1,16},{2,32},{3,48},{4,64},{5,80},{6,96},{7,112},{8,8},{9,2... | collective-permute-start | bytes 331784 | tf_op jit(solution)/shard_map/ppermute | solution.py:395
  179.6 18.4 %collective-permute-done.9 = f32[3,3,24,128]{3,2,1,0:T(8,128)S(1)} collective-permute-done((f32[3,3,24,128]{3,2,1,0:T(8,128)S(1)}, f32[3,3,24,128]{3,2,1,0:T(8,128)S(1)}, u32[]{:S(2)}, u32[]{:S(2)}) %collective-permute-start.9) | collective-permute-done | bytes 110624 | tf_op jit(solution)/shard_map/ppermute | solution.py:395
  (42 shorter events, 22.1 us)
Async XLA Ops:
  2.7 9.6 %copy-start.10 = (f32[3,3,24,128]{3,2,1,0:T(8,128)S(1)}, f32[3,3,24,128]{3,2,1,0:T(8,128)}, u32[]{:S(2)}) copy-start(f32[3,3,24,128]{3,2,1,0:T(8,128)} %get-tuple-element.28) | copy-start | bytes 331780
  2.7 24.6 %all-to-all-start = ((bf16[16,272,128]{2,1,0:T(8,128)(2,1)}), bf16[16,272,128]{2,1,0:T(8,128)(2,1)S(1)}, u32[]{:S(2)}, u32[]{:S(2)}) async-start(bf16[16,272,128]{2,1,0:T(8,128)(2,1)} %get-tuple-element.27), calls=%async_computation | async-start | bytes 2228224 | tf_op jit(solution)/shard_map/all_to_all | solution.py:339
  12.3 22.9 %collective-permute-start.1 = (f32[3,3,24,128]{3,2,1,0:T(8,128)S(1)}, f32[3,3,24,128]{3,2,1,0:T(8,128)S(1)}, u32[]{:S(2)}, u32[]{:S(2)}) collective-permute-start(f32[3,3,24,128]{3,2,1,0:T(8,128)S(1)} %copy-done.10), channel_id=1, source_target_pairs={{0,0},{1,16},{2,32},{3,48},{4,64},{5,80},{6,96},{7,112},{8,8},{9,2... | collective-permute-start | bytes 331784 | tf_op jit(solution)/shard_map/ppermute | solution.py:335
  27.3 40.3 %copy-start.2 = (bf16[16,272,128]{2,1,0:T(8,128)(2,1)}, bf16[16,272,128]{2,1,0:T(8,128)(2,1)S(1)}, u32[]{:S(2)}) copy-start(bf16[16,272,128]{2,1,0:T(8,128)(2,1)S(1)} %all-to-all-done.refs_1_) | copy-start | bytes 3342340
  27.3 40.3 %collective-permute-start = (bf16[16,272,128]{2,1,0:T(8,128)(2,1)S(1)}, bf16[16,272,128]{2,1,0:T(8,128)(2,1)S(1)}, u32[]{:S(2)}, u32[]{:S(2)}) collective-permute-start(bf16[16,272,128]{2,1,0:T(8,128)(2,1)S(1)} %all-to-all-done.refs_1_), channel_id=1, source_target_pairs={{0,1},{1,0},{2,3},{3,2},{4,5},{5,4},{6,7},{7,6},{8,9},{9,8},{10,11... | collective-permute-start | bytes 3342344 | tf_op jit(solution)/shard_map/ppermute | solution.py:340
  36.1 31.5 %all-to-all-start.1 = ((bf16[16,72,128]{2,1,0:T(8,128)(2,1)}), bf16[16,72,128]{2,1,0:T(8,128)(2,1)S(1)}, u32[]{:S(2)}, u32[]{:S(2)}) async-start(bf16[16,72,128]{2,1,0:T(8,128)(2,1)} %bitcast.7), calls=%async_computation.1 | async-start | bytes 589824 | tf_op jit(solution)/shard_map/all_to_all | solution.py:338
  67.7 1.1 copy-start.4
  74.4 22.6 %collective-permute-start.2 = (f32[16,128,128]{2,1,0:T(8,128)}, f32[16,128,128]{2,1,0:T(8,128)S(1)}, u32[]{:S(2)}, u32[]{:S(2)}) collective-permute-start(f32[16,128,128]{2,1,0:T(8,128)} %get-tuple-element.35), channel_id=1, source_target_pairs={{0,1},{1,0},{2,3},{3,2},{4,5},{5,4},{6,7},{7,6},{8,9},{9,8},{10,11... | collective-permute-start | bytes 3145736 | tf_op jit(solution)/shard_map/ppermute | solution.py:367
  76.3 20.6 %all-to-all-start.2 = ((f32[64,1,128]{2,1,0:T(1,128)}), f32[64,1,128]{2,1,0:T(1,128)S(1)}, u32[]{:S(2)}, u32[]{:S(2)}) async-start(f32[64,1,128]{2,1,0:T(1,128)} %get-tuple-element.32), calls=%async_computation.2 | async-start | bytes 65536 | tf_op jit(solution)/shard_map/all_to_all | solution.py:366
  103.4 3.8 %copy-start.9 = (f32[4,128,128]{2,1,0:T(8,128)S(1)}, f32[4,128,128]{2,1,0:T(8,128)}, u32[]{:S(2)}) copy-start(f32[4,128,128]{2,1,0:T(8,128)} %get-tuple-element.38) | copy-start | bytes 786436
  103.4 6.2 %copy-start.8 = (f32[4,128,128]{2,1,0:T(8,128)S(1)}, f32[4,128,128]{2,1,0:T(8,128)}, u32[]{:S(2)}) copy-start(f32[4,128,128]{2,1,0:T(8,128)} %get-tuple-element.39) | copy-start | bytes 786436
  103.4 10.8 %copy-start.7 = (f32[4,128,128]{2,1,0:T(8,128)S(1)}, f32[4,128,128]{2,1,0:T(8,128)}, u32[]{:S(2)}) copy-start(f32[4,128,128]{2,1,0:T(8,128)} %get-tuple-element.40) | copy-start | bytes 786436
  103.4 34.4 %copy-start = (f32[4,128,128]{2,1,0:T(8,128)S(1)}, f32[4,128,128]{2,1,0:T(8,128)}, u32[]{:S(2)}) copy-start(f32[4,128,128]{2,1,0:T(8,128)} %get-tuple-element.37.refs_3_) | copy-start | bytes 786436
  103.4 34.4 %copy-start.1 = (s32[6]{0:T(128)S(1)}, s32[6]{0:T(128)}, u32[]{:S(2)}) copy-start(s32[6]{0:T(128)} %stack.27.refs_0_) | copy-start | bytes 76
  103.4 34.3 %all-to-all-start.3 = ((f32[16,3,24,128]{3,2,1,0:T(8,128)}), f32[16,3,24,128]{3,2,1,0:T(8,128)S(1)}, u32[]{:S(2)}, u32[]{:S(2)}) async-start(f32[16,3,24,128]{3,2,1,0:T(8,128)} %get-tuple-element.36), calls=%async_computation.3 | async-start | bytes 1179648 | tf_op jit(solution)/shard_map/all_to_all | solution.py:378
  107.2 12.4 %collective-permute-start.3 = (f32[4,128,128]{2,1,0:T(8,128)S(1)}, f32[4,128,128]{2,1,0:T(8,128)S(1)}, u32[]{:S(2)}, u32[]{:S(2)}) collective-permute-start(f32[4,128,128]{2,1,0:T(8,128)S(1)} %copy-done.9), channel_id=1, source_target_pairs={{0,128},{128,256},{256,384},{384,0},{1,129},{129,257},{257,385},{3... | collective-permute-start | bytes 786440 | tf_op jit(solution)/shard_map/ppermute | solution.py:307
  109.6 13.9 %collective-permute-start.4 = (f32[4,128,128]{2,1,0:T(8,128)S(1)}, f32[4,128,128]{2,1,0:T(8,128)S(1)}, u32[]{:S(2)}, u32[]{:S(2)}) collective-permute-start(f32[4,128,128]{2,1,0:T(8,128)S(1)} %copy-done.8), channel_id=1, source_target_pairs={{0,256},{128,384},{256,0},{384,128},{1,257},{129,385},{257,1},{385... | collective-permute-start | bytes 786440 | tf_op jit(solution)/shard_map/ppermute | solution.py:307
  114.2 11.8 %collective-permute-start.5 = (f32[4,128,128]{2,1,0:T(8,128)S(1)}, f32[4,128,128]{2,1,0:T(8,128)S(1)}, u32[]{:S(2)}, u32[]{:S(2)}) collective-permute-start(f32[4,128,128]{2,1,0:T(8,128)S(1)} %copy-done.7), channel_id=1, source_target_pairs={{0,384},{128,0},{256,128},{384,256},{1,385},{129,1},{257,129},{385... | collective-permute-start | bytes 786440 | tf_op jit(solution)/shard_map/ppermute | solution.py:307
  139.8 26.6 %all-to-all-start.4 = ((bf16[16,72,128]{2,1,0:T(8,128)(2,1)}), bf16[16,72,128]{2,1,0:T(8,128)(2,1)S(1)}, u32[]{:S(2)}, u32[]{:S(2)}) async-start(bf16[16,72,128]{2,1,0:T(8,128)(2,1)} %bitcast.9), calls=%async_computation.4 | async-start | bytes 589824 | tf_op jit(solution)/shard_map/all_to_all | solution.py:388
  147.2 9.5 %collective-permute-start.6 = (f32[128,128]{1,0:T(8,128)S(1)}, f32[128,128]{1,0:T(8,128)S(1)}, u32[]{:S(2)}, u32[]{:S(2)}) collective-permute-start(f32[128,128]{1,0:T(8,128)S(1)} %get-tuple-element.43), channel_id=1, source_target_pairs={{0,2},{2,4},{4,6},{6,0},{1,3},{3,5},{5,7},{7,1},{8,10},{10,12},{12... | collective-permute-start | bytes 196616 | tf_op jit(solution)/shard_map/ppermute | solution.py:307
  149.1 7.9 %collective-permute-start.7 = (f32[128,128]{1,0:T(8,128)S(1)}, f32[128,128]{1,0:T(8,128)S(1)}, u32[]{:S(2)}, u32[]{:S(2)}) collective-permute-start(f32[128,128]{1,0:T(8,128)S(1)} %get-tuple-element.44), channel_id=1, source_target_pairs={{0,4},{2,6},{4,0},{6,2},{1,5},{3,7},{5,1},{7,3},{8,12},{10,14},{12... | collective-permute-start | bytes 196616 | tf_op jit(solution)/shard_map/ppermute | solution.py:307
  154.8 6.2 %collective-permute-start.8 = (f32[128,128]{1,0:T(8,128)S(1)}, f32[128,128]{1,0:T(8,128)S(1)}, u32[]{:S(2)}, u32[]{:S(2)}) collective-permute-start(f32[128,128]{1,0:T(8,128)S(1)} %get-tuple-element.45), channel_id=1, source_target_pairs={{0,6},{2,0},{4,2},{6,4},{1,7},{3,1},{5,3},{7,5},{8,14},{10,8},{12,... | collective-permute-start | bytes 196616 | tf_op jit(solution)/shard_map/ppermute | solution.py:307
  168.0 30.6 %all-to-all-start.5 = ((bf16[32,144,128]{2,1,0:T(8,128)(2,1)}), bf16[32,144,128]{2,1,0:T(8,128)(2,1)S(1)}, u32[]{:S(2)}, u32[]{:S(2)}) async-start(bf16[32,144,128]{2,1,0:T(8,128)(2,1)} %bitcast.14), calls=%async_computation.5 | async-start | bytes 2359296 | tf_op jit(solution)/shard_map/all_to_all | solution.py:396
  174.0 24.0 %collective-permute-start.9 = (f32[3,3,24,128]{3,2,1,0:T(8,128)S(1)}, f32[3,3,24,128]{3,2,1,0:T(8,128)S(1)}, u32[]{:S(2)}, u32[]{:S(2)}) collective-permute-start(f32[3,3,24,128]{3,2,1,0:T(8,128)S(1)} %get-tuple-element.47), channel_id=1, source_target_pairs={{0,0},{1,16},{2,32},{3,48},{4,64},{5,80},{6,96},{7,112},{8,8},{9,2... | collective-permute-start | bytes 331784 | tf_op jit(solution)/shard_map/ppermute | solution.py:395
  (3 other events, 2.6 us)

commit v8 on v7

--- a/solution.py
+++ b/solution.py
@@ -132,16 +132,16 @@
         terms_ref[rep, BLOCK : 2 * BLOCK, :] = dupper[:, rows]
         terms_ref[rep, 2 * BLOCK : 3 * BLOCK, :] = hidden[:, rows]
     done(2)
-    terms = jnp.concatenate([dgate, dupper], axis=0)
     for target, which in ((keep_ref, core), (give_ref, 1 - core)):
         side = []
         for chip in range(4):
             cols = pl.ds(pl.multiple_of((2 * chip + which) * COLS, COLS), COLS)
             side.append(weights_ref[0 : 2 * BLOCK, cols])
-        back = dot(terms, jnp.concatenate(side, axis=1), 0, 0)
+        side = jnp.concatenate(side, axis=1)
         for rep in range(REPS):
+            back = dot(terms_ref[rep, 0 : 2 * BLOCK, :], side, 0, 0)
             for chip in range(4):
-                target[rep * 4 + chip] = back[rep * TOK : (rep + 1) * TOK, chip * COLS : (chip + 1) * COLS]
+                target[rep * 4 + chip] = back[:, chip * COLS : (chip + 1) * COLS]
     done(5, 6)
     peak = jnp.zeros((3 * BLOCK, COLS), F32)
     for rep in range(REPS):
@@ -162,7 +162,20 @@
     done(4)
 
 
-def quant_kernel(need, done, pos_ref, xs_ref, gs_ref, terms_ref, peaks_ref, bits_ref, row_ref, col_ref, keep_ref, got_ref, out_ref, *back_refs):
+def pair_kernel(pos_ref, keep_ref, got_ref, *back_refs):
+    for step, back_ref in enumerate(back_refs):
+        first = ((pos_ref[4] + step) % 4) * 4
+        for chip in range(4):
+            back_ref[chip] = keep_ref[first + chip] + got_ref[first + chip]
+
+
+def plane_kernel(pos_ref, own_ref, up_ref, across_ref, down_ref, *back_refs):
+    for step, back_ref in enumerate(back_refs):
+        which = (pos_ref[5] + step) % 4
+        back_ref[...] = (own_ref[which] + up_ref[which]) + (across_ref[which] + down_ref[which])
+
+
+def quant_kernel(need, done, pos_ref, xs_ref, gs_ref, terms_ref, peaks_ref, bits_ref, row_ref, col_ref, out_ref, wide_ref):
     need(3, 4)
     spot = pos_ref[1]
     unit = pos_ref[2]
@@ -210,25 +223,22 @@
                 halves[half] = halves[half] + (ratio + turn(ratio + phase))
         for half in range(2):
             result = halves[half] * scale
+            pair = 6 * SHARD * (2 * part + half)
             for mat in range(3):
                 for low in range(2):
                     start = mat * BLOCK + low * SHARD
-                    out_ref[2 * (2 * part + half) + low, mat, :, :] = result[start : start + SHARD]
+                    target = pair + (low * 3 + mat) * SHARD
+                    wide_ref[target : target + SHARD, :] = result[start : start + SHARD]
+            out_ref[pair : pair + 6 * SHARD, :] = wide_ref[pair : pair + 6 * SHARD, :].astype(BF16)
     done(0)
-    need(7, 8)
-    plane = pos_ref[4]
-    for step, back_ref in enumerate(back_refs):
-        first = ((plane + step) % 4) * 4
-        for chip in range(4):
-            back_ref[chip] = keep_ref[first + chip] + got_ref[first + chip]
-        done(1 + step)
-
-
-def adam_kernel(pos_ref, shares_ref, state_ref, own_ref, up_ref, across_ref, down_ref, new_state_ref, coded_ref, *refs):
-    wide_ref = refs[-1]
-    mean_grad = shares_ref[0]
+
+
+def adam_kernel(shares_ref, state_ref, new_state_ref, coded_ref, wide_ref, all_ref):
+    all_ref[...] = shares_ref[...].astype(F32)
+    mean_grad = all_ref[0 : 3 * SHARD]
     for peer in range(1, 16):
-        mean_grad = mean_grad + shares_ref[peer]
+        mean_grad = mean_grad + all_ref[peer * 3 * SHARD : (peer + 1) * 3 * SHARD]
+    mean_grad = mean_grad.reshape(3, SHARD, COLS)
     master = state_ref[0]
     first = BETA_ONE * state_ref[1] + (1.0 - BETA_ONE) * mean_grad
     second = BETA_TWO * state_ref[2] + (1.0 - BETA_TWO) * mean_grad * mean_grad
@@ -237,9 +247,6 @@
     new_state_ref[1] = first
     new_state_ref[2] = second
     spread_coded(eightbit_f32(updated), coded_ref, wide_ref)
-    for step, back_ref in enumerate(refs[:-1]):
-        which = (pos_ref[5] + step) % 4
-        back_ref[...] = (own_ref[which] + up_ref[which]) + (across_ref[which] + down_ref[which])
 
 
 def finish_kernel(ring_ref, own_ref, right_ref, across_ref, left_ref, spread_ref, grad_ref):
@@ -248,17 +255,17 @@
     grad_ref[...] = ((own_ref[...] + right_ref[...]) + (across_ref[...] + left_ref[...])).astype(BF16)
 
 
-def call(kernel, out_shape, smem=0, operands=(), scratch=(), limit=SMALL_LIMIT, first=None):
+def call(kernel, out_shape, smem=0, operands=(), scratch=(), limit=SMALL_LIMIT, first=None, idle=0):
     single = not isinstance(out_shape, tuple)
     outs = (out_shape,) if single else out_shape
-    n_in = len(operands) - smem
+    n_in = len(operands) - smem - idle
     n_out = len(outs)
 
     def body(*refs):
         small = refs[:smem]
         sources = refs[smem : smem + n_in]
-        targets = refs[smem + n_in : smem + n_in + n_out]
-        held = refs[smem + n_in + n_out :]
+        targets = refs[smem + n_in + idle : smem + n_in + idle + n_out]
+        held = refs[smem + n_in + idle + n_out :]
         taken, made, rest, sems = held[:n_in], held[n_in : n_in + n_out], held[n_in + n_out : -1], held[-1]
         loads = [pltpu.make_async_copy(sources[i], taken[i], sems.at[i]) for i in range(n_in)]
         stores = [pltpu.make_async_copy(made[i], targets[i], sems.at[n_in + i]) for i in range(n_out)]
@@ -287,8 +294,8 @@
             store.wait()
 
     anywhere = pl.BlockSpec(memory_space=pl.ANY)
-    specs = [pl.BlockSpec(memory_space=pltpu.SMEM)] * smem + [anywhere] * n_in
-    buffers = [pltpu.VMEM(item.shape, item.dtype) for item in tuple(operands[smem:]) + outs]
+    specs = [pl.BlockSpec(memory_space=pltpu.SMEM)] * smem + [anywhere] * (n_in + idle)
+    buffers = [pltpu.VMEM(item.shape, item.dtype) for item in tuple(operands[smem : smem + n_in]) + outs]
     return pl.pallas_call(
         body,
         out_shape=out_shape,
@@ -365,25 +372,30 @@
     )
     peaks = lax.all_to_all(peak, ("xl", "c") + Z, 0, 0)
     got = lax.ppermute(give, "c", [(0, 1), (1, 0)])
-
-    shares, *back = call(
+    back = call(pair_kernel, (struct((4, TOK, COLS)),) * 4, 1, (pos, keep, got, row_part), idle=1)
+
+    shares = call(
         quant_kernel,
-        (struct((16, 3, SHARD, COLS)),) + (struct((4, TOK, COLS)),) * 4,
+        struct((48 * SHARD, COLS), BF16),
         1,
-        (pos, xs, gs, terms, peaks, bit_widths, row_part, col_part, keep, got),
+        (pos, xs, gs, terms, peaks, bit_widths, row_part, col_part, back[0]),
+        (pltpu.VMEM((48 * SHARD, COLS), F32),),
         limit=LARGE_LIMIT,
-        first=(3, 4, 2, 0, 1, 5, 6, 7, 8),
+        first=(3, 4, 2, 0, 1, 5, 6),
+        idle=1,
     )
     back = [back[0]] + [shift(back[step], "y", step) for step in (1, 2, 3)]
-    shares = lax.all_to_all(shares, Z, 0, 0)
-
-    new_state, ring, *back = call(
+    shares = lax.all_to_all(shares.reshape(16, 3 * SHARD, COLS), Z, 0, 0).reshape(48 * SHARD, COLS)
+
+    new_state, ring = call(
         adam_kernel,
-        (struct((3, 3, SHARD, COLS)), struct((48 * SHARD, COLS), BF16)) + (struct((TOK, COLS)),) * 4,
-        1,
-        (pos, shares, state, *back),
-        wide,
-    )
+        (struct((3, 3, SHARD, COLS)), struct((48 * SHARD, COLS), BF16)),
+        0,
+        (shares, state, *back[1:]),
+        wide + (pltpu.VMEM((48 * SHARD, COLS), F32),),
+        idle=3,
+    )
+    back = call(plane_kernel, (struct((TOK, COLS)),) * 4, 1, (pos, *back))
     back = [back[0]] + [shift(back[step], ("xh", "xl"), step) for step in (1, 2, 3)]
     ring = lax.all_to_all(ring.reshape(16, 3 * SHARD, COLS), Z, 0, 0).reshape(48 * SHARD, COLS)
     ring, grad_in = call(

time: 201 us -> 192 us (0.955)
  waiting for transfers between devices: 94.3 us -> 78 us
  starting transfers between devices: 81.4 us -> 86.5 us
    all_to_all x1, waiting for transfers between devices: 11.8 us -> 0.27 us  [on_device(): lax.all_to_all(shares.reshape(16, 3 * SHARD, COLS), Z, 0, 0)]
    all_to_all x1, starting transfers between devices: 7.35 us -> 11.5 us  [on_device(): lax.all_to_all(ring.reshape(16, 3 * SHARD, COLS), Z, 0, 0)]
    all_to_all x1, waiting for transfers between devices: 11.5 us -> 8.57 us  [on_device(): peaks = lax.all_to_all(peak, ('xl', 'c') + Z, 0, 0)]
    unnamed x22, local copies, waits for them, and re-layouts: 1.26 us -> 3.65 us
    pallas_call x6 -> x8, Pallas kernels: 17.8 us -> 18.6 us  [call(): pl.pallas_call(body, out_shape=out_shape, in_specs=specs, out_specs=anywh...]
  transfers between devices with their start and end apart: 16 -> 16, of which waited for: 12 -> 12; matrix products, arithmetic and copies ran while one was open for 1% -> 1% of each run, Pallas kernels for 0% -> 2%
where the time goes in v8:
time: 192 us; the launch traced here: 191 us
  starting transfers between devices  86.5 us (45%)
  waiting for transfers between devices  78 us (41%)
  Pallas kernels  18.6 us (10%)
  local copies, waits for them, and re-layouts  6.29 us (3%)
    all_to_all x1, waiting for transfers between devices, on_device(): lax.all_to_all(coded.reshape(16, 3 * SHARD, COLS), Z, 0, 0)  20.2 us
    ppermute x6, starting transfers between devices, shift(): return lax.ppermute(value, axes, [(i, (i + step) % 4) for i in range(4)])  19.7 us
    pallas_call x8, Pallas kernels, call(): pl.pallas_call(body, out_shape=out_shape, in_specs=specs, out_specs=anywh...  18.6 us
    ppermute x1, waiting for transfers between devices, on_device(): new_state = lax.ppermute(new_state, Z + TENSOR, pairs)  18.5 us
    ppermute x6, waiting for transfers between devices, shift(): return lax.ppermute(value, axes, [(i, (i + step) % 4) for i in range(4)])  12.7 us
    all_to_all x1, starting transfers between devices, on_device(): lax.all_to_all(ring.reshape(16, 3 * SHARD, COLS), Z, 0, 0)  11.5 us
    all_to_all x1, starting transfers between devices, on_device(): lax.all_to_all(coded.reshape(16, 3 * SHARD, COLS), Z, 0, 0)  10.6 us
    all_to_all x1, starting transfers between devices, on_device(): own = lax.all_to_all(packed, ('y', 'xh', 'xl'), 0, 0)  9.54 us
  transfers between devices with their start and end apart: 16, of which 12 were waited for; matrix products, arithmetic and copies ran while one was open for 1% of the time, Pallas kernels for 2%

profile of v8, /device:TPU:2, one launch (start us, length us, event | category | flops | bytes accessed | tf_op | source)
XLA Modules:
  0.0 191.2 jit_solution(10327432512753364103)
XLA Ops:
  0.6 2.1 %shard_map.119 = (bf16[16,272,128]{2,1,0:T(8,128)(2,1)}, f32[3,3,24,128]{3,2,1,0:T(8,128)}) custom-call(bf16[128,128]{1,0:T(8,128)(2,1)} %refs_0_.1, bf16[128,128]{1,0:T(8,128)(2,1)} %refs_1_.1, s32[1,128]{1,0:T(1,128)} %bitcast.30, f32[3,24,128]{2,1,0:T(8,128)} %refs_3_.1, f32[3,24,128]{2,1,0:T(8,128)} %refs_4_.1, f32[3,24,128]{2,1,0:T(8,128)} %refs_5_.2), custom_call_target="tpu_custom_call" | custom-call | tf_op jit(solution)/shard_map/pallas_call | solution.py:299
  2.7 9.5 %all-to-all-start = ((bf16[16,272,128]{2,1,0:T(8,128)(2,1)}), bf16[16,272,128]{2,1,0:T(8,128)(2,1)S(1)}, u32[]{:S(2)}, u32[]{:S(2)}) async-start(bf16[16,272,128]{2,1,0:T(8,128)(2,1)} %get-tuple-element.26), calls=%async_computation | async-start | bytes 2228224 | tf_op jit(solution)/shard_map/all_to_all | solution.py:346
  12.3 6.7 %collective-permute-start.1 = (f32[3,3,24,128]{3,2,1,0:T(8,128)S(1)}, f32[3,3,24,128]{3,2,1,0:T(8,128)S(1)}, u32[]{:S(2)}, u32[]{:S(2)}) collective-permute-start(f32[3,3,24,128]{3,2,1,0:T(8,128)S(1)} %copy-done.10), channel_id=1, source_target_pairs={{0,0},{1,16},{2,32},{3,48},{4,64},{5,80},{6,96},{7,112},{8,8},{9,2... | collective-permute-start | bytes 331784 | tf_op jit(solution)/shard_map/ppermute | solution.py:342
  19.0 8.3 %all-to-all-done.refs_1_ = bf16[16,272,128]{2,1,0:T(8,128)(2,1)S(1)} async-done(((bf16[16,272,128]{2,1,0:T(8,128)(2,1)}), bf16[16,272,128]{2,1,0:T(8,128)(2,1)S(1)}, u32[]{:S(2)}, u32[]{:S(2)}) %all-to-all-start) | async-done | bytes 1114144 | tf_op jit(solution)/shard_map/all_to_all | solution.py:346
  29.2 5.9 %collective-permute-done.1.refs_0_.refs_1_ = f32[3,3,24,128]{3,2,1,0:T(8,128)S(1)} collective-permute-done((f32[3,3,24,128]{3,2,1,0:T(8,128)S(1)}, f32[3,3,24,128]{3,2,1,0:T(8,128)S(1)}, u32[]{:S(2)}, u32[]{:S(2)}) %collective-permute-start.1) | collective-permute-done | bytes 110624 | tf_op jit(solution)/shard_map/ppermute | solution.py:342
  36.1 10.6 %all-to-all-start.1 = ((bf16[16,72,128]{2,1,0:T(8,128)(2,1)}), bf16[16,72,128]{2,1,0:T(8,128)(2,1)S(1)}, u32[]{:S(2)}, u32[]{:S(2)}) async-start(bf16[16,72,128]{2,1,0:T(8,128)(2,1)} %bitcast.7), calls=%async_computation.1 | async-start | bytes 589824 | tf_op jit(solution)/shard_map/all_to_all | solution.py:345
  47.4 20.2 %all-to-all-done.1 = bf16[16,72,128]{2,1,0:T(8,128)(2,1)S(1)} async-done(((bf16[16,72,128]{2,1,0:T(8,128)(2,1)}), bf16[16,72,128]{2,1,0:T(8,128)(2,1)S(1)}, u32[]{:S(2)}, u32[]{:S(2)}) %all-to-all-start.1) | async-done | bytes 294944 | tf_op jit(solution)/shard_map/all_to_all | solution.py:345
  68.8 5.8 %shard_map.121 = (bf16[512,1024]{1,0:T(8,128)(2,1)}, bf16[512,1024]{1,0:T(8,128)(2,1)}, bf16[4,144,128]{2,1,0:T(8,128)(2,1)}, f32[8,1024]{1,0:T(8,128)}, f32[64,...) custom-call(s32[6]{0:T(128)} %stack.27.refs_0_, bf16[16,272,128]{2,1,0:T(8,128)(2,1)} %copy-done.6, ...), custom_call_target="tpu_custom_call" | custom-call | tf_op jit(solution)/shard_map/pallas_call | solution.py:299
  76.4 8.2 %all-to-all-start.2 = ((f32[64,1,128]{2,1,0:T(1,128)}), f32[64,1,128]{2,1,0:T(1,128)S(1)}, u32[]{:S(2)}, u32[]{:S(2)}) async-start(f32[64,1,128]{2,1,0:T(1,128)} %get-tuple-element.31), calls=%async_computation.2 | async-start | bytes 65536 | tf_op jit(solution)/shard_map/all_to_all | solution.py:373
  88.5 8.6 %all-to-all-done.2.refs_4_ = f32[64,1,128]{2,1,0:T(1,128)S(1)} async-done(((f32[64,1,128]{2,1,0:T(1,128)}), f32[64,1,128]{2,1,0:T(1,128)S(1)}, u32[]{:S(2)}, u32[]{:S(2)}) %all-to-all-start.2) | async-done | bytes 32800 | tf_op jit(solution)/shard_map/all_to_all | solution.py:373
  97.7 4.9 %shard_map.123 = bf16[1152,128]{1,0:T(8,128)(2,1)} custom-call(s32[6]{0:T(128)} %stack.27.refs_0_, bf16[512,1024]{1,0:T(8,128)(2,1)} %get-tuple-element.28.refs_1_, bf16[512,1024]{1,0:T(8,128)(2,1)} %get-tuple-element.29.refs_2_, bf16[4,144,128]{2,1,0:T(8,128)(2,1)} %get-tuple-element.30.refs_3_, f32[64,1,128]{2,1,0:T(1,128)} %copy-done.9, s32[3,24]{1,0:T(4,128)} %refs_5_.3, ...), custom_call_target="tpu_custom_call" | custom-call | tf_op jit(solution)/shard_map/pallas_call | solution.py:299
  102.6 3.7 %all-to-all-start.3 = ((bf16[16,72,128]{2,1,0:T(8,128)(2,1)}), bf16[16,72,128]{2,1,0:T(8,128)(2,1)S(1)}, u32[]{:S(2)}, u32[]{:S(2)}) async-start(bf16[16,72,128]{2,1,0:T(8,128)(2,1)} %bitcast.29), calls=%async_computation.3 | async-start | bytes 589824 | tf_op jit(solution)/shard_map/all_to_all | solution.py:388
  106.3 2.4 %collective-permute-start.3 = (f32[4,128,128]{2,1,0:T(8,128)S(1)}, f32[4,128,128]{2,1,0:T(8,128)S(1)}, u32[]{:S(2)}, u32[]{:S(2)}) collective-permute-start(f32[4,128,128]{2,1,0:T(8,128)S(1)} %get-tuple-element.36), channel_id=1, source_target_pairs={{0,128},{128,256},{256,384},{384,0},{1,129},{129,257},{257,385},{3... | collective-permute-start | bytes 786440 | tf_op jit(solution)/shard_map/ppermute | solution.py:314
  108.8 4.6 %collective-permute-start.4 = (f32[4,128,128]{2,1,0:T(8,128)S(1)}, f32[4,128,128]{2,1,0:T(8,128)S(1)}, u32[]{:S(2)}, u32[]{:S(2)}) collective-permute-start(f32[4,128,128]{2,1,0:T(8,128)S(1)} %get-tuple-element.37), channel_id=1, source_target_pairs={{0,256},{128,384},{256,0},{384,128},{1,257},{129,385},{257,1},{385... | collective-permute-start | bytes 786440 | tf_op jit(solution)/shard_map/ppermute | solution.py:314
  113.4 3.4 %collective-permute-start.5 = (f32[4,128,128]{2,1,0:T(8,128)S(1)}, f32[4,128,128]{2,1,0:T(8,128)S(1)}, u32[]{:S(2)}, u32[]{:S(2)}) collective-permute-start(f32[4,128,128]{2,1,0:T(8,128)S(1)} %get-tuple-element.38), channel_id=1, source_target_pairs={{0,384},{128,0},{256,128},{384,256},{1,385},{129,1},{257,129},{385... | collective-permute-start | bytes 786440 | tf_op jit(solution)/shard_map/ppermute | solution.py:314
  118.7 4.0 %collective-permute-done.4.refs_3_ = f32[4,128,128]{2,1,0:T(8,128)S(1)} collective-permute-done((f32[4,128,128]{2,1,0:T(8,128)S(1)}, f32[4,128,128]{2,1,0:T(8,128)S(1)}, u32[]{:S(2)}, u32[]{:S(2)}) %collective-permute-start.4) | collective-permute-done | bytes 262176 | tf_op jit(solution)/shard_map/ppermute | solution.py:314
  122.7 2.5 %collective-permute-done.5.refs_4_ = f32[4,128,128]{2,1,0:T(8,128)S(1)} collective-permute-done((f32[4,128,128]{2,1,0:T(8,128)S(1)}, f32[4,128,128]{2,1,0:T(8,128)S(1)}, u32[]{:S(2)}, u32[]{:S(2)}) %collective-permute-start.5) | collective-permute-done | bytes 262176 | tf_op jit(solution)/shard_map/ppermute | solution.py:314
  126.8 11.5 %all-to-all-start.4 = ((bf16[16,72,128]{2,1,0:T(8,128)(2,1)}), bf16[16,72,128]{2,1,0:T(8,128)(2,1)S(1)}, u32[]{:S(2)}, u32[]{:S(2)}) async-start(bf16[16,72,128]{2,1,0:T(8,128)(2,1)} %bitcast.11), calls=%async_computation.4 | async-start | bytes 589824 | tf_op jit(solution)/shard_map/all_to_all | solution.py:400
  141.3 5.5 %collective-permute-start.7 = (f32[128,128]{1,0:T(8,128)S(1)}, f32[128,128]{1,0:T(8,128)S(1)}, u32[]{:S(2)}, u32[]{:S(2)}) collective-permute-start(f32[128,128]{1,0:T(8,128)S(1)} %get-tuple-element.42), channel_id=1, source_target_pairs={{0,4},{2,6},{4,0},{6,2},{1,5},{3,7},{5,1},{7,3},{8,12},{10,14},{12... | collective-permute-start | bytes 196616 | tf_op jit(solution)/shard_map/ppermute | solution.py:314
  149.6 3.4 %collective-permute-done.8.refs_4_ = f32[128,128]{1,0:T(8,128)S(1)} collective-permute-done((f32[128,128]{1,0:T(8,128)S(1)}, f32[128,128]{1,0:T(8,128)S(1)}, u32[]{:S(2)}, u32[]{:S(2)}) %collective-permute-start.8) | collective-permute-done | bytes 65568 | tf_op jit(solution)/shard_map/ppermute | solution.py:314
  152.9 3.5 %all-to-all-done.4 = bf16[16,72,128]{2,1,0:T(8,128)(2,1)S(1)} async-done(((bf16[16,72,128]{2,1,0:T(8,128)(2,1)}), bf16[16,72,128]{2,1,0:T(8,128)(2,1)S(1)}, u32[]{:S(2)}, u32[]{:S(2)}) %all-to-all-start.4) | async-done | bytes 294944 | tf_op jit(solution)/shard_map/all_to_all | solution.py:400
  158.1 6.8 %all-to-all-start.5 = ((bf16[32,144,128]{2,1,0:T(8,128)(2,1)}), bf16[32,144,128]{2,1,0:T(8,128)(2,1)S(1)}, u32[]{:S(2)}, u32[]{:S(2)}) async-start(bf16[32,144,128]{2,1,0:T(8,128)(2,1)} %bitcast.16), calls=%async_computation.5 | async-start | bytes 2359296 | tf_op jit(solution)/shard_map/all_to_all | solution.py:408
  164.9 5.9 %collective-permute-start.9 = (f32[3,3,24,128]{3,2,1,0:T(8,128)S(1)}, f32[3,3,24,128]{3,2,1,0:T(8,128)S(1)}, u32[]{:S(2)}, u32[]{:S(2)}) collective-permute-start(f32[3,3,24,128]{3,2,1,0:T(8,128)S(1)} %get-tuple-element.45), channel_id=1, source_target_pairs={{0,0},{1,16},{2,32},{3,48},{4,64},{5,80},{6,96},{7,112},{8,8},{9,2... | collective-permute-start | bytes 331784 | tf_op jit(solution)/shard_map/ppermute | solution.py:407
  170.9 18.5 %collective-permute-done.9 = f32[3,3,24,128]{3,2,1,0:T(8,128)S(1)} collective-permute-done((f32[3,3,24,128]{3,2,1,0:T(8,128)S(1)}, f32[3,3,24,128]{3,2,1,0:T(8,128)S(1)}, u32[]{:S(2)}, u32[]{:S(2)}) %collective-permute-start.9) | collective-permute-done | bytes 110624 | tf_op jit(solution)/shard_map/ppermute | solution.py:407
  (44 shorter events, 23.7 us)
Async XLA Ops:
  2.7 9.6 %copy-start.10 = (f32[3,3,24,128]{3,2,1,0:T(8,128)S(1)}, f32[3,3,24,128]{3,2,1,0:T(8,128)}, u32[]{:S(2)}) copy-start(f32[3,3,24,128]{3,2,1,0:T(8,128)} %get-tuple-element.27) | copy-start | bytes 331780
  2.7 24.6 %all-to-all-start = ((bf16[16,272,128]{2,1,0:T(8,128)(2,1)}), bf16[16,272,128]{2,1,0:T(8,128)(2,1)S(1)}, u32[]{:S(2)}, u32[]{:S(2)}) async-start(bf16[16,272,128]{2,1,0:T(8,128)(2,1)} %get-tuple-element.26), calls=%async_computation | async-start | bytes 2228224 | tf_op jit(solution)/shard_map/all_to_all | solution.py:346
  12.3 22.9 %collective-permute-start.1 = (f32[3,3,24,128]{3,2,1,0:T(8,128)S(1)}, f32[3,3,24,128]{3,2,1,0:T(8,128)S(1)}, u32[]{:S(2)}, u32[]{:S(2)}) collective-permute-start(f32[3,3,24,128]{3,2,1,0:T(8,128)S(1)} %copy-done.10), channel_id=1, source_target_pairs={{0,0},{1,16},{2,32},{3,48},{4,64},{5,80},{6,96},{7,112},{8,8},{9,2... | collective-permute-start | bytes 331784 | tf_op jit(solution)/shard_map/ppermute | solution.py:342
  27.3 40.3 %copy-start.6 = (bf16[16,272,128]{2,1,0:T(8,128)(2,1)}, bf16[16,272,128]{2,1,0:T(8,128)(2,1)S(1)}, u32[]{:S(2)}) copy-start(bf16[16,272,128]{2,1,0:T(8,128)(2,1)S(1)} %all-to-all-done.refs_1_) | copy-start | bytes 3342340
  27.3 40.3 %collective-permute-start = (bf16[16,272,128]{2,1,0:T(8,128)(2,1)S(1)}, bf16[16,272,128]{2,1,0:T(8,128)(2,1)S(1)}, u32[]{:S(2)}, u32[]{:S(2)}) collective-permute-start(bf16[16,272,128]{2,1,0:T(8,128)(2,1)S(1)} %all-to-all-done.refs_1_), channel_id=1, source_target_pairs={{0,1},{1,0},{2,3},{3,2},{4,5},{5,4},{6,7},{7,6},{8,9},{9,8},{10,11... | collective-permute-start | bytes 3342344 | tf_op jit(solution)/shard_map/ppermute | solution.py:347
  36.1 31.5 %all-to-all-start.1 = ((bf16[16,72,128]{2,1,0:T(8,128)(2,1)}), bf16[16,72,128]{2,1,0:T(8,128)(2,1)S(1)}, u32[]{:S(2)}, u32[]{:S(2)}) async-start(bf16[16,72,128]{2,1,0:T(8,128)(2,1)} %bitcast.7), calls=%async_computation.1 | async-start | bytes 589824 | tf_op jit(solution)/shard_map/all_to_all | solution.py:345
  67.6 1.1 copy-start.8
  68.8 16.9 %copy-start.4 = (s32[6]{0:T(128)S(1)}, s32[6]{0:T(128)}, u32[]{:S(2)}) copy-start(s32[6]{0:T(128)} %stack.27.refs_0_) | copy-start | bytes 76
  74.5 11.0 %collective-permute-start.2 = (f32[16,128,128]{2,1,0:T(8,128)}, f32[16,128,128]{2,1,0:T(8,128)S(1)}, u32[]{:S(2)}, u32[]{:S(2)}) collective-permute-start(f32[16,128,128]{2,1,0:T(8,128)} %get-tuple-element.34), channel_id=1, source_target_pairs={{0,1},{1,0},{2,3},{3,2},{4,5},{5,4},{6,7},{7,6},{8,9},{9,8},{10,11... | collective-permute-start | bytes 3145736 | tf_op jit(solution)/shard_map/ppermute | solution.py:374
  76.4 20.6 %all-to-all-start.2 = ((f32[64,1,128]{2,1,0:T(1,128)}), f32[64,1,128]{2,1,0:T(1,128)S(1)}, u32[]{:S(2)}, u32[]{:S(2)}) async-start(f32[64,1,128]{2,1,0:T(1,128)} %get-tuple-element.31), calls=%async_computation.2 | async-start | bytes 65536 | tf_op jit(solution)/shard_map/all_to_all | solution.py:373
  85.6 1.2 copy-start
  86.9 10.2 %copy-start.3 = (f32[144,128]{1,0:T(8,128)}, f32[144,128]{1,0:T(8,128)S(1)}, u32[]{:S(2)}) copy-start(f32[144,128]{1,0:T(8,128)S(1)} %broadcast_in_dim.9.refs_3_.refs_6_) | copy-start | bytes 221188
  102.6 35.6 %copy-start.2 = (f32[4,128,128]{2,1,0:T(8,128)S(1)}, f32[4,128,128]{2,1,0:T(8,128)}, u32[]{:S(2)}) copy-start(f32[4,128,128]{2,1,0:T(8,128)} %copy-done.1) | copy-start | bytes 786436
  102.6 35.6 %copy-start.5 = (s32[6]{0:T(128)S(1)}, s32[6]{0:T(128)}, u32[]{:S(2)}) copy-start(s32[6]{0:T(128)} %stack.27.refs_0_) | copy-start | bytes 76
  102.6 22.8 %all-to-all-start.3 = ((bf16[16,72,128]{2,1,0:T(8,128)(2,1)}), bf16[16,72,128]{2,1,0:T(8,128)(2,1)S(1)}, u32[]{:S(2)}, u32[]{:S(2)}) async-start(bf16[16,72,128]{2,1,0:T(8,128)(2,1)} %bitcast.29), calls=%async_computation.3 | async-start | bytes 589824 | tf_op jit(solution)/shard_map/all_to_all | solution.py:388
  106.3 12.4 %collective-permute-start.3 = (f32[4,128,128]{2,1,0:T(8,128)S(1)}, f32[4,128,128]{2,1,0:T(8,128)S(1)}, u32[]{:S(2)}, u32[]{:S(2)}) collective-permute-start(f32[4,128,128]{2,1,0:T(8,128)S(1)} %get-tuple-element.36), channel_id=1, source_target_pairs={{0,128},{128,256},{256,384},{384,0},{1,129},{129,257},{257,385},{3... | collective-permute-start | bytes 786440 | tf_op jit(solution)/shard_map/ppermute | solution.py:314
  108.8 13.9 %collective-permute-start.4 = (f32[4,128,128]{2,1,0:T(8,128)S(1)}, f32[4,128,128]{2,1,0:T(8,128)S(1)}, u32[]{:S(2)}, u32[]{:S(2)}) collective-permute-start(f32[4,128,128]{2,1,0:T(8,128)S(1)} %get-tuple-element.37), channel_id=1, source_target_pairs={{0,256},{128,384},{256,0},{384,128},{1,257},{129,385},{257,1},{385... | collective-permute-start | bytes 786440 | tf_op jit(solution)/shard_map/ppermute | solution.py:314
  113.4 11.8 %collective-permute-start.5 = (f32[4,128,128]{2,1,0:T(8,128)S(1)}, f32[4,128,128]{2,1,0:T(8,128)S(1)}, u32[]{:S(2)}, u32[]{:S(2)}) collective-permute-start(f32[4,128,128]{2,1,0:T(8,128)S(1)} %get-tuple-element.38), channel_id=1, source_target_pairs={{0,384},{128,0},{256,128},{384,256},{1,385},{129,1},{257,129},{385... | collective-permute-start | bytes 786440 | tf_op jit(solution)/shard_map/ppermute | solution.py:314
  126.8 29.7 %all-to-all-start.4 = ((bf16[16,72,128]{2,1,0:T(8,128)(2,1)}), bf16[16,72,128]{2,1,0:T(8,128)(2,1)S(1)}, u32[]{:S(2)}, u32[]{:S(2)}) async-start(bf16[16,72,128]{2,1,0:T(8,128)(2,1)} %bitcast.11), calls=%async_computation.4 | async-start | bytes 589824 | tf_op jit(solution)/shard_map/all_to_all | solution.py:400
  139.4 9.4 %collective-permute-start.6 = (f32[128,128]{1,0:T(8,128)S(1)}, f32[128,128]{1,0:T(8,128)S(1)}, u32[]{:S(2)}, u32[]{:S(2)}) collective-permute-start(f32[128,128]{1,0:T(8,128)S(1)} %get-tuple-element.41), channel_id=1, source_target_pairs={{0,2},{2,4},{4,6},{6,0},{1,3},{3,5},{5,7},{7,1},{8,10},{10,12},{12... | collective-permute-start | bytes 196616 | tf_op jit(solution)/shard_map/ppermute | solution.py:314
  141.3 8.3 %collective-permute-start.7 = (f32[128,128]{1,0:T(8,128)S(1)}, f32[128,128]{1,0:T(8,128)S(1)}, u32[]{:S(2)}, u32[]{:S(2)}) collective-permute-start(f32[128,128]{1,0:T(8,128)S(1)} %get-tuple-element.42), channel_id=1, source_target_pairs={{0,4},{2,6},{4,0},{6,2},{1,5},{3,7},{5,1},{7,3},{8,12},{10,14},{12... | collective-permute-start | bytes 196616 | tf_op jit(solution)/shard_map/ppermute | solution.py:314
  146.8 6.2 %collective-permute-start.8 = (f32[128,128]{1,0:T(8,128)S(1)}, f32[128,128]{1,0:T(8,128)S(1)}, u32[]{:S(2)}, u32[]{:S(2)}) collective-permute-start(f32[128,128]{1,0:T(8,128)S(1)} %get-tuple-element.43), channel_id=1, source_target_pairs={{0,6},{2,0},{4,2},{6,4},{1,7},{3,1},{5,3},{7,5},{8,14},{10,8},{12,... | collective-permute-start | bytes 196616 | tf_op jit(solution)/shard_map/ppermute | solution.py:314
  158.1 31.9 %all-to-all-start.5 = ((bf16[32,144,128]{2,1,0:T(8,128)(2,1)}), bf16[32,144,128]{2,1,0:T(8,128)(2,1)S(1)}, u32[]{:S(2)}, u32[]{:S(2)}) async-start(bf16[32,144,128]{2,1,0:T(8,128)(2,1)} %bitcast.16), calls=%async_computation.5 | async-start | bytes 2359296 | tf_op jit(solution)/shard_map/all_to_all | solution.py:408
  164.9 24.4 %collective-permute-start.9 = (f32[3,3,24,128]{3,2,1,0:T(8,128)S(1)}, f32[3,3,24,128]{3,2,1,0:T(8,128)S(1)}, u32[]{:S(2)}, u32[]{:S(2)}) collective-permute-start(f32[3,3,24,128]{3,2,1,0:T(8,128)S(1)} %get-tuple-element.45), channel_id=1, source_target_pairs={{0,0},{1,16},{2,32},{3,48},{4,64},{5,80},{6,96},{7,112},{8,8},{9,2... | collective-permute-start | bytes 331784 | tf_op jit(solution)/shard_map/ppermute | solution.py:407
  (3 other events, 2.0 us)

commit v9 on v8

--- a/solution.py
+++ b/solution.py
@@ -74,27 +74,50 @@
         coded_ref[pair * 6 * SHARD : (pair + 1) * 6 * SHARD, :] = narrow
 
 
-def pack_kernel(acts_ref, grad_ref, dither_ref, master_ref, one_ref, two_ref, packed_ref, state_ref):
-    high = (dither_ref[...] >> 3).astype(F32)
-    low = (dither_ref[...] & 7).astype(F32)
+def pack_kernel(acts_ref, grad_ref, dither_ref, *refs):
+    state_in, (packed_ref, state_ref, held_ref, dither_held_ref, sems) = refs[:3], refs[3:]
+    loads = [
+        pltpu.make_async_copy(acts_ref, held_ref.at[pl.ds(0, TOK)], sems.at[0]),
+        pltpu.make_async_copy(grad_ref, held_ref.at[pl.ds(TOK, TOK)], sems.at[1]),
+        pltpu.make_async_copy(dither_ref, dither_held_ref, sems.at[2]),
+    ]
+    copies = [pltpu.make_async_copy(state_in[i], state_ref.at[i], sems.at[3 + i]) for i in range(3)]
+    for copy in loads + copies:
+        copy.start()
+    loads[2].wait()
+    high = (dither_held_ref[...] >> 3).astype(F32)
+    low = (dither_held_ref[...] & 7).astype(F32)
     row = lax.broadcasted_iota(jnp.int32, (16, COLS), 0)
-    extra = jnp.where(row == 0, high, jnp.where(row == 1, low, 0.0)).astype(BF16)
-    for peer in range(16):
-        packed_ref[peer, 0:TOK, :] = acts_ref[...]
-        packed_ref[peer, TOK : 2 * TOK, :] = grad_ref[...]
-        packed_ref[peer, 2 * TOK : PACK, :] = extra
-    state_ref[0] = master_ref[...]
-    state_ref[1] = one_ref[...]
-    state_ref[2] = two_ref[...]
+    held_ref[2 * TOK : PACK, :] = jnp.where(row == 0, high, jnp.where(row == 1, low, 0.0)).astype(BF16)
+    loads[0].wait()
+    loads[1].wait()
+    stores = [pltpu.make_async_copy(held_ref, packed_ref.at[peer], sems.at[6 + peer]) for peer in range(16)]
+    for store in stores:
+        store.start()
+    for copy in copies + stores:
+        copy.wait()
 
 
 def code_kernel(state_ref, coded_ref, wide_ref):
     spread_coded(eightbit_f32(state_ref[0]), coded_ref, wide_ref)
 
 
+def layout_kernel(pos_ref, own_ref, other_ref, xs_ref, gs_ref, col_ref):
+    core = pos_ref[0]
+    for source, which in ((own_ref, core), (other_ref, 1 - core)):
+        for chip in range(4):
+            cols = pl.ds(pl.multiple_of((2 * chip + which) * COLS, COLS), COLS)
+            for rep in range(REPS):
+                rows = slice(rep * TOK, (rep + 1) * TOK)
+                xs_ref[rows, cols] = source[rep * 4 + chip, 0:TOK, :]
+                gs_ref[rows, cols] = source[rep * 4 + chip, TOK : 2 * TOK, :]
+            pair = source[chip, 2 * TOK : PACK, :].astype(F32)
+            dither = pair[0:1] * 8.0 + pair[1:2]
+            col_ref[:, cols] = jnp.broadcast_to(dither * (1.0 / 1024.0), (8, COLS))
+
+
 def front_kernel(need, done, pos_ref, *refs):
-    rows_ref, xs_ref, gs_ref, terms_ref, col_ref, peak_ref, keep_ref, give_ref = refs[2:10]
-    wide_ref, full_ref, weights_ref = refs[10:]
+    xs_ref, gs_ref, rows_ref, terms_ref, peak_ref, keep_ref, give_ref, wide_ref, full_ref, weights_ref = refs
     core = pos_ref[0]
     need(2)
     wide_ref[...] = rows_ref[...].astype(F32)
@@ -105,18 +128,7 @@
             target = mat * BLOCK + (depth % 2) * SHARD
             full_ref[target : target + SHARD, cols] = wide_ref[source : source + SHARD, :]
     weights_ref[...] = full_ref[...].astype(BF16)
-    for side, which in ((0, core), (1, 1 - core)):
-        need(side)
-        for chip in range(4):
-            cols = pl.ds(pl.multiple_of((2 * chip + which) * COLS, COLS), COLS)
-            for rep in range(REPS):
-                rows = slice(rep * TOK, (rep + 1) * TOK)
-                xs_ref[rows, cols] = refs[side][rep * 4 + chip, 0:TOK, :]
-                gs_ref[rows, cols] = refs[side][rep * 4 + chip, TOK : 2 * TOK, :]
-            pair = refs[side][chip, 2 * TOK : PACK, :].astype(F32)
-            dither = pair[0:1] * 8.0 + pair[1:2]
-            col_ref[:, cols] = jnp.broadcast_to(dither * (1.0 / 1024.0), (8, COLS))
-    done(0, 1, 3)
+    need(0, 1)
     front = dot(weights_ref[0 : 2 * BLOCK, :], xs_ref[...], 1, 1)
     delta = dot(weights_ref[2 * BLOCK : 3 * BLOCK, :], gs_ref[...], 1, 1)
     gate = front[0:BLOCK]
@@ -131,7 +143,7 @@
         terms_ref[rep, 0:BLOCK, :] = dgate[:, rows]
         terms_ref[rep, BLOCK : 2 * BLOCK, :] = dupper[:, rows]
         terms_ref[rep, 2 * BLOCK : 3 * BLOCK, :] = hidden[:, rows]
-    done(2)
+    done(0)
     for target, which in ((keep_ref, core), (give_ref, 1 - core)):
         side = []
         for chip in range(4):
@@ -142,7 +154,7 @@
             back = dot(terms_ref[rep, 0 : 2 * BLOCK, :], side, 0, 0)
             for chip in range(4):
                 target[rep * 4 + chip] = back[:, chip * COLS : (chip + 1) * COLS]
-    done(5, 6)
+    done(2, 3)
     peak = jnp.zeros((3 * BLOCK, COLS), F32)
     for rep in range(REPS):
         rows = slice(rep * TOK, (rep + 1) * TOK)
@@ -159,7 +171,7 @@
         top = jnp.max(top, axis=1, keepdims=True)
         packed = jnp.where(lane == group, top, packed)
     peak_ref[...] = jnp.broadcast_to(packed.reshape(1, 1, COLS), peak_ref.shape)
-    done(4)
+    done(1)
 
 
 def pair_kernel(pos_ref, keep_ref, got_ref, *back_refs):
@@ -249,10 +261,13 @@
     spread_coded(eightbit_f32(updated), coded_ref, wide_ref)
 
 
-def finish_kernel(ring_ref, own_ref, right_ref, across_ref, left_ref, spread_ref, grad_ref):
-    for plane in range(4):
-        spread_ref[plane] = ring_ref[...]
+def finish_kernel(ring_ref, own_ref, right_ref, across_ref, left_ref, spread_ref, grad_ref, sems):
+    copies = [pltpu.make_async_copy(ring_ref, spread_ref.at[plane], sems.at[plane]) for plane in range(4)]
+    for copy in copies:
+        copy.start()
     grad_ref[...] = ((own_ref[...] + right_ref[...]) + (across_ref[...] + left_ref[...])).astype(BF16)
+    for copy in copies:
+        copy.wait()
 
 
 def call(kernel, out_shape, smem=0, operands=(), scratch=(), limit=SMALL_LIMIT, first=None, idle=0):
@@ -332,13 +347,18 @@
     pos = jnp.stack([core, spot, unit, z, y, tensor // 2]).astype(jnp.int32)
     pairs = swap_pairs()
 
-    packed, state = call(
+    packed, state = pl.pallas_call(
         pack_kernel,
-        (struct((16, PACK, COLS), BF16), struct((3, 3, SHARD, COLS))),
-        0,
-        (acts, grad_out, col_dither[None], master, moment_one, moment_two),
-        limit=LARGE_LIMIT,
-    )
+        out_shape=(struct((16, PACK, COLS), BF16), struct((3, 3, SHARD, COLS))),
+        in_specs=[pl.BlockSpec(memory_space=pl.ANY)] * 6,
+        out_specs=(pl.BlockSpec(memory_space=pl.ANY),) * 2,
+        scratch_shapes=[
+            pltpu.VMEM((PACK, COLS), BF16),
+            pltpu.VMEM((1, COLS), jnp.int32),
+            pltpu.SemaphoreType.DMA((22,)),
+        ],
+        compiler_params=pltpu.CompilerParams(vmem_limit_bytes=LARGE_LIMIT),
+    )(acts, grad_out, col_dither[None], master, moment_one, moment_two)
     state = lax.ppermute(state, Z + TENSOR, pairs)
     wide = (pltpu.VMEM((6 * SHARD, COLS), F32),)
     coded = call(code_kernel, struct((48 * SHARD, COLS), BF16), 0, (state,), wide)
@@ -349,19 +369,24 @@
     row_part = lax.dynamic_slice(row_dither, (0, BLOCK * (8 * y + tensor)), (3, BLOCK))
     row_part = jnp.broadcast_to(row_part.astype(F32).reshape(3 * BLOCK, 1) * (1.0 / 1024.0), (3 * BLOCK, COLS))
 
-    xs, gs, terms, col_part, peak, keep, give = call(
+    xs, gs, col_part = call(
+        layout_kernel,
+        (struct((REPS * TOK, 1024), BF16), struct((REPS * TOK, 1024), BF16), struct((8, 1024))),
+        1,
+        (pos, own, other, row_part),
+        limit=LARGE_LIMIT,
+        idle=1,
+    )
+    terms, peak, keep, give = call(
         front_kernel,
         (
-            struct((REPS * TOK, 1024), BF16),
-            struct((REPS * TOK, 1024), BF16),
             struct((REPS, 3 * BLOCK, TOK), BF16),
-            struct((8, 1024)),
             struct((64, 1, COLS)),
             struct((16, TOK, COLS)),
             struct((16, TOK, COLS)),
         ),
         1,
-        (pos, own, other, rows),
+        (pos, xs, gs, rows),
         (
             pltpu.VMEM((48 * SHARD, COLS), F32),
             pltpu.VMEM((3 * BLOCK, 1024), F32),
@@ -372,7 +397,7 @@
     )
     peaks = lax.all_to_all(peak, ("xl", "c") + Z, 0, 0)
     got = lax.ppermute(give, "c", [(0, 1), (1, 0)])
-    back = call(pair_kernel, (struct((4, TOK, COLS)),) * 4, 1, (pos, keep, got, row_part), idle=1)
+    back = call(pair_kernel, (struct((4, TOK, COLS)),) * 4, 1, (pos, keep, got))
 
     shares = call(
         quant_kernel,
@@ -398,12 +423,16 @@
     back = call(plane_kernel, (struct((TOK, COLS)),) * 4, 1, (pos, *back))
     back = [back[0]] + [shift(back[step], ("xh", "xl"), step) for step in (1, 2, 3)]
     ring = lax.all_to_all(ring.reshape(16, 3 * SHARD, COLS), Z, 0, 0).reshape(48 * SHARD, COLS)
-    ring, grad_in = call(
+    anywhere = pl.BlockSpec(memory_space=pl.ANY)
+    local = pl.BlockSpec(memory_space=pltpu.VMEM)
+    ring, grad_in = pl.pallas_call(
         finish_kernel,
-        (struct((4, 48 * SHARD, COLS), BF16), struct((TOK, COLS), BF16)),
-        0,
-        (ring, *back),
-    )
+        out_shape=(struct((4, 48 * SHARD, COLS), BF16), struct((TOK, COLS), BF16)),
+        in_specs=[anywhere] + [local] * 4,
+        out_specs=(anywhere, local),
+        scratch_shapes=[pltpu.SemaphoreType.DMA((4,))],
+        compiler_params=pltpu.CompilerParams(vmem_limit_bytes=SMALL_LIMIT),
+    )(ring, *back)
     new_state = lax.ppermute(new_state, Z + TENSOR, pairs)
     ring = lax.all_to_all(ring.reshape(32, 6 * SHARD, COLS), ("y",) + TENSOR, 0, 0)
     new_weights = ring.reshape(32, 2, 3, SHARD, COLS).transpose(2, 0, 1, 3, 4).reshape(3, 64 * SHARD, COLS)

time: 192 us -> 194 us (1.010)
  Pallas kernels: 18.6 us -> 24.7 us
  waiting for transfers between devices: 78 us -> 72.7 us
    pallas_call x0 -> x2, Pallas kernels: none -> 6.33 us  [the longest x1 4.68 us: on_device(): pl.pallas_call(pack_kernel, out_shape=(struct((16, PACK, COLS), BF16), st...]
    all_to_all x1, waiting for transfers between devices: 20.2 us -> 14.1 us  [on_device(): lax.all_to_all(coded.reshape(16, 3 * SHARD, COLS), Z, 0, 0)]
    pallas_call x8 -> x7, Pallas kernels: 18.6 us -> 18.3 us  [call(): pl.pallas_call(body, out_shape=out_shape, in_specs=specs, out_specs=anywh...]
  transfers between devices with their start and end apart: 16 -> 16, of which waited for: 12 -> 12; matrix products, arithmetic and copies ran while one was open for 1% -> 2% of each run, Pallas kernels for 2% -> 4%
where the time goes in v9:
time: 194 us; the launch traced here: 193 us
  starting transfers between devices  86.7 us (45%)
  waiting for transfers between devices  72.7 us (37%)
  Pallas kernels  24.7 us (13%)
  local copies, waits for them, and re-layouts  6.85 us (4%)
    ppermute x6, starting transfers between devices, shift(): return lax.ppermute(value, axes, [(i, (i + step) % 4) for i in range(4)])  19.8 us
    ppermute x1, waiting for transfers between devices, on_device(): new_state = lax.ppermute(new_state, Z + TENSOR, pairs)  18.5 us
    pallas_call x7, Pallas kernels, call(): pl.pallas_call(body, out_shape=out_shape, in_specs=specs, out_specs=anywh...  18.3 us
    all_to_all x1, waiting for transfers between devices, on_device(): lax.all_to_all(coded.reshape(16, 3 * SHARD, COLS), Z, 0, 0)  14.1 us
    ppermute x6, waiting for transfers between devices, shift(): return lax.ppermute(value, axes, [(i, (i + step) % 4) for i in range(4)])  12.6 us
    all_to_all x1, starting transfers between devices, on_device(): lax.all_to_all(ring.reshape(16, 3 * SHARD, COLS), Z, 0, 0)  11.3 us
    all_to_all x1, starting transfers between devices, on_device(): lax.all_to_all(coded.reshape(16, 3 * SHARD, COLS), Z, 0, 0)  10.6 us
    all_to_all x1, starting transfers between devices, on_device(): own = lax.all_to_all(packed, ('y', 'xh', 'xl'), 0, 0)  9.54 us
  transfers between devices with their start and end apart: 16, of which 12 were waited for; matrix products, arithmetic and copies ran while one was open for 2% of the time, Pallas kernels for 4%

profile of v9, /device:TPU:2, one launch (start us, length us, event | category | flops | bytes accessed | tf_op | source)
XLA Modules:
  0.0 192.6 jit_solution(4464348454439697099)
XLA Ops:
  0.6 4.7 %shard_map.119 = (bf16[16,272,128]{2,1,0:T(8,128)(2,1)}, f32[3,3,24,128]{3,2,1,0:T(8,128)}) custom-call(bf16[128,128]{1,0:T(8,128)(2,1)} %acts_ref.1, bf16[128,128]{1,0:T(8,128)(2,1)} %grad_ref.1, s32[1,128]{1,0:T(1,128)} %bitcast.30, f32[3,24,128]{2,1,0:T(8,128)} %refs_0_.1, f32[3,24,128]{2,1,0:T(8,128)} %refs_1_.1, f32[3,24,128]{2,1,0:T(8,128)} %refs_2_.1), custom_call_target="tpu_custom_call" | custom-call | tf_op jit(solution)/shard_map/pallas_call | solution.py:350
  5.3 9.5 %all-to-all-start = ((bf16[16,272,128]{2,1,0:T(8,128)(2,1)}), bf16[16,272,128]{2,1,0:T(8,128)(2,1)S(1)}, u32[]{:S(2)}, u32[]{:S(2)}) async-start(bf16[16,272,128]{2,1,0:T(8,128)(2,1)} %get-tuple-element.26), calls=%async_computation | async-start | bytes 2228224 | tf_op jit(solution)/shard_map/all_to_all | solution.py:366
  14.9 6.7 %collective-permute-start.1 = (f32[3,3,24,128]{3,2,1,0:T(8,128)S(1)}, f32[3,3,24,128]{3,2,1,0:T(8,128)S(1)}, u32[]{:S(2)}, u32[]{:S(2)}) collective-permute-start(f32[3,3,24,128]{3,2,1,0:T(8,128)S(1)} %copy-done.9), channel_id=1, source_target_pairs={{0,0},{1,16},{2,32},{3,48},{4,64},{5,80},{6,96},{7,112},{8,8},{9,2... | collective-permute-start | bytes 331784 | tf_op jit(solution)/shard_map/ppermute | solution.py:362
  21.6 8.3 %all-to-all-done.refs_1_ = bf16[16,272,128]{2,1,0:T(8,128)(2,1)S(1)} async-done(((bf16[16,272,128]{2,1,0:T(8,128)(2,1)}), bf16[16,272,128]{2,1,0:T(8,128)(2,1)S(1)}, u32[]{:S(2)}, u32[]{:S(2)}) %all-to-all-start) | async-done | bytes 1114144 | tf_op jit(solution)/shard_map/all_to_all | solution.py:366
  31.8 5.9 %collective-permute-done.1.refs_0_.refs_1_ = f32[3,3,24,128]{3,2,1,0:T(8,128)S(1)} collective-permute-done((f32[3,3,24,128]{3,2,1,0:T(8,128)S(1)}, f32[3,3,24,128]{3,2,1,0:T(8,128)S(1)}, u32[]{:S(2)}, u32[]{:S(2)}) %collective-permute-start.1) | collective-permute-done | bytes 110624 | tf_op jit(solution)/shard_map/ppermute | solution.py:362
  38.8 10.6 %all-to-all-start.1 = ((bf16[16,72,128]{2,1,0:T(8,128)(2,1)}), bf16[16,72,128]{2,1,0:T(8,128)(2,1)S(1)}, u32[]{:S(2)}, u32[]{:S(2)}) async-start(bf16[16,72,128]{2,1,0:T(8,128)(2,1)} %bitcast.7), calls=%async_computation.1 | async-start | bytes 589824 | tf_op jit(solution)/shard_map/all_to_all | solution.py:365
  51.9 4.2 %shard_map.120 = (bf16[512,1024]{1,0:T(8,128)(2,1)}, bf16[512,1024]{1,0:T(8,128)(2,1)}, f32[8,1024]{1,0:T(8,128)}) custom-call(s32[6]{0:T(128)} %stack.27.refs_0_, bf16[16,272,128]{2,1,0:T(8,128)(2,1)} %copy-done.5, bf16[16,272,128]{2,1,0:T(8,128)(2,1)} %copy-done.7, f32[144,128]{1,0:T(8,128)} %broadcast_in_dim.9.refs_3_.refs_6_), custom_call_target="tpu_custom_call" | custom-call | tf_op jit(solution)/shard_map/pallas_call | solution.py:314
  56.1 14.1 %all-to-all-done.1 = bf16[16,72,128]{2,1,0:T(8,128)(2,1)S(1)} async-done(((bf16[16,72,128]{2,1,0:T(8,128)(2,1)}), bf16[16,72,128]{2,1,0:T(8,128)(2,1)S(1)}, u32[]{:S(2)}, u32[]{:S(2)}) %all-to-all-start.1) | async-done | bytes 294944 | tf_op jit(solution)/shard_map/all_to_all | solution.py:365
  71.0 4.9 %shard_map.122 = (bf16[4,144,128]{2,1,0:T(8,128)(2,1)}, f32[64,1,128]{2,1,0:T(1,128)}, f32[16,128,128]{2,1,0:T(8,128)}, f32[16,128,128]{2,1,0:T(8,128)}) custom-call(s32[6]{0:T(128)} %stack.27.refs_0_, bf16[512,1024]{1,0:T(8,128)(2,1)} %get-tuple-element.27.refs_1_, bf16[512,1024]{1,0:T(8,128)(2,1)} %get-tuple-element.28.refs_2_, bf16[1152,128]{1,0:T(8,128)(2,1)} %bitcast.28), custom_call_target="tpu_custom_call" | custom-call | tf_op jit(solution)/shard_map/pallas_call | solution.py:314
  77.8 8.2 %all-to-all-start.2 = ((f32[64,1,128]{2,1,0:T(1,128)}), f32[64,1,128]{2,1,0:T(1,128)S(1)}, u32[]{:S(2)}, u32[]{:S(2)}) async-start(f32[64,1,128]{2,1,0:T(1,128)} %get-tuple-element.31), calls=%async_computation.2 | async-start | bytes 65536 | tf_op jit(solution)/shard_map/all_to_all | solution.py:398
  89.0 9.5 %all-to-all-done.2.refs_4_ = f32[64,1,128]{2,1,0:T(1,128)S(1)} async-done(((f32[64,1,128]{2,1,0:T(1,128)}), f32[64,1,128]{2,1,0:T(1,128)S(1)}, u32[]{:S(2)}, u32[]{:S(2)}) %all-to-all-start.2) | async-done | bytes 32800 | tf_op jit(solution)/shard_map/all_to_all | solution.py:398
  99.1 4.9 %shard_map.124 = bf16[1152,128]{1,0:T(8,128)(2,1)} custom-call(s32[6]{0:T(128)} %stack.27.refs_0_, bf16[512,1024]{1,0:T(8,128)(2,1)} %get-tuple-element.27.refs_1_, bf16[512,1024]{1,0:T(8,128)(2,1)} %get-tuple-element.28.refs_2_, bf16[4,144,128]{2,1,0:T(8,128)(2,1)} %get-tuple-element.30.refs_3_, f32[64,1,128]{2,1,0:T(1,128)} %copy-done.8, s32[3,24]{1,0:T(4,128)} %refs_5_.1, ...), custom_call_target="tpu_custom_call" | custom-call | tf_op jit(solution)/shard_map/pallas_call | solution.py:314
  104.0 3.7 %all-to-all-start.3 = ((bf16[16,72,128]{2,1,0:T(8,128)(2,1)}), bf16[16,72,128]{2,1,0:T(8,128)(2,1)S(1)}, u32[]{:S(2)}, u32[]{:S(2)}) async-start(bf16[16,72,128]{2,1,0:T(8,128)(2,1)} %bitcast.29), calls=%async_computation.3 | async-start | bytes 589824 | tf_op jit(solution)/shard_map/all_to_all | solution.py:413
  110.2 4.6 %collective-permute-start.4 = (f32[4,128,128]{2,1,0:T(8,128)S(1)}, f32[4,128,128]{2,1,0:T(8,128)S(1)}, u32[]{:S(2)}, u32[]{:S(2)}) collective-permute-start(f32[4,128,128]{2,1,0:T(8,128)S(1)} %get-tuple-element.37), channel_id=1, source_target_pairs={{0,256},{128,384},{256,0},{384,128},{1,257},{129,385},{257,1},{385... | collective-permute-start | bytes 786440 | tf_op jit(solution)/shard_map/ppermute | solution.py:329
  114.7 3.4 %collective-permute-start.5 = (f32[4,128,128]{2,1,0:T(8,128)S(1)}, f32[4,128,128]{2,1,0:T(8,128)S(1)}, u32[]{:S(2)}, u32[]{:S(2)}) collective-permute-start(f32[4,128,128]{2,1,0:T(8,128)S(1)} %get-tuple-element.38), channel_id=1, source_target_pairs={{0,384},{128,0},{256,128},{384,256},{1,385},{129,1},{257,129},{385... | collective-permute-start | bytes 786440 | tf_op jit(solution)/shard_map/ppermute | solution.py:329
  120.1 4.0 %collective-permute-done.4.refs_3_ = f32[4,128,128]{2,1,0:T(8,128)S(1)} collective-permute-done((f32[4,128,128]{2,1,0:T(8,128)S(1)}, f32[4,128,128]{2,1,0:T(8,128)S(1)}, u32[]{:S(2)}, u32[]{:S(2)}) %collective-permute-start.4) | collective-permute-done | bytes 262176 | tf_op jit(solution)/shard_map/ppermute | solution.py:329
  124.0 2.5 %collective-permute-done.5.refs_4_ = f32[4,128,128]{2,1,0:T(8,128)S(1)} collective-permute-done((f32[4,128,128]{2,1,0:T(8,128)S(1)}, f32[4,128,128]{2,1,0:T(8,128)S(1)}, u32[]{:S(2)}, u32[]{:S(2)}) %collective-permute-start.5) | collective-permute-done | bytes 262176 | tf_op jit(solution)/shard_map/ppermute | solution.py:329
  128.2 11.3 %all-to-all-start.4 = ((bf16[16,72,128]{2,1,0:T(8,128)(2,1)}), bf16[16,72,128]{2,1,0:T(8,128)(2,1)S(1)}, u32[]{:S(2)}, u32[]{:S(2)}) async-start(bf16[16,72,128]{2,1,0:T(8,128)(2,1)} %bitcast.11), calls=%async_computation.4 | async-start | bytes 589824 | tf_op jit(solution)/shard_map/all_to_all | solution.py:425
  142.5 5.6 %collective-permute-start.7 = (f32[128,128]{1,0:T(8,128)S(1)}, f32[128,128]{1,0:T(8,128)S(1)}, u32[]{:S(2)}, u32[]{:S(2)}) collective-permute-start(f32[128,128]{1,0:T(8,128)S(1)} %get-tuple-element.42), channel_id=1, source_target_pairs={{0,4},{2,6},{4,0},{6,2},{1,5},{3,7},{5,1},{7,3},{8,12},{10,14},{12... | collective-permute-start | bytes 196616 | tf_op jit(solution)/shard_map/ppermute | solution.py:329
  151.0 3.4 %collective-permute-done.8.left_ref = f32[128,128]{1,0:T(8,128)S(1)} collective-permute-done((f32[128,128]{1,0:T(8,128)S(1)}, f32[128,128]{1,0:T(8,128)S(1)}, u32[]{:S(2)}, u32[]{:S(2)}) %collective-permute-start.8) | collective-permute-done | bytes 65568 | tf_op jit(solution)/shard_map/ppermute | solution.py:329
  154.3 3.3 %all-to-all-done.4 = bf16[16,72,128]{2,1,0:T(8,128)(2,1)S(1)} async-done(((bf16[16,72,128]{2,1,0:T(8,128)(2,1)}), bf16[16,72,128]{2,1,0:T(8,128)(2,1)S(1)}, u32[]{:S(2)}, u32[]{:S(2)}) %all-to-all-start.4) | async-done | bytes 294944 | tf_op jit(solution)/shard_map/all_to_all | solution.py:425
  159.3 7.1 %all-to-all-start.5 = ((bf16[32,144,128]{2,1,0:T(8,128)(2,1)}), bf16[32,144,128]{2,1,0:T(8,128)(2,1)S(1)}, u32[]{:S(2)}, u32[]{:S(2)}) async-start(bf16[32,144,128]{2,1,0:T(8,128)(2,1)} %bitcast.16), calls=%async_computation.5 | async-start | bytes 2359296 | tf_op jit(solution)/shard_map/all_to_all | solution.py:437
  166.4 5.9 %collective-permute-start.9 = (f32[3,3,24,128]{3,2,1,0:T(8,128)S(1)}, f32[3,3,24,128]{3,2,1,0:T(8,128)S(1)}, u32[]{:S(2)}, u32[]{:S(2)}) collective-permute-start(f32[3,3,24,128]{3,2,1,0:T(8,128)S(1)} %get-tuple-element.45), channel_id=1, source_target_pairs={{0,0},{1,16},{2,32},{3,48},{4,64},{5,80},{6,96},{7,112},{8,8},{9,2... | collective-permute-start | bytes 331784 | tf_op jit(solution)/shard_map/ppermute | solution.py:436
  172.3 18.5 %collective-permute-done.9 = f32[3,3,24,128]{3,2,1,0:T(8,128)S(1)} collective-permute-done((f32[3,3,24,128]{3,2,1,0:T(8,128)S(1)}, f32[3,3,24,128]{3,2,1,0:T(8,128)S(1)}, u32[]{:S(2)}, u32[]{:S(2)}) %collective-permute-start.9) | collective-permute-done | bytes 110624 | tf_op jit(solution)/shard_map/ppermute | solution.py:436
  (43 shorter events, 26.9 us)
Async XLA Ops:
  5.3 9.6 %copy-start.9 = (f32[3,3,24,128]{3,2,1,0:T(8,128)S(1)}, f32[3,3,24,128]{3,2,1,0:T(8,128)}, u32[]{:S(2)}) copy-start(f32[3,3,24,128]{3,2,1,0:T(8,128)} %get-tuple-element.29) | copy-start | bytes 331780
  5.3 24.6 %all-to-all-start = ((bf16[16,272,128]{2,1,0:T(8,128)(2,1)}), bf16[16,272,128]{2,1,0:T(8,128)(2,1)S(1)}, u32[]{:S(2)}, u32[]{:S(2)}) async-start(bf16[16,272,128]{2,1,0:T(8,128)(2,1)} %get-tuple-element.26), calls=%async_computation | async-start | bytes 2228224 | tf_op jit(solution)/shard_map/all_to_all | solution.py:366
  14.9 22.9 %collective-permute-start.1 = (f32[3,3,24,128]{3,2,1,0:T(8,128)S(1)}, f32[3,3,24,128]{3,2,1,0:T(8,128)S(1)}, u32[]{:S(2)}, u32[]{:S(2)}) collective-permute-start(f32[3,3,24,128]{3,2,1,0:T(8,128)S(1)} %copy-done.9), channel_id=1, source_target_pairs={{0,0},{1,16},{2,32},{3,48},{4,64},{5,80},{6,96},{7,112},{8,8},{9,2... | collective-permute-start | bytes 331784 | tf_op jit(solution)/shard_map/ppermute | solution.py:362
  29.9 21.8 %copy-start.5 = (bf16[16,272,128]{2,1,0:T(8,128)(2,1)}, bf16[16,272,128]{2,1,0:T(8,128)(2,1)S(1)}, u32[]{:S(2)}) copy-start(bf16[16,272,128]{2,1,0:T(8,128)(2,1)S(1)} %all-to-all-done.refs_1_) | copy-start | bytes 3342340
  29.9 20.9 %collective-permute-start = (bf16[16,272,128]{2,1,0:T(8,128)(2,1)S(1)}, bf16[16,272,128]{2,1,0:T(8,128)(2,1)S(1)}, u32[]{:S(2)}, u32[]{:S(2)}) collective-permute-start(bf16[16,272,128]{2,1,0:T(8,128)(2,1)S(1)} %all-to-all-done.refs_1_), channel_id=1, source_target_pairs={{0,1},{1,0},{2,3},{3,2},{4,5},{5,4},{6,7},{7,6},{8,9},{9,8},{10,11... | collective-permute-start | bytes 3342344 | tf_op jit(solution)/shard_map/ppermute | solution.py:367
  38.8 31.5 %all-to-all-start.1 = ((bf16[16,72,128]{2,1,0:T(8,128)(2,1)}), bf16[16,72,128]{2,1,0:T(8,128)(2,1)S(1)}, u32[]{:S(2)}, u32[]{:S(2)}) async-start(bf16[16,72,128]{2,1,0:T(8,128)(2,1)} %bitcast.7), calls=%async_computation.1 | async-start | bytes 589824 | tf_op jit(solution)/shard_map/all_to_all | solution.py:365
  50.9 1.0 copy-start.7
  70.3 0.7 copy-start.6
  71.0 15.1 %copy-start.3 = (s32[6]{0:T(128)S(1)}, s32[6]{0:T(128)}, u32[]{:S(2)}) copy-start(s32[6]{0:T(128)} %stack.27.refs_0_) | copy-start | bytes 76
  75.9 10.2 %collective-permute-start.2 = (f32[16,128,128]{2,1,0:T(8,128)}, f32[16,128,128]{2,1,0:T(8,128)S(1)}, u32[]{:S(2)}, u32[]{:S(2)}) collective-permute-start(f32[16,128,128]{2,1,0:T(8,128)} %get-tuple-element.34), channel_id=1, source_target_pairs={{0,1},{1,0},{2,3},{3,2},{4,5},{5,4},{6,7},{7,6},{8,9},{9,8},{10,11... | collective-permute-start | bytes 3145736 | tf_op jit(solution)/shard_map/ppermute | solution.py:399
  77.8 20.6 %all-to-all-start.2 = ((f32[64,1,128]{2,1,0:T(1,128)}), f32[64,1,128]{2,1,0:T(1,128)S(1)}, u32[]{:S(2)}, u32[]{:S(2)}) async-start(f32[64,1,128]{2,1,0:T(1,128)} %get-tuple-element.31), calls=%async_computation.2 | async-start | bytes 65536 | tf_op jit(solution)/shard_map/all_to_all | solution.py:398
  86.1 1.2 copy-start
  104.0 35.5 %copy-start.2 = (f32[4,128,128]{2,1,0:T(8,128)S(1)}, f32[4,128,128]{2,1,0:T(8,128)}, u32[]{:S(2)}) copy-start(f32[4,128,128]{2,1,0:T(8,128)} %copy-done.1) | copy-start | bytes 786436
  104.0 35.5 %copy-start.4 = (s32[6]{0:T(128)S(1)}, s32[6]{0:T(128)}, u32[]{:S(2)}) copy-start(s32[6]{0:T(128)} %stack.27.refs_0_) | copy-start | bytes 76
  104.0 22.9 %all-to-all-start.3 = ((bf16[16,72,128]{2,1,0:T(8,128)(2,1)}), bf16[16,72,128]{2,1,0:T(8,128)(2,1)S(1)}, u32[]{:S(2)}, u32[]{:S(2)}) async-start(bf16[16,72,128]{2,1,0:T(8,128)(2,1)} %bitcast.29), calls=%async_computation.3 | async-start | bytes 589824 | tf_op jit(solution)/shard_map/all_to_all | solution.py:413
  107.7 12.4 %collective-permute-start.3 = (f32[4,128,128]{2,1,0:T(8,128)S(1)}, f32[4,128,128]{2,1,0:T(8,128)S(1)}, u32[]{:S(2)}, u32[]{:S(2)}) collective-permute-start(f32[4,128,128]{2,1,0:T(8,128)S(1)} %get-tuple-element.36), channel_id=1, source_target_pairs={{0,128},{128,256},{256,384},{384,0},{1,129},{129,257},{257,385},{3... | collective-permute-start | bytes 786440 | tf_op jit(solution)/shard_map/ppermute | solution.py:329
  110.2 13.9 %collective-permute-start.4 = (f32[4,128,128]{2,1,0:T(8,128)S(1)}, f32[4,128,128]{2,1,0:T(8,128)S(1)}, u32[]{:S(2)}, u32[]{:S(2)}) collective-permute-start(f32[4,128,128]{2,1,0:T(8,128)S(1)} %get-tuple-element.37), channel_id=1, source_target_pairs={{0,256},{128,384},{256,0},{384,128},{1,257},{129,385},{257,1},{385... | collective-permute-start | bytes 786440 | tf_op jit(solution)/shard_map/ppermute | solution.py:329
  114.7 11.8 %collective-permute-start.5 = (f32[4,128,128]{2,1,0:T(8,128)S(1)}, f32[4,128,128]{2,1,0:T(8,128)S(1)}, u32[]{:S(2)}, u32[]{:S(2)}) collective-permute-start(f32[4,128,128]{2,1,0:T(8,128)S(1)} %get-tuple-element.38), channel_id=1, source_target_pairs={{0,384},{128,0},{256,128},{384,256},{1,385},{129,1},{257,129},{385... | collective-permute-start | bytes 786440 | tf_op jit(solution)/shard_map/ppermute | solution.py:329
  128.2 29.4 %all-to-all-start.4 = ((bf16[16,72,128]{2,1,0:T(8,128)(2,1)}), bf16[16,72,128]{2,1,0:T(8,128)(2,1)S(1)}, u32[]{:S(2)}, u32[]{:S(2)}) async-start(bf16[16,72,128]{2,1,0:T(8,128)(2,1)} %bitcast.11), calls=%async_computation.4 | async-start | bytes 589824 | tf_op jit(solution)/shard_map/all_to_all | solution.py:425
  140.6 9.5 %collective-permute-start.6 = (f32[128,128]{1,0:T(8,128)S(1)}, f32[128,128]{1,0:T(8,128)S(1)}, u32[]{:S(2)}, u32[]{:S(2)}) collective-permute-start(f32[128,128]{1,0:T(8,128)S(1)} %get-tuple-element.41), channel_id=1, source_target_pairs={{0,2},{2,4},{4,6},{6,0},{1,3},{3,5},{5,7},{7,1},{8,10},{10,12},{12... | collective-permute-start | bytes 196616 | tf_op jit(solution)/shard_map/ppermute | solution.py:329
  142.5 8.4 %collective-permute-start.7 = (f32[128,128]{1,0:T(8,128)S(1)}, f32[128,128]{1,0:T(8,128)S(1)}, u32[]{:S(2)}, u32[]{:S(2)}) collective-permute-start(f32[128,128]{1,0:T(8,128)S(1)} %get-tuple-element.42), channel_id=1, source_target_pairs={{0,4},{2,6},{4,0},{6,2},{1,5},{3,7},{5,1},{7,3},{8,12},{10,14},{12... | collective-permute-start | bytes 196616 | tf_op jit(solution)/shard_map/ppermute | solution.py:329
  148.2 6.2 %collective-permute-start.8 = (f32[128,128]{1,0:T(8,128)S(1)}, f32[128,128]{1,0:T(8,128)S(1)}, u32[]{:S(2)}, u32[]{:S(2)}) collective-permute-start(f32[128,128]{1,0:T(8,128)S(1)} %get-tuple-element.43), channel_id=1, source_target_pairs={{0,6},{2,0},{4,2},{6,4},{1,7},{3,1},{5,3},{7,5},{8,14},{10,8},{12,... | collective-permute-start | bytes 196616 | tf_op jit(solution)/shard_map/ppermute | solution.py:329
  159.3 32.1 %all-to-all-start.5 = ((bf16[32,144,128]{2,1,0:T(8,128)(2,1)}), bf16[32,144,128]{2,1,0:T(8,128)(2,1)S(1)}, u32[]{:S(2)}, u32[]{:S(2)}) async-start(bf16[32,144,128]{2,1,0:T(8,128)(2,1)} %bitcast.16), calls=%async_computation.5 | async-start | bytes 2359296 | tf_op jit(solution)/shard_map/all_to_all | solution.py:437
  166.4 24.4 %collective-permute-start.9 = (f32[3,3,24,128]{3,2,1,0:T(8,128)S(1)}, f32[3,3,24,128]{3,2,1,0:T(8,128)S(1)}, u32[]{:S(2)}, u32[]{:S(2)}) collective-permute-start(f32[3,3,24,128]{3,2,1,0:T(8,128)S(1)} %get-tuple-element.45), channel_id=1, source_target_pairs={{0,0},{1,16},{2,32},{3,48},{4,64},{5,80},{6,96},{7,112},{8,8},{9,2... | collective-permute-start | bytes 331784 | tf_op jit(solution)/shard_map/ppermute | solution.py:436
  (2 other events, 1.3 us)

commit v10 on v9

--- a/solution.py
+++ b/solution.py
@@ -74,28 +74,18 @@
         coded_ref[pair * 6 * SHARD : (pair + 1) * 6 * SHARD, :] = narrow
 
 
-def pack_kernel(acts_ref, grad_ref, dither_ref, *refs):
-    state_in, (packed_ref, state_ref, held_ref, dither_held_ref, sems) = refs[:3], refs[3:]
-    loads = [
-        pltpu.make_async_copy(acts_ref, held_ref.at[pl.ds(0, TOK)], sems.at[0]),
-        pltpu.make_async_copy(grad_ref, held_ref.at[pl.ds(TOK, TOK)], sems.at[1]),
-        pltpu.make_async_copy(dither_ref, dither_held_ref, sems.at[2]),
-    ]
-    copies = [pltpu.make_async_copy(state_in[i], state_ref.at[i], sems.at[3 + i]) for i in range(3)]
-    for copy in loads + copies:
-        copy.start()
-    loads[2].wait()
-    high = (dither_held_ref[...] >> 3).astype(F32)
-    low = (dither_held_ref[...] & 7).astype(F32)
+def pack_kernel(acts_ref, grad_ref, dither_ref, master_ref, one_ref, two_ref, packed_ref, state_ref):
+    high = (dither_ref[...] >> 3).astype(F32)
+    low = (dither_ref[...] & 7).astype(F32)
     row = lax.broadcasted_iota(jnp.int32, (16, COLS), 0)
-    held_ref[2 * TOK : PACK, :] = jnp.where(row == 0, high, jnp.where(row == 1, low, 0.0)).astype(BF16)
-    loads[0].wait()
-    loads[1].wait()
-    stores = [pltpu.make_async_copy(held_ref, packed_ref.at[peer], sems.at[6 + peer]) for peer in range(16)]
-    for store in stores:
-        store.start()
-    for copy in copies + stores:
-        copy.wait()
+    extra = jnp.where(row == 0, high, jnp.where(row == 1, low, 0.0)).astype(BF16)
+    for peer in range(16):
+        packed_ref[peer, 0:TOK, :] = acts_ref[...]
+        packed_ref[peer, TOK : 2 * TOK, :] = grad_ref[...]
+        packed_ref[peer, 2 * TOK : PACK, :] = extra
+    state_ref[0] = master_ref[...]
+    state_ref[1] = one_ref[...]
+    state_ref[2] = two_ref[...]
 
 
 def code_kernel(state_ref, coded_ref, wide_ref):
@@ -347,18 +337,13 @@
     pos = jnp.stack([core, spot, unit, z, y, tensor // 2]).astype(jnp.int32)
     pairs = swap_pairs()
 
-    packed, state = pl.pallas_call(
+    packed, state = call(
         pack_kernel,
-        out_shape=(struct((16, PACK, COLS), BF16), struct((3, 3, SHARD, COLS))),
-        in_specs=[pl.BlockSpec(memory_space=pl.ANY)] * 6,
-        out_specs=(pl.BlockSpec(memory_space=pl.ANY),) * 2,
-        scratch_shapes=[
-            pltpu.VMEM((PACK, COLS), BF16),
-            pltpu.VMEM((1, COLS), jnp.int32),
-            pltpu.SemaphoreType.DMA((22,)),
-        ],
-        compiler_params=pltpu.CompilerParams(vmem_limit_bytes=LARGE_LIMIT),
-    )(acts, grad_out, col_dither[None], master, moment_one, moment_two)
+        (struct((16, PACK, COLS), BF16), struct((3, 3, SHARD, COLS))),
+        0,
+        (acts, grad_out, col_dither[None], master, moment_one, moment_two),
+        limit=LARGE_LIMIT,
+    )
     state = lax.ppermute(state, Z + TENSOR, pairs)
     wide = (pltpu.VMEM((6 * SHARD, COLS), F32),)
     coded = call(code_kernel, struct((48 * SHARD, COLS), BF16), 0, (state,), wide)

time: 194 us -> 191 us (0.985)
  Pallas kernels: 24.7 us -> 22 us
    pallas_call x1 -> x0, Pallas kernels: 4.68 us -> none  [on_device(): pl.pallas_call(pack_kernel, out_shape=(struct((16, PACK, COLS), BF16), st...]
    pallas_call x7 -> x8, Pallas kernels: 18.3 us -> 20.4 us  [call(): pl.pallas_call(body, out_shape=out_shape, in_specs=specs, out_specs=anywh...]
where the time goes in v10:
time: 191 us; the launch traced here: 190 us
  starting transfers between devices  86.7 us (45%)
  waiting for transfers between devices  72.7 us (38%)
  Pallas kernels  22 us (12%)
  local copies, waits for them, and re-layouts  6.85 us (4%)
    pallas_call x8, Pallas kernels, call(): pl.pallas_call(body, out_shape=out_shape, in_specs=specs, out_specs=anywh...  20.4 us
    ppermute x6, starting transfers between devices, shift(): return lax.ppermute(value, axes, [(i, (i + step) % 4) for i in range(4)])  19.8 us
    ppermute x1, waiting for transfers between devices, on_device(): new_state = lax.ppermute(new_state, Z + TENSOR, pairs)  18.5 us
    all_to_all x1, waiting for transfers between devices, on_device(): lax.all_to_all(coded.reshape(16, 3 * SHARD, COLS), Z, 0, 0)  14.1 us
    ppermute x6, waiting for transfers between devices, shift(): return lax.ppermute(value, axes, [(i, (i + step) % 4) for i in range(4)])  12.6 us
    all_to_all x1, starting transfers between devices, on_device(): lax.all_to_all(ring.reshape(16, 3 * SHARD, COLS), Z, 0, 0)  11.3 us
    all_to_all x1, starting transfers between devices, on_device(): lax.all_to_all(coded.reshape(16, 3 * SHARD, COLS), Z, 0, 0)  10.6 us
    all_to_all x1, starting transfers between devices, on_device(): own = lax.all_to_all(packed, ('y', 'xh', 'xl'), 0, 0)  9.54 us
  transfers between devices with their start and end apart: 16, of which 12 were waited for; matrix products, arithmetic and copies ran while one was open for 2% of the time, Pallas kernels for 4%

profile of v10, /device:TPU:2, one launch (start us, length us, event | category | flops | bytes accessed | tf_op | source)
XLA Modules:
  0.0 190.0 jit_solution(13005299297391176386)
XLA Ops:
  2.7 9.5 %all-to-all-start = ((bf16[16,272,128]{2,1,0:T(8,128)(2,1)}), bf16[16,272,128]{2,1,0:T(8,128)(2,1)S(1)}, u32[]{:S(2)}, u32[]{:S(2)}) async-start(bf16[16,272,128]{2,1,0:T(8,128)(2,1)} %get-tuple-element.26), calls=%async_computation | async-start | bytes 2228224 | tf_op jit(solution)/shard_map/all_to_all | solution.py:351
  12.3 6.7 %collective-permute-start.1 = (f32[3,3,24,128]{3,2,1,0:T(8,128)S(1)}, f32[3,3,24,128]{3,2,1,0:T(8,128)S(1)}, u32[]{:S(2)}, u32[]{:S(2)}) collective-permute-start(f32[3,3,24,128]{3,2,1,0:T(8,128)S(1)} %copy-done.9), channel_id=1, source_target_pairs={{0,0},{1,16},{2,32},{3,48},{4,64},{5,80},{6,96},{7,112},{8,8},{9,2... | collective-permute-start | bytes 331784 | tf_op jit(solution)/shard_map/ppermute | solution.py:347
  19.0 8.3 %all-to-all-done.refs_1_ = bf16[16,272,128]{2,1,0:T(8,128)(2,1)S(1)} async-done(((bf16[16,272,128]{2,1,0:T(8,128)(2,1)}), bf16[16,272,128]{2,1,0:T(8,128)(2,1)S(1)}, u32[]{:S(2)}, u32[]{:S(2)}) %all-to-all-start) | async-done | bytes 1114144 | tf_op jit(solution)/shard_map/all_to_all | solution.py:351
  29.2 5.9 %collective-permute-done.1.refs_0_.refs_1_ = f32[3,3,24,128]{3,2,1,0:T(8,128)S(1)} collective-permute-done((f32[3,3,24,128]{3,2,1,0:T(8,128)S(1)}, f32[3,3,24,128]{3,2,1,0:T(8,128)S(1)}, u32[]{:S(2)}, u32[]{:S(2)}) %collective-permute-start.1) | collective-permute-done | bytes 110624 | tf_op jit(solution)/shard_map/ppermute | solution.py:347
  36.2 10.6 %all-to-all-start.1 = ((bf16[16,72,128]{2,1,0:T(8,128)(2,1)}), bf16[16,72,128]{2,1,0:T(8,128)(2,1)S(1)}, u32[]{:S(2)}, u32[]{:S(2)}) async-start(bf16[16,72,128]{2,1,0:T(8,128)(2,1)} %bitcast.7), calls=%async_computation.1 | async-start | bytes 589824 | tf_op jit(solution)/shard_map/all_to_all | solution.py:350
  49.3 4.2 %shard_map.120 = (bf16[512,1024]{1,0:T(8,128)(2,1)}, bf16[512,1024]{1,0:T(8,128)(2,1)}, f32[8,1024]{1,0:T(8,128)}) custom-call(s32[6]{0:T(128)} %stack.27.refs_0_, bf16[16,272,128]{2,1,0:T(8,128)(2,1)} %copy-done.5, bf16[16,272,128]{2,1,0:T(8,128)(2,1)} %copy-done.7, f32[144,128]{1,0:T(8,128)} %broadcast_in_dim.9.refs_3_.refs_6_), custom_call_target="tpu_custom_call" | custom-call | tf_op jit(solution)/shard_map/pallas_call | solution.py:304
  53.5 14.1 %all-to-all-done.1 = bf16[16,72,128]{2,1,0:T(8,128)(2,1)S(1)} async-done(((bf16[16,72,128]{2,1,0:T(8,128)(2,1)}), bf16[16,72,128]{2,1,0:T(8,128)(2,1)S(1)}, u32[]{:S(2)}, u32[]{:S(2)}) %all-to-all-start.1) | async-done | bytes 294944 | tf_op jit(solution)/shard_map/all_to_all | solution.py:350
  68.4 4.9 %shard_map.122 = (bf16[4,144,128]{2,1,0:T(8,128)(2,1)}, f32[64,1,128]{2,1,0:T(1,128)}, f32[16,128,128]{2,1,0:T(8,128)}, f32[16,128,128]{2,1,0:T(8,128)}) custom-call(s32[6]{0:T(128)} %stack.27.refs_0_, bf16[512,1024]{1,0:T(8,128)(2,1)} %get-tuple-element.27.refs_1_, bf16[512,1024]{1,0:T(8,128)(2,1)} %get-tuple-element.28.refs_2_, bf16[1152,128]{1,0:T(8,128)(2,1)} %bitcast.28), custom_call_target="tpu_custom_call" | custom-call | tf_op jit(solution)/shard_map/pallas_call | solution.py:304
  75.2 8.2 %all-to-all-start.2 = ((f32[64,1,128]{2,1,0:T(1,128)}), f32[64,1,128]{2,1,0:T(1,128)S(1)}, u32[]{:S(2)}, u32[]{:S(2)}) async-start(f32[64,1,128]{2,1,0:T(1,128)} %get-tuple-element.31), calls=%async_computation.2 | async-start | bytes 65536 | tf_op jit(solution)/shard_map/all_to_all | solution.py:383
  86.3 9.5 %all-to-all-done.2.refs_4_ = f32[64,1,128]{2,1,0:T(1,128)S(1)} async-done(((f32[64,1,128]{2,1,0:T(1,128)}), f32[64,1,128]{2,1,0:T(1,128)S(1)}, u32[]{:S(2)}, u32[]{:S(2)}) %all-to-all-start.2) | async-done | bytes 32800 | tf_op jit(solution)/shard_map/all_to_all | solution.py:383
  96.5 4.9 %shard_map.124 = bf16[1152,128]{1,0:T(8,128)(2,1)} custom-call(s32[6]{0:T(128)} %stack.27.refs_0_, bf16[512,1024]{1,0:T(8,128)(2,1)} %get-tuple-element.27.refs_1_, bf16[512,1024]{1,0:T(8,128)(2,1)} %get-tuple-element.28.refs_2_, bf16[4,144,128]{2,1,0:T(8,128)(2,1)} %get-tuple-element.30.refs_3_, f32[64,1,128]{2,1,0:T(1,128)} %copy-done.8, s32[3,24]{1,0:T(4,128)} %refs_5_.3, ...), custom_call_target="tpu_custom_call" | custom-call | tf_op jit(solution)/shard_map/pallas_call | solution.py:304
  101.4 3.7 %all-to-all-start.3 = ((bf16[16,72,128]{2,1,0:T(8,128)(2,1)}), bf16[16,72,128]{2,1,0:T(8,128)(2,1)S(1)}, u32[]{:S(2)}, u32[]{:S(2)}) async-start(bf16[16,72,128]{2,1,0:T(8,128)(2,1)} %bitcast.29), calls=%async_computation.3 | async-start | bytes 589824 | tf_op jit(solution)/shard_map/all_to_all | solution.py:398
  105.1 2.4 %collective-permute-start.3 = (f32[4,128,128]{2,1,0:T(8,128)S(1)}, f32[4,128,128]{2,1,0:T(8,128)S(1)}, u32[]{:S(2)}, u32[]{:S(2)}) collective-permute-start(f32[4,128,128]{2,1,0:T(8,128)S(1)} %get-tuple-element.36), channel_id=1, source_target_pairs={{0,128},{128,256},{256,384},{384,0},{1,129},{129,257},{257,385},{3... | collective-permute-start | bytes 786440 | tf_op jit(solution)/shard_map/ppermute | solution.py:319
  107.5 4.6 %collective-permute-start.4 = (f32[4,128,128]{2,1,0:T(8,128)S(1)}, f32[4,128,128]{2,1,0:T(8,128)S(1)}, u32[]{:S(2)}, u32[]{:S(2)}) collective-permute-start(f32[4,128,128]{2,1,0:T(8,128)S(1)} %get-tuple-element.37), channel_id=1, source_target_pairs={{0,256},{128,384},{256,0},{384,128},{1,257},{129,385},{257,1},{385... | collective-permute-start | bytes 786440 | tf_op jit(solution)/shard_map/ppermute | solution.py:319
  112.1 3.4 %collective-permute-start.5 = (f32[4,128,128]{2,1,0:T(8,128)S(1)}, f32[4,128,128]{2,1,0:T(8,128)S(1)}, u32[]{:S(2)}, u32[]{:S(2)}) collective-permute-start(f32[4,128,128]{2,1,0:T(8,128)S(1)} %get-tuple-element.38), channel_id=1, source_target_pairs={{0,384},{128,0},{256,128},{384,256},{1,385},{129,1},{257,129},{385... | collective-permute-start | bytes 786440 | tf_op jit(solution)/shard_map/ppermute | solution.py:319
  117.5 4.0 %collective-permute-done.4.refs_3_ = f32[4,128,128]{2,1,0:T(8,128)S(1)} collective-permute-done((f32[4,128,128]{2,1,0:T(8,128)S(1)}, f32[4,128,128]{2,1,0:T(8,128)S(1)}, u32[]{:S(2)}, u32[]{:S(2)}) %collective-permute-start.4) | collective-permute-done | bytes 262176 | tf_op jit(solution)/shard_map/ppermute | solution.py:319
  121.4 2.5 %collective-permute-done.5.refs_4_ = f32[4,128,128]{2,1,0:T(8,128)S(1)} collective-permute-done((f32[4,128,128]{2,1,0:T(8,128)S(1)}, f32[4,128,128]{2,1,0:T(8,128)S(1)}, u32[]{:S(2)}, u32[]{:S(2)}) %collective-permute-start.5) | collective-permute-done | bytes 262176 | tf_op jit(solution)/shard_map/ppermute | solution.py:319
  125.6 11.3 %all-to-all-start.4 = ((bf16[16,72,128]{2,1,0:T(8,128)(2,1)}), bf16[16,72,128]{2,1,0:T(8,128)(2,1)S(1)}, u32[]{:S(2)}, u32[]{:S(2)}) async-start(bf16[16,72,128]{2,1,0:T(8,128)(2,1)} %bitcast.11), calls=%async_computation.4 | async-start | bytes 589824 | tf_op jit(solution)/shard_map/all_to_all | solution.py:410
  139.9 5.6 %collective-permute-start.7 = (f32[128,128]{1,0:T(8,128)S(1)}, f32[128,128]{1,0:T(8,128)S(1)}, u32[]{:S(2)}, u32[]{:S(2)}) collective-permute-start(f32[128,128]{1,0:T(8,128)S(1)} %get-tuple-element.42), channel_id=1, source_target_pairs={{0,4},{2,6},{4,0},{6,2},{1,5},{3,7},{5,1},{7,3},{8,12},{10,14},{12... | collective-permute-start | bytes 196616 | tf_op jit(solution)/shard_map/ppermute | solution.py:319
  148.3 3.4 %collective-permute-done.8.left_ref = f32[128,128]{1,0:T(8,128)S(1)} collective-permute-done((f32[128,128]{1,0:T(8,128)S(1)}, f32[128,128]{1,0:T(8,128)S(1)}, u32[]{:S(2)}, u32[]{:S(2)}) %collective-permute-start.8) | collective-permute-done | bytes 65568 | tf_op jit(solution)/shard_map/ppermute | solution.py:319
  151.7 3.3 %all-to-all-done.4 = bf16[16,72,128]{2,1,0:T(8,128)(2,1)S(1)} async-done(((bf16[16,72,128]{2,1,0:T(8,128)(2,1)}), bf16[16,72,128]{2,1,0:T(8,128)(2,1)S(1)}, u32[]{:S(2)}, u32[]{:S(2)}) %all-to-all-start.4) | async-done | bytes 294944 | tf_op jit(solution)/shard_map/all_to_all | solution.py:410
  156.6 7.1 %all-to-all-start.5 = ((bf16[32,144,128]{2,1,0:T(8,128)(2,1)}), bf16[32,144,128]{2,1,0:T(8,128)(2,1)S(1)}, u32[]{:S(2)}, u32[]{:S(2)}) async-start(bf16[32,144,128]{2,1,0:T(8,128)(2,1)} %bitcast.16), calls=%async_computation.5 | async-start | bytes 2359296 | tf_op jit(solution)/shard_map/all_to_all | solution.py:422
  163.7 5.9 %collective-permute-start.9 = (f32[3,3,24,128]{3,2,1,0:T(8,128)S(1)}, f32[3,3,24,128]{3,2,1,0:T(8,128)S(1)}, u32[]{:S(2)}, u32[]{:S(2)}) collective-permute-start(f32[3,3,24,128]{3,2,1,0:T(8,128)S(1)} %get-tuple-element.45), channel_id=1, source_target_pairs={{0,0},{1,16},{2,32},{3,48},{4,64},{5,80},{6,96},{7,112},{8,8},{9,2... | collective-permute-start | bytes 331784 | tf_op jit(solution)/shard_map/ppermute | solution.py:421
  169.7 18.5 %collective-permute-done.9 = f32[3,3,24,128]{3,2,1,0:T(8,128)S(1)} collective-permute-done((f32[3,3,24,128]{3,2,1,0:T(8,128)S(1)}, f32[3,3,24,128]{3,2,1,0:T(8,128)S(1)}, u32[]{:S(2)}, u32[]{:S(2)}) %collective-permute-start.9) | collective-permute-done | bytes 110624 | tf_op jit(solution)/shard_map/ppermute | solution.py:421
  (43 shorter events, 26.5 us)
Async XLA Ops:
  2.7 9.6 %copy-start.9 = (f32[3,3,24,128]{3,2,1,0:T(8,128)S(1)}, f32[3,3,24,128]{3,2,1,0:T(8,128)}, u32[]{:S(2)}) copy-start(f32[3,3,24,128]{3,2,1,0:T(8,128)} %get-tuple-element.29) | copy-start | bytes 331780
  2.7 24.6 %all-to-all-start = ((bf16[16,272,128]{2,1,0:T(8,128)(2,1)}), bf16[16,272,128]{2,1,0:T(8,128)(2,1)S(1)}, u32[]{:S(2)}, u32[]{:S(2)}) async-start(bf16[16,272,128]{2,1,0:T(8,128)(2,1)} %get-tuple-element.26), calls=%async_computation | async-start | bytes 2228224 | tf_op jit(solution)/shard_map/all_to_all | solution.py:351
  12.3 22.9 %collective-permute-start.1 = (f32[3,3,24,128]{3,2,1,0:T(8,128)S(1)}, f32[3,3,24,128]{3,2,1,0:T(8,128)S(1)}, u32[]{:S(2)}, u32[]{:S(2)}) collective-permute-start(f32[3,3,24,128]{3,2,1,0:T(8,128)S(1)} %copy-done.9), channel_id=1, source_target_pairs={{0,0},{1,16},{2,32},{3,48},{4,64},{5,80},{6,96},{7,112},{8,8},{9,2... | collective-permute-start | bytes 331784 | tf_op jit(solution)/shard_map/ppermute | solution.py:347
  27.3 21.8 %copy-start.5 = (bf16[16,272,128]{2,1,0:T(8,128)(2,1)}, bf16[16,272,128]{2,1,0:T(8,128)(2,1)S(1)}, u32[]{:S(2)}) copy-start(bf16[16,272,128]{2,1,0:T(8,128)(2,1)S(1)} %all-to-all-done.refs_1_) | copy-start | bytes 3342340
  27.3 20.9 %collective-permute-start = (bf16[16,272,128]{2,1,0:T(8,128)(2,1)S(1)}, bf16[16,272,128]{2,1,0:T(8,128)(2,1)S(1)}, u32[]{:S(2)}, u32[]{:S(2)}) collective-permute-start(bf16[16,272,128]{2,1,0:T(8,128)(2,1)S(1)} %all-to-all-done.refs_1_), channel_id=1, source_target_pairs={{0,1},{1,0},{2,3},{3,2},{4,5},{5,4},{6,7},{7,6},{8,9},{9,8},{10,11... | collective-permute-start | bytes 3342344 | tf_op jit(solution)/shard_map/ppermute | solution.py:352
  36.2 31.5 %all-to-all-start.1 = ((bf16[16,72,128]{2,1,0:T(8,128)(2,1)}), bf16[16,72,128]{2,1,0:T(8,128)(2,1)S(1)}, u32[]{:S(2)}, u32[]{:S(2)}) async-start(bf16[16,72,128]{2,1,0:T(8,128)(2,1)} %bitcast.7), calls=%async_computation.1 | async-start | bytes 589824 | tf_op jit(solution)/shard_map/all_to_all | solution.py:350
  48.2 1.0 copy-start.7
  67.7 0.7 copy-start.6
  68.4 15.1 %copy-start.3 = (s32[6]{0:T(128)S(1)}, s32[6]{0:T(128)}, u32[]{:S(2)}) copy-start(s32[6]{0:T(128)} %stack.27.refs_0_) | copy-start | bytes 76
  73.3 10.2 %collective-permute-start.2 = (f32[16,128,128]{2,1,0:T(8,128)}, f32[16,128,128]{2,1,0:T(8,128)S(1)}, u32[]{:S(2)}, u32[]{:S(2)}) collective-permute-start(f32[16,128,128]{2,1,0:T(8,128)} %get-tuple-element.34), channel_id=1, source_target_pairs={{0,1},{1,0},{2,3},{3,2},{4,5},{5,4},{6,7},{7,6},{8,9},{9,8},{10,11... | collective-permute-start | bytes 3145736 | tf_op jit(solution)/shard_map/ppermute | solution.py:384
  75.2 20.6 %all-to-all-start.2 = ((f32[64,1,128]{2,1,0:T(1,128)}), f32[64,1,128]{2,1,0:T(1,128)S(1)}, u32[]{:S(2)}, u32[]{:S(2)}) async-start(f32[64,1,128]{2,1,0:T(1,128)} %get-tuple-element.31), calls=%async_computation.2 | async-start | bytes 65536 | tf_op jit(solution)/shard_map/all_to_all | solution.py:383
  83.5 1.2 copy-start
  101.4 35.5 %copy-start.2 = (f32[4,128,128]{2,1,0:T(8,128)S(1)}, f32[4,128,128]{2,1,0:T(8,128)}, u32[]{:S(2)}) copy-start(f32[4,128,128]{2,1,0:T(8,128)} %copy-done.1) | copy-start | bytes 786436
  101.4 35.5 %copy-start.4 = (s32[6]{0:T(128)S(1)}, s32[6]{0:T(128)}, u32[]{:S(2)}) copy-start(s32[6]{0:T(128)} %stack.27.refs_0_) | copy-start | bytes 76
  101.4 22.9 %all-to-all-start.3 = ((bf16[16,72,128]{2,1,0:T(8,128)(2,1)}), bf16[16,72,128]{2,1,0:T(8,128)(2,1)S(1)}, u32[]{:S(2)}, u32[]{:S(2)}) async-start(bf16[16,72,128]{2,1,0:T(8,128)(2,1)} %bitcast.29), calls=%async_computation.3 | async-start | bytes 589824 | tf_op jit(solution)/shard_map/all_to_all | solution.py:398
  105.1 12.4 %collective-permute-start.3 = (f32[4,128,128]{2,1,0:T(8,128)S(1)}, f32[4,128,128]{2,1,0:T(8,128)S(1)}, u32[]{:S(2)}, u32[]{:S(2)}) collective-permute-start(f32[4,128,128]{2,1,0:T(8,128)S(1)} %get-tuple-element.36), channel_id=1, source_target_pairs={{0,128},{128,256},{256,384},{384,0},{1,129},{129,257},{257,385},{3... | collective-permute-start | bytes 786440 | tf_op jit(solution)/shard_map/ppermute | solution.py:319
  107.5 13.9 %collective-permute-start.4 = (f32[4,128,128]{2,1,0:T(8,128)S(1)}, f32[4,128,128]{2,1,0:T(8,128)S(1)}, u32[]{:S(2)}, u32[]{:S(2)}) collective-permute-start(f32[4,128,128]{2,1,0:T(8,128)S(1)} %get-tuple-element.37), channel_id=1, source_target_pairs={{0,256},{128,384},{256,0},{384,128},{1,257},{129,385},{257,1},{385... | collective-permute-start | bytes 786440 | tf_op jit(solution)/shard_map/ppermute | solution.py:319
  112.1 11.8 %collective-permute-start.5 = (f32[4,128,128]{2,1,0:T(8,128)S(1)}, f32[4,128,128]{2,1,0:T(8,128)S(1)}, u32[]{:S(2)}, u32[]{:S(2)}) collective-permute-start(f32[4,128,128]{2,1,0:T(8,128)S(1)} %get-tuple-element.38), channel_id=1, source_target_pairs={{0,384},{128,0},{256,128},{384,256},{1,385},{129,1},{257,129},{385... | collective-permute-start | bytes 786440 | tf_op jit(solution)/shard_map/ppermute | solution.py:319
  125.6 29.4 %all-to-all-start.4 = ((bf16[16,72,128]{2,1,0:T(8,128)(2,1)}), bf16[16,72,128]{2,1,0:T(8,128)(2,1)S(1)}, u32[]{:S(2)}, u32[]{:S(2)}) async-start(bf16[16,72,128]{2,1,0:T(8,128)(2,1)} %bitcast.11), calls=%async_computation.4 | async-start | bytes 589824 | tf_op jit(solution)/shard_map/all_to_all | solution.py:410
  138.0 9.5 %collective-permute-start.6 = (f32[128,128]{1,0:T(8,128)S(1)}, f32[128,128]{1,0:T(8,128)S(1)}, u32[]{:S(2)}, u32[]{:S(2)}) collective-permute-start(f32[128,128]{1,0:T(8,128)S(1)} %get-tuple-element.41), channel_id=1, source_target_pairs={{0,2},{2,4},{4,6},{6,0},{1,3},{3,5},{5,7},{7,1},{8,10},{10,12},{12... | collective-permute-start | bytes 196616 | tf_op jit(solution)/shard_map/ppermute | solution.py:319
  139.9 8.4 %collective-permute-start.7 = (f32[128,128]{1,0:T(8,128)S(1)}, f32[128,128]{1,0:T(8,128)S(1)}, u32[]{:S(2)}, u32[]{:S(2)}) collective-permute-start(f32[128,128]{1,0:T(8,128)S(1)} %get-tuple-element.42), channel_id=1, source_target_pairs={{0,4},{2,6},{4,0},{6,2},{1,5},{3,7},{5,1},{7,3},{8,12},{10,14},{12... | collective-permute-start | bytes 196616 | tf_op jit(solution)/shard_map/ppermute | solution.py:319
  145.6 6.2 %collective-permute-start.8 = (f32[128,128]{1,0:T(8,128)S(1)}, f32[128,128]{1,0:T(8,128)S(1)}, u32[]{:S(2)}, u32[]{:S(2)}) collective-permute-start(f32[128,128]{1,0:T(8,128)S(1)} %get-tuple-element.43), channel_id=1, source_target_pairs={{0,6},{2,0},{4,2},{6,4},{1,7},{3,1},{5,3},{7,5},{8,14},{10,8},{12,... | collective-permute-start | bytes 196616 | tf_op jit(solution)/shard_map/ppermute | solution.py:319
  156.6 32.1 %all-to-all-start.5 = ((bf16[32,144,128]{2,1,0:T(8,128)(2,1)}), bf16[32,144,128]{2,1,0:T(8,128)(2,1)S(1)}, u32[]{:S(2)}, u32[]{:S(2)}) async-start(bf16[32,144,128]{2,1,0:T(8,128)(2,1)} %bitcast.16), calls=%async_computation.5 | async-start | bytes 2359296 | tf_op jit(solution)/shard_map/all_to_all | solution.py:422
  163.7 24.4 %collective-permute-start.9 = (f32[3,3,24,128]{3,2,1,0:T(8,128)S(1)}, f32[3,3,24,128]{3,2,1,0:T(8,128)S(1)}, u32[]{:S(2)}, u32[]{:S(2)}) collective-permute-start(f32[3,3,24,128]{3,2,1,0:T(8,128)S(1)} %get-tuple-element.45), channel_id=1, source_target_pairs={{0,0},{1,16},{2,32},{3,48},{4,64},{5,80},{6,96},{7,112},{8,8},{9,2... | collective-permute-start | bytes 331784 | tf_op jit(solution)/shard_map/ppermute | solution.py:421
  (2 other events, 1.3 us)

commit v11 on v10

--- a/solution.py
+++ b/solution.py
@@ -109,7 +109,6 @@
 def front_kernel(need, done, pos_ref, *refs):
     xs_ref, gs_ref, rows_ref, terms_ref, peak_ref, keep_ref, give_ref, wide_ref, full_ref, weights_ref = refs
     core = pos_ref[0]
-    need(2)
     wide_ref[...] = rows_ref[...].astype(F32)
     for depth in range(16):
         cols = slice((depth // 2) * COLS, (depth // 2 + 1) * COLS)
@@ -178,7 +177,7 @@
 
 
 def quant_kernel(need, done, pos_ref, xs_ref, gs_ref, terms_ref, peaks_ref, bits_ref, row_ref, col_ref, out_ref, wide_ref):
-    need(3, 4)
+    need(4)
     spot = pos_ref[1]
     unit = pos_ref[2]
     depth = pos_ref[3]
@@ -260,7 +259,7 @@
         copy.wait()
 
 
-def call(kernel, out_shape, smem=0, operands=(), scratch=(), limit=SMALL_LIMIT, first=None, idle=0):
+def call(kernel, out_shape, smem=0, operands=(), scratch=(), limit=SMALL_LIMIT, first=None, idle=0, near=None):
     single = not isinstance(out_shape, tuple)
     outs = (out_shape,) if single else out_shape
     n_in = len(operands) - smem - idle
@@ -272,7 +271,11 @@
         targets = refs[smem + n_in + idle : smem + n_in + idle + n_out]
         held = refs[smem + n_in + idle + n_out :]
         taken, made, rest, sems = held[:n_in], held[n_in : n_in + n_out], held[n_in + n_out : -1], held[-1]
-        loads = [pltpu.make_async_copy(sources[i], taken[i], sems.at[i]) for i in range(n_in)]
+        if near is not None:
+            taken = taken[:near] + (sources[near],) + taken[near + 1 :]
+        loads = [
+            None if i == near else pltpu.make_async_copy(sources[i], taken[i], sems.at[i]) for i in range(n_in)
+        ]
         stores = [pltpu.make_async_copy(made[i], targets[i], sems.at[n_in + i]) for i in range(n_out)]
         if first is None:
             for load in loads:
@@ -300,7 +303,11 @@
 
     anywhere = pl.BlockSpec(memory_space=pl.ANY)
     specs = [pl.BlockSpec(memory_space=pltpu.SMEM)] * smem + [anywhere] * (n_in + idle)
+    if near is not None:
+        specs[smem + near] = pl.BlockSpec(memory_space=pltpu.VMEM)
     buffers = [pltpu.VMEM(item.shape, item.dtype) for item in tuple(operands[smem : smem + n_in]) + outs]
+    if near is not None:
+        buffers[near] = pltpu.VMEM((8, COLS), F32)
     return pl.pallas_call(
         body,
         out_shape=out_shape,
@@ -378,7 +385,8 @@
             pltpu.VMEM((3 * BLOCK, 1024), BF16),
         ),
         limit=LARGE_LIMIT,
-        first=(2, 0, 1),
+        first=(0, 1),
+        near=2,
     )
     peaks = lax.all_to_all(peak, ("xl", "c") + Z, 0, 0)
     got = lax.ppermute(give, "c", [(0, 1), (1, 0)])
@@ -391,8 +399,9 @@
         (pos, xs, gs, terms, peaks, bit_widths, row_part, col_part, back[0]),
         (pltpu.VMEM((48 * SHARD, COLS), F32),),
         limit=LARGE_LIMIT,
-        first=(3, 4, 2, 0, 1, 5, 6),
+        first=(4, 2, 0, 1, 5, 6),
         idle=1,
+        near=3,
     )
     back = [back[0]] + [shift(back[step], "y", step) for step in (1, 2, 3)]
     shares = lax.all_to_all(shares.reshape(16, 3 * SHARD, COLS), Z, 0, 0).reshape(48 * SHARD, COLS)

time: 191 us -> 191 us (level)
  no operation moved by 1% of the time
where the time goes in v11:
time: 191 us; the launch traced here: 190 us
  starting transfers between devices  86.7 us (45%)
  waiting for transfers between devices  72.7 us (38%)
  Pallas kernels  22.2 us (12%)
  local copies, waits for them, and re-layouts  6.85 us (4%)
    pallas_call x8, Pallas kernels, call(): pl.pallas_call(body, out_shape=out_shape, in_specs=specs, out_specs=anywh...  20.6 us
    ppermute x6, starting transfers between devices, shift(): return lax.ppermute(value, axes, [(i, (i + step) % 4) for i in range(4)])  19.9 us
    ppermute x1, waiting for transfers between devices, on_device(): new_state = lax.ppermute(new_state, Z + TENSOR, pairs)  18.5 us
    all_to_all x1, waiting for transfers between devices, on_device(): lax.all_to_all(coded.reshape(16, 3 * SHARD, COLS), Z, 0, 0)  14.1 us
    ppermute x6, waiting for transfers between devices, shift(): return lax.ppermute(value, axes, [(i, (i + step) % 4) for i in range(4)])  12.6 us
    all_to_all x1, starting transfers between devices, on_device(): lax.all_to_all(ring.reshape(16, 3 * SHARD, COLS), Z, 0, 0)  11.3 us
    all_to_all x1, starting transfers between devices, on_device(): lax.all_to_all(coded.reshape(16, 3 * SHARD, COLS), Z, 0, 0)  10.6 us
    all_to_all x1, starting transfers between devices, on_device(): own = lax.all_to_all(packed, ('y', 'xh', 'xl'), 0, 0)  9.54 us
  transfers between devices with their start and end apart: 16, of which 12 were waited for; matrix products, arithmetic and copies ran while one was open for 2% of the time, Pallas kernels for 4%

profile of v11, /device:TPU:2, one launch (start us, length us, event | category | flops | bytes accessed | tf_op | source)
XLA Modules:
  0.0 190.2 jit_solution(7256262393658104121)
XLA Ops:
  2.7 9.5 %all-to-all-start = ((bf16[16,272,128]{2,1,0:T(8,128)(2,1)}), bf16[16,272,128]{2,1,0:T(8,128)(2,1)S(1)}, u32[]{:S(2)}, u32[]{:S(2)}) async-start(bf16[16,272,128]{2,1,0:T(8,128)(2,1)} %get-tuple-element.26), calls=%async_computation | async-start | bytes 2228224 | tf_op jit(solution)/shard_map/all_to_all | solution.py:358
  12.3 6.7 %collective-permute-start.1 = (f32[3,3,24,128]{3,2,1,0:T(8,128)S(1)}, f32[3,3,24,128]{3,2,1,0:T(8,128)S(1)}, u32[]{:S(2)}, u32[]{:S(2)}) collective-permute-start(f32[3,3,24,128]{3,2,1,0:T(8,128)S(1)} %copy-done.9), channel_id=1, source_target_pairs={{0,0},{1,16},{2,32},{3,48},{4,64},{5,80},{6,96},{7,112},{8,8},{9,2... | collective-permute-start | bytes 331784 | tf_op jit(solution)/shard_map/ppermute | solution.py:354
  19.0 8.3 %all-to-all-done.refs_1_ = bf16[16,272,128]{2,1,0:T(8,128)(2,1)S(1)} async-done(((bf16[16,272,128]{2,1,0:T(8,128)(2,1)}), bf16[16,272,128]{2,1,0:T(8,128)(2,1)S(1)}, u32[]{:S(2)}, u32[]{:S(2)}) %all-to-all-start) | async-done | bytes 1114144 | tf_op jit(solution)/shard_map/all_to_all | solution.py:358
  29.2 5.9 %collective-permute-done.1.refs_0_.refs_1_ = f32[3,3,24,128]{3,2,1,0:T(8,128)S(1)} collective-permute-done((f32[3,3,24,128]{3,2,1,0:T(8,128)S(1)}, f32[3,3,24,128]{3,2,1,0:T(8,128)S(1)}, u32[]{:S(2)}, u32[]{:S(2)}) %collective-permute-start.1) | collective-permute-done | bytes 110624 | tf_op jit(solution)/shard_map/ppermute | solution.py:354
  36.2 10.6 %all-to-all-start.1 = ((bf16[16,72,128]{2,1,0:T(8,128)(2,1)}), bf16[16,72,128]{2,1,0:T(8,128)(2,1)S(1)}, u32[]{:S(2)}, u32[]{:S(2)}) async-start(bf16[16,72,128]{2,1,0:T(8,128)(2,1)} %bitcast.7), calls=%async_computation.1 | async-start | bytes 589824 | tf_op jit(solution)/shard_map/all_to_all | solution.py:357
  49.3 4.2 %shard_map.120 = (bf16[512,1024]{1,0:T(8,128)(2,1)}, bf16[512,1024]{1,0:T(8,128)(2,1)}, f32[8,1024]{1,0:T(8,128)}) custom-call(s32[6]{0:T(128)} %stack.27.refs_0_, bf16[16,272,128]{2,1,0:T(8,128)(2,1)} %copy-done.5, bf16[16,272,128]{2,1,0:T(8,128)(2,1)} %copy-done.7, f32[144,128]{1,0:T(8,128)} %broadcast_in_dim.9.refs_3_.refs_6_), custom_call_target="tpu_custom_call" | custom-call | tf_op jit(solution)/shard_map/pallas_call | solution.py:311
  53.5 14.1 %all-to-all-done.1 = bf16[16,72,128]{2,1,0:T(8,128)(2,1)S(1)} async-done(((bf16[16,72,128]{2,1,0:T(8,128)(2,1)}), bf16[16,72,128]{2,1,0:T(8,128)(2,1)S(1)}, u32[]{:S(2)}, u32[]{:S(2)}) %all-to-all-start.1) | async-done | bytes 294944 | tf_op jit(solution)/shard_map/all_to_all | solution.py:357
  68.4 5.0 %shard_map.122 = (bf16[4,144,128]{2,1,0:T(8,128)(2,1)}, f32[64,1,128]{2,1,0:T(1,128)}, f32[16,128,128]{2,1,0:T(8,128)}, f32[16,128,128]{2,1,0:T(8,128)}) custom-call(s32[6]{0:T(128)} %stack.27.refs_0_, bf16[512,1024]{1,0:T(8,128)(2,1)} %get-tuple-element.27.refs_1_, bf16[512,1024]{1,0:T(8,128)(2,1)} %get-tuple-element.28.refs_2_, bf16[1152,128]{1,0:T(8,128)(2,1)} %bitcast.28), custom_call_target="tpu_custom_call" | custom-call | tf_op jit(solution)/shard_map/pallas_call | solution.py:311
  75.3 8.2 %all-to-all-start.2 = ((f32[64,1,128]{2,1,0:T(1,128)}), f32[64,1,128]{2,1,0:T(1,128)S(1)}, u32[]{:S(2)}, u32[]{:S(2)}) async-start(f32[64,1,128]{2,1,0:T(1,128)} %get-tuple-element.31), calls=%async_computation.2 | async-start | bytes 65536 | tf_op jit(solution)/shard_map/all_to_all | solution.py:391
  86.4 9.5 %all-to-all-done.2.refs_4_ = f32[64,1,128]{2,1,0:T(1,128)S(1)} async-done(((f32[64,1,128]{2,1,0:T(1,128)}), f32[64,1,128]{2,1,0:T(1,128)S(1)}, u32[]{:S(2)}, u32[]{:S(2)}) %all-to-all-start.2) | async-done | bytes 32800 | tf_op jit(solution)/shard_map/all_to_all | solution.py:391
  96.5 5.0 %shard_map.124 = bf16[1152,128]{1,0:T(8,128)(2,1)} custom-call(s32[6]{0:T(128)} %stack.27.refs_0_, bf16[512,1024]{1,0:T(8,128)(2,1)} %get-tuple-element.27.refs_1_, bf16[512,1024]{1,0:T(8,128)(2,1)} %get-tuple-element.28.refs_2_, bf16[4,144,128]{2,1,0:T(8,128)(2,1)} %get-tuple-element.30.refs_3_, f32[64,1,128]{2,1,0:T(1,128)} %copy-done.8, s32[3,24]{1,0:T(4,128)} %refs_5_.3, ...), custom_call_target="tpu_custom_call" | custom-call | tf_op jit(solution)/shard_map/pallas_call | solution.py:311
  101.6 3.7 %all-to-all-start.3 = ((bf16[16,72,128]{2,1,0:T(8,128)(2,1)}), bf16[16,72,128]{2,1,0:T(8,128)(2,1)S(1)}, u32[]{:S(2)}, u32[]{:S(2)}) async-start(bf16[16,72,128]{2,1,0:T(8,128)(2,1)} %bitcast.29), calls=%async_computation.3 | async-start | bytes 589824 | tf_op jit(solution)/shard_map/all_to_all | solution.py:407
  105.3 2.4 %collective-permute-start.3 = (f32[4,128,128]{2,1,0:T(8,128)S(1)}, f32[4,128,128]{2,1,0:T(8,128)S(1)}, u32[]{:S(2)}, u32[]{:S(2)}) collective-permute-start(f32[4,128,128]{2,1,0:T(8,128)S(1)} %get-tuple-element.36), channel_id=1, source_target_pairs={{0,128},{128,256},{256,384},{384,0},{1,129},{129,257},{257,385},{3... | collective-permute-start | bytes 786440 | tf_op jit(solution)/shard_map/ppermute | solution.py:326
  107.7 4.6 %collective-permute-start.4 = (f32[4,128,128]{2,1,0:T(8,128)S(1)}, f32[4,128,128]{2,1,0:T(8,128)S(1)}, u32[]{:S(2)}, u32[]{:S(2)}) collective-permute-start(f32[4,128,128]{2,1,0:T(8,128)S(1)} %get-tuple-element.37), channel_id=1, source_target_pairs={{0,256},{128,384},{256,0},{384,128},{1,257},{129,385},{257,1},{385... | collective-permute-start | bytes 786440 | tf_op jit(solution)/shard_map/ppermute | solution.py:326
  112.3 3.4 %collective-permute-start.5 = (f32[4,128,128]{2,1,0:T(8,128)S(1)}, f32[4,128,128]{2,1,0:T(8,128)S(1)}, u32[]{:S(2)}, u32[]{:S(2)}) collective-permute-start(f32[4,128,128]{2,1,0:T(8,128)S(1)} %get-tuple-element.38), channel_id=1, source_target_pairs={{0,384},{128,0},{256,128},{384,256},{1,385},{129,1},{257,129},{385... | collective-permute-start | bytes 786440 | tf_op jit(solution)/shard_map/ppermute | solution.py:326
  117.6 3.9 %collective-permute-done.4.refs_3_ = f32[4,128,128]{2,1,0:T(8,128)S(1)} collective-permute-done((f32[4,128,128]{2,1,0:T(8,128)S(1)}, f32[4,128,128]{2,1,0:T(8,128)S(1)}, u32[]{:S(2)}, u32[]{:S(2)}) %collective-permute-start.4) | collective-permute-done | bytes 262176 | tf_op jit(solution)/shard_map/ppermute | solution.py:326
  121.6 2.5 %collective-permute-done.5.refs_4_ = f32[4,128,128]{2,1,0:T(8,128)S(1)} collective-permute-done((f32[4,128,128]{2,1,0:T(8,128)S(1)}, f32[4,128,128]{2,1,0:T(8,128)S(1)}, u32[]{:S(2)}, u32[]{:S(2)}) %collective-permute-start.5) | collective-permute-done | bytes 262176 | tf_op jit(solution)/shard_map/ppermute | solution.py:326
  125.8 11.3 %all-to-all-start.4 = ((bf16[16,72,128]{2,1,0:T(8,128)(2,1)}), bf16[16,72,128]{2,1,0:T(8,128)(2,1)S(1)}, u32[]{:S(2)}, u32[]{:S(2)}) async-start(bf16[16,72,128]{2,1,0:T(8,128)(2,1)} %bitcast.11), calls=%async_computation.4 | async-start | bytes 589824 | tf_op jit(solution)/shard_map/all_to_all | solution.py:419
  140.1 5.6 %collective-permute-start.7 = (f32[128,128]{1,0:T(8,128)S(1)}, f32[128,128]{1,0:T(8,128)S(1)}, u32[]{:S(2)}, u32[]{:S(2)}) collective-permute-start(f32[128,128]{1,0:T(8,128)S(1)} %get-tuple-element.42), channel_id=1, source_target_pairs={{0,4},{2,6},{4,0},{6,2},{1,5},{3,7},{5,1},{7,3},{8,12},{10,14},{12... | collective-permute-start | bytes 196616 | tf_op jit(solution)/shard_map/ppermute | solution.py:326
  148.5 3.4 %collective-permute-done.8.left_ref = f32[128,128]{1,0:T(8,128)S(1)} collective-permute-done((f32[128,128]{1,0:T(8,128)S(1)}, f32[128,128]{1,0:T(8,128)S(1)}, u32[]{:S(2)}, u32[]{:S(2)}) %collective-permute-start.8) | collective-permute-done | bytes 65568 | tf_op jit(solution)/shard_map/ppermute | solution.py:326
  151.9 3.3 %all-to-all-done.4 = bf16[16,72,128]{2,1,0:T(8,128)(2,1)S(1)} async-done(((bf16[16,72,128]{2,1,0:T(8,128)(2,1)}), bf16[16,72,128]{2,1,0:T(8,128)(2,1)S(1)}, u32[]{:S(2)}, u32[]{:S(2)}) %all-to-all-start.4) | async-done | bytes 294944 | tf_op jit(solution)/shard_map/all_to_all | solution.py:419
  156.8 7.1 %all-to-all-start.5 = ((bf16[32,144,128]{2,1,0:T(8,128)(2,1)}), bf16[32,144,128]{2,1,0:T(8,128)(2,1)S(1)}, u32[]{:S(2)}, u32[]{:S(2)}) async-start(bf16[32,144,128]{2,1,0:T(8,128)(2,1)} %bitcast.16), calls=%async_computation.5 | async-start | bytes 2359296 | tf_op jit(solution)/shard_map/all_to_all | solution.py:431
  163.9 5.9 %collective-permute-start.9 = (f32[3,3,24,128]{3,2,1,0:T(8,128)S(1)}, f32[3,3,24,128]{3,2,1,0:T(8,128)S(1)}, u32[]{:S(2)}, u32[]{:S(2)}) collective-permute-start(f32[3,3,24,128]{3,2,1,0:T(8,128)S(1)} %get-tuple-element.45), channel_id=1, source_target_pairs={{0,0},{1,16},{2,32},{3,48},{4,64},{5,80},{6,96},{7,112},{8,8},{9,2... | collective-permute-start | bytes 331784 | tf_op jit(solution)/shard_map/ppermute | solution.py:430
  169.8 18.5 %collective-permute-done.9 = f32[3,3,24,128]{3,2,1,0:T(8,128)S(1)} collective-permute-done((f32[3,3,24,128]{3,2,1,0:T(8,128)S(1)}, f32[3,3,24,128]{3,2,1,0:T(8,128)S(1)}, u32[]{:S(2)}, u32[]{:S(2)}) %collective-permute-start.9) | collective-permute-done | bytes 110624 | tf_op jit(solution)/shard_map/ppermute | solution.py:430
  (43 shorter events, 26.5 us)
Async XLA Ops:
  2.7 9.6 %copy-start.9 = (f32[3,3,24,128]{3,2,1,0:T(8,128)S(1)}, f32[3,3,24,128]{3,2,1,0:T(8,128)}, u32[]{:S(2)}) copy-start(f32[3,3,24,128]{3,2,1,0:T(8,128)} %get-tuple-element.29) | copy-start | bytes 331780
  2.7 24.6 %all-to-all-start = ((bf16[16,272,128]{2,1,0:T(8,128)(2,1)}), bf16[16,272,128]{2,1,0:T(8,128)(2,1)S(1)}, u32[]{:S(2)}, u32[]{:S(2)}) async-start(bf16[16,272,128]{2,1,0:T(8,128)(2,1)} %get-tuple-element.26), calls=%async_computation | async-start | bytes 2228224 | tf_op jit(solution)/shard_map/all_to_all | solution.py:358
  12.3 22.9 %collective-permute-start.1 = (f32[3,3,24,128]{3,2,1,0:T(8,128)S(1)}, f32[3,3,24,128]{3,2,1,0:T(8,128)S(1)}, u32[]{:S(2)}, u32[]{:S(2)}) collective-permute-start(f32[3,3,24,128]{3,2,1,0:T(8,128)S(1)} %copy-done.9), channel_id=1, source_target_pairs={{0,0},{1,16},{2,32},{3,48},{4,64},{5,80},{6,96},{7,112},{8,8},{9,2... | collective-permute-start | bytes 331784 | tf_op jit(solution)/shard_map/ppermute | solution.py:354
  27.3 21.8 %copy-start.5 = (bf16[16,272,128]{2,1,0:T(8,128)(2,1)}, bf16[16,272,128]{2,1,0:T(8,128)(2,1)S(1)}, u32[]{:S(2)}) copy-start(bf16[16,272,128]{2,1,0:T(8,128)(2,1)S(1)} %all-to-all-done.refs_1_) | copy-start | bytes 3342340
  27.3 20.9 %collective-permute-start = (bf16[16,272,128]{2,1,0:T(8,128)(2,1)S(1)}, bf16[16,272,128]{2,1,0:T(8,128)(2,1)S(1)}, u32[]{:S(2)}, u32[]{:S(2)}) collective-permute-start(bf16[16,272,128]{2,1,0:T(8,128)(2,1)S(1)} %all-to-all-done.refs_1_), channel_id=1, source_target_pairs={{0,1},{1,0},{2,3},{3,2},{4,5},{5,4},{6,7},{7,6},{8,9},{9,8},{10,11... | collective-permute-start | bytes 3342344 | tf_op jit(solution)/shard_map/ppermute | solution.py:359
  36.2 31.5 %all-to-all-start.1 = ((bf16[16,72,128]{2,1,0:T(8,128)(2,1)}), bf16[16,72,128]{2,1,0:T(8,128)(2,1)S(1)}, u32[]{:S(2)}, u32[]{:S(2)}) async-start(bf16[16,72,128]{2,1,0:T(8,128)(2,1)} %bitcast.7), calls=%async_computation.1 | async-start | bytes 589824 | tf_op jit(solution)/shard_map/all_to_all | solution.py:357
  48.2 1.0 copy-start.7
  67.7 0.7 copy-start.6
  68.4 15.2 %copy-start.3 = (s32[6]{0:T(128)S(1)}, s32[6]{0:T(128)}, u32[]{:S(2)}) copy-start(s32[6]{0:T(128)} %stack.27.refs_0_) | copy-start | bytes 76
  73.4 10.2 %collective-permute-start.2 = (f32[16,128,128]{2,1,0:T(8,128)}, f32[16,128,128]{2,1,0:T(8,128)S(1)}, u32[]{:S(2)}, u32[]{:S(2)}) collective-permute-start(f32[16,128,128]{2,1,0:T(8,128)} %get-tuple-element.34), channel_id=1, source_target_pairs={{0,1},{1,0},{2,3},{3,2},{4,5},{5,4},{6,7},{7,6},{8,9},{9,8},{10,11... | collective-permute-start | bytes 3145736 | tf_op jit(solution)/shard_map/ppermute | solution.py:392
  75.3 20.6 %all-to-all-start.2 = ((f32[64,1,128]{2,1,0:T(1,128)}), f32[64,1,128]{2,1,0:T(1,128)S(1)}, u32[]{:S(2)}, u32[]{:S(2)}) async-start(f32[64,1,128]{2,1,0:T(1,128)} %get-tuple-element.31), calls=%async_computation.2 | async-start | bytes 65536 | tf_op jit(solution)/shard_map/all_to_all | solution.py:391
  83.6 1.2 copy-start
  101.6 35.5 %copy-start.2 = (f32[4,128,128]{2,1,0:T(8,128)S(1)}, f32[4,128,128]{2,1,0:T(8,128)}, u32[]{:S(2)}) copy-start(f32[4,128,128]{2,1,0:T(8,128)} %copy-done.1) | copy-start | bytes 786436
  101.6 35.5 %copy-start.4 = (s32[6]{0:T(128)S(1)}, s32[6]{0:T(128)}, u32[]{:S(2)}) copy-start(s32[6]{0:T(128)} %stack.27.refs_0_) | copy-start | bytes 76
  101.6 22.9 %all-to-all-start.3 = ((bf16[16,72,128]{2,1,0:T(8,128)(2,1)}), bf16[16,72,128]{2,1,0:T(8,128)(2,1)S(1)}, u32[]{:S(2)}, u32[]{:S(2)}) async-start(bf16[16,72,128]{2,1,0:T(8,128)(2,1)} %bitcast.29), calls=%async_computation.3 | async-start | bytes 589824 | tf_op jit(solution)/shard_map/all_to_all | solution.py:407
  105.3 12.4 %collective-permute-start.3 = (f32[4,128,128]{2,1,0:T(8,128)S(1)}, f32[4,128,128]{2,1,0:T(8,128)S(1)}, u32[]{:S(2)}, u32[]{:S(2)}) collective-permute-start(f32[4,128,128]{2,1,0:T(8,128)S(1)} %get-tuple-element.36), channel_id=1, source_target_pairs={{0,128},{128,256},{256,384},{384,0},{1,129},{129,257},{257,385},{3... | collective-permute-start | bytes 786440 | tf_op jit(solution)/shard_map/ppermute | solution.py:326
  107.7 13.9 %collective-permute-start.4 = (f32[4,128,128]{2,1,0:T(8,128)S(1)}, f32[4,128,128]{2,1,0:T(8,128)S(1)}, u32[]{:S(2)}, u32[]{:S(2)}) collective-permute-start(f32[4,128,128]{2,1,0:T(8,128)S(1)} %get-tuple-element.37), channel_id=1, source_target_pairs={{0,256},{128,384},{256,0},{384,128},{1,257},{129,385},{257,1},{385... | collective-permute-start | bytes 786440 | tf_op jit(solution)/shard_map/ppermute | solution.py:326
  112.3 11.8 %collective-permute-start.5 = (f32[4,128,128]{2,1,0:T(8,128)S(1)}, f32[4,128,128]{2,1,0:T(8,128)S(1)}, u32[]{:S(2)}, u32[]{:S(2)}) collective-permute-start(f32[4,128,128]{2,1,0:T(8,128)S(1)} %get-tuple-element.38), channel_id=1, source_target_pairs={{0,384},{128,0},{256,128},{384,256},{1,385},{129,1},{257,129},{385... | collective-permute-start | bytes 786440 | tf_op jit(solution)/shard_map/ppermute | solution.py:326
  125.8 29.4 %all-to-all-start.4 = ((bf16[16,72,128]{2,1,0:T(8,128)(2,1)}), bf16[16,72,128]{2,1,0:T(8,128)(2,1)S(1)}, u32[]{:S(2)}, u32[]{:S(2)}) async-start(bf16[16,72,128]{2,1,0:T(8,128)(2,1)} %bitcast.11), calls=%async_computation.4 | async-start | bytes 589824 | tf_op jit(solution)/shard_map/all_to_all | solution.py:419
  138.2 9.5 %collective-permute-start.6 = (f32[128,128]{1,0:T(8,128)S(1)}, f32[128,128]{1,0:T(8,128)S(1)}, u32[]{:S(2)}, u32[]{:S(2)}) collective-permute-start(f32[128,128]{1,0:T(8,128)S(1)} %get-tuple-element.41), channel_id=1, source_target_pairs={{0,2},{2,4},{4,6},{6,0},{1,3},{3,5},{5,7},{7,1},{8,10},{10,12},{12... | collective-permute-start | bytes 196616 | tf_op jit(solution)/shard_map/ppermute | solution.py:326
  140.1 8.4 %collective-permute-start.7 = (f32[128,128]{1,0:T(8,128)S(1)}, f32[128,128]{1,0:T(8,128)S(1)}, u32[]{:S(2)}, u32[]{:S(2)}) collective-permute-start(f32[128,128]{1,0:T(8,128)S(1)} %get-tuple-element.42), channel_id=1, source_target_pairs={{0,4},{2,6},{4,0},{6,2},{1,5},{3,7},{5,1},{7,3},{8,12},{10,14},{12... | collective-permute-start | bytes 196616 | tf_op jit(solution)/shard_map/ppermute | solution.py:326
  145.7 6.2 %collective-permute-start.8 = (f32[128,128]{1,0:T(8,128)S(1)}, f32[128,128]{1,0:T(8,128)S(1)}, u32[]{:S(2)}, u32[]{:S(2)}) collective-permute-start(f32[128,128]{1,0:T(8,128)S(1)} %get-tuple-element.43), channel_id=1, source_target_pairs={{0,6},{2,0},{4,2},{6,4},{1,7},{3,1},{5,3},{7,5},{8,14},{10,8},{12,... | collective-permute-start | bytes 196616 | tf_op jit(solution)/shard_map/ppermute | solution.py:326
  156.8 32.1 %all-to-all-start.5 = ((bf16[32,144,128]{2,1,0:T(8,128)(2,1)}), bf16[32,144,128]{2,1,0:T(8,128)(2,1)S(1)}, u32[]{:S(2)}, u32[]{:S(2)}) async-start(bf16[32,144,128]{2,1,0:T(8,128)(2,1)} %bitcast.16), calls=%async_computation.5 | async-start | bytes 2359296 | tf_op jit(solution)/shard_map/all_to_all | solution.py:431
  163.9 24.4 %collective-permute-start.9 = (f32[3,3,24,128]{3,2,1,0:T(8,128)S(1)}, f32[3,3,24,128]{3,2,1,0:T(8,128)S(1)}, u32[]{:S(2)}, u32[]{:S(2)}) collective-permute-start(f32[3,3,24,128]{3,2,1,0:T(8,128)S(1)} %get-tuple-element.45), channel_id=1, source_target_pairs={{0,0},{1,16},{2,32},{3,48},{4,64},{5,80},{6,96},{7,112},{8,8},{9,2... | collective-permute-start | bytes 331784 | tf_op jit(solution)/shard_map/ppermute | solution.py:430
  (2 other events, 1.3 us)

commit v12 on v10

--- a/solution.py
+++ b/solution.py
@@ -401,9 +401,9 @@
         adam_kernel,
         (struct((3, 3, SHARD, COLS)), struct((48 * SHARD, COLS), BF16)),
         0,
-        (shares, state, *back[1:]),
+        (shares, state, back[1], back[2]),
         wide + (pltpu.VMEM((48 * SHARD, COLS), F32),),
-        idle=3,
+        idle=2,
     )
     back = call(plane_kernel, (struct((TOK, COLS)),) * 4, 1, (pos, *back))
     back = [back[0]] + [shift(back[step], ("xh", "xl"), step) for step in (1, 2, 3)]

time: 191 us -> 192 us (level)
  waiting for transfers between devices: 72.7 us -> 77.6 us
  starting transfers between devices: 86.7 us -> 82.6 us
    ppermute x6, waiting for transfers between devices: 12.6 us -> 19.8 us  [shift(): return lax.ppermute(value, axes, [(i, (i + step) % 4) for i in range(4)])]
    all_to_all x1, waiting for transfers between devices: 3.26 us -> 0.01 us  [on_device(): lax.all_to_all(ring.reshape(16, 3 * SHARD, COLS), Z, 0, 0)]
    all_to_all x1, waiting for transfers between devices: 0.41 us -> 2.91 us  [on_device(): lax.all_to_all(shares.reshape(16, 3 * SHARD, COLS), Z, 0, 0)]
    all_to_all x1, starting transfers between devices: 11.3 us -> 8.76 us  [on_device(): lax.all_to_all(ring.reshape(16, 3 * SHARD, COLS), Z, 0, 0)]
  transfers between devices with their start and end apart: 16 -> 16, of which waited for: 12 -> 11; matrix products, arithmetic and copies ran while one was open for 2% -> 2% of each run, Pallas kernels for 4% -> 4%
where the time goes in v12:
time: 192 us; the launch traced here: 191 us
  starting transfers between devices  82.6 us (43%)
  waiting for transfers between devices  77.6 us (40%)
  Pallas kernels  22 us (11%)
  local copies, waits for them, and re-layouts  6.85 us (4%)
    pallas_call x8, Pallas kernels, call(): pl.pallas_call(body, out_shape=out_shape, in_specs=specs, out_specs=anywh...  20.4 us
    ppermute x6, waiting for transfers between devices, shift(): return lax.ppermute(value, axes, [(i, (i + step) % 4) for i in range(4)])  19.8 us
    ppermute x6, starting transfers between devices, shift(): return lax.ppermute(value, axes, [(i, (i + step) % 4) for i in range(4)])  18.8 us
    ppermute x1, waiting for transfers between devices, on_device(): new_state = lax.ppermute(new_state, Z + TENSOR, pairs)  16.9 us
    all_to_all x1, waiting for transfers between devices, on_device(): lax.all_to_all(coded.reshape(16, 3 * SHARD, COLS), Z, 0, 0)  14.1 us
    all_to_all x1, starting transfers between devices, on_device(): lax.all_to_all(coded.reshape(16, 3 * SHARD, COLS), Z, 0, 0)  10.6 us
    all_to_all x1, starting transfers between devices, on_device(): own = lax.all_to_all(packed, ('y', 'xh', 'xl'), 0, 0)  9.54 us
    all_to_all x1, waiting for transfers between devices, on_device(): peaks = lax.all_to_all(peak, ('xl', 'c') + Z, 0, 0)  9.51 us
  transfers between devices with their start and end apart: 16, of which 11 were waited for; matrix products, arithmetic and copies ran while one was open for 2% of the time, Pallas kernels for 4%

profile of v12, /device:TPU:2, one launch (start us, length us, event | category | flops | bytes accessed | tf_op | source)
XLA Modules:
  0.0 190.8 jit_solution(3836826486501566338)
XLA Ops:
  2.7 9.5 %all-to-all-start = ((bf16[16,272,128]{2,1,0:T(8,128)(2,1)}), bf16[16,272,128]{2,1,0:T(8,128)(2,1)S(1)}, u32[]{:S(2)}, u32[]{:S(2)}) async-start(bf16[16,272,128]{2,1,0:T(8,128)(2,1)} %get-tuple-element.26), calls=%async_computation | async-start | bytes 2228224 | tf_op jit(solution)/shard_map/all_to_all | solution.py:351
  12.3 6.7 %collective-permute-start.1 = (f32[3,3,24,128]{3,2,1,0:T(8,128)S(1)}, f32[3,3,24,128]{3,2,1,0:T(8,128)S(1)}, u32[]{:S(2)}, u32[]{:S(2)}) collective-permute-start(f32[3,3,24,128]{3,2,1,0:T(8,128)S(1)} %copy-done.9), channel_id=1, source_target_pairs={{0,0},{1,16},{2,32},{3,48},{4,64},{5,80},{6,96},{7,112},{8,8},{9,2... | collective-permute-start | bytes 331784 | tf_op jit(solution)/shard_map/ppermute | solution.py:347
  19.0 8.3 %all-to-all-done.refs_1_ = bf16[16,272,128]{2,1,0:T(8,128)(2,1)S(1)} async-done(((bf16[16,272,128]{2,1,0:T(8,128)(2,1)}), bf16[16,272,128]{2,1,0:T(8,128)(2,1)S(1)}, u32[]{:S(2)}, u32[]{:S(2)}) %all-to-all-start) | async-done | bytes 1114144 | tf_op jit(solution)/shard_map/all_to_all | solution.py:351
  29.2 5.9 %collective-permute-done.1.refs_0_.refs_1_ = f32[3,3,24,128]{3,2,1,0:T(8,128)S(1)} collective-permute-done((f32[3,3,24,128]{3,2,1,0:T(8,128)S(1)}, f32[3,3,24,128]{3,2,1,0:T(8,128)S(1)}, u32[]{:S(2)}, u32[]{:S(2)}) %collective-permute-start.1) | collective-permute-done | bytes 110624 | tf_op jit(solution)/shard_map/ppermute | solution.py:347
  36.2 10.6 %all-to-all-start.1 = ((bf16[16,72,128]{2,1,0:T(8,128)(2,1)}), bf16[16,72,128]{2,1,0:T(8,128)(2,1)S(1)}, u32[]{:S(2)}, u32[]{:S(2)}) async-start(bf16[16,72,128]{2,1,0:T(8,128)(2,1)} %bitcast.7), calls=%async_computation.1 | async-start | bytes 589824 | tf_op jit(solution)/shard_map/all_to_all | solution.py:350
  49.3 4.2 %shard_map.120 = (bf16[512,1024]{1,0:T(8,128)(2,1)}, bf16[512,1024]{1,0:T(8,128)(2,1)}, f32[8,1024]{1,0:T(8,128)}) custom-call(s32[6]{0:T(128)} %stack.27.refs_0_, bf16[16,272,128]{2,1,0:T(8,128)(2,1)} %copy-done.5, bf16[16,272,128]{2,1,0:T(8,128)(2,1)} %copy-done.7, f32[144,128]{1,0:T(8,128)} %broadcast_in_dim.9.refs_3_.refs_6_), custom_call_target="tpu_custom_call" | custom-call | tf_op jit(solution)/shard_map/pallas_call | solution.py:304
  53.5 14.1 %all-to-all-done.1 = bf16[16,72,128]{2,1,0:T(8,128)(2,1)S(1)} async-done(((bf16[16,72,128]{2,1,0:T(8,128)(2,1)}), bf16[16,72,128]{2,1,0:T(8,128)(2,1)S(1)}, u32[]{:S(2)}, u32[]{:S(2)}) %all-to-all-start.1) | async-done | bytes 294944 | tf_op jit(solution)/shard_map/all_to_all | solution.py:350
  68.4 4.9 %shard_map.122 = (bf16[4,144,128]{2,1,0:T(8,128)(2,1)}, f32[64,1,128]{2,1,0:T(1,128)}, f32[16,128,128]{2,1,0:T(8,128)}, f32[16,128,128]{2,1,0:T(8,128)}) custom-call(s32[6]{0:T(128)} %stack.27.refs_0_, bf16[512,1024]{1,0:T(8,128)(2,1)} %get-tuple-element.27.refs_1_, bf16[512,1024]{1,0:T(8,128)(2,1)} %get-tuple-element.28.refs_2_, bf16[1152,128]{1,0:T(8,128)(2,1)} %bitcast.28), custom_call_target="tpu_custom_call" | custom-call | tf_op jit(solution)/shard_map/pallas_call | solution.py:304
  75.2 8.2 %all-to-all-start.2 = ((f32[64,1,128]{2,1,0:T(1,128)}), f32[64,1,128]{2,1,0:T(1,128)S(1)}, u32[]{:S(2)}, u32[]{:S(2)}) async-start(f32[64,1,128]{2,1,0:T(1,128)} %get-tuple-element.31), calls=%async_computation.2 | async-start | bytes 65536 | tf_op jit(solution)/shard_map/all_to_all | solution.py:383
  86.3 9.5 %all-to-all-done.2.refs_4_ = f32[64,1,128]{2,1,0:T(1,128)S(1)} async-done(((f32[64,1,128]{2,1,0:T(1,128)}), f32[64,1,128]{2,1,0:T(1,128)S(1)}, u32[]{:S(2)}, u32[]{:S(2)}) %all-to-all-start.2) | async-done | bytes 32800 | tf_op jit(solution)/shard_map/all_to_all | solution.py:383
  96.5 4.9 %shard_map.124 = bf16[1152,128]{1,0:T(8,128)(2,1)} custom-call(s32[6]{0:T(128)} %stack.27.refs_0_, bf16[512,1024]{1,0:T(8,128)(2,1)} %get-tuple-element.27.refs_1_, bf16[512,1024]{1,0:T(8,128)(2,1)} %get-tuple-element.28.refs_2_, bf16[4,144,128]{2,1,0:T(8,128)(2,1)} %get-tuple-element.30.refs_3_, f32[64,1,128]{2,1,0:T(1,128)} %copy-done.8, s32[3,24]{1,0:T(4,128)} %refs_5_.3, ...), custom_call_target="tpu_custom_call" | custom-call | tf_op jit(solution)/shard_map/pallas_call | solution.py:304
  101.4 3.7 %all-to-all-start.3 = ((bf16[16,72,128]{2,1,0:T(8,128)(2,1)}), bf16[16,72,128]{2,1,0:T(8,128)(2,1)S(1)}, u32[]{:S(2)}, u32[]{:S(2)}) async-start(bf16[16,72,128]{2,1,0:T(8,128)(2,1)} %bitcast.29), calls=%async_computation.3 | async-start | bytes 589824 | tf_op jit(solution)/shard_map/all_to_all | solution.py:398
  107.5 4.6 %collective-permute-start.4 = (f32[4,128,128]{2,1,0:T(8,128)S(1)}, f32[4,128,128]{2,1,0:T(8,128)S(1)}, u32[]{:S(2)}, u32[]{:S(2)}) collective-permute-start(f32[4,128,128]{2,1,0:T(8,128)S(1)} %get-tuple-element.37), channel_id=1, source_target_pairs={{0,256},{128,384},{256,0},{384,128},{1,257},{129,385},{257,1},{385... | collective-permute-start | bytes 786440 | tf_op jit(solution)/shard_map/ppermute | solution.py:319
  112.1 5.3 %collective-permute-done.3.refs_2_ = f32[4,128,128]{2,1,0:T(8,128)S(1)} collective-permute-done((f32[4,128,128]{2,1,0:T(8,128)S(1)}, f32[4,128,128]{2,1,0:T(8,128)S(1)}, u32[]{:S(2)}, u32[]{:S(2)}) %collective-permute-start.3) | collective-permute-done | bytes 262176 | tf_op jit(solution)/shard_map/ppermute | solution.py:319
  117.5 4.0 %collective-permute-done.4.refs_3_ = f32[4,128,128]{2,1,0:T(8,128)S(1)} collective-permute-done((f32[4,128,128]{2,1,0:T(8,128)S(1)}, f32[4,128,128]{2,1,0:T(8,128)S(1)}, u32[]{:S(2)}, u32[]{:S(2)}) %collective-permute-start.4) | collective-permute-done | bytes 262176 | tf_op jit(solution)/shard_map/ppermute | solution.py:319
  121.4 2.9 %all-to-all-done.3 = bf16[16,72,128]{2,1,0:T(8,128)(2,1)S(1)} async-done(((bf16[16,72,128]{2,1,0:T(8,128)(2,1)}), bf16[16,72,128]{2,1,0:T(8,128)(2,1)S(1)}, u32[]{:S(2)}, u32[]{:S(2)}) %all-to-all-start.3) | async-done | bytes 294944 | tf_op jit(solution)/shard_map/all_to_all | solution.py:398
  125.6 8.8 %all-to-all-start.4 = ((bf16[16,72,128]{2,1,0:T(8,128)(2,1)}), bf16[16,72,128]{2,1,0:T(8,128)(2,1)S(1)}, u32[]{:S(2)}, u32[]{:S(2)}) async-start(bf16[16,72,128]{2,1,0:T(8,128)(2,1)} %bitcast.11), calls=%async_computation.4 | async-start | bytes 589824 | tf_op jit(solution)/shard_map/all_to_all | solution.py:410
  136.3 6.3 %collective-permute-done.5.refs_4_ = f32[4,128,128]{2,1,0:T(8,128)S(1)} collective-permute-done((f32[4,128,128]{2,1,0:T(8,128)S(1)}, f32[4,128,128]{2,1,0:T(8,128)S(1)}, u32[]{:S(2)}, u32[]{:S(2)}) %collective-permute-start.5) | collective-permute-done | bytes 262176 | tf_op jit(solution)/shard_map/ppermute | solution.py:319
  143.8 3.1 %collective-permute-start.6 = (f32[128,128]{1,0:T(8,128)S(1)}, f32[128,128]{1,0:T(8,128)S(1)}, u32[]{:S(2)}, u32[]{:S(2)}) collective-permute-start(f32[128,128]{1,0:T(8,128)S(1)} %get-tuple-element.41), channel_id=1, source_target_pairs={{0,2},{2,4},{4,6},{6,0},{1,3},{3,5},{5,7},{7,1},{8,10},{10,12},{12... | collective-permute-start | bytes 196616 | tf_op jit(solution)/shard_map/ppermute | solution.py:319
  146.8 4.9 %collective-permute-start.7 = (f32[128,128]{1,0:T(8,128)S(1)}, f32[128,128]{1,0:T(8,128)S(1)}, u32[]{:S(2)}, u32[]{:S(2)}) collective-permute-start(f32[128,128]{1,0:T(8,128)S(1)} %get-tuple-element.42), channel_id=1, source_target_pairs={{0,4},{2,6},{4,0},{6,2},{1,5},{3,7},{5,1},{7,3},{8,12},{10,14},{12... | collective-permute-start | bytes 196616 | tf_op jit(solution)/shard_map/ppermute | solution.py:319
  154.6 3.3 %collective-permute-done.8.left_ref = f32[128,128]{1,0:T(8,128)S(1)} collective-permute-done((f32[128,128]{1,0:T(8,128)S(1)}, f32[128,128]{1,0:T(8,128)S(1)}, u32[]{:S(2)}, u32[]{:S(2)}) %collective-permute-start.8) | collective-permute-done | bytes 65568 | tf_op jit(solution)/shard_map/ppermute | solution.py:319
  159.6 5.3 %all-to-all-start.5 = ((bf16[32,144,128]{2,1,0:T(8,128)(2,1)}), bf16[32,144,128]{2,1,0:T(8,128)(2,1)S(1)}, u32[]{:S(2)}, u32[]{:S(2)}) async-start(bf16[32,144,128]{2,1,0:T(8,128)(2,1)} %bitcast.16), calls=%async_computation.5 | async-start | bytes 2359296 | tf_op jit(solution)/shard_map/all_to_all | solution.py:422
  164.9 7.1 %collective-permute-start.9 = (f32[3,3,24,128]{3,2,1,0:T(8,128)S(1)}, f32[3,3,24,128]{3,2,1,0:T(8,128)S(1)}, u32[]{:S(2)}, u32[]{:S(2)}) collective-permute-start(f32[3,3,24,128]{3,2,1,0:T(8,128)S(1)} %get-tuple-element.45), channel_id=1, source_target_pairs={{0,0},{1,16},{2,32},{3,48},{4,64},{5,80},{6,96},{7,112},{8,8},{9,2... | collective-permute-start | bytes 331784 | tf_op jit(solution)/shard_map/ppermute | solution.py:421
  172.0 16.9 %collective-permute-done.9 = f32[3,3,24,128]{3,2,1,0:T(8,128)S(1)} collective-permute-done((f32[3,3,24,128]{3,2,1,0:T(8,128)S(1)}, f32[3,3,24,128]{3,2,1,0:T(8,128)S(1)}, u32[]{:S(2)}, u32[]{:S(2)}) %collective-permute-start.9) | collective-permute-done | bytes 110624 | tf_op jit(solution)/shard_map/ppermute | solution.py:421
  (43 shorter events, 26.6 us)
Async XLA Ops:
  2.7 9.6 %copy-start.9 = (f32[3,3,24,128]{3,2,1,0:T(8,128)S(1)}, f32[3,3,24,128]{3,2,1,0:T(8,128)}, u32[]{:S(2)}) copy-start(f32[3,3,24,128]{3,2,1,0:T(8,128)} %get-tuple-element.29) | copy-start | bytes 331780
  2.7 24.6 %all-to-all-start = ((bf16[16,272,128]{2,1,0:T(8,128)(2,1)}), bf16[16,272,128]{2,1,0:T(8,128)(2,1)S(1)}, u32[]{:S(2)}, u32[]{:S(2)}) async-start(bf16[16,272,128]{2,1,0:T(8,128)(2,1)} %get-tuple-element.26), calls=%async_computation | async-start | bytes 2228224 | tf_op jit(solution)/shard_map/all_to_all | solution.py:351
  12.3 22.9 %collective-permute-start.1 = (f32[3,3,24,128]{3,2,1,0:T(8,128)S(1)}, f32[3,3,24,128]{3,2,1,0:T(8,128)S(1)}, u32[]{:S(2)}, u32[]{:S(2)}) collective-permute-start(f32[3,3,24,128]{3,2,1,0:T(8,128)S(1)} %copy-done.9), channel_id=1, source_target_pairs={{0,0},{1,16},{2,32},{3,48},{4,64},{5,80},{6,96},{7,112},{8,8},{9,2... | collective-permute-start | bytes 331784 | tf_op jit(solution)/shard_map/ppermute | solution.py:347
  27.3 21.8 %copy-start.5 = (bf16[16,272,128]{2,1,0:T(8,128)(2,1)}, bf16[16,272,128]{2,1,0:T(8,128)(2,1)S(1)}, u32[]{:S(2)}) copy-start(bf16[16,272,128]{2,1,0:T(8,128)(2,1)S(1)} %all-to-all-done.refs_1_) | copy-start | bytes 3342340
  27.3 20.9 %collective-permute-start = (bf16[16,272,128]{2,1,0:T(8,128)(2,1)S(1)}, bf16[16,272,128]{2,1,0:T(8,128)(2,1)S(1)}, u32[]{:S(2)}, u32[]{:S(2)}) collective-permute-start(bf16[16,272,128]{2,1,0:T(8,128)(2,1)S(1)} %all-to-all-done.refs_1_), channel_id=1, source_target_pairs={{0,1},{1,0},{2,3},{3,2},{4,5},{5,4},{6,7},{7,6},{8,9},{9,8},{10,11... | collective-permute-start | bytes 3342344 | tf_op jit(solution)/shard_map/ppermute | solution.py:352
  36.2 31.5 %all-to-all-start.1 = ((bf16[16,72,128]{2,1,0:T(8,128)(2,1)}), bf16[16,72,128]{2,1,0:T(8,128)(2,1)S(1)}, u32[]{:S(2)}, u32[]{:S(2)}) async-start(bf16[16,72,128]{2,1,0:T(8,128)(2,1)} %bitcast.7), calls=%async_computation.1 | async-start | bytes 589824 | tf_op jit(solution)/shard_map/all_to_all | solution.py:350
  48.2 1.0 copy-start.7
  67.7 0.7 copy-start.6
  68.4 15.1 %copy-start.3 = (s32[6]{0:T(128)S(1)}, s32[6]{0:T(128)}, u32[]{:S(2)}) copy-start(s32[6]{0:T(128)} %stack.27.refs_0_) | copy-start | bytes 76
  73.3 10.2 %collective-permute-start.2 = (f32[16,128,128]{2,1,0:T(8,128)}, f32[16,128,128]{2,1,0:T(8,128)S(1)}, u32[]{:S(2)}, u32[]{:S(2)}) collective-permute-start(f32[16,128,128]{2,1,0:T(8,128)} %get-tuple-element.34), channel_id=1, source_target_pairs={{0,1},{1,0},{2,3},{3,2},{4,5},{5,4},{6,7},{7,6},{8,9},{9,8},{10,11... | collective-permute-start | bytes 3145736 | tf_op jit(solution)/shard_map/ppermute | solution.py:384
  75.2 20.6 %all-to-all-start.2 = ((f32[64,1,128]{2,1,0:T(1,128)}), f32[64,1,128]{2,1,0:T(1,128)S(1)}, u32[]{:S(2)}, u32[]{:S(2)}) async-start(f32[64,1,128]{2,1,0:T(1,128)} %get-tuple-element.31), calls=%async_computation.2 | async-start | bytes 65536 | tf_op jit(solution)/shard_map/all_to_all | solution.py:383
  83.5 1.2 copy-start
  101.4 41.3 %copy-start.2 = (f32[4,128,128]{2,1,0:T(8,128)S(1)}, f32[4,128,128]{2,1,0:T(8,128)}, u32[]{:S(2)}) copy-start(f32[4,128,128]{2,1,0:T(8,128)} %copy-done.1) | copy-start | bytes 786436
  101.4 41.2 %copy-start.4 = (s32[6]{0:T(128)S(1)}, s32[6]{0:T(128)}, u32[]{:S(2)}) copy-start(s32[6]{0:T(128)} %stack.27.refs_0_) | copy-start | bytes 76
  101.4 22.9 %all-to-all-start.3 = ((bf16[16,72,128]{2,1,0:T(8,128)(2,1)}), bf16[16,72,128]{2,1,0:T(8,128)(2,1)S(1)}, u32[]{:S(2)}, u32[]{:S(2)}) async-start(bf16[16,72,128]{2,1,0:T(8,128)(2,1)} %bitcast.29), calls=%async_computation.3 | async-start | bytes 589824 | tf_op jit(solution)/shard_map/all_to_all | solution.py:398
  105.1 12.4 %collective-permute-start.3 = (f32[4,128,128]{2,1,0:T(8,128)S(1)}, f32[4,128,128]{2,1,0:T(8,128)S(1)}, u32[]{:S(2)}, u32[]{:S(2)}) collective-permute-start(f32[4,128,128]{2,1,0:T(8,128)S(1)} %get-tuple-element.36), channel_id=1, source_target_pairs={{0,128},{128,256},{256,384},{384,0},{1,129},{129,257},{257,385},{3... | collective-permute-start | bytes 786440 | tf_op jit(solution)/shard_map/ppermute | solution.py:319
  107.5 13.9 %collective-permute-start.4 = (f32[4,128,128]{2,1,0:T(8,128)S(1)}, f32[4,128,128]{2,1,0:T(8,128)S(1)}, u32[]{:S(2)}, u32[]{:S(2)}) collective-permute-start(f32[4,128,128]{2,1,0:T(8,128)S(1)} %get-tuple-element.37), channel_id=1, source_target_pairs={{0,256},{128,384},{256,0},{384,128},{1,257},{129,385},{257,1},{385... | collective-permute-start | bytes 786440 | tf_op jit(solution)/shard_map/ppermute | solution.py:319
  125.6 32.3 %all-to-all-start.4 = ((bf16[16,72,128]{2,1,0:T(8,128)(2,1)}), bf16[16,72,128]{2,1,0:T(8,128)(2,1)S(1)}, u32[]{:S(2)}, u32[]{:S(2)}) async-start(bf16[16,72,128]{2,1,0:T(8,128)(2,1)} %bitcast.11), calls=%async_computation.4 | async-start | bytes 589824 | tf_op jit(solution)/shard_map/all_to_all | solution.py:410
  134.4 8.3 %collective-permute-start.5 = (f32[4,128,128]{2,1,0:T(8,128)S(1)}, f32[4,128,128]{2,1,0:T(8,128)S(1)}, u32[]{:S(2)}, u32[]{:S(2)}) collective-permute-start(f32[4,128,128]{2,1,0:T(8,128)S(1)} %get-tuple-element.39), channel_id=1, source_target_pairs={{0,384},{128,0},{256,128},{384,256},{1,385},{129,1},{257,129},{385... | collective-permute-start | bytes 786440 | tf_op jit(solution)/shard_map/ppermute | solution.py:319
  143.8 9.9 %collective-permute-start.6 = (f32[128,128]{1,0:T(8,128)S(1)}, f32[128,128]{1,0:T(8,128)S(1)}, u32[]{:S(2)}, u32[]{:S(2)}) collective-permute-start(f32[128,128]{1,0:T(8,128)S(1)} %get-tuple-element.41), channel_id=1, source_target_pairs={{0,2},{2,4},{4,6},{6,0},{1,3},{3,5},{5,7},{7,1},{8,10},{10,12},{12... | collective-permute-start | bytes 196616 | tf_op jit(solution)/shard_map/ppermute | solution.py:319
  146.8 7.8 %collective-permute-start.7 = (f32[128,128]{1,0:T(8,128)S(1)}, f32[128,128]{1,0:T(8,128)S(1)}, u32[]{:S(2)}, u32[]{:S(2)}) collective-permute-start(f32[128,128]{1,0:T(8,128)S(1)} %get-tuple-element.42), channel_id=1, source_target_pairs={{0,4},{2,6},{4,0},{6,2},{1,5},{3,7},{5,1},{7,3},{8,12},{10,14},{12... | collective-permute-start | bytes 196616 | tf_op jit(solution)/shard_map/ppermute | solution.py:319
  151.8 6.2 %collective-permute-start.8 = (f32[128,128]{1,0:T(8,128)S(1)}, f32[128,128]{1,0:T(8,128)S(1)}, u32[]{:S(2)}, u32[]{:S(2)}) collective-permute-start(f32[128,128]{1,0:T(8,128)S(1)} %get-tuple-element.43), channel_id=1, source_target_pairs={{0,6},{2,0},{4,2},{6,4},{1,7},{3,1},{5,3},{7,5},{8,14},{10,8},{12,... | collective-permute-start | bytes 196616 | tf_op jit(solution)/shard_map/ppermute | solution.py:319
  159.6 30.0 %all-to-all-start.5 = ((bf16[32,144,128]{2,1,0:T(8,128)(2,1)}), bf16[32,144,128]{2,1,0:T(8,128)(2,1)S(1)}, u32[]{:S(2)}, u32[]{:S(2)}) async-start(bf16[32,144,128]{2,1,0:T(8,128)(2,1)} %bitcast.16), calls=%async_computation.5 | async-start | bytes 2359296 | tf_op jit(solution)/shard_map/all_to_all | solution.py:422
  164.9 24.1 %collective-permute-start.9 = (f32[3,3,24,128]{3,2,1,0:T(8,128)S(1)}, f32[3,3,24,128]{3,2,1,0:T(8,128)S(1)}, u32[]{:S(2)}, u32[]{:S(2)}) collective-permute-start(f32[3,3,24,128]{3,2,1,0:T(8,128)S(1)} %get-tuple-element.45), channel_id=1, source_target_pairs={{0,0},{1,16},{2,32},{3,48},{4,64},{5,80},{6,96},{7,112},{8,8},{9,2... | collective-permute-start | bytes 331784 | tf_op jit(solution)/shard_map/ppermute | solution.py:421
  (2 other events, 1.3 us)
